TPU v7x, 32 devices: a whole 2x2x4 slice. The times are simulated.
32 devices in a mesh: dp: 16 (over z, x, core), fsdp: 2 (over y).
Axes of the slice: x: 2, y: 2, z: 4, core: 2. Of those that a mesh axis runs over, the one named last changes fastest.
Arguments:
- image_maps: bfloat16 [64, 8, 8, 3072], P(('dp', 'fsdp')), may hold values from -6 to 6
- dw_kernel: bfloat16 [49, 3072], P(None, 'fsdp'), may hold values from -0.5 to 0.55
- channel_terms: bfloat16 [4, 3072], P(None, 'fsdp'), may hold values from 0.099609375 to 1.8984375
- head_weight: bfloat16 [3072, 1152], P('fsdp'), may hold values from -0.5 to 0.5
- text_feats: bfloat16 [64, 1152], P(('dp', 'fsdp')), may hold values from -6 to 6
Outputs:
- image_grads: bfloat16 [64, 8, 8, 3072], P(('dp', 'fsdp'))
- kernel_grads: float32 [49, 3072], P(None, 'fsdp')
- term_grads: float32 [4, 3072], P(None, 'fsdp')
- head_grads: float32 [3072, 1152], P('fsdp')
- text_grads: float32 [64, 1152], P(('dp', 'fsdp'))
All inputs are finite; a program needn't handle non-finite values.
Results may differ from a plain program's by a relative error of at most 0.017.
Values may be sent and summed in bfloat16 or wider, within the bound.
No kernel may reach another device: no remote copies, remote signals or barrier semaphores. Data moves between devices by JAX's collectives and lax.ppermute only.
A program may use at most 192 MiB of HBM per device.

v0:
```python
import jax
import jax.numpy as jnp
from jax import lax
from jax.sharding import PartitionSpec as P

EPS = 1e-06
LOGIT_SCALE = 10.0
LOGIT_BIAS = -2.0


def shifted(value, axis, steps):
    count = lax.axis_size(axis)
    pairs = [(source, (source + steps) % count) for source in range(count)]
    return lax.ppermute(value, axis, pairs)


def depthwise(inputs, kernel):
    ker_side = 7
    reach = ker_side // 2
    height = inputs.shape[1]
    width = inputs.shape[2]
    padded = jnp.pad(inputs, ((0, 0), (reach, reach), (reach, reach), (0, 0)))
    mixed = jnp.zeros_like(inputs)
    for row_tap in range(ker_side):
        for col_tap in range(ker_side):
            mixed = (
                mixed
                + padded[:, row_tap : row_tap + height, col_tap : col_tap + width, :]
                * kernel[row_tap * ker_side + col_tap]
            )
    return mixed


def block_pool(inputs, kernel, conv_bias, norm_gain, layer_scale):
    mixed = depthwise(inputs, kernel) + conv_bias
    row_mean = jnp.mean(mixed, axis=3, keepdims=True)
    centered = mixed - row_mean
    row_var = jnp.mean(centered * centered, axis=3, keepdims=True)
    output = inputs + layer_scale * (centered * lax.rsqrt(row_var + EPS) * norm_gain)
    return jnp.mean(output, axis=(1, 2))


def head_norm(pooled, head_gain):
    row_mean = jnp.mean(pooled, axis=1, keepdims=True)
    centered = pooled - row_mean
    row_var = jnp.mean(centered * centered, axis=1, keepdims=True)
    return centered * lax.rsqrt(row_var + EPS) * head_gain


def to_unit(vectors):
    return vectors * lax.rsqrt(jnp.sum(vectors * vectors, axis=1, keepdims=True) + EPS)


def pair_terms(unit_bf, text_piece, anchor, cycle_home, first_col):
    logits = (
        LOGIT_SCALE
        * lax.dot_general(
            unit_bf, text_piece, (((1,), (1,)), ((), ())), preferred_element_type=jnp.float32
        )
        + LOGIT_BIAS
    )
    rows_here = lax.broadcasted_iota(jnp.int32, logits.shape, 0)
    cols_here = lax.broadcasted_iota(jnp.int32, logits.shape, 1)
    positive = jnp.where(
        (anchor == cycle_home) & (cols_here == rows_here + first_col), 1.0, 0.0
    ).astype(jnp.float32)
    weights = (jax.nn.sigmoid(logits) - positive).astype(jnp.bfloat16)
    unit_part = LOGIT_SCALE * jnp.dot(weights, text_piece, preferred_element_type=jnp.float32)
    text_part = LOGIT_SCALE * lax.dot_general(
        weights, unit_bf, (((0,), (0,)), ((), ())), preferred_element_type=jnp.float32
    )
    return (unit_part, text_part)


def per_device(image_maps, dw_kernel, channel_terms, head_weight, text_feats):
    images_here = image_maps.shape[0]
    embed_width = text_feats.shape[1]
    cycle_size = lax.axis_size("dp")
    cycle_home = lax.axis_index("dp")
    member = lax.axis_index("fsdp")
    kernel_all, terms_raw = (
        lax.all_gather(dw_kernel, "fsdp", axis=1, tiled=True),
        lax.all_gather(channel_terms, "fsdp", axis=1, tiled=True),
    )
    kernel = kernel_all.astype(jnp.float32)
    terms_all = terms_raw.astype(jnp.float32)
    inputs = image_maps.astype(jnp.float32)
    pooled, block_back = jax.vjp(
        block_pool, inputs, kernel, terms_all[0], terms_all[1], terms_all[2]
    )
    normed, head_back = jax.vjp(head_norm, pooled, terms_all[3])
    pooled_bf = normed.astype(jnp.bfloat16)
    head_all = lax.all_gather(head_weight, "fsdp", axis=0, tiled=True)
    embed = jnp.dot(pooled_bf, head_all, preferred_element_type=jnp.float32)
    unit_vec, unit_back = jax.vjp(to_unit, embed)
    unit_bf = unit_vec.astype(jnp.bfloat16)
    text_unit, text_back = jax.vjp(to_unit, text_feats.astype(jnp.float32))
    own_text = text_unit.astype(jnp.bfloat16)
    first_col = member * images_here
    zero_unit = jnp.zeros((images_here, embed_width), jnp.float32)
    text_block = lax.all_gather(own_text, "fsdp", axis=0, tiled=True)
    block_rows = text_block.shape[0]

    def turn(turn_index, state_tuple):
        text_piece, grad_accum, unit_sum = state_tuple
        moved = shifted(text_piece, "dp", 1)
        anchor = (cycle_home - turn_index) % cycle_size
        unit_part, text_part = pair_terms(unit_bf, text_piece, anchor, cycle_home, first_col)
        grad_accum = shifted((grad_accum + text_part).astype(jnp.bfloat16), "dp", 1).astype(
            jnp.float32
        )
        return (moved, grad_accum, unit_sum + unit_part)

    start_state = (text_block, jnp.zeros((block_rows, embed_width), jnp.float32), zero_unit)
    text_piece, grad_accum, unit_sum = lax.fori_loop(0, cycle_size - 1, turn, start_state)
    anchor = (cycle_home - (cycle_size - 1)) % cycle_size
    unit_part, text_part = pair_terms(unit_bf, text_piece, anchor, cycle_home, first_col)
    text_accum = shifted((grad_accum + text_part).astype(jnp.bfloat16), "dp", 1).astype(jnp.float32)
    unit_sum = unit_sum + unit_part
    mine_text = lax.psum_scatter(
        text_accum.astype(jnp.bfloat16), "fsdp", scatter_dimension=0, tiled=True
    ).astype(jnp.float32)
    text_grads = text_back(mine_text)[0]
    embed_grad = unit_back(unit_sum)[0].astype(jnp.bfloat16)
    pooled_grad = lax.dot_general(
        embed_grad, head_all, (((1,), (1,)), ((), ())), preferred_element_type=jnp.float32
    )
    head_part = lax.psum_scatter(
        lax.dot_general(
            pooled_bf, embed_grad, (((0,), (0,)), ((), ())), preferred_element_type=jnp.float32
        ).astype(jnp.bfloat16),
        "fsdp",
        scatter_dimension=0,
        tiled=True,
    )
    pool_grad, gain_grad = head_back(pooled_grad)
    image_grad, kernel_grad, bias_grad, norm_grad, scale_grad = block_back(pool_grad)
    channel_grad = jnp.stack([bias_grad, norm_grad, scale_grad, gain_grad])
    kernel_part, terms_part = (
        lax.psum_scatter(
            kernel_grad.astype(jnp.bfloat16), "fsdp", scatter_dimension=1, tiled=True
        ).astype(jnp.float32),
        lax.psum_scatter(
            channel_grad.astype(jnp.bfloat16), "fsdp", scatter_dimension=1, tiled=True
        ).astype(jnp.float32),
    )
    head_grads, kernel_grads, term_grads = (
        lax.psum(head_part, "dp").astype(jnp.float32),
        lax.psum(kernel_part.astype(jnp.bfloat16), "dp").astype(jnp.float32),
        lax.psum(terms_part.astype(jnp.bfloat16), "dp").astype(jnp.float32),
    )
    return (image_grad.astype(jnp.bfloat16), kernel_grads, term_grads, head_grads, text_grads)


def solution(mesh):
    in_specs = (
        P(("dp", "fsdp"), None, None, None),
        P(None, "fsdp"),
        P(None, "fsdp"),
        P("fsdp", None),
        P(("dp", "fsdp"), None),
    )
    out_specs = (
        P(("dp", "fsdp"), None, None, None),
        P(None, "fsdp"),
        P(None, "fsdp"),
        P("fsdp", None),
        P(("dp", "fsdp"), None),
    )
    return jax.shard_map(
        per_device, mesh=mesh, in_specs=in_specs, out_specs=out_specs, check_vma=False
    )
```

profile of v0, /device:TPU:0, one launch (start us, length us, event | category | flops | bytes accessed | tf_op | source)
XLA Modules:
  0.0 466.3 jit_solution(9153076778696779375)
XLA Ops:
  7.2 0.7 all-gather.3.cloned.1.call-update
  8.8 0.7 copy-done.78
  10.1 5.2 %all-gather = bf16[2,2,1152]{2,1,0:T(2,128)(2,1)S(1)} all-gather(bf16[1,2,1152]{2,1,0:T(2,128)(2,1)S(1)} %fusion.33), channel_id=1, replica_groups=mesh['dp'=16,'fsdp'=2] {'fsdp'}, dimensions={0}, use_global_device_ids=true | all-gather | bytes 13824 | tf_op jit(solution)/shard_map/all_gather | solution.py:101
  15.4 4.4 all_gather.13
  19.8 9.1 %all_gather.14 = bf16[49,3072]{1,0:T(8,128)(2,1)S(1)} all-gather(bf16[49,1536]{1,0:T(8,128)(2,1)S(1)} %copy-done.6), channel_id=1, replica_groups=mesh['dp'=16,'fsdp'=2] {'fsdp'}, dimensions={1}, use_global_device_ids=true | all-gather | bytes 451584 | tf_op jit(solution)/shard_map/all_gather | solution.py:82
  30.2 14.5 %fusion.42 = (f32[2,8,8]{2,1,0:T(8,128)S(1)}, f32[2,8,8,3072]{3,2,1,0:T(8,128)S(1)}) fusion(f32[3072]{0:T(1024)S(1)} %bitcast.245, f32[3072]{0:T(1024)S(1)} %bitcast.149, f32[3072]{0:T(1024)S(1)} %bitcast.147, f32[3072]{0:T(1024)S(1)} %bitcast.167, f32[3072]{0:T(1024)S(1)} %bitcast.165, f32[3072]{0:T(1024)S(1)} %bitcast.163, f32[3072]{0:T(1024)S(1)} %bitcast.161, ...), kind=kLoop, calls=%fused_computation.242 | loop fusion | flops 39321472 | bytes 4547072 | tf_op jit(solution)/shard_map/jvp()/reduce_sum | solution.py:36
  45.2 0.8 copy-done.3
  46.9 55.1 %all-gather.3.cloned.1.call-done = bf16[3072,1152]{1,0:T(8,128)(2,1)} async-done(((bf16[1536,1152]{1,0:T(8,128)(2,1)}), bf16[3072,1152]{1,0:T(8,128)(2,1)}) %all-gather.3.cloned.1.call-update) | async-done | bytes 7077904 | tf_op jit(solution)/shard_map/all_gather | solution.py:93
  102.0 4.2 multiply_reduce_fusion.56
  106.3 95.1 %while.20 = (s32[]{:T(128)}, bf16[4,1152]{1,0:T(4,128)(2,1)S(1)}, f32[4,1152]{1,0:T(4,128)S(1)}, f32[2,1152]{1,0:T(2,128)S(1)}, bf16[2,1152]{1,0:T(2,128)(2,1)S(...) while((s32[]{:T(128)}, bf16[4,1152]{1,0:T(4,128)(2,1)S(1)}, ...), condition=%wide.region_8.9_spmd.clone, body=%wide.region_7.8_spmd.clone.sunk | while | flops 85346 | bytes 193935 | solution.py:115
  106.8 2.1 collective-permute-start.1
  109.0 3.8 collective-permute-done.1
  113.5 5.6 %collective-permute-done.1 = bf16[4,1152]{1,0:T(4,128)(2,1)S(1)} collective-permute-done((bf16[4,1152]{1,0:T(4,128)(2,1)S(1)}, bf16[4,1152]{1,0:T(4,128)(2,1)S(1)}, u32[]{:S(2)}, u32[]{:S(2)}) %collective-permute-start.1) | collective-permute-done | bytes 9248 | tf_op jit(solution)/shard_map/while/body/eval_jaxpr/ppermute | solution.py:14
  119.8 5.6 %collective-permute-done.1 = bf16[4,1152]{1,0:T(4,128)(2,1)S(1)} collective-permute-done((bf16[4,1152]{1,0:T(4,128)(2,1)S(1)}, bf16[4,1152]{1,0:T(4,128)(2,1)S(1)}, u32[]{:S(2)}, u32[]{:S(2)}) %collective-permute-start.1) | collective-permute-done | bytes 9248 | tf_op jit(solution)/shard_map/while/body/eval_jaxpr/ppermute | solution.py:14
  126.2 5.6 %collective-permute-done.1 = bf16[4,1152]{1,0:T(4,128)(2,1)S(1)} collective-permute-done((bf16[4,1152]{1,0:T(4,128)(2,1)S(1)}, bf16[4,1152]{1,0:T(4,128)(2,1)S(1)}, u32[]{:S(2)}, u32[]{:S(2)}) %collective-permute-start.1) | collective-permute-done | bytes 9248 | tf_op jit(solution)/shard_map/while/body/eval_jaxpr/ppermute | solution.py:14
  132.5 5.6 %collective-permute-done.1 = bf16[4,1152]{1,0:T(4,128)(2,1)S(1)} collective-permute-done((bf16[4,1152]{1,0:T(4,128)(2,1)S(1)}, bf16[4,1152]{1,0:T(4,128)(2,1)S(1)}, u32[]{:S(2)}, u32[]{:S(2)}) %collective-permute-start.1) | collective-permute-done | bytes 9248 | tf_op jit(solution)/shard_map/while/body/eval_jaxpr/ppermute | solution.py:14
  138.8 5.6 %collective-permute-done.1 = bf16[4,1152]{1,0:T(4,128)(2,1)S(1)} collective-permute-done((bf16[4,1152]{1,0:T(4,128)(2,1)S(1)}, bf16[4,1152]{1,0:T(4,128)(2,1)S(1)}, u32[]{:S(2)}, u32[]{:S(2)}) %collective-permute-start.1) | collective-permute-done | bytes 9248 | tf_op jit(solution)/shard_map/while/body/eval_jaxpr/ppermute | solution.py:14
  145.1 5.6 %collective-permute-done.1 = bf16[4,1152]{1,0:T(4,128)(2,1)S(1)} collective-permute-done((bf16[4,1152]{1,0:T(4,128)(2,1)S(1)}, bf16[4,1152]{1,0:T(4,128)(2,1)S(1)}, u32[]{:S(2)}, u32[]{:S(2)}) %collective-permute-start.1) | collective-permute-done | bytes 9248 | tf_op jit(solution)/shard_map/while/body/eval_jaxpr/ppermute | solution.py:14
  151.5 5.6 %collective-permute-done.1 = bf16[4,1152]{1,0:T(4,128)(2,1)S(1)} collective-permute-done((bf16[4,1152]{1,0:T(4,128)(2,1)S(1)}, bf16[4,1152]{1,0:T(4,128)(2,1)S(1)}, u32[]{:S(2)}, u32[]{:S(2)}) %collective-permute-start.1) | collective-permute-done | bytes 9248 | tf_op jit(solution)/shard_map/while/body/eval_jaxpr/ppermute | solution.py:14
  157.8 5.6 %collective-permute-done.1 = bf16[4,1152]{1,0:T(4,128)(2,1)S(1)} collective-permute-done((bf16[4,1152]{1,0:T(4,128)(2,1)S(1)}, bf16[4,1152]{1,0:T(4,128)(2,1)S(1)}, u32[]{:S(2)}, u32[]{:S(2)}) %collective-permute-start.1) | collective-permute-done | bytes 9248 | tf_op jit(solution)/shard_map/while/body/eval_jaxpr/ppermute | solution.py:14
  164.1 5.6 %collective-permute-done.1 = bf16[4,1152]{1,0:T(4,128)(2,1)S(1)} collective-permute-done((bf16[4,1152]{1,0:T(4,128)(2,1)S(1)}, bf16[4,1152]{1,0:T(4,128)(2,1)S(1)}, u32[]{:S(2)}, u32[]{:S(2)}) %collective-permute-start.1) | collective-permute-done | bytes 9248 | tf_op jit(solution)/shard_map/while/body/eval_jaxpr/ppermute | solution.py:14
  170.4 5.6 %collective-permute-done.1 = bf16[4,1152]{1,0:T(4,128)(2,1)S(1)} collective-permute-done((bf16[4,1152]{1,0:T(4,128)(2,1)S(1)}, bf16[4,1152]{1,0:T(4,128)(2,1)S(1)}, u32[]{:S(2)}, u32[]{:S(2)}) %collective-permute-start.1) | collective-permute-done | bytes 9248 | tf_op jit(solution)/shard_map/while/body/eval_jaxpr/ppermute | solution.py:14
  176.8 5.6 %collective-permute-done.1 = bf16[4,1152]{1,0:T(4,128)(2,1)S(1)} collective-permute-done((bf16[4,1152]{1,0:T(4,128)(2,1)S(1)}, bf16[4,1152]{1,0:T(4,128)(2,1)S(1)}, u32[]{:S(2)}, u32[]{:S(2)}) %collective-permute-start.1) | collective-permute-done | bytes 9248 | tf_op jit(solution)/shard_map/while/body/eval_jaxpr/ppermute | solution.py:14
  183.1 5.6 %collective-permute-done.1 = bf16[4,1152]{1,0:T(4,128)(2,1)S(1)} collective-permute-done((bf16[4,1152]{1,0:T(4,128)(2,1)S(1)}, bf16[4,1152]{1,0:T(4,128)(2,1)S(1)}, u32[]{:S(2)}, u32[]{:S(2)}) %collective-permute-start.1) | collective-permute-done | bytes 9248 | tf_op jit(solution)/shard_map/while/body/eval_jaxpr/ppermute | solution.py:14
  189.4 5.6 %collective-permute-done.1 = bf16[4,1152]{1,0:T(4,128)(2,1)S(1)} collective-permute-done((bf16[4,1152]{1,0:T(4,128)(2,1)S(1)}, bf16[4,1152]{1,0:T(4,128)(2,1)S(1)}, u32[]{:S(2)}, u32[]{:S(2)}) %collective-permute-start.1) | collective-permute-done | bytes 9248 | tf_op jit(solution)/shard_map/while/body/eval_jaxpr/ppermute | solution.py:14
  195.7 5.6 %collective-permute-done.1 = bf16[4,1152]{1,0:T(4,128)(2,1)S(1)} collective-permute-done((bf16[4,1152]{1,0:T(4,128)(2,1)S(1)}, bf16[4,1152]{1,0:T(4,128)(2,1)S(1)}, u32[]{:S(2)}, u32[]{:S(2)}) %collective-permute-start.1) | collective-permute-done | bytes 9248 | tf_op jit(solution)/shard_map/while/body/eval_jaxpr/ppermute | solution.py:14
  202.6 5.6 %multiply_reduce_fusion.51 = (bf16[3072]{0:T(1024)(128)(2,1)}, f32[2]{0:T(128)S(1)}, f32[2,3072]{1,0:T(2,128)S(1)}) fusion(f32[2]{0:T(128)S(1)} %fusion.34, f32[2]{0:T(128)S(1)} %broadcast_multiply_fusion.50, f32[2,3072]{1,0:T(2,128)S(1)} %add_reduce_fusion, f32[3072]{0:T(1024)S(1)} %bitcast.135, bf16[3072,1152]{1,0:T(8,128)(2,1)} %all-gather.3.cloned.1.call-done, ...), kind=kOutput, calls=%fused_computation.200 | convolution fusion | flops 14213374 | bytes 7163944 | tf_op jit(solution)/shard_map/dot_general | solution.py:125
  208.9 1.5 fusion.16
  210.4 3.6 fusion.39
  214.1 3.3 multiply_reduce_fusion.49
  217.4 3.7 multiply_reduce_fusion.48
  221.1 2.2 add_convert_fusion
  223.6 5.1 %convolution_convert_fusion = bf16[3072,1152]{1,0:T(8,128)(2,1)} fusion(f32[2,1152]{1,0:T(2,128)S(1)} %get-tuple-element.402, f32[2,1152]{1,0:T(2,128)S(1)} %copy-done.60, f32[2]{0:T(128)S(1)} %copy-done.77, f32[2]{0:T(128)S(1)} %copy-done.73, f32[2]{0:T(128)S(1)} %copy-done.68, f32[3072]{0:T(1024)S(1)} %bitcast.137, f32[2,3072]{1,0:T(2,128)S(1)} %add_reduce_fusion, ...), kind=kOutput, calls=%fused_computation.63 | convolution fusion | flops 17736960 | bytes 7133216 | tf_op jit(solution)/shard_map/dot_general | solution.py:129
  230.8 1.2 copy.10
  232.2 7.0 %broadcast_multiply_fusion.2 = (f32[2,8,8,3072]{3,2,1,0:T(8,128)}, f32[2,8,8,3072]{3,2,1,0:T(8,128)}, f32[2,8,8,3072]{3,2,1,0:T(8,128)}, f32[2,8,8,3072]{3,2,1,0...) fusion(f32[2,8,8,3072]{3,2,1,0:T(8,128)S(1)} %get-tuple-element, ...), kind=kLoop, calls=%fused_computation.150 | loop fusion | flops 5111808 | bytes 22179840 | tf_op jit(solution)/shard_map/transpose(jvp())/mul | solution.py:28
  239.4 9.6 %broadcast_multiply_fusion = (f32[2,8,8,3072]{3,2,1,0:T(8,128)}, f32[2,8,8,3072]{3,2,1,0:T(8,128)S(1)}, f32[2,8,8,3072]{3,2,1,0:T(8,128)}, f32[2,8,8,3072]{3,2,1...) fusion(f32[2,8,8,3072]{3,2,1,0:T(8,128)S(1)} %get-tuple-element, ...), kind=kLoop, calls=%fused_computation.148 | loop fusion | flops 7077888 | bytes 30105600 | tf_op jit(solution)/shard_map/transpose(jvp())/mul | solution.py:28
  249.0 9.6 %broadcast_multiply_fusion.1 = (f32[2,8,8,3072]{3,2,1,0:T(8,128)}, f32[2,8,8,3072]{3,2,1,0:T(8,128)}, f32[2,8,8,3072]{3,2,1,0:T(8,128)}, f32[2,8,8,3072]{3,2,1,0...) fusion(f32[2,8,8,3072]{3,2,1,0:T(8,128)S(1)} %get-tuple-element, ...), kind=kLoop, calls=%fused_computation.149 | loop fusion | flops 7077888 | bytes 30105600 | tf_op jit(solution)/shard_map/transpose(jvp())/mul | solution.py:28
  259.0 62.8 %reduce-scatter.8.cloned.1.call-done = bf16[1536,1152]{1,0:T(8,128)(2,1)} async-done(((bf16[3072,1152]{1,0:T(8,128)(2,1)}), bf16[1536,1152]{1,0:T(8,128)(2,1)}) %reduce-scatter.8.cloned.1.call-update) | async-done | bytes 3538960 | tf_op jit(solution)/shard_map/reduce_scatter | solution.py:128
  321.9 28.7 %pad_add_fusion = f32[2,14,14,3072]{3,2,1,0:T(8,128)} fusion(f32[2,8,8,3072]{3,2,1,0:T(8,128)} %get-tuple-element.306, f32[2,8,8,3072]{3,2,1,0:T(8,128)} %get-tuple-element.307, f32[2,8,8,3072]{3,2,1,0:T(8,128)} %get-tuple-element.308, f32[2,8,8,3072]{3,2,1,0:T(8,128)} %get-tuple-element.309, f32[2,8,8,3072]{3,2,1,0:T(8,128)} %get-tuple-element.310, ...), kind=kLoop, calls=%fused_computation.64 | loop fusion | flops 50577408 | bytes 72450048 | tf_op jit(solution)/shard_map/transpose(jvp())/add_any | solution.py:28
  350.7 5.0 %fusion.18 = bf16[2,8,8,3072]{3,2,1,0:T(8,128)(2,1)} fusion(f32[2,8,8,3072]{3,2,1,0:T(8,128)S(1)} %get-tuple-element.300, f32[2,8,8,3072]{3,2,1,0:T(8,128)S(1)} %copy-done.5, f32[2,8,8,3072]{3,2,1,0:T(8,128)} %get-tuple-element.302, f32[2,8,8,3072]{3,2,1,0:T(8,128)} %get-tuple-element.303, f32[2,8,8,3072]{3,2,1,0:T(8,128)} %get-tuple-element.304, ...), kind=kLoop, calls=%fused_computation.79 | loop fusion | flops 3145728 | bytes 11821056 | tf_op jit(solution)/shard_map/convert_element_type | solution.py:152
  355.7 5.0 %all-reduce.99 = bf16[4,1152]{1,0:T(4,128)(2,1)S(1)} all-reduce(bf16[4,1152]{1,0:T(4,128)(2,1)S(1)} %collective-permute-done.2), channel_id=5, replica_groups=mesh['dp'=16,'fsdp'=2] {'fsdp'}, use_global_device_ids=true, to_apply=%region_73.74.clone | all-reduce | flops 4608 | bytes 18432
  360.9 0.7 add_add_fusion.3
  361.6 1.2 copy.11
  362.7 61.2 %psum.22 = bf16[4,1536]{1,0:T(4,128)(2,1)S(1)} all-reduce(bf16[4,1536]{1,0:T(4,128)(2,1)S(1)} %copy.11), channel_id=1, replica_groups=mesh['dp'=16,'fsdp'=2] {'dp'}, use_global_device_ids=true, to_apply=%region_70.71 | all-reduce | flops 6144 | bytes 24576 | tf_op jit(solution)/shard_map/psum | solution.py:150
  423.9 0.6 convert_element_type.102
  424.5 28.1 %all-reduce.103.cloned.1.call-done = (bf16[49,1536]{1,0:T(8,128)(2,1)}, bf16[1536,1152]{1,0:T(8,128)(2,1)}) async-done(((bf16[49,1536]{1,0:T(8,128)(2,1)}, bf16[1536,1152]{1,0:T(8,128)(2,1)}), (bf16[49,1536]{1,0:T(8,128)(2,1)}, bf16[1536,1152]{1,0:T(8,128)(2,1)})) %all-reduce.103.cloned.1.call-update) | async-done | bytes 3689488 | tf_op jit(solution)/shard_map/psum | solution.py:149
  452.7 1.7 convert_element_type.101
  454.3 5.4 %convert_element_type.104 = f32[1536,1152]{1,0:T(8,128)} convert(bf16[1536,1152]{1,0:T(8,128)(2,1)} %get-tuple-element.293) | non-fusion elementwise | flops 1769472 | bytes 10616832 | tf_op jit(solution)/shard_map/convert_element_type | solution.py:148
  (362 shorter events, 17.0 us)
Async XLA Ops:
  7.2 94.8 %all-gather.3.cloned.1.call-start = ((), (), s32[]{:S(2)}) async-start(), calls=%async_computation.3 | async-start | bytes 10616832 | tf_op jit(solution)/shard_map/all_gather | solution.py:93
  7.9 251.1 %reduce-scatter.6.cloned.1.call-start = ((), (), s32[]{:S(2)}) async-start(), calls=%async_computation.4 | async-start | bytes 516096 | tf_op jit(solution)/shard_map/reduce_scatter | solution.py:140
  8.7 36.0 %copy-start = (f32[2,8,8,3072]{3,2,1,0:T(8,128)}, f32[2,8,8,3072]{3,2,1,0:T(8,128)S(1)}, u32[]{:S(2)}) copy-start(f32[2,8,8,3072]{3,2,1,0:T(8,128)S(1)} %convert_element_type.92) | copy-start | bytes 4718596
  29.7 14.9 %copy-start.7 = (f32[1,3072]{1,0:T(1,128)}, f32[1,3072]{1,0:T(1,128)S(1)}, u32[]{:S(2)}) copy-start(f32[1,3072]{1,0:T(1,128)S(1)} %get-tuple-element.380) | copy-start | bytes 36868
  29.8 14.9 %copy-start.9 = (f32[1,3072]{1,0:T(1,128)}, f32[1,3072]{1,0:T(1,128)S(1)}, u32[]{:S(2)}) copy-start(f32[1,3072]{1,0:T(1,128)S(1)} %get-tuple-element.381) | copy-start | bytes 36868
  29.8 14.9 %copy-start.49 = (f32[1,3072]{1,0:T(1,128)}, f32[1,3072]{1,0:T(1,128)S(1)}, u32[]{:S(2)}) copy-start(f32[1,3072]{1,0:T(1,128)S(1)} %get-tuple-element.382) | copy-start | bytes 36868
  29.8 14.9 %copy-start.51 = (f32[1,3072]{1,0:T(1,128)}, f32[1,3072]{1,0:T(1,128)S(1)}, u32[]{:S(2)}) copy-start(f32[1,3072]{1,0:T(1,128)S(1)} %get-tuple-element.383) | copy-start | bytes 36868
  29.8 14.9 %copy-start.53 = (f32[1,3072]{1,0:T(1,128)}, f32[1,3072]{1,0:T(1,128)S(1)}, u32[]{:S(2)}) copy-start(f32[1,3072]{1,0:T(1,128)S(1)} %get-tuple-element.384) | copy-start | bytes 36868
  29.8 14.9 %copy-start.55 = (f32[1,3072]{1,0:T(1,128)}, f32[1,3072]{1,0:T(1,128)S(1)}, u32[]{:S(2)}) copy-start(f32[1,3072]{1,0:T(1,128)S(1)} %get-tuple-element.385) | copy-start | bytes 36868
  46.7 161.5 %copy-start.65 = (f32[2]{0:T(128)}, f32[2]{0:T(128)S(1)}, u32[]{:S(2)}) copy-start(f32[2]{0:T(128)S(1)} %broadcast_multiply_fusion.50) | copy-start | bytes 28
  46.9 161.3 %copy-start.67 = (f32[2]{0:T(128)}, f32[2]{0:T(128)S(1)}, u32[]{:S(2)}) copy-start(f32[2]{0:T(128)S(1)} %fusion.34) | copy-start | bytes 28
  102.0 99.5 %copy-start.85 = (s32[2]{0:T(128)S(1)}, s32[2]{0:T(128)}, u32[]{:S(2)}) copy-start(s32[2]{0:T(128)} %iota_add_fusion.1) | copy-start | bytes 28
  106.2 102.0 %copy-start.72 = (f32[2]{0:T(128)}, f32[2]{0:T(128)S(1)}, u32[]{:S(2)}) copy-start(f32[2]{0:T(128)S(1)} %add_rsqrt_fusion) | copy-start | bytes 28
  106.3 6.5 %collective-permute-start = (bf16[4,1152]{1,0:T(4,128)(2,1)S(1)}, bf16[4,1152]{1,0:T(4,128)(2,1)S(1)}, u32[]{:S(2)}, u32[]{:S(2)}) collective-permute-start(bf16[4,1152]{1,0:T(4,128)(2,1)S(1)} %copy.17), channel_id=1, source_target_pairs={{0,2},{2,4},{4,6},{6,8},{8,10},{10,12},{12,14},{14,16},{16,18},{18... | collective-permute-start | bytes 27656 | tf_op jit(solution)/shard_map/while/body/eval_jaxpr/ppermute | solution.py:14
  106.8 6.0 %collective-permute-start.1 = (bf16[4,1152]{1,0:T(4,128)(2,1)S(1)}, bf16[4,1152]{1,0:T(4,128)(2,1)S(1)}, u32[]{:S(2)}, u32[]{:S(2)}) collective-permute-start(bf16[4,1152]{1,0:T(4,128)(2,1)S(1)} %fusion.77), channel_id=1, source_target_pairs={{0,2},{2,4},{4,6},{6,8},{8,10},{10,12},{12,14},{14,16},{16,18},{18... | collective-permute-start | bytes 27656 | tf_op jit(solution)/shard_map/while/body/eval_jaxpr/ppermute | solution.py:14
  112.9 6.3 %collective-permute-start = (bf16[4,1152]{1,0:T(4,128)(2,1)S(1)}, bf16[4,1152]{1,0:T(4,128)(2,1)S(1)}, u32[]{:S(2)}, u32[]{:S(2)}) collective-permute-start(bf16[4,1152]{1,0:T(4,128)(2,1)S(1)} %copy.17), channel_id=1, source_target_pairs={{0,2},{2,4},{4,6},{6,8},{8,10},{10,12},{12,14},{14,16},{16,18},{18... | collective-permute-start | bytes 27656 | tf_op jit(solution)/shard_map/while/body/eval_jaxpr/ppermute | solution.py:14
  113.3 5.8 %collective-permute-start.1 = (bf16[4,1152]{1,0:T(4,128)(2,1)S(1)}, bf16[4,1152]{1,0:T(4,128)(2,1)S(1)}, u32[]{:S(2)}, u32[]{:S(2)}) collective-permute-start(bf16[4,1152]{1,0:T(4,128)(2,1)S(1)} %fusion.77), channel_id=1, source_target_pairs={{0,2},{2,4},{4,6},{6,8},{8,10},{10,12},{12,14},{14,16},{16,18},{18... | collective-permute-start | bytes 27656 | tf_op jit(solution)/shard_map/while/body/eval_jaxpr/ppermute | solution.py:14
  119.2 6.3 %collective-permute-start = (bf16[4,1152]{1,0:T(4,128)(2,1)S(1)}, bf16[4,1152]{1,0:T(4,128)(2,1)S(1)}, u32[]{:S(2)}, u32[]{:S(2)}) collective-permute-start(bf16[4,1152]{1,0:T(4,128)(2,1)S(1)} %copy.17), channel_id=1, source_target_pairs={{0,2},{2,4},{4,6},{6,8},{8,10},{10,12},{12,14},{14,16},{16,18},{18... | collective-permute-start | bytes 27656 | tf_op jit(solution)/shard_map/while/body/eval_jaxpr/ppermute | solution.py:14
  119.6 5.8 %collective-permute-start.1 = (bf16[4,1152]{1,0:T(4,128)(2,1)S(1)}, bf16[4,1152]{1,0:T(4,128)(2,1)S(1)}, u32[]{:S(2)}, u32[]{:S(2)}) collective-permute-start(bf16[4,1152]{1,0:T(4,128)(2,1)S(1)} %fusion.77), channel_id=1, source_target_pairs={{0,2},{2,4},{4,6},{6,8},{8,10},{10,12},{12,14},{14,16},{16,18},{18... | collective-permute-start | bytes 27656 | tf_op jit(solution)/shard_map/while/body/eval_jaxpr/ppermute | solution.py:14
  125.5 6.3 %collective-permute-start = (bf16[4,1152]{1,0:T(4,128)(2,1)S(1)}, bf16[4,1152]{1,0:T(4,128)(2,1)S(1)}, u32[]{:S(2)}, u32[]{:S(2)}) collective-permute-start(bf16[4,1152]{1,0:T(4,128)(2,1)S(1)} %copy.17), channel_id=1, source_target_pairs={{0,2},{2,4},{4,6},{6,8},{8,10},{10,12},{12,14},{14,16},{16,18},{18... | collective-permute-start | bytes 27656 | tf_op jit(solution)/shard_map/while/body/eval_jaxpr/ppermute | solution.py:14
  126.0 5.8 %collective-permute-start.1 = (bf16[4,1152]{1,0:T(4,128)(2,1)S(1)}, bf16[4,1152]{1,0:T(4,128)(2,1)S(1)}, u32[]{:S(2)}, u32[]{:S(2)}) collective-permute-start(bf16[4,1152]{1,0:T(4,128)(2,1)S(1)} %fusion.77), channel_id=1, source_target_pairs={{0,2},{2,4},{4,6},{6,8},{8,10},{10,12},{12,14},{14,16},{16,18},{18... | collective-permute-start | bytes 27656 | tf_op jit(solution)/shard_map/while/body/eval_jaxpr/ppermute | solution.py:14
  131.8 6.3 %collective-permute-start = (bf16[4,1152]{1,0:T(4,128)(2,1)S(1)}, bf16[4,1152]{1,0:T(4,128)(2,1)S(1)}, u32[]{:S(2)}, u32[]{:S(2)}) collective-permute-start(bf16[4,1152]{1,0:T(4,128)(2,1)S(1)} %copy.17), channel_id=1, source_target_pairs={{0,2},{2,4},{4,6},{6,8},{8,10},{10,12},{12,14},{14,16},{16,18},{18... | collective-permute-start | bytes 27656 | tf_op jit(solution)/shard_map/while/body/eval_jaxpr/ppermute | solution.py:14
  132.3 5.8 %collective-permute-start.1 = (bf16[4,1152]{1,0:T(4,128)(2,1)S(1)}, bf16[4,1152]{1,0:T(4,128)(2,1)S(1)}, u32[]{:S(2)}, u32[]{:S(2)}) collective-permute-start(bf16[4,1152]{1,0:T(4,128)(2,1)S(1)} %fusion.77), channel_id=1, source_target_pairs={{0,2},{2,4},{4,6},{6,8},{8,10},{10,12},{12,14},{14,16},{16,18},{18... | collective-permute-start | bytes 27656 | tf_op jit(solution)/shard_map/while/body/eval_jaxpr/ppermute | solution.py:14
  138.2 6.3 %collective-permute-start = (bf16[4,1152]{1,0:T(4,128)(2,1)S(1)}, bf16[4,1152]{1,0:T(4,128)(2,1)S(1)}, u32[]{:S(2)}, u32[]{:S(2)}) collective-permute-start(bf16[4,1152]{1,0:T(4,128)(2,1)S(1)} %copy.17), channel_id=1, source_target_pairs={{0,2},{2,4},{4,6},{6,8},{8,10},{10,12},{12,14},{14,16},{16,18},{18... | collective-permute-start | bytes 27656 | tf_op jit(solution)/shard_map/while/body/eval_jaxpr/ppermute | solution.py:14
  138.6 5.8 %collective-permute-start.1 = (bf16[4,1152]{1,0:T(4,128)(2,1)S(1)}, bf16[4,1152]{1,0:T(4,128)(2,1)S(1)}, u32[]{:S(2)}, u32[]{:S(2)}) collective-permute-start(bf16[4,1152]{1,0:T(4,128)(2,1)S(1)} %fusion.77), channel_id=1, source_target_pairs={{0,2},{2,4},{4,6},{6,8},{8,10},{10,12},{12,14},{14,16},{16,18},{18... | collective-permute-start | bytes 27656 | tf_op jit(solution)/shard_map/while/body/eval_jaxpr/ppermute | solution.py:14
  144.5 6.3 %collective-permute-start = (bf16[4,1152]{1,0:T(4,128)(2,1)S(1)}, bf16[4,1152]{1,0:T(4,128)(2,1)S(1)}, u32[]{:S(2)}, u32[]{:S(2)}) collective-permute-start(bf16[4,1152]{1,0:T(4,128)(2,1)S(1)} %copy.17), channel_id=1, source_target_pairs={{0,2},{2,4},{4,6},{6,8},{8,10},{10,12},{12,14},{14,16},{16,18},{18... | collective-permute-start | bytes 27656 | tf_op jit(solution)/shard_map/while/body/eval_jaxpr/ppermute | solution.py:14
  144.9 5.8 %collective-permute-start.1 = (bf16[4,1152]{1,0:T(4,128)(2,1)S(1)}, bf16[4,1152]{1,0:T(4,128)(2,1)S(1)}, u32[]{:S(2)}, u32[]{:S(2)}) collective-permute-start(bf16[4,1152]{1,0:T(4,128)(2,1)S(1)} %fusion.77), channel_id=1, source_target_pairs={{0,2},{2,4},{4,6},{6,8},{8,10},{10,12},{12,14},{14,16},{16,18},{18... | collective-permute-start | bytes 27656 | tf_op jit(solution)/shard_map/while/body/eval_jaxpr/ppermute | solution.py:14
  150.8 6.3 %collective-permute-start = (bf16[4,1152]{1,0:T(4,128)(2,1)S(1)}, bf16[4,1152]{1,0:T(4,128)(2,1)S(1)}, u32[]{:S(2)}, u32[]{:S(2)}) collective-permute-start(bf16[4,1152]{1,0:T(4,128)(2,1)S(1)} %copy.17), channel_id=1, source_target_pairs={{0,2},{2,4},{4,6},{6,8},{8,10},{10,12},{12,14},{14,16},{16,18},{18... | collective-permute-start | bytes 27656 | tf_op jit(solution)/shard_map/while/body/eval_jaxpr/ppermute | solution.py:14
  151.3 5.8 %collective-permute-start.1 = (bf16[4,1152]{1,0:T(4,128)(2,1)S(1)}, bf16[4,1152]{1,0:T(4,128)(2,1)S(1)}, u32[]{:S(2)}, u32[]{:S(2)}) collective-permute-start(bf16[4,1152]{1,0:T(4,128)(2,1)S(1)} %fusion.77), channel_id=1, source_target_pairs={{0,2},{2,4},{4,6},{6,8},{8,10},{10,12},{12,14},{14,16},{16,18},{18... | collective-permute-start | bytes 27656 | tf_op jit(solution)/shard_map/while/body/eval_jaxpr/ppermute | solution.py:14
  157.1 6.3 %collective-permute-start = (bf16[4,1152]{1,0:T(4,128)(2,1)S(1)}, bf16[4,1152]{1,0:T(4,128)(2,1)S(1)}, u32[]{:S(2)}, u32[]{:S(2)}) collective-permute-start(bf16[4,1152]{1,0:T(4,128)(2,1)S(1)} %copy.17), channel_id=1, source_target_pairs={{0,2},{2,4},{4,6},{6,8},{8,10},{10,12},{12,14},{14,16},{16,18},{18... | collective-permute-start | bytes 27656 | tf_op jit(solution)/shard_map/while/body/eval_jaxpr/ppermute | solution.py:14
  157.6 5.8 %collective-permute-start.1 = (bf16[4,1152]{1,0:T(4,128)(2,1)S(1)}, bf16[4,1152]{1,0:T(4,128)(2,1)S(1)}, u32[]{:S(2)}, u32[]{:S(2)}) collective-permute-start(bf16[4,1152]{1,0:T(4,128)(2,1)S(1)} %fusion.77), channel_id=1, source_target_pairs={{0,2},{2,4},{4,6},{6,8},{8,10},{10,12},{12,14},{14,16},{16,18},{18... | collective-permute-start | bytes 27656 | tf_op jit(solution)/shard_map/while/body/eval_jaxpr/ppermute | solution.py:14
  163.5 6.3 %collective-permute-start = (bf16[4,1152]{1,0:T(4,128)(2,1)S(1)}, bf16[4,1152]{1,0:T(4,128)(2,1)S(1)}, u32[]{:S(2)}, u32[]{:S(2)}) collective-permute-start(bf16[4,1152]{1,0:T(4,128)(2,1)S(1)} %copy.17), channel_id=1, source_target_pairs={{0,2},{2,4},{4,6},{6,8},{8,10},{10,12},{12,14},{14,16},{16,18},{18... | collective-permute-start | bytes 27656 | tf_op jit(solution)/shard_map/while/body/eval_jaxpr/ppermute | solution.py:14
  163.9 5.8 %collective-permute-start.1 = (bf16[4,1152]{1,0:T(4,128)(2,1)S(1)}, bf16[4,1152]{1,0:T(4,128)(2,1)S(1)}, u32[]{:S(2)}, u32[]{:S(2)}) collective-permute-start(bf16[4,1152]{1,0:T(4,128)(2,1)S(1)} %fusion.77), channel_id=1, source_target_pairs={{0,2},{2,4},{4,6},{6,8},{8,10},{10,12},{12,14},{14,16},{16,18},{18... | collective-permute-start | bytes 27656 | tf_op jit(solution)/shard_map/while/body/eval_jaxpr/ppermute | solution.py:14
  169.8 6.3 %collective-permute-start = (bf16[4,1152]{1,0:T(4,128)(2,1)S(1)}, bf16[4,1152]{1,0:T(4,128)(2,1)S(1)}, u32[]{:S(2)}, u32[]{:S(2)}) collective-permute-start(bf16[4,1152]{1,0:T(4,128)(2,1)S(1)} %copy.17), channel_id=1, source_target_pairs={{0,2},{2,4},{4,6},{6,8},{8,10},{10,12},{12,14},{14,16},{16,18},{18... | collective-permute-start | bytes 27656 | tf_op jit(solution)/shard_map/while/body/eval_jaxpr/ppermute | solution.py:14
  170.2 5.8 %collective-permute-start.1 = (bf16[4,1152]{1,0:T(4,128)(2,1)S(1)}, bf16[4,1152]{1,0:T(4,128)(2,1)S(1)}, u32[]{:S(2)}, u32[]{:S(2)}) collective-permute-start(bf16[4,1152]{1,0:T(4,128)(2,1)S(1)} %fusion.77), channel_id=1, source_target_pairs={{0,2},{2,4},{4,6},{6,8},{8,10},{10,12},{12,14},{14,16},{16,18},{18... | collective-permute-start | bytes 27656 | tf_op jit(solution)/shard_map/while/body/eval_jaxpr/ppermute | solution.py:14
  176.1 6.3 %collective-permute-start = (bf16[4,1152]{1,0:T(4,128)(2,1)S(1)}, bf16[4,1152]{1,0:T(4,128)(2,1)S(1)}, u32[]{:S(2)}, u32[]{:S(2)}) collective-permute-start(bf16[4,1152]{1,0:T(4,128)(2,1)S(1)} %copy.17), channel_id=1, source_target_pairs={{0,2},{2,4},{4,6},{6,8},{8,10},{10,12},{12,14},{14,16},{16,18},{18... | collective-permute-start | bytes 27656 | tf_op jit(solution)/shard_map/while/body/eval_jaxpr/ppermute | solution.py:14
  176.6 5.8 %collective-permute-start.1 = (bf16[4,1152]{1,0:T(4,128)(2,1)S(1)}, bf16[4,1152]{1,0:T(4,128)(2,1)S(1)}, u32[]{:S(2)}, u32[]{:S(2)}) collective-permute-start(bf16[4,1152]{1,0:T(4,128)(2,1)S(1)} %fusion.77), channel_id=1, source_target_pairs={{0,2},{2,4},{4,6},{6,8},{8,10},{10,12},{12,14},{14,16},{16,18},{18... | collective-permute-start | bytes 27656 | tf_op jit(solution)/shard_map/while/body/eval_jaxpr/ppermute | solution.py:14
  182.4 6.3 %collective-permute-start = (bf16[4,1152]{1,0:T(4,128)(2,1)S(1)}, bf16[4,1152]{1,0:T(4,128)(2,1)S(1)}, u32[]{:S(2)}, u32[]{:S(2)}) collective-permute-start(bf16[4,1152]{1,0:T(4,128)(2,1)S(1)} %copy.17), channel_id=1, source_target_pairs={{0,2},{2,4},{4,6},{6,8},{8,10},{10,12},{12,14},{14,16},{16,18},{18... | collective-permute-start | bytes 27656 | tf_op jit(solution)/shard_map/while/body/eval_jaxpr/ppermute | solution.py:14
  182.9 5.8 %collective-permute-start.1 = (bf16[4,1152]{1,0:T(4,128)(2,1)S(1)}, bf16[4,1152]{1,0:T(4,128)(2,1)S(1)}, u32[]{:S(2)}, u32[]{:S(2)}) collective-permute-start(bf16[4,1152]{1,0:T(4,128)(2,1)S(1)} %fusion.77), channel_id=1, source_target_pairs={{0,2},{2,4},{4,6},{6,8},{8,10},{10,12},{12,14},{14,16},{16,18},{18... | collective-permute-start | bytes 27656 | tf_op jit(solution)/shard_map/while/body/eval_jaxpr/ppermute | solution.py:14
  188.8 6.3 %collective-permute-start = (bf16[4,1152]{1,0:T(4,128)(2,1)S(1)}, bf16[4,1152]{1,0:T(4,128)(2,1)S(1)}, u32[]{:S(2)}, u32[]{:S(2)}) collective-permute-start(bf16[4,1152]{1,0:T(4,128)(2,1)S(1)} %copy.17), channel_id=1, source_target_pairs={{0,2},{2,4},{4,6},{6,8},{8,10},{10,12},{12,14},{14,16},{16,18},{18... | collective-permute-start | bytes 27656 | tf_op jit(solution)/shard_map/while/body/eval_jaxpr/ppermute | solution.py:14
  189.2 5.8 %collective-permute-start.1 = (bf16[4,1152]{1,0:T(4,128)(2,1)S(1)}, bf16[4,1152]{1,0:T(4,128)(2,1)S(1)}, u32[]{:S(2)}, u32[]{:S(2)}) collective-permute-start(bf16[4,1152]{1,0:T(4,128)(2,1)S(1)} %fusion.77), channel_id=1, source_target_pairs={{0,2},{2,4},{4,6},{6,8},{8,10},{10,12},{12,14},{14,16},{16,18},{18... | collective-permute-start | bytes 27656 | tf_op jit(solution)/shard_map/while/body/eval_jaxpr/ppermute | solution.py:14
  195.1 6.3 %collective-permute-start = (bf16[4,1152]{1,0:T(4,128)(2,1)S(1)}, bf16[4,1152]{1,0:T(4,128)(2,1)S(1)}, u32[]{:S(2)}, u32[]{:S(2)}) collective-permute-start(bf16[4,1152]{1,0:T(4,128)(2,1)S(1)} %copy.17), channel_id=1, source_target_pairs={{0,2},{2,4},{4,6},{6,8},{8,10},{10,12},{12,14},{14,16},{16,18},{18... | collective-permute-start | bytes 27656 | tf_op jit(solution)/shard_map/while/body/eval_jaxpr/ppermute | solution.py:14
  195.5 5.8 %collective-permute-start.1 = (bf16[4,1152]{1,0:T(4,128)(2,1)S(1)}, bf16[4,1152]{1,0:T(4,128)(2,1)S(1)}, u32[]{:S(2)}, u32[]{:S(2)}) collective-permute-start(bf16[4,1152]{1,0:T(4,128)(2,1)S(1)} %fusion.77), channel_id=1, source_target_pairs={{0,2},{2,4},{4,6},{6,8},{8,10},{10,12},{12,14},{14,16},{16,18},{18... | collective-permute-start | bytes 27656 | tf_op jit(solution)/shard_map/while/body/eval_jaxpr/ppermute | solution.py:14
  223.4 98.5 %reduce-scatter.8.cloned.1.call-start = ((), (), s32[]{:S(2)}) async-start(), calls=%async_computation.5 | async-start | bytes 10616832 | tf_op jit(solution)/shard_map/reduce_scatter | solution.py:128
  228.8 132.8 %reduce-scatter.10.cloned.1.call-start = ((), (), s32[]{:S(2)}) async-start(), calls=%async_computation.6 | async-start | bytes 1179648
  258.6 194.0 %all-reduce.103.cloned.1.call-start = ((), (), s32[]{:S(2)}) async-start(), calls=%async_computation.7 | async-start | bytes 7421952 | tf_op jit(solution)/shard_map/psum | solution.py:149
  258.9 96.7 %collective-permute-start.2 = (bf16[4,1152]{1,0:T(4,128)(2,1)S(1)}, bf16[4,1152]{1,0:T(4,128)(2,1)S(1)}, u32[]{:S(2)}, u32[]{:S(2)}) collective-permute-start(bf16[4,1152]{1,0:T(4,128)(2,1)S(1)} %fusion.11), channel_id=1, source_target_pairs={{0,2},{2,4},{4,6},{6,8},{8,10},{10,12},{12,14},{14,16},{16,18},{18... | collective-permute-start | bytes 27656 | tf_op jit(solution)/shard_map/ppermute | solution.py:14
  321.9 28.7 %copy-start.5 = (f32[2,8,8,3072]{3,2,1,0:T(8,128)S(1)}, f32[2,8,8,3072]{3,2,1,0:T(8,128)}, u32[]{:S(2)}) copy-start(f32[2,8,8,3072]{3,2,1,0:T(8,128)} %get-tuple-element.301) | copy-start | bytes 4718596
  (76 other events, 607.8 us)
Sparse Core Ops, SparseCore 0:
  9.6 92.3 all-gather.2
  223.5 9.8 reduce-scatter.5
  236.2 85.5 reduce-scatter.7
  324.0 17.4 reduce-scatter.9
  345.2 107.4 all-reduce.102
where the time goes:
time: 467 us; the launch traced here: 466 us
  waiting for transfers between devices  230 us (49%)
  other arithmetic  100 us (21%)
  blocking collectives  85 us (18%)
  matrix products  22.4 us (5%)
  between operations  15.8 us (3%)
  local copies, waits for them, and re-layouts  7.71 us (2%)
    ppermute x31, waiting for transfers between devices, shifted(): return lax.ppermute(value, axis, pairs)  82.8 us
    reduce_scatter x1, waiting for transfers between devices, per_device(): lax.psum_scatter(lax.dot_general(pooled_bf, embed_grad, (((0,), (0,)), ((...  62.8 us
    psum x1, blocking collectives, per_device(): lax.psum(terms_part.astype(jnp.bfloat16), 'dp').astype(jnp.float32)  61.2 us
    all_gather x1, waiting for transfers between devices, per_device(): head_all = lax.all_gather(head_weight, 'fsdp', axis=0, tiled=True)  55.1 us
    add_any x1, other arithmetic, depthwise(): padded[:, row_tap:row_tap + height, col_tap:col_tap + width, :]  28.7 us
    psum x1, waiting for transfers between devices, per_device(): lax.psum(kernel_part.astype(jnp.bfloat16), 'dp').astype(jnp.float32)  28.1 us
    mul x3, other arithmetic, depthwise(): padded[:, row_tap:row_tap + height, col_tap:col_tap + width, :]  26.2 us
    reduce_sum x1, other arithmetic, block_pool(): row_mean = jnp.mean(mixed, axis=3, keepdims=True)  14.5 us
  transfers between devices with their start and end apart: 36, of which 18 were waited for; matrix products, arithmetic and copies ran while one was open for 20% of the time, Pallas kernels for 0%

commit v1 on v0

v1 whole, which is shorter than its diff:
```python
import jax
import jax.numpy as jnp
from jax import lax
from jax.sharding import PartitionSpec as P

EPS = 1e-06
LOGIT_SCALE = 10.0
LOGIT_BIAS = -2.0
KER = 7
BF = jnp.bfloat16
F32 = jnp.float32


def swap(value, axis, mask):
    count = lax.axis_size(axis)
    return lax.ppermute(value, axis, [(source, source ^ mask) for source in range(count)])


def tree_gather(value, axis, masks):
    for mask in masks:
        value = jnp.concatenate([value, swap(value, axis, mask)], axis=0)
    return value


def bits_up(count):
    masks = []
    mask = 1
    while mask < count:
        masks.append(mask)
        mask *= 2
    return masks


def depthwise(inputs, kernel):
    reach = KER // 2
    height = inputs.shape[1]
    width = inputs.shape[2]
    padded = jnp.pad(inputs, ((0, 0), (reach, reach), (reach, reach), (0, 0)))
    mixed = jnp.zeros_like(inputs)
    for row_tap in range(KER):
        for col_tap in range(KER):
            mixed = (
                mixed
                + padded[:, row_tap : row_tap + height, col_tap : col_tap + width, :]
                * kernel[row_tap * KER + col_tap]
            )
    return mixed


def block_pool(inputs, kernel, conv_bias, norm_gain, layer_scale):
    mixed = depthwise(inputs, kernel) + conv_bias
    row_mean = jnp.mean(mixed, axis=3, keepdims=True)
    centered = mixed - row_mean
    row_var = jnp.mean(centered * centered, axis=3, keepdims=True)
    output = inputs + layer_scale * (centered * lax.rsqrt(row_var + EPS) * norm_gain)
    return jnp.mean(output, axis=(1, 2))


def head_norm(pooled, head_gain):
    row_mean = jnp.mean(pooled, axis=1, keepdims=True)
    centered = pooled - row_mean
    row_var = jnp.mean(centered * centered, axis=1, keepdims=True)
    return centered * lax.rsqrt(row_var + EPS) * head_gain


def to_unit(vectors):
    return vectors * lax.rsqrt(jnp.sum(vectors * vectors, axis=1, keepdims=True) + EPS)


def pick(value, index, width):
    return lax.dynamic_slice_in_dim(value, index * width, width, axis=value.ndim - 1)


def join_slices(pieces, member):
    count = len(pieces)
    if count == 1:
        return pieces[0]
    if count == 2:
        low = jnp.where(member == 0, pieces[0], pieces[1])
        high = jnp.where(member == 0, pieces[1], pieces[0])
        return jnp.concatenate([low, high], axis=-1)
    stacked = jnp.stack(pieces)
    return jnp.concatenate(
        [lax.dynamic_index_in_dim(stacked, member ^ s, keepdims=False) for s in range(count)], axis=-1
    )


def reduce_terms(value, member, core, members, dp_masks):
    rows, channels = value.shape
    share = channels // members
    half = share // 2
    split = value.reshape(rows, members, 2, half)
    keep = lax.dynamic_index_in_dim(split, core, axis=2, keepdims=False)
    give = lax.dynamic_index_in_dim(split, 1 - core, axis=2, keepdims=False).astype(BF)
    chip = keep.astype(BF).astype(F32) + swap(give, "dp", 1).astype(F32)
    total = lax.dynamic_index_in_dim(chip, member, axis=1, keepdims=False).astype(BF).astype(F32)
    for m in range(1, members):
        part = lax.dynamic_index_in_dim(chip, member ^ m, axis=1, keepdims=False).astype(BF)
        total = total + swap(part, "fsdp", m).astype(F32)
    for mask in dp_masks:
        sent = total.astype(BF)
        total = sent.astype(F32) + swap(sent, "dp", mask).astype(F32)
    sent = total.astype(BF)
    other = swap(sent, "dp", 1)
    low = jnp.where(core == 0, sent, other)
    high = jnp.where(core == 0, other, sent)
    return jnp.concatenate([low, high], axis=1).astype(F32)


def per_device(image_maps, dw_kernel, channel_terms, head_weight, text_feats):
    rows = image_maps.shape[0]
    members = lax.axis_size("fsdp")
    member = lax.axis_index("fsdp")
    core = lax.axis_index("dp") % 2
    pair_masks = bits_up(members)
    dp_masks = bits_up(lax.axis_size("dp"))
    down = dp_masks[::-1]
    share = head_weight.shape[0]

    weights = jnp.concatenate([dw_kernel, channel_terms], axis=0)
    weights = join_slices([weights] + [swap(weights, "fsdp", m) for m in range(1, members)], member)
    kernel = weights[: KER * KER].astype(F32)
    terms = weights[KER * KER :].astype(F32)

    text_unit, text_back = jax.vjp(to_unit, text_feats.astype(F32))
    own_text = text_unit.astype(BF)
    text_all = tree_gather(tree_gather(own_text, "fsdp", pair_masks), "dp", down)

    inputs = image_maps.astype(F32)
    pooled, block_back = jax.vjp(block_pool, inputs, kernel, terms[0], terms[1], terms[2])
    normed, head_back = jax.vjp(head_norm, pooled, terms[3])
    pooled_bf = normed.astype(BF)

    group = jnp.concatenate(
        [pick(pooled_bf, member, share)]
        + [swap(pick(pooled_bf, member ^ m, share), "fsdp", m) for m in range(1, members)],
        axis=0,
    )
    partial = jnp.dot(group, head_weight, preferred_element_type=F32)
    embed = partial
    for m in range(1, members):
        other = swap(partial, "fsdp", m)
        embed = embed + jnp.concatenate(
            [other[(k ^ m) * rows : (k ^ m) * rows + rows] for k in range(members)], axis=0
        )
    unit_vec, unit_back = jax.vjp(to_unit, embed)
    unit_bf = unit_vec.astype(BF)

    def pair_weights(images, texts):
        logits = (
            LOGIT_SCALE
            * lax.dot_general(images, texts, (((1,), (1,)), ((), ())), preferred_element_type=F32)
            + LOGIT_BIAS
        )
        here = lax.broadcasted_iota(jnp.int32, logits.shape, 0)
        there = lax.broadcasted_iota(jnp.int32, logits.shape, 1)
        positive = jnp.where(here == there, 1.0, 0.0).astype(F32)
        return (jax.nn.sigmoid(logits) - positive).astype(BF)

    unit_sum = LOGIT_SCALE * jnp.dot(
        pair_weights(unit_bf, text_all), text_all, preferred_element_type=F32
    )
    embed_grad = unit_back(unit_sum)[0].astype(BF)
    grad_part = lax.dot_general(
        embed_grad, head_weight, (((1,), (1,)), ((), ())), preferred_element_type=F32
    )
    pooled_grad = join_slices(
        [grad_part[:rows]]
        + [swap(grad_part[m * rows : m * rows + rows], "fsdp", m) for m in range(1, members)],
        member,
    )

    packed = tree_gather(jnp.concatenate([group, embed_grad, unit_bf], axis=1), "dp", down)
    group_all = packed[:, :share]
    width = embed_grad.shape[1]
    grad_all = packed[:, share : share + width]
    unit_all = packed[:, share + width :]

    pool_grad, gain_grad = head_back(pooled_grad)
    image_grad, kernel_grad, bias_grad, norm_grad, scale_grad = block_back(pool_grad)
    sums = jnp.concatenate(
        [kernel_grad, jnp.stack([bias_grad, norm_grad, scale_grad, gain_grad])], axis=0
    )
    sums = reduce_terms(sums, member, core, members, dp_masks[1:])

    head_grads = lax.dot_general(
        group_all, grad_all, (((0,), (0,)), ((), ())), preferred_element_type=F32
    )
    text_sum = LOGIT_SCALE * lax.dot_general(
        pair_weights(unit_all, own_text),
        unit_all,
        (((0,), (0,)), ((), ())),
        preferred_element_type=F32,
    )
    text_grads = text_back(text_sum)[0]
    return (
        image_grad.astype(BF),
        sums[: KER * KER],
        sums[KER * KER :],
        head_grads,
        text_grads,
    )


def solution(mesh):
    in_specs = (
        P(("dp", "fsdp"), None, None, None),
        P(None, "fsdp"),
        P(None, "fsdp"),
        P("fsdp", None),
        P(("dp", "fsdp"), None),
    )
    out_specs = (
        P(("dp", "fsdp"), None, None, None),
        P(None, "fsdp"),
        P(None, "fsdp"),
        P("fsdp", None),
        P(("dp", "fsdp"), None),
    )
    return jax.shard_map(
        per_device, mesh=mesh, in_specs=in_specs, out_specs=out_specs, check_vma=False
    )
```

time: 467 us -> 178 us (0.38)
  waiting for transfers between devices: 230 us -> 9.54 us
  blocking collectives: 85 us -> 0 us
  starting transfers between devices: 4.29 us -> 24.6 us
  between operations: 15.8 us -> 2.46 us
  other arithmetic: 100 us -> 113 us
  matrix products: 22.4 us -> 10.7 us
  local copies, waits for them, and re-layouts: 7.71 us -> 16.8 us
    ppermute x31 -> x19, waiting for transfers between devices: 82.8 us -> 9.54 us  [swap(): lax.ppermute(value, axis, [(source, source ^ mask) for source in range(co...]
    reduce_scatter x2 -> x0, waiting for transfers between devices: 62.9 us -> none  [the longest x1 62.8 us: per_device(): lax.psum_scatter(lax.dot_general(pooled_bf, embed_grad, (((0,), (0,)), ((...]
    psum x1 -> x0, blocking collectives: 61.2 us -> none  [per_device(): lax.psum(terms_part.astype(jnp.bfloat16), 'dp').astype(jnp.float32)]
    all_gather x1 -> x0, waiting for transfers between devices: 55.1 us -> none  [per_device(): head_all = lax.all_gather(head_weight, 'fsdp', axis=0, tiled=True)]
    psum x1 -> x0, waiting for transfers between devices: 28.1 us -> none  [per_device(): lax.psum(kernel_part.astype(jnp.bfloat16), 'dp').astype(jnp.float32)]
    ppermute x31 -> x19, starting transfers between devices: 3.91 us -> 24.6 us  [swap(): lax.ppermute(value, axis, [(source, source ^ mask) for source in range(co...]
    all_gather x3 -> x0, blocking collectives: 18.7 us -> none  [the longest x1 9.07 us: per_device(): lax.all_gather(dw_kernel, 'fsdp', axis=1, tiled=True)]
    dot_general x51 -> x5, matrix products: 22.4 us -> 10.7 us  [the longest x1 5.23 us: per_device(): lax.dot_general(group_all, grad_all, (((0,), (0,)), ((), ())), preferred_...]
  transfers between devices with their start and end apart: 36 -> 19, of which waited for: 18 -> 6; matrix products, arithmetic and copies ran while one was open for 20% -> 72% of each run, Pallas kernels for 0% -> 0%
where the time goes in v1:
time: 178 us; the launch traced here: 177 us
  other arithmetic  113 us (63%)
  starting transfers between devices  24.6 us (14%)
  local copies, waits for them, and re-layouts  16.8 us (9%)
  matrix products  10.7 us (6%)
  waiting for transfers between devices  9.54 us (5%)
  between operations  2.46 us (1%)
    add_any x1, other arithmetic, depthwise(): padded[:, row_tap:row_tap + height, col_tap:col_tap + width, :]  28.3 us
    mul x3, other arithmetic, depthwise(): padded[:, row_tap:row_tap + height, col_tap:col_tap + width, :]  27 us
    ppermute x19, starting transfers between devices, swap(): lax.ppermute(value, axis, [(source, source ^ mask) for source in range(co...  24.6 us
    reduce_sum x1, other arithmetic, block_pool(): row_mean = jnp.mean(mixed, axis=3, keepdims=True)  14.8 us
    concatenate x3, local copies, waits for them, and re-layouts, tree_gather(): value = jnp.concatenate([value, swap(value, axis, mask)], axis=0)  10.7 us
    ppermute x19, waiting for transfers between devices, swap(): lax.ppermute(value, axis, [(source, source ^ mask) for source in range(co...  9.54 us
    reduce_sum x2, other arithmetic, depthwise(): padded[:, row_tap:row_tap + height, col_tap:col_tap + width, :]  7.01 us
    dot_general x1, matrix products, per_device(): lax.dot_general(group_all, grad_all, (((0,), (0,)), ((), ())), preferred_...  5.23 us
  transfers between devices with their start and end apart: 19, of which 6 were waited for; matrix products, arithmetic and copies ran while one was open for 72% of the time, Pallas kernels for 0%

profile of v1, /device:TPU:0, one launch (start us, length us, event | category | flops | bytes accessed | tf_op | source)
XLA Modules:
  0.0 177.2 jit_solution(6792336725576857380)
XLA Ops:
  0.6 1.0 fusion.36
  1.6 0.8 fusion.37
  2.5 3.0 %collective-permute-start.3 = (bf16[2,1152]{1,0:T(2,128)(2,1)S(1)}, bf16[2,1152]{1,0:T(2,128)(2,1)S(1)}, u32[]{:S(2)}, u32[]{:S(2)}) collective-permute-start(bf16[2,1152]{1,0:T(2,128)(2,1)S(1)} %fusion.37), channel_id=1, source_target_pairs={{0,1},{1,0},{2,3},{3,2},{4,5},{5,4},{6,7},{7,6},{8,9},{9,8},{10,11... | collective-permute-start | bytes 13832 | tf_op jit(solution)/shard_map/ppermute | solution.py:16
  5.5 1.6 collective-permute-done.3
  7.1 3.2 %collective-permute-start.4 = (bf16[4,1152]{1,0:T(4,128)(2,1)S(1)}, bf16[4,1152]{1,0:T(4,128)(2,1)S(1)}, u32[]{:S(2)}, u32[]{:S(2)}) collective-permute-start(bf16[4,1152]{1,0:T(4,128)(2,1)S(1)} %pad_maximum_fusion.9), channel_id=1, source_target_pairs={{0,16},{2,18},{4,20},{6,22},{8,24},{10,26},{12,28},{14,30},{16,0},... | collective-permute-start | bytes 27656 | tf_op jit(solution)/shard_map/ppermute | solution.py:16
  10.2 1.6 collective-permute-done.4
  13.1 1.9 %collective-permute-start.5 = (bf16[8,1152]{1,0:T(8,128)(2,1)}, bf16[8,1152]{1,0:T(8,128)(2,1)}, u32[]{:S(2)}, u32[]{:S(2)}) collective-permute-start(bf16[8,1152]{1,0:T(8,128)(2,1)} %pad_maximum_fusion.7), channel_id=1, source_target_pairs={{0,8},{2,10},{4,12},{6,14},{8,0},{10,2},{12,4},{14,6},{16,24},{18,... | collective-permute-start | bytes 55304 | tf_op jit(solution)/shard_map/ppermute | solution.py:16
  15.0 1.6 pad_maximum_fusion.1
  16.6 1.5 collective-permute-start
  18.1 2.4 %convert_element_type.106 = f32[2,8,8,3072]{3,2,1,0:T(8,128)} convert(bf16[2,8,8,3072]{3,2,1,0:T(8,128)(2,1)} %param.5) | non-fusion elementwise | flops 393216 | bytes 2359296 | tf_op jit(solution)/shard_map/convert_element_type | solution.py:129
  21.3 1.6 collective-permute-start.6
  22.9 1.1 broadcast_select_fusion.1
  27.2 14.8 %fusion.64 = (f32[2,8,8]{2,1,0:T(8,128)S(1)}, f32[2,8,8,3072]{3,2,1,0:T(8,128)S(1)}) fusion(f32[3072]{0:T(1024)S(1)} %bitcast.204, f32[3072]{0:T(1024)S(1)} %bitcast.139, f32[3072]{0:T(1024)S(1)} %bitcast.133, f32[3072]{0:T(1024)S(1)} %bitcast.141, f32[3072]{0:T(1024)S(1)} %bitcast.143, f32[3072]{0:T(1024)S(1)} %bitcast.145, f32[3072]{0:T(1024)S(1)} %bitcast.147, ...), kind=kLoop, calls=%fused_computation.344 | loop fusion | flops 39321472 | bytes 4547072 | tf_op jit(solution)/shard_map/jvp()/reduce_sum | solution.py:52
  45.3 1.0 collective-permute-start.1
  46.2 4.1 %concatenate.76 = bf16[32,1152]{1,0:T(8,128)(2,1)} concatenate(bf16[2,1152]{1,0:T(2,128)(2,1)S(1)} %fusion.37, bf16[2,1152]{1,0:T(2,128)(2,1)} %copy-done.38, bf16[4,1152]{1,0:T(4,128)(2,1)} %copy-done.33, bf16[8,1152]{1,0:T(8,128)(2,1)} %collective-permute-done.5, bf16[16,1152]{1,0:T(8,128)(2,1)} %collective-permute-done.6), dimensions={0} | concatenate | bytes 147456 | tf_op jit(solution)/shard_map/concatenate | solution.py:21
  50.3 1.9 %fusion.32 = f32[4,1152]{1,0:T(4,128)} fusion(bf16[1536,1152]{1,0:T(8,128)(2,1)S(1)} %copy-done, bf16[2,1536]{1,0:T(2,128)(2,1)} %collective-permute-done.1, bf16[2,1536]{1,0:T(2,128)(2,1)S(1)} %get-tuple-element.195), kind=kOutput, calls=%fused_computation.287 | convolution fusion | flops 14180352 | bytes 3569664 | tf_op jit(solution)/shard_map/dot_general | solution.py:139
  52.2 1.1 collective-permute-start.2
  53.2 5.6 %concatenate.77 = bf16[64,1152]{1,0:T(8,128)(2,1)} concatenate(bf16[2,1152]{1,0:T(2,128)(2,1)S(1)} %fusion.37, bf16[2,1152]{1,0:T(2,128)(2,1)} %copy-done.38, bf16[4,1152]{1,0:T(4,128)(2,1)} %copy-done.33, bf16[8,1152]{1,0:T(8,128)(2,1)} %collective-permute-done.5, bf16[16,1152]{1,0:T(8,128)(2,1)} %collective-permute-done.6, bf16[32,1152]{1,0:T(8,128)(2,1)} %collective-permute-done.7), dimensions={0} | concatenate | bytes 294912 | tf_op jit(solution)/shard_map/concatenate | solution.py:21
  58.8 0.8 fusion.66
  59.6 0.9 multiply_reduce_fusion.56
  61.8 2.1 %multiply_reduce_fusion.55 = (f32[4]{0:T(128)S(1)}, f32[4,1152]{1,0:T(4,128)}) fusion(f32[4,1152]{1,0:T(4,128)} %copy-done.24, bf16[64,1152]{1,0:T(8,128)(2,1)} %concatenate.77, f32[4]{0:T(128)S(1)} %add_rsqrt_fusion.1), kind=kOutput, calls=%fused_computation.228 | convolution fusion | flops 1204988 | bytes 184352 | tf_op jit(solution)/shard_map/dot_general | solution.py:160
  63.9 0.8 fusion.30
  64.8 1.0 fusion.71
  65.9 1.0 collective-permute-start.8
  67.6 2.7 %collective-permute-start.15 = (bf16[4,3840]{1,0:T(4,128)(2,1)S(1)}, bf16[4,3840]{1,0:T(4,128)(2,1)S(1)}, u32[]{:S(2)}, u32[]{:S(2)}) collective-permute-start(bf16[4,3840]{1,0:T(4,128)(2,1)S(1)} %pad_maximum_fusion.5), channel_id=1, source_target_pairs={{0,16},{2,18},{4,20},{6,22},{8,24},{10,26},{12,28},{14,30},{16,0},... | collective-permute-start | bytes 92168 | tf_op jit(solution)/shard_map/ppermute | solution.py:16
  71.9 1.5 multiply_reduce_fusion
  73.5 3.6 %fusion.61 = (bf16[3072]{0:T(1024)(128)(2,1)}, f32[3072]{0:T(1024)S(1)}, f32[3072]{0:T(1024)S(1)}, f32[3072]{0:T(1024)S(1)}, f32[3072]{0:T(1024)S(1)}, /*index=5...) fusion(bf16[2,8,8,3072]{3,2,1,0:T(8,128)(2,1)S(1)} %copy-done.7, ...), kind=kLoop, calls=%fused_computation.342 | loop fusion | flops 14112768 | bytes 5722112 | tf_op jit(solution)/shard_map/transpose(jvp())/reduce_sum | solution.py:51
  77.3 10.5 %broadcast_multiply_fusion = (f32[2,8,8,3072]{3,2,1,0:T(8,128)}, f32[2,8,8,3072]{3,2,1,0:T(8,128)}, f32[2,8,8,3072]{3,2,1,0:T(8,128)}, f32[2,8,8,3072]{3,2,1,0:T...) fusion(f32[2,8,8,3072]{3,2,1,0:T(8,128)S(1)} %get-tuple-element, ...), kind=kLoop, calls=%fused_computation.137 | loop fusion | flops 7077888 | bytes 30105600 | tf_op jit(solution)/shard_map/transpose(jvp())/mul | solution.py:44
  88.1 9.4 %broadcast_multiply_fusion.1 = (f32[2,8,8,3072]{3,2,1,0:T(8,128)}, f32[2,8,8,3072]{3,2,1,0:T(8,128)}, f32[2,8,8,3072]{3,2,1,0:T(8,128)}, f32[2,8,8,3072]{3,2,1,0...) fusion(f32[2,8,8,3072]{3,2,1,0:T(8,128)S(1)} %get-tuple-element, ...), kind=kLoop, calls=%fused_computation.138 | loop fusion | flops 7077888 | bytes 30105600 | tf_op jit(solution)/shard_map/transpose(jvp())/mul | solution.py:44
  97.6 7.1 %broadcast_multiply_fusion.2 = (f32[2,8,8,3072]{3,2,1,0:T(8,128)}, f32[2,8,8,3072]{3,2,1,0:T(8,128)}, f32[2,8,8,3072]{3,2,1,0:T(8,128)}, f32[2,8,8,3072]{3,2,1,0...) fusion(f32[2,8,8,3072]{3,2,1,0:T(8,128)S(1)} %get-tuple-element, ...), kind=kLoop, calls=%fused_computation.139 | loop fusion | flops 5111808 | bytes 22179840 | tf_op jit(solution)/shard_map/transpose(jvp())/mul | solution.py:44
  104.7 3.3 %multiply_reduce_fusion.49 = (f32[3072]{0:T(1024)S(1)}, f32[3072]{0:T(1024)S(1)}, f32[3072]{0:T(1024)S(1)}, f32[3072]{0:T(1024)S(1)}, f32[3072]{0:T(1024)S(1)}, ...) fusion(f32[2,8,8,3072]{3,2,1,0:T(8,128)S(1)} %get-tuple-element, ...), kind=kLoop, calls=%fused_computation.113 | loop fusion | flops 14100480 | bytes 3366912 | tf_op jit(solution)/shard_map/transpose(jvp())/reduce_sum | solution.py:44
  108.0 3.7 %multiply_reduce_fusion.48 = (f32[3072]{0:T(1024)S(1)}, f32[3072]{0:T(1024)S(1)}, f32[3072]{0:T(1024)S(1)}, f32[3072]{0:T(1024)S(1)}, f32[3072]{0:T(1024)S(1)}, ...) fusion(f32[2,8,8,3072]{3,2,1,0:T(8,128)S(1)} %get-tuple-element, ...), kind=kLoop, calls=%fused_computation.112 | loop fusion | flops 14100480 | bytes 3366912 | tf_op jit(solution)/shard_map/transpose(jvp())/reduce_sum | solution.py:44
  111.8 1.6 pad_add_fusion.7
  113.9 1.3 dynamic-slice_convert_fusion
  116.1 28.3 %pad_add_fusion = f32[2,14,14,3072]{3,2,1,0:T(8,128)} fusion(f32[2,8,8,3072]{3,2,1,0:T(8,128)} %get-tuple-element.88, f32[2,8,8,3072]{3,2,1,0:T(8,128)} %get-tuple-element.89, f32[2,8,8,3072]{3,2,1,0:T(8,128)} %get-tuple-element.90, f32[2,8,8,3072]{3,2,1,0:T(8,128)} %get-tuple-element.91, f32[2,8,8,3072]{3,2,1,0:T(8,128)} %get-tuple-element.92, ...), kind=kLoop, calls=%fused_computation.48 | loop fusion | flops 50577408 | bytes 72450048 | tf_op jit(solution)/shard_map/transpose(jvp())/add_any | solution.py:44
  144.4 0.8 pad_maximum_fusion.3
  145.8 1.2 bitcast_add_fusion
  147.3 1.1 collective-permute-start.10
  148.4 1.3 collective-permute-done.16
  150.5 1.6 collective-permute-start.17
  152.1 1.5 collective-permute-start.11
  153.6 2.8 %collective-permute-done.17 = bf16[16,3840]{1,0:T(8,128)(2,1)S(1)} collective-permute-done((bf16[16,3840]{1,0:T(8,128)(2,1)S(1)}, bf16[16,3840]{1,0:T(8,128)(2,1)S(1)}, u32[]{:S(2)}, u32[]{:S(2)}) %collective-permute-start.17) | collective-permute-done | bytes 122912 | tf_op jit(solution)/shard_map/ppermute | solution.py:16
  157.4 0.9 collective-permute-start.12
  158.3 5.0 %fusion.5 = bf16[2,8,8,3072]{3,2,1,0:T(8,128)(2,1)} fusion(f32[2,8,8,3072]{3,2,1,0:T(8,128)S(1)} %copy-done.8, f32[2,8,8,3072]{3,2,1,0:T(8,128)S(1)} %copy-done.9, f32[2,8,8,3072]{3,2,1,0:T(8,128)} %get-tuple-element.84, f32[2,8,8,3072]{3,2,1,0:T(8,128)} %get-tuple-element.85, f32[2,8,8,3072]{3,2,1,0:T(8,128)} %get-tuple-element.86, ...), kind=kLoop, calls=%fused_computation.58 | loop fusion | flops 3145728 | bytes 11821056 | tf_op jit(solution)/shard_map/convert_element_type | solution.py:197
  163.4 2.0 %collective-permute-start.13 = (bf16[53,768]{1,0:T(8,128)(2,1)S(1)}, bf16[53,768]{1,0:T(8,128)(2,1)S(1)}, u32[]{:S(2)}, u32[]{:S(2)}) collective-permute-start(bf16[53,768]{1,0:T(8,128)(2,1)S(1)} %add_convert_fusion.1), channel_id=1, source_target_pairs={{0,16},{2,18},{4,20},{6,22},{8,24},{10,26},{12,28},{14,30},{16,0},... | collective-permute-start | bytes 244232 | tf_op jit(solution)/shard_map/ppermute | solution.py:16
  165.4 1.0 concatenate.90
  168.4 2.1 %collective-permute-done.13 = bf16[53,768]{1,0:T(8,128)(2,1)S(1)} collective-permute-done((bf16[53,768]{1,0:T(8,128)(2,1)S(1)}, bf16[53,768]{1,0:T(8,128)(2,1)S(1)}, u32[]{:S(2)}, u32[]{:S(2)}) %collective-permute-start.13) | collective-permute-done | bytes 81440 | tf_op jit(solution)/shard_map/ppermute | solution.py:16
  170.6 5.2 %fusion.24 = f32[1536,1152]{1,0:T(8,128)} fusion(bf16[64,3840]{1,0:T(8,128)(2,1)} %copy-done.11), kind=kOutput, calls=%fused_computation.191 | convolution fusion | flops 226492416 | bytes 7421952 | tf_op jit(solution)/shard_map/dot_general | solution.py:186
  (329 shorter events, 18.9 us)
Async XLA Ops:
  0.6 49.7 %copy-start = (bf16[1536,1152]{1,0:T(8,128)(2,1)S(1)}, bf16[1536,1152]{1,0:T(8,128)(2,1)}, u32[]{:S(2)}) copy-start(bf16[1536,1152]{1,0:T(8,128)(2,1)} %param.8) | copy-start | bytes 10616836
  2.5 4.6 %collective-permute-start.3 = (bf16[2,1152]{1,0:T(2,128)(2,1)S(1)}, bf16[2,1152]{1,0:T(2,128)(2,1)S(1)}, u32[]{:S(2)}, u32[]{:S(2)}) collective-permute-start(bf16[2,1152]{1,0:T(2,128)(2,1)S(1)} %fusion.37), channel_id=1, source_target_pairs={{0,1},{1,0},{2,3},{3,2},{4,5},{5,4},{6,7},{7,6},{8,9},{9,8},{10,11... | collective-permute-start | bytes 13832 | tf_op jit(solution)/shard_map/ppermute | solution.py:16
  7.0 16.9 %copy-start.38 = (bf16[2,1152]{1,0:T(2,128)(2,1)}, bf16[2,1152]{1,0:T(2,128)(2,1)S(1)}, u32[]{:S(2)}) copy-start(bf16[2,1152]{1,0:T(2,128)(2,1)S(1)} %collective-permute-done.3) | copy-start | bytes 13828
  7.1 4.8 %collective-permute-start.4 = (bf16[4,1152]{1,0:T(4,128)(2,1)S(1)}, bf16[4,1152]{1,0:T(4,128)(2,1)S(1)}, u32[]{:S(2)}, u32[]{:S(2)}) collective-permute-start(bf16[4,1152]{1,0:T(4,128)(2,1)S(1)} %pad_maximum_fusion.9), channel_id=1, source_target_pairs={{0,16},{2,18},{4,20},{6,22},{8,24},{10,26},{12,28},{14,30},{16,0},... | collective-permute-start | bytes 27656 | tf_op jit(solution)/shard_map/ppermute | solution.py:16
  13.1 7.5 %collective-permute-start.5 = (bf16[8,1152]{1,0:T(8,128)(2,1)}, bf16[8,1152]{1,0:T(8,128)(2,1)}, u32[]{:S(2)}, u32[]{:S(2)}) collective-permute-start(bf16[8,1152]{1,0:T(8,128)(2,1)} %pad_maximum_fusion.7), channel_id=1, source_target_pairs={{0,8},{2,10},{4,12},{6,14},{8,0},{10,2},{12,4},{14,6},{16,24},{18,... | collective-permute-start | bytes 55304 | tf_op jit(solution)/shard_map/ppermute | solution.py:16
  16.6 6.3 %collective-permute-start = (bf16[53,1536]{1,0:T(8,128)(2,1)}, bf16[53,1536]{1,0:T(8,128)(2,1)}, u32[]{:S(2)}, u32[]{:S(2)}) collective-permute-start(bf16[53,1536]{1,0:T(8,128)(2,1)} %pad_maximum_fusion.1), channel_id=1, source_target_pairs={{0,1},{1,0},{2,3},{3,2},{4,5},{5,4},{6,7},{7,6},{8,9},{9,8},{10,11... | collective-permute-start | bytes 488456 | tf_op jit(solution)/shard_map/ppermute | solution.py:16
  21.3 24.9 %collective-permute-start.6 = (bf16[16,1152]{1,0:T(8,128)(2,1)S(1)}, bf16[16,1152]{1,0:T(8,128)(2,1)}, u32[]{:S(2)}, u32[]{:S(2)}) collective-permute-start(bf16[16,1152]{1,0:T(8,128)(2,1)S(1)} %pad_maximum_fusion.4), channel_id=1, source_target_pairs={{0,4},{2,6},{4,0},{6,2},{8,12},{10,14},{12,8},{14,10},{16,20},{18,... | collective-permute-start | bytes 110600 | tf_op jit(solution)/shard_map/ppermute | solution.py:16
  24.1 18.0 %copy-start.39 = (f32[1,3072]{1,0:T(1,128)}, f32[1,3072]{1,0:T(1,128)S(1)}, u32[]{:S(2)}) copy-start(f32[1,3072]{1,0:T(1,128)S(1)} %get-tuple-element.178) | copy-start | bytes 36868
  24.1 18.0 %copy-start.41 = (f32[1,3072]{1,0:T(1,128)}, f32[1,3072]{1,0:T(1,128)S(1)}, u32[]{:S(2)}) copy-start(f32[1,3072]{1,0:T(1,128)S(1)} %get-tuple-element.175) | copy-start | bytes 36868
  24.1 18.0 %copy-start.43 = (f32[1,3072]{1,0:T(1,128)}, f32[1,3072]{1,0:T(1,128)S(1)}, u32[]{:S(2)}) copy-start(f32[1,3072]{1,0:T(1,128)S(1)} %get-tuple-element.176) | copy-start | bytes 36868
  24.1 18.0 %copy-start.45 = (f32[1,3072]{1,0:T(1,128)}, f32[1,3072]{1,0:T(1,128)S(1)}, u32[]{:S(2)}) copy-start(f32[1,3072]{1,0:T(1,128)S(1)} %get-tuple-element.177) | copy-start | bytes 36868
  24.2 17.9 %copy-start.47 = (f32[1,3072]{1,0:T(1,128)}, f32[1,3072]{1,0:T(1,128)S(1)}, u32[]{:S(2)}) copy-start(f32[1,3072]{1,0:T(1,128)S(1)} %get-tuple-element.131) | copy-start | bytes 36868
  24.2 17.9 %copy-start.49 = (f32[1,3072]{1,0:T(1,128)}, f32[1,3072]{1,0:T(1,128)S(1)}, u32[]{:S(2)}) copy-start(f32[1,3072]{1,0:T(1,128)S(1)} %get-tuple-element.132) | copy-start | bytes 36868
  24.2 17.9 %copy-start.51 = (f32[1,3072]{1,0:T(1,128)}, f32[1,3072]{1,0:T(1,128)S(1)}, u32[]{:S(2)}) copy-start(f32[1,3072]{1,0:T(1,128)S(1)} %get-tuple-element.133) | copy-start | bytes 36868
  24.2 17.9 %copy-start.53 = (f32[1,3072]{1,0:T(1,128)}, f32[1,3072]{1,0:T(1,128)S(1)}, u32[]{:S(2)}) copy-start(f32[1,3072]{1,0:T(1,128)S(1)} %get-tuple-element.134) | copy-start | bytes 36868
  24.3 17.9 %copy-start.55 = (f32[1,3072]{1,0:T(1,128)}, f32[1,3072]{1,0:T(1,128)S(1)}, u32[]{:S(2)}) copy-start(f32[1,3072]{1,0:T(1,128)S(1)} %get-tuple-element.135) | copy-start | bytes 36868
  24.3 17.9 %copy-start.57 = (f32[1,3072]{1,0:T(1,128)}, f32[1,3072]{1,0:T(1,128)S(1)}, u32[]{:S(2)}) copy-start(f32[1,3072]{1,0:T(1,128)S(1)} %get-tuple-element.136) | copy-start | bytes 36868
  24.3 17.9 %copy-start.59 = (f32[1,3072]{1,0:T(1,128)}, f32[1,3072]{1,0:T(1,128)S(1)}, u32[]{:S(2)}) copy-start(f32[1,3072]{1,0:T(1,128)S(1)} %get-tuple-element.137) | copy-start | bytes 36868
  24.3 17.9 %copy-start.61 = (f32[1,3072]{1,0:T(1,128)}, f32[1,3072]{1,0:T(1,128)S(1)}, u32[]{:S(2)}) copy-start(f32[1,3072]{1,0:T(1,128)S(1)} %get-tuple-element.138) | copy-start | bytes 36868
  24.3 17.9 %copy-start.107 = (f32[1,3072]{1,0:T(1,128)}, f32[1,3072]{1,0:T(1,128)S(1)}, u32[]{:S(2)}) copy-start(f32[1,3072]{1,0:T(1,128)S(1)} %get-tuple-element.130) | copy-start | bytes 36868
  25.0 17.2 %copy-start.63 = (f32[1,3072]{1,0:T(1,128)}, f32[1,3072]{1,0:T(1,128)S(1)}, u32[]{:S(2)}) copy-start(f32[1,3072]{1,0:T(1,128)S(1)} %get-tuple-element.140) | copy-start | bytes 36868
  25.0 17.2 %copy-start.65 = (f32[1,3072]{1,0:T(1,128)}, f32[1,3072]{1,0:T(1,128)S(1)}, u32[]{:S(2)}) copy-start(f32[1,3072]{1,0:T(1,128)S(1)} %get-tuple-element.141) | copy-start | bytes 36868
  25.0 17.2 %copy-start.67 = (f32[1,3072]{1,0:T(1,128)}, f32[1,3072]{1,0:T(1,128)S(1)}, u32[]{:S(2)}) copy-start(f32[1,3072]{1,0:T(1,128)S(1)} %get-tuple-element.142) | copy-start | bytes 36868
  25.0 17.2 %copy-start.69 = (f32[1,3072]{1,0:T(1,128)}, f32[1,3072]{1,0:T(1,128)S(1)}, u32[]{:S(2)}) copy-start(f32[1,3072]{1,0:T(1,128)S(1)} %get-tuple-element.143) | copy-start | bytes 36868
  25.0 17.3 %copy-start.71 = (f32[1,3072]{1,0:T(1,128)}, f32[1,3072]{1,0:T(1,128)S(1)}, u32[]{:S(2)}) copy-start(f32[1,3072]{1,0:T(1,128)S(1)} %get-tuple-element.144) | copy-start | bytes 36868
  25.0 17.3 %copy-start.73 = (f32[1,3072]{1,0:T(1,128)}, f32[1,3072]{1,0:T(1,128)S(1)}, u32[]{:S(2)}) copy-start(f32[1,3072]{1,0:T(1,128)S(1)} %get-tuple-element.145) | copy-start | bytes 36868
  25.0 17.3 %copy-start.75 = (f32[1,3072]{1,0:T(1,128)}, f32[1,3072]{1,0:T(1,128)S(1)}, u32[]{:S(2)}) copy-start(f32[1,3072]{1,0:T(1,128)S(1)} %get-tuple-element.146) | copy-start | bytes 36868
  25.0 17.3 %copy-start.77 = (f32[1,3072]{1,0:T(1,128)}, f32[1,3072]{1,0:T(1,128)S(1)}, u32[]{:S(2)}) copy-start(f32[1,3072]{1,0:T(1,128)S(1)} %get-tuple-element.147) | copy-start | bytes 36868
  25.7 16.6 %copy-start.87 = (f32[1,3072]{1,0:T(1,128)}, f32[1,3072]{1,0:T(1,128)S(1)}, u32[]{:S(2)}) copy-start(f32[1,3072]{1,0:T(1,128)S(1)} %get-tuple-element.153) | copy-start | bytes 36868
  25.7 16.6 %copy-start.89 = (f32[1,3072]{1,0:T(1,128)}, f32[1,3072]{1,0:T(1,128)S(1)}, u32[]{:S(2)}) copy-start(f32[1,3072]{1,0:T(1,128)S(1)} %get-tuple-element.154) | copy-start | bytes 36868
  27.2 16.8 %copy-start.31 = (f32[1,3072]{1,0:T(1,128)}, f32[1,3072]{1,0:T(1,128)S(1)}, u32[]{:S(2)}) copy-start(f32[1,3072]{1,0:T(1,128)S(1)} %get-tuple-element.187) | copy-start | bytes 36868
  45.3 5.0 %collective-permute-start.1 = (bf16[2,1536]{1,0:T(2,128)(2,1)}, bf16[2,1536]{1,0:T(2,128)(2,1)}, u32[]{:S(2)}, u32[]{:S(2)}) collective-permute-start(bf16[2,1536]{1,0:T(2,128)(2,1)} %get-tuple-element.196), channel_id=1, source_target_pairs={{0,1},{1,0},{2,3},{3,2},{4,5},{5,4},{6,7},{7,6},{8,9},{9,8},{10,11... | collective-permute-start | bytes 18440 | tf_op jit(solution)/shard_map/ppermute | solution.py:16
  50.3 2.9 %collective-permute-start.7 = (bf16[32,1152]{1,0:T(8,128)(2,1)}, bf16[32,1152]{1,0:T(8,128)(2,1)}, u32[]{:S(2)}, u32[]{:S(2)}) collective-permute-start(bf16[32,1152]{1,0:T(8,128)(2,1)} %concatenate.76), channel_id=1, source_target_pairs={{0,2},{2,0},{4,6},{6,4},{8,10},{10,8},{12,14},{14,12},{16,18},{18,... | collective-permute-start | bytes 221192 | tf_op jit(solution)/shard_map/ppermute | solution.py:16
  52.2 6.6 %collective-permute-start.2 = (f32[4,1152]{1,0:T(4,128)}, f32[4,1152]{1,0:T(4,128)}, u32[]{:S(2)}, u32[]{:S(2)}) collective-permute-start(f32[4,1152]{1,0:T(4,128)} %fusion.32), channel_id=1, source_target_pairs={{0,1},{1,0},{2,3},{3,2},{4,5},{5,4},{6,7},{7,6},{8,9},{9,8},{10,11... | collective-permute-start | bytes 55304 | tf_op jit(solution)/shard_map/ppermute | solution.py:16
  65.9 4.4 %collective-permute-start.8 = (f32[2,1536]{1,0:T(2,128)S(1)}, f32[2,1536]{1,0:T(2,128)S(1)}, u32[]{:S(2)}, u32[]{:S(2)}) collective-permute-start(f32[2,1536]{1,0:T(2,128)S(1)} %slice.457), channel_id=1, source_target_pairs={{0,1},{1,0},{2,3},{3,2},{4,5},{5,4},{6,7},{7,6},{8,9},{9,8},{10,11... | collective-permute-start | bytes 36872 | tf_op jit(solution)/shard_map/ppermute | solution.py:16
  67.6 76.7 %collective-permute-start.15 = (bf16[4,3840]{1,0:T(4,128)(2,1)S(1)}, bf16[4,3840]{1,0:T(4,128)(2,1)S(1)}, u32[]{:S(2)}, u32[]{:S(2)}) collective-permute-start(bf16[4,3840]{1,0:T(4,128)(2,1)S(1)} %pad_maximum_fusion.5), channel_id=1, source_target_pairs={{0,16},{2,18},{4,20},{6,22},{8,24},{10,26},{12,28},{14,30},{16,0},... | collective-permute-start | bytes 92168 | tf_op jit(solution)/shard_map/ppermute | solution.py:16
  116.0 29.7 %collective-permute-start.9 = (bf16[53,2,768]{2,1,0:T(2,128)(2,1)}, bf16[53,2,768]{2,1,0:T(2,128)(2,1)S(1)}, u32[]{:S(2)}, u32[]{:S(2)}) collective-permute-start(bf16[53,2,768]{2,1,0:T(2,128)(2,1)} %copy.13), channel_id=1, source_target_pairs={{0,2},{2,0},{4,6},{6,4},{8,10},{10,8},{12,14},{14,12},{16,18},{18,... | collective-permute-start | bytes 488456 | tf_op jit(solution)/shard_map/ppermute | solution.py:16
  116.1 28.3 %copy-start.26 = (bf16[4,1152]{1,0:T(4,128)(2,1)S(1)}, bf16[4,1152]{1,0:T(4,128)(2,1)}, u32[]{:S(2)}) copy-start(bf16[4,1152]{1,0:T(4,128)(2,1)} %multiply_convert_fusion.1) | copy-start | bytes 27652
  116.1 28.3 %copy-start.30 = (bf16[2,1536]{1,0:T(2,128)(2,1)S(1)}, bf16[2,1536]{1,0:T(2,128)(2,1)}, u32[]{:S(2)}) copy-start(bf16[2,1536]{1,0:T(2,128)(2,1)} %copy-done.28) | copy-start | bytes 18436
  116.1 42.2 %copy-start.9 = (f32[2,8,8,3072]{3,2,1,0:T(8,128)S(1)}, f32[2,8,8,3072]{3,2,1,0:T(8,128)}, u32[]{:S(2)}) copy-start(f32[2,8,8,3072]{3,2,1,0:T(8,128)} %get-tuple-element.83) | copy-start | bytes 4718596
  145.2 4.5 %collective-permute-start.16 = (bf16[8,3840]{1,0:T(8,128)(2,1)S(1)}, bf16[8,3840]{1,0:T(8,128)(2,1)S(1)}, u32[]{:S(2)}, u32[]{:S(2)}) collective-permute-start(bf16[8,3840]{1,0:T(8,128)(2,1)S(1)} %pad_maximum_fusion.3), channel_id=1, source_target_pairs={{0,8},{2,10},{4,12},{6,14},{8,0},{10,2},{12,4},{14,6},{16,24},{18,... | collective-permute-start | bytes 184328 | tf_op jit(solution)/shard_map/ppermute | solution.py:16
  147.3 4.7 %collective-permute-start.10 = (bf16[53,768]{1,0:T(8,128)(2,1)S(1)}, bf16[53,768]{1,0:T(8,128)(2,1)S(1)}, u32[]{:S(2)}, u32[]{:S(2)}) collective-permute-start(bf16[53,768]{1,0:T(8,128)(2,1)S(1)} %bitcast.203), channel_id=1, source_target_pairs={{0,1},{1,0},{2,3},{3,2},{4,5},{5,4},{6,7},{7,6},{8,9},{9,8},{10,11... | collective-permute-start | bytes 244232 | tf_op jit(solution)/shard_map/ppermute | solution.py:16
  150.5 5.9 %collective-permute-start.17 = (bf16[16,3840]{1,0:T(8,128)(2,1)S(1)}, bf16[16,3840]{1,0:T(8,128)(2,1)S(1)}, u32[]{:S(2)}, u32[]{:S(2)}) collective-permute-start(bf16[16,3840]{1,0:T(8,128)(2,1)S(1)} %pad_maximum_fusion.2), channel_id=1, source_target_pairs={{0,4},{2,6},{4,0},{6,2},{8,12},{10,14},{12,8},{14,10},{16,20},{18,... | collective-permute-start | bytes 368648 | tf_op jit(solution)/shard_map/ppermute | solution.py:16
  152.1 5.3 %collective-permute-start.11 = (bf16[53,768]{1,0:T(8,128)(2,1)S(1)}, bf16[53,768]{1,0:T(8,128)(2,1)S(1)}, u32[]{:S(2)}, u32[]{:S(2)}) collective-permute-start(bf16[53,768]{1,0:T(8,128)(2,1)S(1)} %fusion.26), channel_id=1, source_target_pairs={{0,4},{2,6},{4,0},{6,2},{8,12},{10,14},{12,8},{14,10},{16,20},{18,... | collective-permute-start | bytes 244232 | tf_op jit(solution)/shard_map/ppermute | solution.py:16
  157.2 8.1 %collective-permute-start.18 = (bf16[32,3840]{1,0:T(8,128)(2,1)S(1)}, bf16[32,3840]{1,0:T(8,128)(2,1)}, u32[]{:S(2)}, u32[]{:S(2)}) collective-permute-start(bf16[32,3840]{1,0:T(8,128)(2,1)S(1)} %pad_maximum_fusion), channel_id=1, source_target_pairs={{0,2},{2,0},{4,6},{6,4},{8,10},{10,8},{12,14},{14,12},{16,18},{18,... | collective-permute-start | bytes 737288 | tf_op jit(solution)/shard_map/ppermute | solution.py:16
  157.4 6.0 %collective-permute-start.12 = (bf16[53,768]{1,0:T(8,128)(2,1)S(1)}, bf16[53,768]{1,0:T(8,128)(2,1)S(1)}, u32[]{:S(2)}, u32[]{:S(2)}) collective-permute-start(bf16[53,768]{1,0:T(8,128)(2,1)S(1)} %add_convert_fusion.2), channel_id=1, source_target_pairs={{0,8},{2,10},{4,12},{6,14},{8,0},{10,2},{12,4},{14,6},{16,24},{18,... | collective-permute-start | bytes 244232 | tf_op jit(solution)/shard_map/ppermute | solution.py:16
  163.4 7.1 %collective-permute-start.13 = (bf16[53,768]{1,0:T(8,128)(2,1)S(1)}, bf16[53,768]{1,0:T(8,128)(2,1)S(1)}, u32[]{:S(2)}, u32[]{:S(2)}) collective-permute-start(bf16[53,768]{1,0:T(8,128)(2,1)S(1)} %add_convert_fusion.1), channel_id=1, source_target_pairs={{0,16},{2,18},{4,20},{6,22},{8,24},{10,26},{12,28},{14,30},{16,0},... | collective-permute-start | bytes 244232 | tf_op jit(solution)/shard_map/ppermute | solution.py:16
  170.5 5.3 %collective-permute-start.14 = (bf16[53,768]{1,0:T(8,128)(2,1)S(1)}, bf16[53,768]{1,0:T(8,128)(2,1)S(1)}, u32[]{:S(2)}, u32[]{:S(2)}) collective-permute-start(bf16[53,768]{1,0:T(8,128)(2,1)S(1)} %add_convert_fusion), channel_id=1, source_target_pairs={{0,2},{2,0},{4,6},{6,4},{8,10},{10,8},{12,14},{14,12},{16,18},{18,... | collective-permute-start | bytes 244232 | tf_op jit(solution)/shard_map/ppermute | solution.py:16
  (95 other events, 758.2 us)

commit v2 on v1

v2 whole, which is shorter than its diff:
```python
import jax
import jax.numpy as jnp
from jax import lax
from jax.experimental import pallas as pl
from jax.experimental.pallas import tpu as pltpu
from jax.sharding import PartitionSpec as P

EPS = 1e-06
LOGIT_SCALE = 10.0
LOGIT_BIAS = -2.0
KER = 7
REACH = KER // 2
TAPS = KER * KER
LANES = 128
ROWS_PAD = 64
BF = jnp.bfloat16
F32 = jnp.float32


def swap(value, axis, mask):
    count = lax.axis_size(axis)
    return lax.ppermute(value, axis, [(source, source ^ mask) for source in range(count)])


def tree_gather(value, axis, masks):
    for mask in masks:
        value = jnp.concatenate([value, swap(value, axis, mask)], axis=0)
    return value


def bits_up(count):
    masks = []
    mask = 1
    while mask < count:
        masks.append(mask)
        mask *= 2
    return masks


def params(mebibytes):
    return pltpu.CompilerParams(vmem_limit_bytes=mebibytes * 1024 * 1024)


VM = pl.BlockSpec(memory_space=pltpu.VMEM)
SM = pl.BlockSpec(memory_space=pltpu.SMEM)


def lane_block(index, width):
    return pl.ds(pl.multiple_of(index * width, LANES), width)


def shift_cols(value, step):
    if step == 0:
        return value
    width = value.shape[0]
    rolled = pltpu.roll(value, (-step) % width, 0)
    col = lax.broadcasted_iota(jnp.int32, value.shape, 0)
    inside = (col < width - step) if step > 0 else (col >= -step)
    return jnp.where(inside, rolled, 0.0)


def conv_rows(rows, tap_row, flip):
    height = len(rows)
    sums = [None] * height
    for b in range(KER):
        moved = [shift_cols(row, b - REACH) for row in rows]
        for a in range(KER):
            tap = (KER - 1 - a) * KER + (KER - 1 - b) if flip else a * KER + b
            weight = tap_row(tap)
            for h in range(max(0, REACH - a), min(height, height + REACH - a)):
                term = moved[h + a - REACH] * weight
                sums[h] = term if sums[h] is None else sums[h] + term
    return sums


def forward_kernel(members, member_ref, x_ref, *refs):
    kernel_refs, refs = refs[:members], refs[members:]
    term_refs, refs = refs[:members], refs[members:]
    piece_refs, refs = refs[:members], refs[members:]
    weight_ref, mixed_ref, mean_ref, rstd_ref, hatsum_ref, hat_ref, hrstd_ref, sum_ref, pool_ref = refs
    images, height, width, channels = x_ref.shape
    share = channels // members
    tiles = channels // LANES
    cells = height * width
    member = member_ref[0]
    for m in range(members):
        lanes = lane_block(member ^ m, share)
        weight_ref[0:TAPS, lanes] = kernel_refs[m][...].astype(F32)
        weight_ref[TAPS : TAPS + 4, lanes] = term_refs[m][...].astype(F32)
    sum_ref[...] = jnp.zeros_like(sum_ref)

    @pl.loop(0, tiles)
    def _(t):
        lanes = lane_block(t, LANES)
        bias = weight_ref[TAPS : TAPS + 1, lanes]
        for i in range(images):
            rows = [x_ref[i, h, :, lanes].astype(F32) for h in range(height)]
            sums = conv_rows(rows, lambda tap: weight_ref[tap : tap + 1, lanes], False)
            for h in range(height):
                value = sums[h] + bias
                mixed_ref[i, h, :, lanes] = value
                sum_ref[i, h] += value

    mean = jnp.sum(sum_ref[...], axis=-1, keepdims=True) * (1.0 / channels)
    mean_ref[...] = jnp.broadcast_to(mean, mean_ref.shape)
    sum_ref[...] = jnp.zeros_like(sum_ref)

    @pl.loop(0, tiles)
    def _(t):
        lanes = lane_block(t, LANES)
        for i in range(images):
            for h in range(height):
                value = mixed_ref[i, h, :, lanes] - mean_ref[i, h]
                sum_ref[i, h] += value * value

    var = jnp.sum(sum_ref[...], axis=-1, keepdims=True) * (1.0 / channels)
    rstd_ref[...] = jnp.broadcast_to(lax.rsqrt(var + EPS), rstd_ref.shape)

    @pl.loop(0, tiles)
    def _(t):
        lanes = lane_block(t, LANES)
        scale = weight_ref[TAPS + 1 : TAPS + 2, lanes] * weight_ref[TAPS + 2 : TAPS + 3, lanes]
        for i in range(images):
            hats = jnp.zeros((width, LANES), F32)
            plain = jnp.zeros((width, LANES), F32)
            for h in range(height):
                hats = hats + (mixed_ref[i, h, :, lanes] - mean_ref[i, h]) * rstd_ref[i, h]
                plain = plain + x_ref[i, h, :, lanes].astype(F32)
            hat_row = jnp.sum(hats, axis=0, keepdims=True)
            hatsum_ref[i : i + 1, lanes] = hat_row
            pool_ref[i : i + 1, lanes] = (
                jnp.sum(plain, axis=0, keepdims=True) + scale * hat_row
            ) * (1.0 / cells)

    pooled = pool_ref[...]
    centered = pooled - jnp.mean(pooled, axis=1, keepdims=True)
    head_rstd = lax.rsqrt(jnp.mean(centered * centered, axis=1, keepdims=True) + EPS)
    hat = centered * head_rstd
    hat_ref[...] = hat
    hrstd_ref[...] = jnp.broadcast_to(head_rstd, hrstd_ref.shape)
    pool_ref[...] = hat * weight_ref[TAPS + 3 : TAPS + 4, :]
    for m in range(members):
        piece_refs[m][...] = pool_ref[:, lane_block(member ^ m, share)].astype(BF)


def forward_block(member, image_maps, kernels, terms):
    images, height, width, channels = image_maps.shape
    members = len(kernels)
    share = channels // members
    shape = jax.ShapeDtypeStruct
    cell = (images, height, width, LANES)
    outs = [shape((images, share), BF)] * members + [
        shape((TAPS + 7, channels), F32),
        shape(image_maps.shape, F32),
        shape(cell, F32),
        shape(cell, F32),
        shape((images, channels), F32),
        shape((images, channels), F32),
        shape((images, LANES), F32),
    ]
    result = pl.pallas_call(
        lambda *refs: forward_kernel(members, *refs),
        out_shape=outs,
        in_specs=[SM, VM] + [VM] * (2 * members),
        out_specs=[VM] * len(outs),
        scratch_shapes=[pltpu.VMEM(cell, F32), pltpu.VMEM((images, channels), F32)],
        compiler_params=params(24),
        name="forward_block",
    )(member, image_maps, *kernels, *terms)
    return result[:members], result[members:]


def head_kernel(members, *refs):
    group = jnp.concatenate([ref[...].astype(F32) for ref in refs[:members]], axis=0).astype(BF)
    weight_ref, group_ref, out_ref = refs[members:]
    group_ref[...] = group
    out_ref[...] = jnp.dot(group, weight_ref[...], preferred_element_type=F32)


def head_project(pieces, head_weight):
    members = len(pieces)
    share, embed_width = head_weight.shape
    rows = members * pieces[0].shape[0]
    return pl.pallas_call(
        lambda *refs: head_kernel(members, *refs),
        out_shape=[
            jax.ShapeDtypeStruct((rows, share), BF),
            jax.ShapeDtypeStruct((rows, embed_width), F32),
        ],
        in_specs=[VM] * (members + 1),
        out_specs=[VM, VM],
        compiler_params=params(24),
        name="head_project",
    )(*pieces, head_weight)


def pair_weights(images, texts):
    logits = (
        LOGIT_SCALE
        * lax.dot_general(images, texts, (((1,), (1,)), ((), ())), preferred_element_type=F32)
        + LOGIT_BIAS
    )
    here = lax.broadcasted_iota(jnp.int32, logits.shape, 0)
    there = lax.broadcasted_iota(jnp.int32, logits.shape, 1)
    positive = jnp.where(here == there, 1.0, 0.0).astype(F32)
    return (jax.nn.sigmoid(logits) - positive).astype(BF)


def loss_kernel(members, *refs):
    partials, refs = refs[:members], refs[members:]
    text_ref, weight_ref, unit_ref, grad_ref = refs[:4]
    piece_refs = refs[4:]
    total_rows = partials[0].shape[0]
    rows = total_rows // members
    embed = partials[0][...]
    for m in range(1, members):
        embed = embed + jnp.concatenate(
            [partials[m][(k ^ m) * rows : (k ^ m) * rows + rows, :] for k in range(members)], axis=0
        )
    inv = lax.rsqrt(jnp.sum(embed * embed, axis=1, keepdims=True) + EPS)
    unit = embed * inv
    unit_bf = unit.astype(BF)
    unit_ref[...] = unit_bf
    texts = text_ref[...]
    unit_grad = LOGIT_SCALE * jnp.dot(
        pair_weights(unit_bf, texts), texts, preferred_element_type=F32
    )
    along = jnp.sum(unit * unit_grad, axis=1, keepdims=True)
    embed_grad = (inv * (unit_grad - unit * along)).astype(BF)
    grad_ref[...] = embed_grad
    part = lax.dot_general(
        embed_grad, weight_ref[...], (((1,), (1,)), ((), ())), preferred_element_type=F32
    )
    for m in range(members):
        piece_refs[m][...] = part[m * rows : m * rows + rows]


def loss_block(partials, text_all, head_weight):
    members = len(partials)
    total_rows, embed_width = partials[0].shape
    share = head_weight.shape[0]
    shape = jax.ShapeDtypeStruct
    result = pl.pallas_call(
        lambda *refs: loss_kernel(members, *refs),
        out_shape=[
            shape((total_rows, embed_width), BF),
            shape((total_rows, embed_width), BF),
        ]
        + [shape((total_rows // members, share), F32)] * members,
        in_specs=[VM] * (members + 2),
        out_specs=[VM] * (members + 2),
        compiler_params=params(24),
        name="loss_block",
    )(*partials, text_all, head_weight)
    return result[0], result[1], result[2:]


def terms_kernel(members, place_ref, *refs):
    grad_refs, refs = refs[:members], refs[members:]
    x_ref, weight_ref, mixed_ref, mean_ref, rstd_ref, hatsum_ref, hat_ref, hrstd_ref = refs[:8]
    keep_ref, give_ref, flow_ref, shared_ref, full_ref, scaled_ref, dot_ref, sums_ref, taps_ref = refs[8:]
    images, height, width, channels = x_ref.shape
    share = channels // members
    tiles = channels // LANES
    cells = height * width
    member = place_ref[0]
    core = place_ref[1]
    for m in range(members):
        full_ref[:, lane_block(member ^ m, share)] = grad_refs[m][...]
    grad = full_ref[...]
    hat = hat_ref[...]
    sums_ref[...] = jnp.zeros_like(sums_ref)
    sums_ref[TAPS + 3 : TAPS + 4, :] = jnp.sum(grad * hat, axis=0, keepdims=True)
    inner = grad * weight_ref[TAPS + 3 : TAPS + 4, :]
    shared = (
        hrstd_ref[:, 0:1]
        * (
            inner
            - jnp.mean(inner, axis=1, keepdims=True)
            - hat * jnp.mean(inner * hat, axis=1, keepdims=True)
        )
        * (1.0 / cells)
    )
    shared_ref[...] = shared
    gain = weight_ref[TAPS + 1 : TAPS + 2, :]
    scale = weight_ref[TAPS + 2 : TAPS + 3, :]
    hat_grad = shared * hatsum_ref[...]
    hat_total = jnp.sum(hat_grad, axis=0, keepdims=True)
    sums_ref[TAPS + 1 : TAPS + 2, :] = hat_total * scale
    sums_ref[TAPS + 2 : TAPS + 3, :] = hat_total * gain
    scaled = shared * (gain * scale)
    scaled_mean = jnp.mean(scaled, axis=1, keepdims=True)
    scaled_ref[...] = scaled - scaled_mean
    dot_ref[...] = jnp.zeros_like(dot_ref)

    @pl.loop(0, tiles)
    def _(t):
        lanes = lane_block(t, LANES)
        for i in range(images):
            factor = scaled_ref[i : i + 1, lanes]
            for h in range(height):
                dot_ref[i, h] += factor * (mixed_ref[i, h, :, lanes] - mean_ref[i, h])

    dots = jnp.sum(dot_ref[...], axis=-1, keepdims=True) * (1.0 / channels)
    dot_ref[...] = jnp.broadcast_to(dots, dot_ref.shape) * rstd_ref[...] * rstd_ref[...]

    @pl.loop(0, tiles)
    def _(t):
        lanes = lane_block(t, LANES)
        flows = []
        for i in range(images):
            factor = scaled_ref[i : i + 1, lanes]
            flow_rows = []
            for h in range(height):
                centered = mixed_ref[i, h, :, lanes] - mean_ref[i, h]
                flow = rstd_ref[i, h] * (factor - centered * dot_ref[i, h])
                flow_ref[i, h, :, lanes] = flow
                flow_rows.append(flow)
            flows.append(flow_rows)
        bias = flows[0][0]
        for i in range(images):
            for h in range(height):
                if i or h:
                    bias = bias + flows[i][h]
        taps_ref[TAPS * width : TAPS * width + width, :] = bias
        for b in range(KER):
            totals = [None] * KER
            for i in range(images):
                moved = [shift_cols(x_ref[i, h, :, lanes].astype(F32), b - REACH) for h in range(height)]
                for a in range(KER):
                    for h in range(max(0, REACH - a), min(height, height + REACH - a)):
                        term = flows[i][h] * moved[h + a - REACH]
                        totals[a] = term if totals[a] is None else totals[a] + term
            for a in range(KER):
                tap = a * KER + b
                taps_ref[tap * width : tap * width + width, :] = totals[a]
        rows = TAPS + 1
        total = taps_ref[pl.ds(0, rows, stride=width), :]
        for s in range(1, width):
            total = total + taps_ref[pl.ds(s, rows, stride=width), :]
        sums_ref[0:rows, lanes] = total

    half = ROWS_PAD // 2
    for m in range(members):
        lanes = lane_block(member ^ m, share)
        keep_ref[m] = sums_ref[pl.ds(pl.multiple_of(core * half, half), half), lanes].astype(BF)
        give_ref[m] = sums_ref[pl.ds(pl.multiple_of((1 - core) * half, half), half), lanes].astype(BF)


def terms_block(place, grads, image_maps, weights, mixed, mean, rstd, hatsum, hat, hrstd):
    images, height, width, channels = image_maps.shape
    members = len(grads)
    share = channels // members
    shape = jax.ShapeDtypeStruct
    half = shape((members, ROWS_PAD // 2, share), BF)
    return pl.pallas_call(
        lambda *refs: terms_kernel(members, *refs),
        out_shape=[half, half, shape(image_maps.shape, F32), shape((images, channels), F32)],
        in_specs=[SM] + [VM] * (members + 8),
        out_specs=[VM] * 4,
        scratch_shapes=[
            pltpu.VMEM((images, channels), F32),
            pltpu.VMEM((images, channels), F32),
            pltpu.VMEM((images, height, width, LANES), F32),
            pltpu.VMEM((ROWS_PAD, channels), F32),
            pltpu.VMEM(((TAPS + 1) * width, LANES), F32),
        ],
        compiler_params=params(24),
        name="terms_block",
    )(place, *grads, image_maps, weights, mixed, mean, rstd, hatsum, hat, hrstd)


def images_kernel(flow_ref, weight_ref, shared_ref, out_ref):
    images, height, width, channels = flow_ref.shape

    @pl.loop(0, channels // LANES)
    def _(t):
        lanes = lane_block(t, LANES)
        for i in range(images):
            rows = [flow_ref[i, h, :, lanes] for h in range(height)]
            sums = conv_rows(rows, lambda tap: weight_ref[tap : tap + 1, lanes], True)
            for h in range(height):
                out_ref[i, h, :, lanes] = (sums[h] + shared_ref[i : i + 1, lanes]).astype(BF)


def images_block(flow, weights, shared):
    return pl.pallas_call(
        images_kernel,
        out_shape=jax.ShapeDtypeStruct(flow.shape, BF),
        in_specs=[VM] * 3,
        out_specs=VM,
        compiler_params=params(24),
        cost_estimate=pl.CostEstimate(
            flops=2 * TAPS * flow.size, bytes_accessed=6 * flow.size, transcendentals=0
        ),
        name="images_block",
    )(flow, weights, shared)


def to_unit(vectors):
    return vectors * lax.rsqrt(jnp.sum(vectors * vectors, axis=1, keepdims=True) + EPS)


def reduce_terms(keep, give, core, members, dp_masks):
    chip = keep.astype(F32) + swap(give, "dp", 1).astype(F32)
    sent = chip.astype(BF)
    total = sent[0].astype(F32)
    for m in range(1, members):
        total = total + swap(sent[m], "fsdp", m).astype(F32)
    for mask in dp_masks:
        sent = total.astype(BF)
        total = sent.astype(F32) + swap(sent, "dp", mask).astype(F32)
    sent = total.astype(BF)
    other = swap(sent, "dp", 1)
    low = jnp.where(core == 0, sent, other)
    high = jnp.where(core == 0, other, sent)
    return jnp.concatenate([low, high], axis=0).astype(F32)


def per_device(image_maps, dw_kernel, channel_terms, head_weight, text_feats):
    rows = image_maps.shape[0]
    members = lax.axis_size("fsdp")
    member = lax.axis_index("fsdp")
    core = lax.axis_index("dp") % 2
    place = jnp.stack([member, core]).astype(jnp.int32)
    others = range(1, members)
    pair_masks = bits_up(members)
    dp_masks = bits_up(lax.axis_size("dp"))
    down = dp_masks[::-1]
    share, width = head_weight.shape

    kernels = [dw_kernel] + [swap(dw_kernel, "fsdp", m) for m in others]
    terms = [channel_terms] + [swap(channel_terms, "fsdp", m) for m in others]

    text_unit, text_back = jax.vjp(to_unit, text_feats.astype(F32))
    own_text = text_unit.astype(BF)
    text_all = tree_gather(tree_gather(own_text, "fsdp", pair_masks), "dp", down)

    pieces, saved = forward_block(place, image_maps, kernels, terms)
    weights = saved[0]
    pieces = [pieces[0]] + [swap(pieces[m], "fsdp", m) for m in others]
    group, partial = head_project(pieces, head_weight)
    partials = [partial] + [swap(partial, "fsdp", m) for m in others]
    unit_bf, embed_grad, grads = loss_block(partials, text_all, head_weight)
    grads = [grads[0]] + [swap(grads[m], "fsdp", m) for m in others]

    keep, give, flow, shared = terms_block(place, grads, image_maps, *saved)
    image_grads = images_block(flow, weights, shared)

    packed = tree_gather(jnp.concatenate([group, embed_grad, unit_bf], axis=1), "dp", down)
    group_all = packed[:, :share]
    grad_all = packed[:, share : share + width]
    unit_all = packed[:, share + width :]

    sums = reduce_terms(keep, give, core, members, dp_masks[1:])

    head_grads = lax.dot_general(
        group_all, grad_all, (((0,), (0,)), ((), ())), preferred_element_type=F32
    )
    text_sum = LOGIT_SCALE * lax.dot_general(
        pair_weights(unit_all, own_text),
        unit_all,
        (((0,), (0,)), ((), ())),
        preferred_element_type=F32,
    )
    text_grads = text_back(text_sum)[0]
    return (image_grads, sums[:TAPS], sums[TAPS : TAPS + 4], head_grads, text_grads)


def solution(mesh):
    in_specs = (
        P(("dp", "fsdp"), None, None, None),
        P(None, "fsdp"),
        P(None, "fsdp"),
        P("fsdp", None),
        P(("dp", "fsdp"), None),
    )
    out_specs = (
        P(("dp", "fsdp"), None, None, None),
        P(None, "fsdp"),
        P(None, "fsdp"),
        P("fsdp", None),
        P(("dp", "fsdp"), None),
    )
    return jax.shard_map(
        per_device, mesh=mesh, in_specs=in_specs, out_specs=out_specs, check_vma=False
    )
```

time: 178 us -> 91 us (0.51)
  other arithmetic: 113 us -> 3.38 us
  Pallas kernels: 0 us -> 22.9 us
  waiting for transfers between devices: 9.54 us -> 25.9 us
  local copies, waits for them, and re-layouts: 16.8 us -> 5.89 us
  matrix products: 10.7 us -> 4.65 us
  starting transfers between devices: 24.6 us -> 27.1 us
    add_any x2 -> x0, other arithmetic: 29.8 us -> none  [the longest x1 28.3 us: depthwise(): padded[:, row_tap:row_tap + height, col_tap:col_tap + width, :]]
    reduce_sum x12 -> x0, other arithmetic: 29.5 us -> none  [the longest x1 14.8 us: block_pool(): row_mean = jnp.mean(mixed, axis=3, keepdims=True)]
    mul x3 -> x0, other arithmetic: 27 us -> none  [depthwise(): padded[:, row_tap:row_tap + height, col_tap:col_tap + width, :]]
    pallas_call x0 -> x5, Pallas kernels: none -> 22.9 us  [the longest x1 7.68 us: forward_block(): pl.pallas_call(lambda *refs: forward_kernel(members, *refs), out_shape=ou...]
    ppermute x19 -> x20, waiting for transfers between devices: 9.54 us -> 25.9 us  [swap(): lax.ppermute(value, axis, [(source, source ^ mask) for source in range(co...]
    convert_element_type x9 -> x2, other arithmetic: 11.4 us -> 0.08 us  [the longest x1 0.05 us: reduce_terms(): sent = chip.astype(BF)]
    concatenate x3, local copies, waits for them, and re-layouts: 10.7 us -> 0.31 us  [tree_gather(): value = jnp.concatenate([value, swap(value, axis, mask)], axis=0)]
    dot_general x3 -> x0, matrix products: 4.98 us -> none  [the longest x1 2.11 us: per_device(): jnp.dot(pair_weights(unit_bf, text_all), text_all, preferred_element_type...]
  transfers between devices with their start and end apart: 19 -> 20, of which waited for: 6 -> 14; matrix products, arithmetic and copies ran while one was open for 72% -> 7% of each run, Pallas kernels for 0% -> 23%
where the time goes in v2:
time: 91 us; the launch traced here: 90.6 us
  starting transfers between devices  27.1 us (30%)
  waiting for transfers between devices  25.9 us (28%)
  Pallas kernels  22.9 us (25%)
  local copies, waits for them, and re-layouts  5.89 us (6%)
  matrix products  4.65 us (5%)
  other arithmetic  3.38 us (4%)
    ppermute x20, starting transfers between devices, swap(): lax.ppermute(value, axis, [(source, source ^ mask) for source in range(co...  27.1 us
    ppermute x20, waiting for transfers between devices, swap(): lax.ppermute(value, axis, [(source, source ^ mask) for source in range(co...  25.9 us
    pallas_call x1, Pallas kernels, forward_block(): pl.pallas_call(lambda *refs: forward_kernel(members, *refs), out_shape=ou...  7.68 us
    pallas_call x1, Pallas kernels, terms_block(): pl.pallas_call(lambda *refs: terms_kernel(members, *refs), out_shape=[hal...  7.07 us
    pallas_call x1, Pallas kernels, images_block(): pl.pallas_call(images_kernel, out_shape=jax.ShapeDtypeStruct(flow.shape,...  6.13 us
    unnamed x16, local copies, waits for them, and re-layouts  4.81 us
    dot_general x1, matrix products, per_device(): lax.dot_general(group_all, grad_all, (((0,), (0,)), ((), ())), preferred_...  4.08 us
  transfers between devices with their start and end apart: 20, of which 14 were waited for; matrix products, arithmetic and copies ran while one was open for 7% of the time, Pallas kernels for 23%

profile of v2, /device:TPU:0, one launch (start us, length us, event | category | flops | bytes accessed | tf_op | source)
XLA Modules:
  0.0 90.6 jit_solution(12633463767418938064)
XLA Ops:
  0.6 0.8 fusion.19
  1.5 0.8 fusion.20
  2.2 3.0 %collective-permute-start.4 = (bf16[2,1152]{1,0:T(2,128)(2,1)S(1)}, bf16[2,1152]{1,0:T(2,128)(2,1)S(1)}, u32[]{:S(2)}, u32[]{:S(2)}) collective-permute-start(bf16[2,1152]{1,0:T(2,128)(2,1)S(1)} %fusion.20), channel_id=1, source_target_pairs={{0,1},{1,0},{2,3},{3,2},{4,5},{5,4},{6,7},{7,6},{8,9},{9,8},{10,11... | collective-permute-start | bytes 13832 | tf_op jit(solution)/shard_map/ppermute | solution.py:22
  5.2 1.6 %collective-permute-done.4 = bf16[2,1152]{1,0:T(2,128)(2,1)S(1)} collective-permute-done((bf16[2,1152]{1,0:T(2,128)(2,1)S(1)}, bf16[2,1152]{1,0:T(2,128)(2,1)S(1)}, u32[]{:S(2)}, u32[]{:S(2)}) %collective-permute-start.4) | collective-permute-done | bytes 4640 | tf_op jit(solution)/shard_map/ppermute | solution.py:22
  6.8 3.2 %collective-permute-start.5 = (bf16[4,1152]{1,0:T(4,128)(2,1)S(1)}, bf16[4,1152]{1,0:T(4,128)(2,1)S(1)}, u32[]{:S(2)}, u32[]{:S(2)}) collective-permute-start(bf16[4,1152]{1,0:T(4,128)(2,1)S(1)} %pad_maximum_fusion.5), channel_id=1, source_target_pairs={{0,16},{2,18},{4,20},{6,22},{8,24},{10,26},{12,28},{14,30},{16,0},... | collective-permute-start | bytes 27656 | tf_op jit(solution)/shard_map/ppermute | solution.py:22
  10.0 1.6 %collective-permute-done.5 = bf16[4,1152]{1,0:T(4,128)(2,1)S(1)} collective-permute-done((bf16[4,1152]{1,0:T(4,128)(2,1)S(1)}, bf16[4,1152]{1,0:T(4,128)(2,1)S(1)}, u32[]{:S(2)}, u32[]{:S(2)}) %collective-permute-start.5) | collective-permute-done | bytes 9248 | tf_op jit(solution)/shard_map/ppermute | solution.py:22
  11.6 2.0 %collective-permute-start.6 = (bf16[8,1152]{1,0:T(8,128)(2,1)S(1)}, bf16[8,1152]{1,0:T(8,128)(2,1)S(1)}, u32[]{:S(2)}, u32[]{:S(2)}) collective-permute-start(bf16[8,1152]{1,0:T(8,128)(2,1)S(1)} %pad_maximum_fusion.4), channel_id=1, source_target_pairs={{0,8},{2,10},{4,12},{6,14},{8,0},{10,2},{12,4},{14,6},{16,24},{18,... | collective-permute-start | bytes 55304 | tf_op jit(solution)/shard_map/ppermute | solution.py:22
  13.6 1.5 %collective-permute-start = (bf16[49,1536]{1,0:T(8,128)(2,1)}, bf16[49,1536]{1,0:T(8,128)(2,1)S(1)}, u32[]{:S(2)}, u32[]{:S(2)}) collective-permute-start(bf16[49,1536]{1,0:T(8,128)(2,1)} %refs_2_.2), channel_id=1, source_target_pairs={{0,1},{1,0},{2,3},{3,2},{4,5},{5,4},{6,7},{7,6},{8,9},{9,8},{10,11... | collective-permute-start | bytes 451592 | tf_op jit(solution)/shard_map/ppermute | solution.py:22
  15.1 0.3 collective-permute-done.6
  15.5 1.9 %collective-permute-start.7 = (bf16[16,1152]{1,0:T(8,128)(2,1)S(1)}, bf16[16,1152]{1,0:T(8,128)(2,1)S(1)}, u32[]{:S(2)}, u32[]{:S(2)}) collective-permute-start(bf16[16,1152]{1,0:T(8,128)(2,1)S(1)} %pad_maximum_fusion.3), channel_id=1, source_target_pairs={{0,4},{2,6},{4,0},{6,2},{8,12},{10,14},{12,8},{14,10},{16,20},{18,... | collective-permute-start | bytes 110600 | tf_op jit(solution)/shard_map/ppermute | solution.py:22
  17.4 1.5 %collective-permute-start.1 = (bf16[4,1536]{1,0:T(4,128)(2,1)}, bf16[4,1536]{1,0:T(4,128)(2,1)S(1)}, u32[]{:S(2)}, u32[]{:S(2)}) collective-permute-start(bf16[4,1536]{1,0:T(4,128)(2,1)} %refs_4_.1), channel_id=1, source_target_pairs={{0,1},{1,0},{2,3},{3,2},{4,5},{5,4},{6,7},{7,6},{8,9},{9,8},{10,11... | collective-permute-start | bytes 36872 | tf_op jit(solution)/shard_map/ppermute | solution.py:22
  18.9 0.6 collective-permute-done.7
  19.7 1.5 %collective-permute-done.1.refs_5_ = bf16[4,1536]{1,0:T(4,128)(2,1)S(1)} collective-permute-done((bf16[4,1536]{1,0:T(4,128)(2,1)}, bf16[4,1536]{1,0:T(4,128)(2,1)S(1)}, u32[]{:S(2)}, u32[]{:S(2)}) %collective-permute-start.1) | collective-permute-done | bytes 12320 | tf_op jit(solution)/shard_map/ppermute | solution.py:22
  21.3 1.1 %copy-done.2 = bf16[2,8,8,3072]{3,2,1,0:T(8,128)(2,1)S(1)} copy-done((bf16[2,8,8,3072]{3,2,1,0:T(8,128)(2,1)S(1)}, bf16[2,8,8,3072]{3,2,1,0:T(8,128)(2,1)}, u32[]{:S(2)}) %copy-start.2) | copy-done | bytes 786456
  22.4 0.9 %copy-done.4 = bf16[49,1536]{1,0:T(8,128)(2,1)S(1)} copy-done((bf16[49,1536]{1,0:T(8,128)(2,1)S(1)}, bf16[49,1536]{1,0:T(8,128)(2,1)}, u32[]{:S(2)}) %copy-start.4) | copy-done | bytes 150552
  23.3 0.7 copy-done.5
  24.0 7.7 %forward_block.1 = (bf16[2,1536]{1,0:T(2,128)(2,1)S(1)}, bf16[2,1536]{1,0:T(2,128)(2,1)S(1)}, f32[56,3072]{1,0:T(8,128)S(1)}, f32[2,8,8,3072]{3,2,1,0:T(8,128)S(...) custom-call(s32[2]{0:T(128)S(1)} %pad_add_fusion.refs_0_, ...), custom_call_target="tpu_custom_call" | custom-call | tf_op jit(solution)/shard_map/forward_block/pallas_call | solution.py:161
  31.7 1.6 %collective-permute-start.2 = (bf16[2,1536]{1,0:T(2,128)(2,1)S(1)}, bf16[2,1536]{1,0:T(2,128)(2,1)S(1)}, u32[]{:S(2)}, u32[]{:S(2)}) collective-permute-start(bf16[2,1536]{1,0:T(2,128)(2,1)S(1)} %get-tuple-element.25), channel_id=1, source_target_pairs={{0,1},{1,0},{2,3},{3,2},{4,5},{5,4},{6,7},{7,6},{8,9},{9,8},{10,11... | collective-permute-start | bytes 18440 | tf_op jit(solution)/shard_map/ppermute | solution.py:22
  33.3 0.1 concatenate.44.refs_2_
  33.4 2.0 %collective-permute-done.2.refs_1_ = bf16[2,1536]{1,0:T(2,128)(2,1)S(1)} collective-permute-done((bf16[2,1536]{1,0:T(2,128)(2,1)S(1)}, bf16[2,1536]{1,0:T(2,128)(2,1)S(1)}, u32[]{:S(2)}, u32[]{:S(2)}) %collective-permute-start.2) | collective-permute-done | bytes 6176 | tf_op jit(solution)/shard_map/ppermute | solution.py:22
  35.4 2.0 %copy-done = bf16[1536,1152]{1,0:T(8,128)(2,1)S(1)} copy-done((bf16[1536,1152]{1,0:T(8,128)(2,1)S(1)}, bf16[1536,1152]{1,0:T(8,128)(2,1)}, u32[]{:S(2)}) %copy-start) | copy-done | bytes 3538968
  37.4 0.6 head_project.1
  38.0 1.6 %collective-permute-start.3 = (f32[4,1152]{1,0:T(4,128)S(1)}, f32[4,1152]{1,0:T(4,128)S(1)}, u32[]{:S(2)}, u32[]{:S(2)}) collective-permute-start(f32[4,1152]{1,0:T(4,128)S(1)} %get-tuple-element.26.refs_0_), channel_id=1, source_target_pairs={{0,1},{1,0},{2,3},{3,2},{4,5},{5,4},{6,7},{7,6},{8,9},{9,8},{10,11... | collective-permute-start | bytes 55304 | tf_op jit(solution)/shard_map/ppermute | solution.py:22
  39.6 2.2 %collective-permute-done.3.refs_1_ = f32[4,1152]{1,0:T(4,128)S(1)} collective-permute-done((f32[4,1152]{1,0:T(4,128)S(1)}, f32[4,1152]{1,0:T(4,128)S(1)}, u32[]{:S(2)}, u32[]{:S(2)}) %collective-permute-start.3) | collective-permute-done | bytes 18464 | tf_op jit(solution)/shard_map/ppermute | solution.py:22
  41.8 1.5 %loss_block.1 = (bf16[4,1152]{1,0:T(4,128)(2,1)S(1)}, bf16[4,1152]{1,0:T(4,128)(2,1)S(1)}, f32[2,1536]{1,0:T(2,128)S(1)}, f32[2,1536]{1,0:T(2,128)S(1)}) custom-call(f32[4,1152]{1,0:T(4,128)S(1)} %get-tuple-element.26.refs_0_, f32[4,1152]{1,0:T(4,128)S(1)} %collective-permute-done.3.refs_1_, bf16[64,1152]{1,0:T(8,128)(2,1)S(1)} %concatenate.44.refs_2_, ...), custom_call_target="tpu_custom_call" | custom-call | tf_op jit(solution)/shard_map/loss_block/pallas_call | solution.py:243
  43.3 2.7 %collective-permute-start.16 = (bf16[4,3840]{1,0:T(4,128)(2,1)S(1)}, bf16[4,3840]{1,0:T(4,128)(2,1)S(1)}, u32[]{:S(2)}, u32[]{:S(2)}) collective-permute-start(bf16[4,3840]{1,0:T(4,128)(2,1)S(1)} %constant_dynamic-update-slice_fusion), channel_id=1, source_target_pairs={{0,16},{2,18},{4,20},{6,22},{8,24},{10,26},{12,28},{14,30},{16,0},... | collective-permute-start | bytes 92168 | tf_op jit(solution)/shard_map/ppermute | solution.py:22
  46.0 1.5 %collective-permute-start.9 = (f32[2,1536]{1,0:T(2,128)S(1)}, f32[2,1536]{1,0:T(2,128)S(1)}, u32[]{:S(2)}, u32[]{:S(2)}) collective-permute-start(f32[2,1536]{1,0:T(2,128)S(1)} %get-tuple-element.28), channel_id=1, source_target_pairs={{0,1},{1,0},{2,3},{3,2},{4,5},{5,4},{6,7},{7,6},{8,9},{9,8},{10,11... | collective-permute-start | bytes 36872 | tf_op jit(solution)/shard_map/ppermute | solution.py:22
  47.5 2.2 %collective-permute-done.9.refs_2_ = f32[2,1536]{1,0:T(2,128)S(1)} collective-permute-done((f32[2,1536]{1,0:T(2,128)S(1)}, f32[2,1536]{1,0:T(2,128)S(1)}, u32[]{:S(2)}, u32[]{:S(2)}) %collective-permute-start.9) | collective-permute-done | bytes 12320 | tf_op jit(solution)/shard_map/ppermute | solution.py:22
  49.7 7.1 %terms_block.1 = (bf16[2,32,1536]{2,1,0:T(8,128)(2,1)S(1)}, bf16[2,32,1536]{2,1,0:T(8,128)(2,1)S(1)}, f32[2,8,8,3072]{3,2,1,0:T(8,128)S(1)}, f32[2,3072]{1,0:T(2,128)S(1)}) custom-call(s32[2]{0:T(128)S(1)} %pad_add_fusion.refs_0_, f32[2,1536]{1,0:T(2,128)S(1)} %get-tuple-element.27.refs_1_, f32[2,1536]{1,0:T(2,128)S(1)} %collective-permute-done.9.refs_2_, ...), custom_call_target="tpu_custom_call" | custom-call | tf_op jit(solution)/shard_map/terms_block/pallas_call | solution.py:356
  56.8 6.1 %images_block.1 = bf16[2,8,8,3072]{3,2,1,0:T(8,128)(2,1)} custom-call(f32[2,8,8,3072]{3,2,1,0:T(8,128)S(1)} %get-tuple-element.36.flow_ref, f32[56,3072]{1,0:T(8,128)S(1)} %get-tuple-element.29.refs_4_.weight_ref, f32[2,3072]{1,0:T(2,128)S(1)} %get-tuple-element.37.shared_ref), custom_call_target="tpu_custom_call" | custom-call | flops 38535168 | bytes 2359296 | tf_op jit(solution)/shard_map/images_block/pallas_call | solution.py:387
  63.0 1.6 %collective-permute-start.17 = (bf16[8,3840]{1,0:T(8,128)(2,1)S(1)}, bf16[8,3840]{1,0:T(8,128)(2,1)S(1)}, u32[]{:S(2)}, u32[]{:S(2)}) collective-permute-start(bf16[8,3840]{1,0:T(8,128)(2,1)S(1)} %pad_maximum_fusion.2), channel_id=1, source_target_pairs={{0,8},{2,10},{4,12},{6,14},{8,0},{10,2},{12,4},{14,6},{16,24},{18,... | collective-permute-start | bytes 184328 | tf_op jit(solution)/shard_map/ppermute | solution.py:22
  64.7 1.6 %collective-permute-start.11 = (bf16[32,1536]{1,0:T(8,128)(2,1)S(1)}, bf16[32,1536]{1,0:T(8,128)(2,1)S(1)}, u32[]{:S(2)}, u32[]{:S(2)}) collective-permute-start(bf16[32,1536]{1,0:T(8,128)(2,1)S(1)} %slice_bitcast_fusion), channel_id=1, source_target_pairs={{0,1},{1,0},{2,3},{3,2},{4,5},{5,4},{6,7},{7,6},{8,9},{9,8},{10,11... | collective-permute-start | bytes 294920 | tf_op jit(solution)/shard_map/ppermute | solution.py:22
  66.3 1.2 %collective-permute-done.17 = bf16[8,3840]{1,0:T(8,128)(2,1)S(1)} collective-permute-done((bf16[8,3840]{1,0:T(8,128)(2,1)S(1)}, bf16[8,3840]{1,0:T(8,128)(2,1)S(1)}, u32[]{:S(2)}, u32[]{:S(2)}) %collective-permute-start.17) | collective-permute-done | bytes 61472 | tf_op jit(solution)/shard_map/ppermute | solution.py:22
  67.5 0.6 collective-permute-start.18
  68.1 1.6 %collective-permute-done.11 = bf16[32,1536]{1,0:T(8,128)(2,1)S(1)} collective-permute-done((bf16[32,1536]{1,0:T(8,128)(2,1)S(1)}, bf16[32,1536]{1,0:T(8,128)(2,1)S(1)}, u32[]{:S(2)}, u32[]{:S(2)}) %collective-permute-start.11) | collective-permute-done | bytes 98336 | tf_op jit(solution)/shard_map/ppermute | solution.py:22
  69.7 0.6 collective-permute-start.12
  70.3 3.0 %collective-permute-done.18 = bf16[16,3840]{1,0:T(8,128)(2,1)S(1)} collective-permute-done((bf16[16,3840]{1,0:T(8,128)(2,1)S(1)}, bf16[16,3840]{1,0:T(8,128)(2,1)S(1)}, u32[]{:S(2)}, u32[]{:S(2)}) %collective-permute-start.18) | collective-permute-done | bytes 122912 | tf_op jit(solution)/shard_map/ppermute | solution.py:22
  73.5 1.2 %collective-permute-done.12 = bf16[32,1536]{1,0:T(8,128)(2,1)S(1)} collective-permute-done((bf16[32,1536]{1,0:T(8,128)(2,1)S(1)}, bf16[32,1536]{1,0:T(8,128)(2,1)S(1)}, u32[]{:S(2)}, u32[]{:S(2)}) %collective-permute-start.12) | collective-permute-done | bytes 98336 | tf_op jit(solution)/shard_map/ppermute | solution.py:22
  74.7 1.6 %collective-permute-start.13 = (bf16[32,1536]{1,0:T(8,128)(2,1)S(1)}, bf16[32,1536]{1,0:T(8,128)(2,1)S(1)}, u32[]{:S(2)}, u32[]{:S(2)}) collective-permute-start(bf16[32,1536]{1,0:T(8,128)(2,1)S(1)} %add_convert_fusion.3), channel_id=1, source_target_pairs={{0,8},{2,10},{4,12},{6,14},{8,0},{10,2},{12,4},{14,6},{16,24},{18,... | collective-permute-start | bytes 294920 | tf_op jit(solution)/shard_map/ppermute | solution.py:22
  76.3 0.2 concatenate.50
  76.5 0.6 fusion.21
  77.1 2.3 %collective-permute-done.13 = bf16[32,1536]{1,0:T(8,128)(2,1)S(1)} collective-permute-done((bf16[32,1536]{1,0:T(8,128)(2,1)S(1)}, bf16[32,1536]{1,0:T(8,128)(2,1)S(1)}, u32[]{:S(2)}, u32[]{:S(2)}) %collective-permute-start.13) | collective-permute-done | bytes 98336 | tf_op jit(solution)/shard_map/ppermute | solution.py:22
  79.4 0.4 collective-permute-start.14
  79.8 0.7 add_add_fusion
  80.5 4.5 %collective-permute-done.14 = bf16[32,1536]{1,0:T(8,128)(2,1)S(1)} collective-permute-done((bf16[32,1536]{1,0:T(8,128)(2,1)S(1)}, bf16[32,1536]{1,0:T(8,128)(2,1)S(1)}, u32[]{:S(2)}, u32[]{:S(2)}) %collective-permute-start.14) | collective-permute-done | bytes 98336 | tf_op jit(solution)/shard_map/ppermute | solution.py:22
  85.1 4.1 %fusion.8 = f32[1536,1152]{1,0:T(8,128)} fusion(bf16[64,3840]{1,0:T(8,128)(2,1)S(1)} %concatenate.50), kind=kOutput, calls=%fused_computation.11 | convolution fusion | flops 226492416 | bytes 7421952 | tf_op jit(solution)/shard_map/dot_general | solution.py:457
  89.2 0.6 maximum_convert_fusion.1
  89.8 0.8 slice.30
  (41 shorter events, 0.9 us)
Async XLA Ops:
  2.2 4.6 %collective-permute-start.4 = (bf16[2,1152]{1,0:T(2,128)(2,1)S(1)}, bf16[2,1152]{1,0:T(2,128)(2,1)S(1)}, u32[]{:S(2)}, u32[]{:S(2)}) collective-permute-start(bf16[2,1152]{1,0:T(2,128)(2,1)S(1)} %fusion.20), channel_id=1, source_target_pairs={{0,1},{1,0},{2,3},{3,2},{4,5},{5,4},{6,7},{7,6},{8,9},{9,8},{10,11... | collective-permute-start | bytes 13832 | tf_op jit(solution)/shard_map/ppermute | solution.py:22
  6.8 4.8 %collective-permute-start.5 = (bf16[4,1152]{1,0:T(4,128)(2,1)S(1)}, bf16[4,1152]{1,0:T(4,128)(2,1)S(1)}, u32[]{:S(2)}, u32[]{:S(2)}) collective-permute-start(bf16[4,1152]{1,0:T(4,128)(2,1)S(1)} %pad_maximum_fusion.5), channel_id=1, source_target_pairs={{0,16},{2,18},{4,20},{6,22},{8,24},{10,26},{12,28},{14,30},{16,0},... | collective-permute-start | bytes 27656 | tf_op jit(solution)/shard_map/ppermute | solution.py:22
  11.6 3.8 %collective-permute-start.6 = (bf16[8,1152]{1,0:T(8,128)(2,1)S(1)}, bf16[8,1152]{1,0:T(8,128)(2,1)S(1)}, u32[]{:S(2)}, u32[]{:S(2)}) collective-permute-start(bf16[8,1152]{1,0:T(8,128)(2,1)S(1)} %pad_maximum_fusion.4), channel_id=1, source_target_pairs={{0,8},{2,10},{4,12},{6,14},{8,0},{10,2},{12,4},{14,6},{16,24},{18,... | collective-permute-start | bytes 55304 | tf_op jit(solution)/shard_map/ppermute | solution.py:22
  13.6 7.7 %collective-permute-start = (bf16[49,1536]{1,0:T(8,128)(2,1)}, bf16[49,1536]{1,0:T(8,128)(2,1)S(1)}, u32[]{:S(2)}, u32[]{:S(2)}) collective-permute-start(bf16[49,1536]{1,0:T(8,128)(2,1)} %refs_2_.2), channel_id=1, source_target_pairs={{0,1},{1,0},{2,3},{3,2},{4,5},{5,4},{6,7},{7,6},{8,9},{9,8},{10,11... | collective-permute-start | bytes 451592 | tf_op jit(solution)/shard_map/ppermute | solution.py:22
  15.5 4.0 %collective-permute-start.7 = (bf16[16,1152]{1,0:T(8,128)(2,1)S(1)}, bf16[16,1152]{1,0:T(8,128)(2,1)S(1)}, u32[]{:S(2)}, u32[]{:S(2)}) collective-permute-start(bf16[16,1152]{1,0:T(8,128)(2,1)S(1)} %pad_maximum_fusion.3), channel_id=1, source_target_pairs={{0,4},{2,6},{4,0},{6,2},{8,12},{10,14},{12,8},{14,10},{16,20},{18,... | collective-permute-start | bytes 110600 | tf_op jit(solution)/shard_map/ppermute | solution.py:22
  17.4 3.9 %collective-permute-start.1 = (bf16[4,1536]{1,0:T(4,128)(2,1)}, bf16[4,1536]{1,0:T(4,128)(2,1)S(1)}, u32[]{:S(2)}, u32[]{:S(2)}) collective-permute-start(bf16[4,1536]{1,0:T(4,128)(2,1)} %refs_4_.1), channel_id=1, source_target_pairs={{0,1},{1,0},{2,3},{3,2},{4,5},{5,4},{6,7},{7,6},{8,9},{9,8},{10,11... | collective-permute-start | bytes 36872 | tf_op jit(solution)/shard_map/ppermute | solution.py:22
  19.6 13.7 %collective-permute-start.8 = (bf16[32,1152]{1,0:T(8,128)(2,1)S(1)}, bf16[32,1152]{1,0:T(8,128)(2,1)S(1)}, u32[]{:S(2)}, u32[]{:S(2)}) collective-permute-start(bf16[32,1152]{1,0:T(8,128)(2,1)S(1)} %concatenate.43), channel_id=1, source_target_pairs={{0,2},{2,0},{4,6},{6,4},{8,10},{10,8},{12,14},{14,12},{16,18},{18,... | collective-permute-start | bytes 221192 | tf_op jit(solution)/shard_map/ppermute | solution.py:22
  21.3 1.1 %copy-start.2 = (bf16[2,8,8,3072]{3,2,1,0:T(8,128)(2,1)S(1)}, bf16[2,8,8,3072]{3,2,1,0:T(8,128)(2,1)}, u32[]{:S(2)}) copy-start(bf16[2,8,8,3072]{3,2,1,0:T(8,128)(2,1)} %refs_3_.3) | copy-start | bytes 2359300
  22.4 0.9 %copy-start.4 = (bf16[49,1536]{1,0:T(8,128)(2,1)S(1)}, bf16[49,1536]{1,0:T(8,128)(2,1)}, u32[]{:S(2)}) copy-start(bf16[49,1536]{1,0:T(8,128)(2,1)} %refs_2_.2) | copy-start | bytes 451588
  23.3 0.7 copy-start.5
  31.7 3.7 %collective-permute-start.2 = (bf16[2,1536]{1,0:T(2,128)(2,1)S(1)}, bf16[2,1536]{1,0:T(2,128)(2,1)S(1)}, u32[]{:S(2)}, u32[]{:S(2)}) collective-permute-start(bf16[2,1536]{1,0:T(2,128)(2,1)S(1)} %get-tuple-element.25), channel_id=1, source_target_pairs={{0,1},{1,0},{2,3},{3,2},{4,5},{5,4},{6,7},{7,6},{8,9},{9,8},{10,11... | collective-permute-start | bytes 18440 | tf_op jit(solution)/shard_map/ppermute | solution.py:22
  35.4 2.0 %copy-start = (bf16[1536,1152]{1,0:T(8,128)(2,1)S(1)}, bf16[1536,1152]{1,0:T(8,128)(2,1)}, u32[]{:S(2)}) copy-start(bf16[1536,1152]{1,0:T(8,128)(2,1)} %refs_3_.2) | copy-start | bytes 10616836
  37.4 4.4 %copy-start.1 = (bf16[1536,1152]{1,0:T(8,128)(2,1)S(1)}, bf16[1536,1152]{1,0:T(8,128)(2,1)}, u32[]{:S(2)}) copy-start(bf16[1536,1152]{1,0:T(8,128)(2,1)} %refs_3_.2) | copy-start | bytes 10616836
  37.4 12.2 %copy-start.3 = (bf16[2,8,8,3072]{3,2,1,0:T(8,128)(2,1)S(1)}, bf16[2,8,8,3072]{3,2,1,0:T(8,128)(2,1)}, u32[]{:S(2)}) copy-start(bf16[2,8,8,3072]{3,2,1,0:T(8,128)(2,1)} %refs_3_.3) | copy-start | bytes 2359300
  38.0 3.8 %collective-permute-start.3 = (f32[4,1152]{1,0:T(4,128)S(1)}, f32[4,1152]{1,0:T(4,128)S(1)}, u32[]{:S(2)}, u32[]{:S(2)}) collective-permute-start(f32[4,1152]{1,0:T(4,128)S(1)} %get-tuple-element.26.refs_0_), channel_id=1, source_target_pairs={{0,1},{1,0},{2,3},{3,2},{4,5},{5,4},{6,7},{7,6},{8,9},{9,8},{10,11... | collective-permute-start | bytes 55304 | tf_op jit(solution)/shard_map/ppermute | solution.py:22
  43.3 19.7 %collective-permute-start.16 = (bf16[4,3840]{1,0:T(4,128)(2,1)S(1)}, bf16[4,3840]{1,0:T(4,128)(2,1)S(1)}, u32[]{:S(2)}, u32[]{:S(2)}) collective-permute-start(bf16[4,3840]{1,0:T(4,128)(2,1)S(1)} %constant_dynamic-update-slice_fusion), channel_id=1, source_target_pairs={{0,16},{2,18},{4,20},{6,22},{8,24},{10,26},{12,28},{14,30},{16,0},... | collective-permute-start | bytes 92168 | tf_op jit(solution)/shard_map/ppermute | solution.py:22
  46.0 3.7 %collective-permute-start.9 = (f32[2,1536]{1,0:T(2,128)S(1)}, f32[2,1536]{1,0:T(2,128)S(1)}, u32[]{:S(2)}, u32[]{:S(2)}) collective-permute-start(f32[2,1536]{1,0:T(2,128)S(1)} %get-tuple-element.28), channel_id=1, source_target_pairs={{0,1},{1,0},{2,3},{3,2},{4,5},{5,4},{6,7},{7,6},{8,9},{9,8},{10,11... | collective-permute-start | bytes 36872 | tf_op jit(solution)/shard_map/ppermute | solution.py:22
  56.7 19.7 %copy-start.6 = (bf16[2,1152]{1,0:T(2,128)(2,1)S(1)}, bf16[2,1152]{1,0:T(2,128)(2,1)}, u32[]{:S(2)}) copy-start(bf16[2,1152]{1,0:T(2,128)(2,1)} %param.9) | copy-start | bytes 13828
  56.8 7.9 %collective-permute-start.10 = (bf16[2,32,1536]{2,1,0:T(8,128)(2,1)S(1)}, bf16[2,32,1536]{2,1,0:T(8,128)(2,1)S(1)}, u32[]{:S(2)}, u32[]{:S(2)}) collective-permute-start(bf16[2,32,1536]{2,1,0:T(8,128)(2,1)S(1)} %get-tuple-element.39), channel_id=1, source_target_pairs={{0,2},{2,0},{4,6},{6,4},{8,10},{10,8},{12,14},{14,12},{16,18},{18,... | collective-permute-start | bytes 589832 | tf_op jit(solution)/shard_map/ppermute | solution.py:22
  63.0 4.5 %collective-permute-start.17 = (bf16[8,3840]{1,0:T(8,128)(2,1)S(1)}, bf16[8,3840]{1,0:T(8,128)(2,1)S(1)}, u32[]{:S(2)}, u32[]{:S(2)}) collective-permute-start(bf16[8,3840]{1,0:T(8,128)(2,1)S(1)} %pad_maximum_fusion.2), channel_id=1, source_target_pairs={{0,8},{2,10},{4,12},{6,14},{8,0},{10,2},{12,4},{14,6},{16,24},{18,... | collective-permute-start | bytes 184328 | tf_op jit(solution)/shard_map/ppermute | solution.py:22
  64.7 5.0 %collective-permute-start.11 = (bf16[32,1536]{1,0:T(8,128)(2,1)S(1)}, bf16[32,1536]{1,0:T(8,128)(2,1)S(1)}, u32[]{:S(2)}, u32[]{:S(2)}) collective-permute-start(bf16[32,1536]{1,0:T(8,128)(2,1)S(1)} %slice_bitcast_fusion), channel_id=1, source_target_pairs={{0,1},{1,0},{2,3},{3,2},{4,5},{5,4},{6,7},{7,6},{8,9},{9,8},{10,11... | collective-permute-start | bytes 294920 | tf_op jit(solution)/shard_map/ppermute | solution.py:22
  67.5 5.8 %collective-permute-start.18 = (bf16[16,3840]{1,0:T(8,128)(2,1)S(1)}, bf16[16,3840]{1,0:T(8,128)(2,1)S(1)}, u32[]{:S(2)}, u32[]{:S(2)}) collective-permute-start(bf16[16,3840]{1,0:T(8,128)(2,1)S(1)} %pad_maximum_fusion.1), channel_id=1, source_target_pairs={{0,4},{2,6},{4,0},{6,2},{8,12},{10,14},{12,8},{14,10},{16,20},{18,... | collective-permute-start | bytes 368648 | tf_op jit(solution)/shard_map/ppermute | solution.py:22
  69.7 4.9 %collective-permute-start.12 = (bf16[32,1536]{1,0:T(8,128)(2,1)S(1)}, bf16[32,1536]{1,0:T(8,128)(2,1)S(1)}, u32[]{:S(2)}, u32[]{:S(2)}) collective-permute-start(bf16[32,1536]{1,0:T(8,128)(2,1)S(1)} %fusion.10), channel_id=1, source_target_pairs={{0,4},{2,6},{4,0},{6,2},{8,12},{10,14},{12,8},{14,10},{16,20},{18,... | collective-permute-start | bytes 294920 | tf_op jit(solution)/shard_map/ppermute | solution.py:22
  73.4 2.9 %collective-permute-start.19 = (bf16[32,3840]{1,0:T(8,128)(2,1)S(1)}, bf16[32,3840]{1,0:T(8,128)(2,1)S(1)}, u32[]{:S(2)}, u32[]{:S(2)}) collective-permute-start(bf16[32,3840]{1,0:T(8,128)(2,1)S(1)} %pad_maximum_fusion), channel_id=1, source_target_pairs={{0,2},{2,0},{4,6},{6,4},{8,10},{10,8},{12,14},{14,12},{16,18},{18,... | collective-permute-start | bytes 737288 | tf_op jit(solution)/shard_map/ppermute | solution.py:22
  74.7 4.7 %collective-permute-start.13 = (bf16[32,1536]{1,0:T(8,128)(2,1)S(1)}, bf16[32,1536]{1,0:T(8,128)(2,1)S(1)}, u32[]{:S(2)}, u32[]{:S(2)}) collective-permute-start(bf16[32,1536]{1,0:T(8,128)(2,1)S(1)} %add_convert_fusion.3), channel_id=1, source_target_pairs={{0,8},{2,10},{4,12},{6,14},{8,0},{10,2},{12,4},{14,6},{16,24},{18,... | collective-permute-start | bytes 294920 | tf_op jit(solution)/shard_map/ppermute | solution.py:22
  79.4 5.6 %collective-permute-start.14 = (bf16[32,1536]{1,0:T(8,128)(2,1)S(1)}, bf16[32,1536]{1,0:T(8,128)(2,1)S(1)}, u32[]{:S(2)}, u32[]{:S(2)}) collective-permute-start(bf16[32,1536]{1,0:T(8,128)(2,1)S(1)} %add_convert_fusion.2), channel_id=1, source_target_pairs={{0,16},{2,18},{4,20},{6,22},{8,24},{10,26},{12,28},{14,30},{16,0},... | collective-permute-start | bytes 294920 | tf_op jit(solution)/shard_map/ppermute | solution.py:22
  85.0 4.2 %collective-permute-start.15 = (bf16[32,1536]{1,0:T(8,128)(2,1)S(1)}, bf16[32,1536]{1,0:T(8,128)(2,1)S(1)}, u32[]{:S(2)}, u32[]{:S(2)}) collective-permute-start(bf16[32,1536]{1,0:T(8,128)(2,1)S(1)} %add_convert_fusion.1), channel_id=1, source_target_pairs={{0,2},{2,0},{4,6},{6,4},{8,10},{10,8},{12,14},{14,12},{16,18},{18,... | collective-permute-start | bytes 294920 | tf_op jit(solution)/shard_map/ppermute | solution.py:22

commit v3 on v2

v3 whole, which is shorter than its diff:
```python
import jax
import jax.numpy as jnp
from jax import lax
from jax.experimental import pallas as pl
from jax.experimental.pallas import tpu as pltpu
from jax.sharding import PartitionSpec as P

EPS = 1e-06
LOGIT_SCALE = 10.0
LOGIT_BIAS = -2.0
KER = 7
REACH = KER // 2
TAPS = KER * KER
LANES = 128
ROWS_PAD = 64
HALF_PAD = ROWS_PAD // 2
TERM_ROW = 56
BF = jnp.bfloat16
F32 = jnp.float32


def swap(value, axis, mask):
    count = lax.axis_size(axis)
    return lax.ppermute(value, axis, [(source, source ^ mask) for source in range(count)])


def tree_gather(value, axis, masks):
    for mask in masks:
        value = jnp.concatenate([value, swap(value, axis, mask)], axis=0)
    return value


def bits_up(count):
    masks = []
    mask = 1
    while mask < count:
        masks.append(mask)
        mask *= 2
    return masks


def params(mebibytes):
    return pltpu.CompilerParams(vmem_limit_bytes=mebibytes * 1024 * 1024)


def far(arrays):
    return [pltpu.with_memory_space_constraint(value, pltpu.HBM) for value in arrays]


def near(arrays):
    return [pltpu.with_memory_space_constraint(value, pltpu.VMEM) for value in arrays]


VM = pl.BlockSpec(memory_space=pltpu.VMEM)
SM = pl.BlockSpec(memory_space=pltpu.SMEM)
HB = pl.BlockSpec(memory_space=pltpu.HBM)
ANY = pl.BlockSpec(memory_space=pl.ANY)
SHAPE = jax.ShapeDtypeStruct


def lane_block(index, width):
    return pl.ds(pl.multiple_of(index * width, LANES), width)


def shift_cols(value, step):
    if step == 0:
        return value
    width = value.shape[0]
    rolled = pltpu.roll(value, (-step) % width, 0)
    col = lax.broadcasted_iota(jnp.int32, value.shape, 0)
    inside = (col < width - step) if step > 0 else (col >= -step)
    return jnp.where(inside, rolled, 0.0)


def conv_rows(rows, tap_row, flip):
    height = len(rows)
    sums = [None] * height
    for b in range(KER):
        moved = [shift_cols(row, b - REACH) for row in rows]
        for a in range(KER):
            tap = (KER - 1 - a) * KER + (KER - 1 - b) if flip else a * KER + b
            weight = tap_row(tap)
            for h in range(max(0, REACH - a), min(height, height + REACH - a)):
                term = moved[h + a - REACH] * weight
                sums[h] = term if sums[h] is None else sums[h] + term
    return sums


def stack_rows(low, high, order):
    def kernel(low_ref, high_ref, order_ref, out_ref):
        both = jnp.concatenate([low_ref[...].astype(F32), high_ref[...].astype(F32)], axis=0)
        out_ref[...] = both.astype(out_ref.dtype)

    rows, width = low.shape
    return pl.pallas_call(
        kernel,
        out_shape=SHAPE((2 * rows, width), low.dtype),
        in_specs=[VM, VM, ANY],
        out_specs=VM,
        compiler_params=params(24),
        name="stack_rows",
    )(low, high, order)


def add_all(values, order):
    def kernel(*refs):
        total = refs[0][...].astype(F32)
        for ref in refs[1:-2]:
            total = total + ref[...].astype(F32)
        refs[-1][...] = total.astype(BF)

    return pl.pallas_call(
        kernel,
        out_shape=SHAPE(values[0].shape, BF),
        in_specs=[VM] * len(values) + [ANY],
        out_specs=VM,
        compiler_params=params(24),
        name="add_all",
    )(*values, order)


def chip_sums(keep, give):
    members = keep.shape[0]

    def kernel(keep_ref, give_ref, *out_refs):
        for m in range(members):
            out_refs[m][...] = (keep_ref[m].astype(F32) + give_ref[m].astype(F32)).astype(BF)

    return pl.pallas_call(
        kernel,
        out_shape=[SHAPE(keep.shape[1:], BF)] * members,
        in_specs=[VM, VM],
        out_specs=[VM] * members,
        compiler_params=params(24),
        name="chip_sums",
    )(keep, give)


def tile_of(base_piece, t, member, share):
    per_piece = share // LANES
    piece = base_piece + t // per_piece
    return lane_block((member ^ piece) * per_piece + t % per_piece, LANES)


def conv_tiles(tiles, base_piece, member, share, x_ref, weight_ref, mixed_ref, sum_ref):
    images, height = x_ref.shape[:2]

    @pl.loop(0, tiles)
    def _(t):
        lanes = lane_block(t, LANES)
        source = tile_of(base_piece, t, member, share)
        bias = weight_ref[TERM_ROW : TERM_ROW + 1, lanes]
        for i in range(images):
            rows = [x_ref[i, h, :, source].astype(F32) for h in range(height)]
            sums = conv_rows(rows, lambda tap: weight_ref[tap : tap + 1, lanes], False)
            for h in range(height):
                value = sums[h] + bias
                mixed_ref[i, h, :, lanes] = value
                sum_ref[i, h] += value


def own_kernel(
    members, place_ref, x_hbm, kernel_hbm, term_hbm, mixed_ref, sum_ref, weight_ref, x_ref, kernel_ref, term_ref, sems
):
    share = kernel_hbm.shape[1]
    member = place_ref[0]
    copies = [
        pltpu.make_async_copy(kernel_hbm, kernel_ref, sems.at[0]),
        pltpu.make_async_copy(term_hbm, term_ref, sems.at[1]),
    ]
    for m in range(members):
        lanes = lane_block(member ^ m, share)
        copies.append(
            pltpu.make_async_copy(
                x_hbm.at[:, :, :, lanes], x_ref.at[:, :, :, lanes], sems.at[2 + m]
            )
        )
    for copy in copies:
        copy.start()
    sum_ref[...] = jnp.zeros_like(sum_ref)
    for copy in copies[:3]:
        copy.wait()
    weight_ref[0:TAPS, :] = kernel_ref[...].astype(F32)
    weight_ref[TERM_ROW : TERM_ROW + 4, :] = term_ref[...].astype(F32)
    conv_tiles(share // LANES, 0, member, share, x_ref, weight_ref, mixed_ref, sum_ref)
    for copy in copies[3:]:
        copy.wait()


def own_block(place, image_maps, dw_kernel, channel_terms):
    images, height, width, channels = image_maps.shape
    share = dw_kernel.shape[1]
    members = channels // share
    return pl.pallas_call(
        lambda *refs: own_kernel(members, *refs),
        out_shape=[
            SHAPE((images, height, width, share), F32),
            SHAPE((images, height, width, LANES), F32),
            SHAPE((ROWS_PAD, share), F32),
            SHAPE(image_maps.shape, BF),
        ],
        in_specs=[SM, HB, HB, HB],
        out_specs=[VM] * 4,
        scratch_shapes=[
            pltpu.VMEM(dw_kernel.shape, BF),
            pltpu.VMEM(channel_terms.shape, BF),
            pltpu.SemaphoreType.DMA((2 + members,)),
        ],
        compiler_params=params(24),
        name="own_block",
    )(place, *far([image_maps, dw_kernel, channel_terms]))


def forward_kernel(members, place_ref, head_hbm, x_ref, mixed_own, sum_own, weight_own, order_ref, *refs):
    kernel_refs, refs = refs[: members - 1], refs[members - 1 :]
    term_refs, refs = refs[: members - 1], refs[members - 1 :]
    piece_refs, refs = refs[:members], refs[members:]
    head_ref, weight_rest, mixed_rest, mean_ref, rstd_ref, hatsum_ref, hat_ref, hrstd_ref, sum_ref, pool_ref, sem = refs
    images, height, width, channels = x_ref.shape
    share = channels // members
    cells = height * width
    member = place_ref[0]
    head_copy = pltpu.make_async_copy(head_hbm, head_ref, sem)
    head_copy.start()
    for m in range(1, members):
        lanes = slice((m - 1) * share, m * share)
        weight_rest[0:TAPS, lanes] = kernel_refs[m - 1][...].astype(F32)
        weight_rest[TERM_ROW : TERM_ROW + 4, lanes] = term_refs[m - 1][...].astype(F32)
    sum_ref[...] = sum_own[...]
    own_tiles = share // LANES
    rest_tiles = (members - 1) * own_tiles
    conv_tiles(rest_tiles, 1, member, share, x_ref, weight_rest, mixed_rest, sum_ref)
    parts = [(0, own_tiles, mixed_own, weight_own), (1, rest_tiles, mixed_rest, weight_rest)]

    mean = jnp.sum(sum_ref[...], axis=-1, keepdims=True) * (1.0 / channels)
    mean_ref[...] = jnp.broadcast_to(mean, mean_ref.shape)
    sum_ref[...] = jnp.zeros_like(sum_ref)
    for base, tiles, mixed_ref, weight_ref in parts:

        @pl.loop(0, tiles)
        def _(t):
            lanes = lane_block(t, LANES)
            for i in range(images):
                for h in range(height):
                    value = mixed_ref[i, h, :, lanes] - mean_ref[i, h]
                    sum_ref[i, h] += value * value

    var = jnp.sum(sum_ref[...], axis=-1, keepdims=True) * (1.0 / channels)
    rstd_ref[...] = jnp.broadcast_to(lax.rsqrt(var + EPS), rstd_ref.shape)
    for base, tiles, mixed_ref, weight_ref in parts:

        @pl.loop(0, tiles)
        def _(t):
            lanes = lane_block(t, LANES)
            wide = lane_block(t + base * own_tiles, LANES)
            source = tile_of(base, t, member, share)
            scale = (
                weight_ref[TERM_ROW + 1 : TERM_ROW + 2, lanes]
                * weight_ref[TERM_ROW + 2 : TERM_ROW + 3, lanes]
            )
            for i in range(images):
                hats = jnp.zeros((width, LANES), F32)
                plain = jnp.zeros((width, LANES), F32)
                for h in range(height):
                    hats = hats + (mixed_ref[i, h, :, lanes] - mean_ref[i, h]) * rstd_ref[i, h]
                    plain = plain + x_ref[i, h, :, source].astype(F32)
                hat_row = jnp.sum(hats, axis=0, keepdims=True)
                hatsum_ref[i : i + 1, wide] = hat_row
                pool_ref[i : i + 1, wide] = (
                    jnp.sum(plain, axis=0, keepdims=True) + scale * hat_row
                ) * (1.0 / cells)

    pooled = pool_ref[...]
    centered = pooled - jnp.mean(pooled, axis=1, keepdims=True)
    head_rstd = lax.rsqrt(jnp.mean(centered * centered, axis=1, keepdims=True) + EPS)
    hat = centered * head_rstd
    hat_ref[...] = hat
    hrstd_ref[...] = jnp.broadcast_to(head_rstd, hrstd_ref.shape)
    for m in range(members):
        gain = (
            weight_own[TERM_ROW + 3 : TERM_ROW + 4, :]
            if m == 0
            else weight_rest[TERM_ROW + 3 : TERM_ROW + 4, (m - 1) * share : m * share]
        )
        piece_refs[m][...] = (hat[:, m * share : (m + 1) * share] * gain).astype(BF)
    head_copy.wait()


def forward_block(place, head_weight, x_here, own, order, kernels, terms):
    images, height, width, channels = x_here.shape
    members = len(kernels) + 1
    share = channels // members
    cell = (images, height, width, LANES)
    outs = [SHAPE((images, share), BF)] * members + [
        SHAPE(head_weight.shape, BF),
        SHAPE((ROWS_PAD, channels - share), F32),
        SHAPE((images, height, width, channels - share), F32),
        SHAPE(cell, F32),
        SHAPE(cell, F32),
        SHAPE((images, channels), F32),
        SHAPE((images, channels), F32),
        SHAPE((images, LANES), F32),
    ]
    result = pl.pallas_call(
        lambda *refs: forward_kernel(members, *refs),
        out_shape=outs,
        in_specs=[SM, HB, VM, VM, VM, VM, ANY] + [VM] * (2 * (members - 1)),
        out_specs=[VM] * len(outs),
        scratch_shapes=[
            pltpu.VMEM(cell, F32),
            pltpu.VMEM((images, channels), F32),
            pltpu.SemaphoreType.DMA,
        ],
        compiler_params=params(24),
        name="forward_block",
    )(place, *far([head_weight]), *near([x_here, *own]), order, *near([*kernels, *terms]))
    return result[:members], result[members], result[members + 1], result[members + 2], result[members + 3 :]


def head_kernel(members, *refs):
    group = jnp.concatenate([ref[...].astype(F32) for ref in refs[:members]], axis=0).astype(BF)
    weight_ref, group_ref, out_ref = refs[members:]
    group_ref[...] = group
    out_ref[...] = jnp.dot(group, weight_ref[...], preferred_element_type=F32)


def head_project(pieces, head_weight):
    members = len(pieces)
    share, embed_width = head_weight.shape
    rows = members * pieces[0].shape[0]
    return pl.pallas_call(
        lambda *refs: head_kernel(members, *refs),
        out_shape=[SHAPE((rows, share), BF), SHAPE((rows, embed_width), F32)],
        in_specs=[VM] * (members + 1),
        out_specs=[VM, VM],
        compiler_params=params(24),
        name="head_project",
    )(*near([*pieces, head_weight]))


def inverse_norm(vectors):
    return lax.rsqrt(jnp.sum(vectors * vectors, axis=1, keepdims=True) + EPS)


def pair_weights(images, texts):
    logits = (
        LOGIT_SCALE
        * lax.dot_general(images, texts, (((1,), (1,)), ((), ())), preferred_element_type=F32)
        + LOGIT_BIAS
    )
    here = lax.broadcasted_iota(jnp.int32, logits.shape, 0)
    there = lax.broadcasted_iota(jnp.int32, logits.shape, 1)
    positive = jnp.where(here == there, 1.0, 0.0).astype(F32)
    return (jax.nn.sigmoid(logits) - positive).astype(BF)


def unit_back(unit, inverse, grad):
    return inverse * (grad - unit * jnp.sum(unit * grad, axis=1, keepdims=True))


def loss_kernel(members, *refs):
    partials, refs = refs[:members], refs[members:]
    text_low, text_high, group_ref, weight_ref, packed_ref = refs[:5]
    piece_refs = refs[5:]
    total_rows, width = partials[0].shape
    rows = total_rows // members
    share = group_ref.shape[1]
    embed = partials[0][...]
    for m in range(1, members):
        embed = embed + jnp.concatenate(
            [partials[m][(k ^ m) * rows : (k ^ m) * rows + rows, :] for k in range(members)], axis=0
        )
    inverse = inverse_norm(embed)
    unit = embed * inverse
    unit_bf = unit.astype(BF)
    raw = jnp.concatenate([text_low[...], text_high[...]], axis=0).astype(F32)
    texts = (raw * inverse_norm(raw)).astype(BF)
    unit_grad = LOGIT_SCALE * jnp.dot(
        pair_weights(unit_bf, texts), texts, preferred_element_type=F32
    )
    embed_grad = unit_back(unit, inverse, unit_grad).astype(BF)
    packed_ref[:, 0:share] = group_ref[...]
    packed_ref[:, share : share + width] = embed_grad
    packed_ref[:, share + width : share + 2 * width] = unit_bf
    part = lax.dot_general(
        embed_grad, weight_ref[...], (((1,), (1,)), ((), ())), preferred_element_type=F32
    )
    for m in range(members):
        piece_refs[m][...] = part[m * rows : m * rows + rows]


def loss_block(partials, texts, group, head_weight):
    members = len(partials)
    total_rows, embed_width = partials[0].shape
    share = head_weight.shape[0]
    result = pl.pallas_call(
        lambda *refs: loss_kernel(members, *refs),
        out_shape=[SHAPE((total_rows, share + 2 * embed_width), BF)]
        + [SHAPE((total_rows // members, share), F32)] * members,
        in_specs=[VM] * (members + 4),
        out_specs=[VM] * (members + 1),
        compiler_params=params(24),
        name="loss_block",
    )(*near([*partials, *texts, group, head_weight]))
    return result[0], result[1:]


def terms_kernel(members, place_ref, *refs):
    grad_refs, refs = refs[:members], refs[members:]
    order_ref, x_ref, weight_own, weight_rest, mixed_own, mixed_rest, mean_ref, rstd_ref, hatsum_ref, hat_ref, hrstd_ref = refs[:11]
    keep_ref, give_ref, flow_ref, shared_ref, scaled_ref, dot_ref, sums_ref, taps_ref = refs[11:]
    images, height, width, channels = x_ref.shape
    share = channels // members
    own_tiles = share // LANES
    rest_tiles = (members - 1) * own_tiles
    cells = height * width
    member = place_ref[0]
    core = place_ref[1]
    parts = [(0, own_tiles, mixed_own), (1, rest_tiles, mixed_rest)]

    def term_row(row):
        return jnp.concatenate(
            [weight_own[TERM_ROW + row : TERM_ROW + row + 1, :], weight_rest[TERM_ROW + row : TERM_ROW + row + 1, :]],
            axis=1,
        )

    grad = jnp.concatenate([ref[...] for ref in grad_refs], axis=1)
    hat = hat_ref[...]
    sums_ref[...] = jnp.zeros_like(sums_ref)
    sums_ref[TERM_ROW + 3 : TERM_ROW + 4, :] = jnp.sum(grad * hat, axis=0, keepdims=True)
    inner = grad * term_row(3)
    shared = (
        hrstd_ref[:, 0:1]
        * (
            inner
            - jnp.mean(inner, axis=1, keepdims=True)
            - hat * jnp.mean(inner * hat, axis=1, keepdims=True)
        )
        * (1.0 / cells)
    )
    shared_ref[...] = shared
    gain = term_row(1)
    scale = term_row(2)
    hat_total = jnp.sum(shared * hatsum_ref[...], axis=0, keepdims=True)
    sums_ref[TERM_ROW + 1 : TERM_ROW + 2, :] = hat_total * scale
    sums_ref[TERM_ROW + 2 : TERM_ROW + 3, :] = hat_total * gain
    scaled = shared * (gain * scale)
    scaled_ref[...] = scaled - jnp.mean(scaled, axis=1, keepdims=True)
    dot_ref[...] = jnp.zeros_like(dot_ref)
    for base, tiles, mixed_ref in parts:

        @pl.loop(0, tiles)
        def _(t):
            lanes = lane_block(t, LANES)
            wide = lane_block(t + base * own_tiles, LANES)
            for i in range(images):
                factor = scaled_ref[i : i + 1, wide]
                for h in range(height):
                    dot_ref[i, h] += factor * (mixed_ref[i, h, :, lanes] - mean_ref[i, h])

    dots = jnp.sum(dot_ref[...], axis=-1, keepdims=True) * (1.0 / channels)
    dot_ref[...] = jnp.broadcast_to(dots, dot_ref.shape) * rstd_ref[...] * rstd_ref[...]
    for base, tiles, mixed_ref in parts:

        @pl.loop(0, tiles)
        def _(t):
            lanes = lane_block(t, LANES)
            wide = lane_block(t + base * own_tiles, LANES)
            source = tile_of(base, t, member, share)
            flows = []
            for i in range(images):
                factor = scaled_ref[i : i + 1, wide]
                flow_rows = []
                for h in range(height):
                    centered = mixed_ref[i, h, :, lanes] - mean_ref[i, h]
                    flow = rstd_ref[i, h] * (factor - centered * dot_ref[i, h])
                    flow_ref[i, h, :, wide] = flow
                    flow_rows.append(flow)
                flows.append(flow_rows)
            bias = flows[0][0]
            for i in range(images):
                for h in range(height):
                    if i or h:
                        bias = bias + flows[i][h]
            taps_ref[TAPS * width : TAPS * width + width, :] = bias
            for b in range(KER):
                totals = [None] * KER
                for i in range(images):
                    moved = [
                        shift_cols(x_ref[i, h, :, source].astype(F32), b - REACH)
                        for h in range(height)
                    ]
                    for a in range(KER):
                        for h in range(max(0, REACH - a), min(height, height + REACH - a)):
                            term = flows[i][h] * moved[h + a - REACH]
                            totals[a] = term if totals[a] is None else totals[a] + term
                for a in range(KER):
                    tap = a * KER + b
                    taps_ref[tap * width : tap * width + width, :] = totals[a]
            rows = TAPS + 1
            total = taps_ref[pl.ds(0, rows, stride=width), :]
            for s in range(1, width):
                total = total + taps_ref[pl.ds(s, rows, stride=width), :]
            sums_ref[0:TAPS, wide] = total[0:TAPS]
            sums_ref[TERM_ROW : TERM_ROW + 1, wide] = total[TAPS : TAPS + 1]

    for m in range(members):
        lanes = slice(m * share, (m + 1) * share)
        keep_ref[m] = sums_ref[pl.ds(pl.multiple_of(core * HALF_PAD, HALF_PAD), HALF_PAD), lanes].astype(BF)
        give_ref[m] = sums_ref[pl.ds(pl.multiple_of((1 - core) * HALF_PAD, HALF_PAD), HALF_PAD), lanes].astype(BF)


def terms_block(place, grads, order, x_here, weights, mixed, saved):
    images, height, width, channels = x_here.shape
    members = len(grads)
    share = channels // members
    half = SHAPE((members, HALF_PAD, share), BF)
    return pl.pallas_call(
        lambda *refs: terms_kernel(members, *refs),
        out_shape=[half, half, SHAPE(x_here.shape, F32), SHAPE((images, channels), F32)],
        in_specs=[SM] + [VM] * members + [ANY] + [VM] * 10,
        out_specs=[VM] * 4,
        scratch_shapes=[
            pltpu.VMEM((images, channels), F32),
            pltpu.VMEM((images, height, width, LANES), F32),
            pltpu.VMEM((ROWS_PAD, channels), F32),
            pltpu.VMEM(((TAPS + 1) * width, LANES), F32),
        ],
        compiler_params=params(24),
        name="terms_block",
    )(place, *near(grads), order, *near([x_here, *weights, *mixed, *saved]))


def images_kernel(image, place_ref, flow_ref, weight_own, weight_rest, shared_ref, out_ref, token_ref):
    height, width, channels = flow_ref.shape[1:]
    share = weight_own.shape[1]
    own_tiles = share // LANES
    step = pl.program_id(0)
    token_ref[...] = jnp.zeros_like(token_ref)

    def piece(weight_ref, first):
        @pl.loop(0, own_tiles)
        def _(t):
            lanes = lane_block(t, LANES)
            wide = lane_block(t + step * own_tiles, LANES)
            near_lanes = lane_block(t + (step - first) * own_tiles, LANES)
            rows = [flow_ref[image, h, :, wide] for h in range(height)]
            sums = conv_rows(rows, lambda tap: weight_ref[tap : tap + 1, near_lanes], True)
            for h in range(height):
                out_ref[0, h, :, lanes] = (sums[h] + shared_ref[image : image + 1, wide]).astype(BF)

    @pl.when(step == 0)
    def _():
        piece(weight_own, 0)

    @pl.when(step != 0)
    def _():
        piece(weight_rest, 1)


def image_block(image, place, flow, weights, shared, order, out):
    first = out is None
    share = weights[0].shape[1]
    members = flow.shape[3] // share
    operands = [place, *near([flow, *weights, shared]), order] + ([] if first else [out])

    def kernel(*refs):
        images_kernel(image, *refs[:5], refs[-2], refs[-1])

    return pl.pallas_call(
        kernel,
        grid_spec=pltpu.PrefetchScalarGridSpec(
            num_scalar_prefetch=1,
            grid=(members,),
            in_specs=[VM, VM, VM, VM, ANY] + ([] if first else [HB]),
            out_specs=[
                pl.BlockSpec(
                    (1,) + flow.shape[1:3] + (share,),
                    lambda step, place_ref: (image, 0, 0, place_ref[0] ^ step),
                ),
                pl.BlockSpec((8, LANES), lambda step, place_ref: (0, 0)),
            ],
        ),
        out_shape=[SHAPE(flow.shape, BF), SHAPE((8, LANES), F32)],
        input_output_aliases={} if first else {6: 0},
        compiler_params=params(24),
        name="image_block",
    )(*operands)


def head_grads_kernel(block, packed_low, packed_high, text_ref, order_ref, head_ref, text_grad_ref):
    share = packed_low.shape[1] - 2 * text_ref.shape[1]
    width = text_ref.shape[1]
    step = pl.program_id(0)
    lanes = lane_block(step, block)
    grads = slice(share, share + width)
    images = jnp.concatenate([packed_low[:, lanes], packed_high[:, lanes]], axis=0)
    grad = jnp.concatenate([packed_low[:, grads], packed_high[:, grads]], axis=0)
    head_ref[...] = lax.dot_general(
        images, grad, (((0,), (0,)), ((), ())), preferred_element_type=F32
    )

    @pl.when(step == 0)
    def _():
        units = slice(share + width, share + 2 * width)
        unit_all = jnp.concatenate([packed_low[:, units], packed_high[:, units]], axis=0)
        raw = text_ref[...].astype(F32)
        inverse = inverse_norm(raw)
        unit = raw * inverse
        pairs = pair_weights(unit_all, unit.astype(BF))
        text_sum = LOGIT_SCALE * lax.dot_general(
            pairs, unit_all, (((0,), (0,)), ((), ())), preferred_element_type=F32
        )
        text_grad_ref[...] = unit_back(unit, inverse, text_sum)


def head_grads_block(packed, text_feats, share, order):
    rows, width = text_feats.shape
    block = 256 if share % 256 == 0 else LANES
    return pl.pallas_call(
        lambda *refs: head_grads_kernel(block, *refs),
        grid=(share // block,),
        out_shape=[SHAPE((share, width), F32), SHAPE((rows, width), F32)],
        in_specs=[VM, VM, VM, ANY],
        out_specs=[
            pl.BlockSpec((block, width), lambda step: (step, 0)),
            pl.BlockSpec((rows, width), lambda step: (0, 0)),
        ],
        compiler_params=params(24),
        name="head_grads_block",
    )(*near(packed), text_feats, order)


def split_kernel(place_ref, own_ref, other_ref, kernel_ref, term_ref):
    core = place_ref[1]
    rest = TAPS - HALF_PAD
    terms = slice(TERM_ROW - HALF_PAD, TERM_ROW - HALF_PAD + 4)

    def write(low_ref, high_ref):
        kernel_ref[0:HALF_PAD, :] = low_ref[...].astype(F32)
        high = high_ref[...].astype(F32)
        kernel_ref[HALF_PAD:TAPS, :] = high[0:rest]
        term_ref[...] = high[terms]

    @pl.when(core == 0)
    def _():
        write(own_ref, other_ref)

    @pl.when(core != 0)
    def _():
        write(other_ref, own_ref)


def split_block(place, own, other):
    share = own.shape[1]
    return pl.pallas_call(
        split_kernel,
        out_shape=[SHAPE((TAPS, share), F32), SHAPE((4, share), F32)],
        in_specs=[SM, VM, VM],
        out_specs=[VM, VM],
        compiler_params=params(24),
        name="split_block",
    )(place, *near([own, other]))


def per_device(image_maps, dw_kernel, channel_terms, head_weight, text_feats):
    members = lax.axis_size("fsdp")
    member = lax.axis_index("fsdp")
    core = lax.axis_index("dp") % 2
    place = jnp.stack([member, core]).astype(jnp.int32)
    others = range(1, members)
    pair_masks = bits_up(members)
    dp_masks = bits_up(lax.axis_size("dp"))
    down = dp_masks[::-1]
    share = head_weight.shape[0]

    kernels = [swap(dw_kernel, "fsdp", m) for m in others]
    terms = [swap(channel_terms, "fsdp", m) for m in others]
    mixed_own, sum_own, weight_own, x_here = own_block(place, image_maps, dw_kernel, channel_terms)

    text_rows = text_feats
    for mask in pair_masks:
        text_rows = stack_rows(text_rows, swap(text_rows, "fsdp", mask), sum_own)
    text_rows = stack_rows(text_rows, swap(text_rows, "dp", 1), (terms or [sum_own])[-1])
    text_masks = down[:-1]
    pieces, head_here, weight_rest, mixed_rest, saved = forward_block(
        place, head_weight, x_here, (mixed_own, sum_own, weight_own), text_rows, kernels, terms
    )
    weights = (weight_own, weight_rest)
    far_rows = swap(text_rows, "dp", text_masks[0])
    pieces = [pieces[0]] + [swap(pieces[m], "fsdp", m) for m in others]
    group, partial = head_project(pieces, head_here)
    orders = [saved[4]] + [partial] * len(text_masks)
    for mask, order in zip(text_masks[1:], orders):
        text_rows = stack_rows(text_rows, far_rows, order)
        far_rows = swap(text_rows, "dp", mask)
    texts = (text_rows, far_rows)

    partials = [partial] + [swap(partial, "fsdp", m) for m in others]
    packed, grads = loss_block(partials, texts, group, head_here)
    grads = [grads[0]] + [swap(grads[m], "fsdp", m) for m in others]

    packed = stack_rows(packed, swap(packed, "dp", down[0]), packed)
    keep, give, flow, shared = terms_block(
        place, grads, packed, x_here, weights, (mixed_own, mixed_rest), saved
    )
    for mask in down[1:-1]:
        packed = stack_rows(packed, swap(packed, "dp", mask), shared)
    packed = (packed, swap(packed, "dp", down[-1]))

    chip = chip_sums(keep, swap(give, "dp", 1))
    image_grads, token = image_block(0, place, flow, weights, shared, chip[0], None)
    sent = add_all([chip[0]] + [swap(chip[m], "fsdp", m) for m in others], token)
    for image in range(1, image_maps.shape[0]):
        image_grads, token = image_block(image, place, flow, weights, shared, sent, image_grads)
    ring_masks = dp_masks[1:]
    for mask in ring_masks[:-1]:
        sent = add_all([sent, swap(sent, "dp", mask)], token)
    head_grads, text_grads = head_grads_block(packed, text_feats, share, sent)
    sent = add_all([sent, swap(sent, "dp", ring_masks[-1])], text_grads)
    kernel_grads, term_grads = split_block(place, sent, swap(sent, "dp", 1))
    return (image_grads, kernel_grads, term_grads, head_grads, text_grads)


def solution(mesh):
    in_specs = (
        P(("dp", "fsdp"), None, None, None),
        P(None, "fsdp"),
        P(None, "fsdp"),
        P("fsdp", None),
        P(("dp", "fsdp"), None),
    )
    out_specs = (
        P(("dp", "fsdp"), None, None, None),
        P(None, "fsdp"),
        P(None, "fsdp"),
        P("fsdp", None),
        P(("dp", "fsdp"), None),
    )
    return jax.shard_map(
        per_device, mesh=mesh, in_specs=in_specs, out_specs=out_specs, check_vma=False
    )
```

time: 91 us -> 76.1 us (0.84)
  Pallas kernels: 22.9 us -> 33.6 us
  starting transfers between devices: 27.1 us -> 18.1 us
  matrix products: 4.65 us -> 0 us
  local copies, waits for them, and re-layouts: 5.89 us -> 1.39 us
  waiting for transfers between devices: 25.9 us -> 21.9 us
  other arithmetic: 3.38 us -> 0.07 us
    pallas_call x3 -> x19, Pallas kernels: 8.15 us -> 21.3 us  [the longest x2 8.31 us: image_block(): pl.pallas_call(kernel, grid_spec=pltpu.PrefetchScalarGridSpec(num_scalar_...]
    ppermute x20, starting transfers between devices: 27.1 us -> 18.1 us  [swap(): lax.ppermute(value, axis, [(source, source ^ mask) for source in range(co...]
    dot_general x2 -> x0, matrix products: 4.65 us -> none  [the longest x1 4.08 us: per_device(): lax.dot_general(group_all, grad_all, (((0,), (0,)), ((), ())), preferred_...]
    ppermute x20, waiting for transfers between devices: 25.9 us -> 21.9 us  [swap(): lax.ppermute(value, axis, [(source, source ^ mask) for source in range(co...]
    unnamed x16 -> x6, local copies, waits for them, and re-layouts: 4.81 us -> 1.39 us
    pallas_call x1, Pallas kernels: 7.68 us -> 5.07 us  [forward_block(): pl.pallas_call(lambda *refs: forward_kernel(members, *refs), out_shape=ou...]
    convert_element_type x7 -> x0, other arithmetic: 0.95 us -> none  [the longest x1 0.77 us: per_device(): own_text = text_unit.astype(BF)]
  transfers between devices with their start and end apart: 20 -> 20, of which waited for: 14 -> 9; matrix products, arithmetic and copies ran while one was open for 7% -> 0% of each run, Pallas kernels for 23% -> 31%
where the time goes in v3:
time: 76.1 us; the launch traced here: 75.9 us
  Pallas kernels  33.6 us (44%)
  waiting for transfers between devices  21.9 us (29%)
  starting transfers between devices  18.1 us (24%)
  local copies, waits for them, and re-layouts  1.39 us (2%)
  between operations  0.8 us (1%)
    ppermute x20, waiting for transfers between devices, swap(): lax.ppermute(value, axis, [(source, source ^ mask) for source in range(co...  21.9 us
    ppermute x20, starting transfers between devices, swap(): lax.ppermute(value, axis, [(source, source ^ mask) for source in range(co...  18.1 us
    pallas_call x2, Pallas kernels, image_block(): pl.pallas_call(kernel, grid_spec=pltpu.PrefetchScalarGridSpec(num_scalar_...  8.31 us
    pallas_call x1, Pallas kernels, terms_block(): pl.pallas_call(lambda *refs: terms_kernel(members, *refs), out_shape=[hal...  7.19 us
    pallas_call x1, Pallas kernels, forward_block(): pl.pallas_call(lambda *refs: forward_kernel(members, *refs), out_shape=ou...  5.07 us
    pallas_call x1, Pallas kernels, head_grads_block(): pl.pallas_call(lambda *refs: head_grads_kernel(block, *refs), grid=(share...  5.04 us
    pallas_call x1, Pallas kernels, own_block(): pl.pallas_call(lambda *refs: own_kernel(members, *refs), out_shape=[SHAPE...  4.41 us
  transfers between devices with their start and end apart: 20, of which 9 were waited for; matrix products, arithmetic and copies ran while one was open for 0% of the time, Pallas kernels for 31%

profile of v3, /device:TPU:0, one launch (start us, length us, event | category | flops | bytes accessed | tf_op | source)
XLA Modules:
  0.0 75.9 jit_solution(13342430928993798823)
XLA Ops:
  0.6 3.0 %collective-permute-start.3 = (bf16[49,1536]{1,0:T(8,128)(2,1)}, bf16[49,1536]{1,0:T(8,128)(2,1)S(1)}, u32[]{:S(2)}, u32[]{:S(2)}) collective-permute-start(bf16[49,1536]{1,0:T(8,128)(2,1)} %refs_2_.2), channel_id=1, source_target_pairs={{0,1},{1,0},{2,3},{3,2},{4,5},{5,4},{6,7},{7,6},{8,9},{9,8},{10,11... | collective-permute-start | bytes 451592 | tf_op jit(solution)/shard_map/ppermute | solution.py:24
  3.7 0.1 collective-permute-start
  3.7 1.9 %collective-permute-start.2 = (bf16[4,1536]{1,0:T(4,128)(2,1)}, bf16[4,1536]{1,0:T(4,128)(2,1)S(1)}, u32[]{:S(2)}, u32[]{:S(2)}) collective-permute-start(bf16[4,1536]{1,0:T(4,128)(2,1)} %refs_3_.1), channel_id=1, source_target_pairs={{0,1},{1,0},{2,3},{3,2},{4,5},{5,4},{6,7},{7,6},{8,9},{9,8},{10,11... | collective-permute-start | bytes 36872 | tf_op jit(solution)/shard_map/ppermute | solution.py:24
  5.7 0.1 pad_add_fusion.refs_0_.place_ref
  5.8 4.4 %own_block.1 = (f32[2,8,8,1536]{3,2,1,0:T(8,128)S(1)}, f32[2,8,8,128]{3,2,1,0:T(8,128)S(1)}, f32[64,1536]{1,0:T(8,128)S(1)}, bf16[2,8,8,3072]{3,2,1,0:T(8,128)(2,1)S(1)}) custom-call(s32[2]{0:T(128)S(1)} %pad_add_fusion.refs_0_.place_ref, bf16[2,8,8,3072]{3,2,1,0:T(8,128)(2,1)} %refs_1_.2, bf16[49,1536]{1,0:T(8,128)(2,1)} %refs_2_.2, bf16[4,1536]{1,0:T(4,128)(2,1)} %refs_3_.1), custom_call_target="tpu_custom_call" | custom-call | tf_op jit(solution)/shard_map/own_block/pallas_call | solution.py:194
  10.2 0.0 collective-permute-done.high_ref
  10.2 0.0 copy-start
  10.2 0.7 copy-done
  10.9 0.1 collective-permute-start.1
  11.0 1.1 %collective-permute-done.1.high_ref = bf16[4,1152]{1,0:T(4,128)(2,1)S(1)} collective-permute-done((bf16[4,1152]{1,0:T(4,128)(2,1)S(1)}, bf16[4,1152]{1,0:T(4,128)(2,1)S(1)}, u32[]{:S(2)}, u32[]{:S(2)}) %collective-permute-start.1) | collective-permute-done | bytes 9248 | tf_op jit(solution)/shard_map/ppermute | solution.py:24
  12.2 2.7 %collective-permute-start.6 = (bf16[8,1152]{1,0:T(8,128)(2,1)S(1)}, bf16[8,1152]{1,0:T(8,128)(2,1)S(1)}, u32[]{:S(2)}, u32[]{:S(2)}) collective-permute-start(bf16[8,1152]{1,0:T(8,128)(2,1)S(1)} %stack_rows.8.refs_6_.low_ref), channel_id=1, source_target_pairs={{0,16},{2,18},{4,20},{6,22},{8,24},{10,26},{12,28},{14,30},{16,0},... | collective-permute-start | bytes 55304 | tf_op jit(solution)/shard_map/ppermute | solution.py:24
  14.8 0.0 collective-permute-done.3.refs_7_
  14.8 5.1 %forward_block.1 = (bf16[2,1536]{1,0:T(2,128)(2,1)S(1)}, bf16[2,1536]{1,0:T(2,128)(2,1)S(1)}, bf16[1536,1152]{1,0:T(8,128)(2,1)S(1)}, f32[64,1536]{1,0:T(8,128)S...) custom-call(s32[2]{0:T(128)S(1)} %pad_add_fusion.refs_0_.place_ref, ...), custom_call_target="tpu_custom_call" | custom-call | tf_op jit(solution)/shard_map/forward_block/pallas_call | solution.py:304
  19.9 0.0 collective-permute-done.6.high_ref
  19.9 1.6 %collective-permute-start.7 = (bf16[16,1152]{1,0:T(8,128)(2,1)S(1)}, bf16[16,1152]{1,0:T(8,128)(2,1)S(1)}, u32[]{:S(2)}, u32[]{:S(2)}) collective-permute-start(bf16[16,1152]{1,0:T(8,128)(2,1)S(1)} %stack_rows.9.low_ref), channel_id=1, source_target_pairs={{0,8},{2,10},{4,12},{6,14},{8,0},{10,2},{12,4},{14,6},{16,24},{18,... | collective-permute-start | bytes 110600 | tf_op jit(solution)/shard_map/ppermute | solution.py:24
  21.6 0.5 collective-permute-start.4
  22.1 3.1 %collective-permute-done.4.refs_1_ = bf16[2,1536]{1,0:T(2,128)(2,1)S(1)} collective-permute-done((bf16[2,1536]{1,0:T(2,128)(2,1)S(1)}, bf16[2,1536]{1,0:T(2,128)(2,1)S(1)}, u32[]{:S(2)}, u32[]{:S(2)}) %collective-permute-start.4) | collective-permute-done | bytes 6176 | tf_op jit(solution)/shard_map/ppermute | solution.py:24
  25.2 0.6 head_project.1
  25.8 1.6 %collective-permute-start.8 = (bf16[32,1152]{1,0:T(8,128)(2,1)S(1)}, bf16[32,1152]{1,0:T(8,128)(2,1)S(1)}, u32[]{:S(2)}, u32[]{:S(2)}) collective-permute-start(bf16[32,1152]{1,0:T(8,128)(2,1)S(1)} %stack_rows.10.refs_2_), channel_id=1, source_target_pairs={{0,4},{2,6},{4,0},{6,2},{8,12},{10,14},{12,8},{14,10},{16,20},{18,... | collective-permute-start | bytes 221192 | tf_op jit(solution)/shard_map/ppermute | solution.py:24
  27.3 0.5 collective-permute-start.5
  27.8 3.3 %collective-permute-done.5.refs_1_ = f32[4,1152]{1,0:T(4,128)S(1)} collective-permute-done((f32[4,1152]{1,0:T(4,128)S(1)}, f32[4,1152]{1,0:T(4,128)S(1)}, u32[]{:S(2)}, u32[]{:S(2)}) %collective-permute-start.5) | collective-permute-done | bytes 18464 | tf_op jit(solution)/shard_map/ppermute | solution.py:24
  31.1 1.5 %loss_block.1 = (bf16[4,3840]{1,0:T(4,128)(2,1)S(1)}, f32[2,1536]{1,0:T(2,128)S(1)}, f32[2,1536]{1,0:T(2,128)S(1)}) custom-call(f32[4,1152]{1,0:T(4,128)S(1)} %get-tuple-element.45.order_ref.refs_0_, f32[4,1152]{1,0:T(4,128)S(1)} %collective-permute-done.5.refs_1_, bf16[32,1152]{1,0:T(8,128)(2,1)S(1)} %stack_rows.10.refs_2_, ...), custom_call_target="tpu_custom_call" | custom-call | tf_op jit(solution)/shard_map/loss_block/pallas_call | solution.py:396
  32.6 0.4 collective-permute-start.10
  32.9 0.5 collective-permute-start.9
  33.4 4.2 %collective-permute-done.10.high_ref = bf16[4,3840]{1,0:T(4,128)(2,1)S(1)} collective-permute-done((bf16[4,3840]{1,0:T(4,128)(2,1)S(1)}, bf16[4,3840]{1,0:T(4,128)(2,1)S(1)}, u32[]{:S(2)}, u32[]{:S(2)}) %collective-permute-start.10) | collective-permute-done | bytes 30752 | tf_op jit(solution)/shard_map/ppermute | solution.py:24
  37.6 0.0 collective-permute-done.9.refs_2_
  37.6 7.2 %terms_block.1 = (bf16[2,32,1536]{2,1,0:T(8,128)(2,1)S(1)}, bf16[2,32,1536]{2,1,0:T(8,128)(2,1)S(1)}, f32[2,8,8,3072]{3,2,1,0:T(8,128)S(1)}, f32[2,3072]{1,0:T(2,128)S(1)}) custom-call(s32[2]{0:T(128)S(1)} %pad_add_fusion.refs_0_.place_ref, f32[2,1536]{1,0:T(2,128)S(1)} %get-tuple-element.48.refs_1_, f32[2,1536]{1,0:T(2,128)S(1)} %collective-permute-done.9.refs_2_, ...), custom_call_target="tpu_custom_call" | custom-call | tf_op jit(solution)/shard_map/terms_block/pallas_call | solution.py:518
  44.8 0.1 collective-permute-start.11
  44.9 0.3 collective-permute-start.16
  45.2 1.1 %collective-permute-done.11.give_ref = bf16[2,32,1536]{2,1,0:T(8,128)(2,1)S(1)} collective-permute-done((bf16[2,32,1536]{2,1,0:T(8,128)(2,1)S(1)}, bf16[2,32,1536]{2,1,0:T(8,128)(2,1)S(1)}, u32[]{:S(2)}, u32[]{:S(2)}) %collective-permute-start.11) | collective-permute-done | bytes 196640 | tf_op jit(solution)/shard_map/ppermute | solution.py:24
  46.3 0.1 chip_sums.1
  46.4 0.6 collective-permute-start.12
  46.9 2.4 %collective-permute-done.16.high_ref = bf16[8,3840]{1,0:T(8,128)(2,1)S(1)} collective-permute-done((bf16[8,3840]{1,0:T(8,128)(2,1)S(1)}, bf16[8,3840]{1,0:T(8,128)(2,1)S(1)}, u32[]{:S(2)}, u32[]{:S(2)}) %collective-permute-start.16) | collective-permute-done | bytes 61472 | tf_op jit(solution)/shard_map/ppermute | solution.py:24
  49.3 0.7 collective-permute-start.17
  50.0 4.1 %image_block.2 = (bf16[2,8,8,3072]{3,2,1,0:T(8,128)(2,1)}, f32[8,128]{1,0:T(8,128)S(1)}) custom-call(s32[2]{0:T(128)S(1)} %pad_add_fusion.refs_0_.place_ref, f32[2,8,8,3072]{3,2,1,0:T(8,128)S(1)} %get-tuple-element.57.refs_1_, f32[64,1536]{1,0:T(8,128)S(1)} %get-tuple-element.41.refs_5_.refs_2_, f32[64,1536]{1,0:T(8,128)S(1)} %get-tuple-element.51.refs_6_.refs_3_, ...), custom_call_target="tpu_custom_call" | custom-call | tf_op jit(solution)/shard_map/image_block/pallas_call | solution.py:570
  54.2 1.5 %collective-permute-start.13 = (bf16[32,1536]{1,0:T(8,128)(2,1)S(1)}, bf16[32,1536]{1,0:T(8,128)(2,1)S(1)}, u32[]{:S(2)}, u32[]{:S(2)}) collective-permute-start(bf16[32,1536]{1,0:T(8,128)(2,1)S(1)} %add_all.4.refs_5_.refs_0_), channel_id=1, source_target_pairs={{0,4},{2,6},{4,0},{6,2},{8,12},{10,14},{12,8},{14,10},{16,20},{18,... | collective-permute-start | bytes 294920 | tf_op jit(solution)/shard_map/ppermute | solution.py:24
  55.7 0.0 collective-permute-done.17.high_ref
  55.7 0.1 collective-permute-start.18
  55.8 4.2 %image_block.3 = (bf16[2,8,8,3072]{3,2,1,0:T(8,128)(2,1)}, f32[8,128]{1,0:T(8,128)S(1)}) custom-call(s32[2]{0:T(128)S(1)} %pad_add_fusion.refs_0_.place_ref, f32[2,8,8,3072]{3,2,1,0:T(8,128)S(1)} %get-tuple-element.57.refs_1_, f32[64,1536]{1,0:T(8,128)S(1)} %get-tuple-element.41.refs_5_.refs_2_, ...), custom_call_target="tpu_custom_call", output_to_operand_aliasing={{0}: (6, {})} | custom-call | tf_op jit(solution)/shard_map/image_block/pallas_call | solution.py:570
  60.0 0.3 collective-permute-start.14
  60.3 4.9 %collective-permute-done.14.refs_1_ = bf16[32,1536]{1,0:T(8,128)(2,1)S(1)} collective-permute-done((bf16[32,1536]{1,0:T(8,128)(2,1)S(1)}, bf16[32,1536]{1,0:T(8,128)(2,1)S(1)}, u32[]{:S(2)}, u32[]{:S(2)}) %collective-permute-start.14) | collective-permute-done | bytes 98336 | tf_op jit(solution)/shard_map/ppermute | solution.py:24
  65.2 1.6 %collective-permute-start.15 = (bf16[32,1536]{1,0:T(8,128)(2,1)S(1)}, bf16[32,1536]{1,0:T(8,128)(2,1)S(1)}, u32[]{:S(2)}, u32[]{:S(2)}) collective-permute-start(bf16[32,1536]{1,0:T(8,128)(2,1)S(1)} %add_all.6.refs_3_.refs_0_), channel_id=1, source_target_pairs={{0,16},{2,18},{4,20},{6,22},{8,24},{10,26},{12,28},{14,30},{16,0},... | collective-permute-start | bytes 294920 | tf_op jit(solution)/shard_map/ppermute | solution.py:24
  66.9 5.0 %head_grads_block.1 = (f32[1536,1152]{1,0:T(8,128)}, f32[2,1152]{1,0:T(2,128)}) custom-call(bf16[32,3840]{1,0:T(8,128)(2,1)S(1)} %stack_rows.13.refs_0_, bf16[32,3840]{1,0:T(8,128)(2,1)S(1)} %collective-permute-done.18.refs_1_, bf16[2,1152]{1,0:T(2,128)(2,1)S(1)} %copy-done.1, bf16[32,1536]{1,0:T(8,128)(2,1)S(1)} %add_all.6.refs_3_.refs_0_), custom_call_target="tpu_custom_call" | custom-call | tf_op jit(solution)/shard_map/head_grads_block/pallas_call | solution.py:620
  71.9 0.5 collective-permute-done.15.refs_1_
  72.5 0.7 copy-done.2
  73.2 0.1 collective-permute-start.19
  73.3 1.3 %collective-permute-done.19.other_ref = bf16[32,1536]{1,0:T(8,128)(2,1)S(1)} collective-permute-done((bf16[32,1536]{1,0:T(8,128)(2,1)S(1)}, bf16[32,1536]{1,0:T(8,128)(2,1)S(1)}, u32[]{:S(2)}, u32[]{:S(2)}) %collective-permute-start.19) | collective-permute-done | bytes 98336 | tf_op jit(solution)/shard_map/ppermute | solution.py:24
  74.6 1.3 %split_block.1 = (f32[49,1536]{1,0:T(8,128)}, f32[4,1536]{1,0:T(4,128)}) custom-call(s32[2]{0:T(128)S(1)} %pad_add_fusion.refs_0_.place_ref, bf16[32,1536]{1,0:T(8,128)(2,1)S(1)} %add_all.7.own_ref, bf16[32,1536]{1,0:T(8,128)(2,1)S(1)} %collective-permute-done.19.other_ref), custom_call_target="tpu_custom_call" | custom-call | tf_op jit(solution)/shard_map/split_block/pallas_call | solution.py:656
  (20 shorter events, 0.2 us)
Async XLA Ops:
  0.6 14.2 %collective-permute-start.3 = (bf16[49,1536]{1,0:T(8,128)(2,1)}, bf16[49,1536]{1,0:T(8,128)(2,1)S(1)}, u32[]{:S(2)}, u32[]{:S(2)}) collective-permute-start(bf16[49,1536]{1,0:T(8,128)(2,1)} %refs_2_.2), channel_id=1, source_target_pairs={{0,1},{1,0},{2,3},{3,2},{4,5},{5,4},{6,7},{7,6},{8,9},{9,8},{10,11... | collective-permute-start | bytes 451592 | tf_op jit(solution)/shard_map/ppermute | solution.py:24
  3.7 6.5 %collective-permute-start = (bf16[2,1152]{1,0:T(2,128)(2,1)}, bf16[2,1152]{1,0:T(2,128)(2,1)S(1)}, u32[]{:S(2)}, u32[]{:S(2)}) collective-permute-start(bf16[2,1152]{1,0:T(2,128)(2,1)} %refs_2_.3), channel_id=1, source_target_pairs={{0,1},{1,0},{2,3},{3,2},{4,5},{5,4},{6,7},{7,6},{8,9},{9,8},{10,11... | collective-permute-start | bytes 13832 | tf_op jit(solution)/shard_map/ppermute | solution.py:24
  3.7 7.2 %collective-permute-start.2 = (bf16[4,1536]{1,0:T(4,128)(2,1)}, bf16[4,1536]{1,0:T(4,128)(2,1)S(1)}, u32[]{:S(2)}, u32[]{:S(2)}) collective-permute-start(bf16[4,1536]{1,0:T(4,128)(2,1)} %refs_3_.1), channel_id=1, source_target_pairs={{0,1},{1,0},{2,3},{3,2},{4,5},{5,4},{6,7},{7,6},{8,9},{9,8},{10,11... | collective-permute-start | bytes 36872 | tf_op jit(solution)/shard_map/ppermute | solution.py:24
  10.2 0.7 copy-start
  10.9 1.2 %collective-permute-start.1 = (bf16[4,1152]{1,0:T(4,128)(2,1)S(1)}, bf16[4,1152]{1,0:T(4,128)(2,1)S(1)}, u32[]{:S(2)}, u32[]{:S(2)}) collective-permute-start(bf16[4,1152]{1,0:T(4,128)(2,1)S(1)} %stack_rows.7.low_ref), channel_id=1, source_target_pairs={{0,2},{2,0},{4,6},{6,4},{8,10},{10,8},{12,14},{14,12},{16,18},{18,... | collective-permute-start | bytes 27656 | tf_op jit(solution)/shard_map/ppermute | solution.py:24
  12.2 7.7 %collective-permute-start.6 = (bf16[8,1152]{1,0:T(8,128)(2,1)S(1)}, bf16[8,1152]{1,0:T(8,128)(2,1)S(1)}, u32[]{:S(2)}, u32[]{:S(2)}) collective-permute-start(bf16[8,1152]{1,0:T(8,128)(2,1)S(1)} %stack_rows.8.refs_6_.low_ref), channel_id=1, source_target_pairs={{0,16},{2,18},{4,20},{6,22},{8,24},{10,26},{12,28},{14,30},{16,0},... | collective-permute-start | bytes 55304 | tf_op jit(solution)/shard_map/ppermute | solution.py:24
  19.9 5.8 %collective-permute-start.7 = (bf16[16,1152]{1,0:T(8,128)(2,1)S(1)}, bf16[16,1152]{1,0:T(8,128)(2,1)S(1)}, u32[]{:S(2)}, u32[]{:S(2)}) collective-permute-start(bf16[16,1152]{1,0:T(8,128)(2,1)S(1)} %stack_rows.9.low_ref), channel_id=1, source_target_pairs={{0,8},{2,10},{4,12},{6,14},{8,0},{10,2},{12,4},{14,6},{16,24},{18,... | collective-permute-start | bytes 110600 | tf_op jit(solution)/shard_map/ppermute | solution.py:24
  21.6 3.6 %collective-permute-start.4 = (bf16[2,1536]{1,0:T(2,128)(2,1)S(1)}, bf16[2,1536]{1,0:T(2,128)(2,1)S(1)}, u32[]{:S(2)}, u32[]{:S(2)}) collective-permute-start(bf16[2,1536]{1,0:T(2,128)(2,1)S(1)} %get-tuple-element.43), channel_id=1, source_target_pairs={{0,1},{1,0},{2,3},{3,2},{4,5},{5,4},{6,7},{7,6},{8,9},{9,8},{10,11... | collective-permute-start | bytes 18440 | tf_op jit(solution)/shard_map/ppermute | solution.py:24
  25.8 5.3 %collective-permute-start.8 = (bf16[32,1152]{1,0:T(8,128)(2,1)S(1)}, bf16[32,1152]{1,0:T(8,128)(2,1)S(1)}, u32[]{:S(2)}, u32[]{:S(2)}) collective-permute-start(bf16[32,1152]{1,0:T(8,128)(2,1)S(1)} %stack_rows.10.refs_2_), channel_id=1, source_target_pairs={{0,4},{2,6},{4,0},{6,2},{8,12},{10,14},{12,8},{14,10},{16,20},{18,... | collective-permute-start | bytes 221192 | tf_op jit(solution)/shard_map/ppermute | solution.py:24
  27.3 3.8 %collective-permute-start.5 = (f32[4,1152]{1,0:T(4,128)S(1)}, f32[4,1152]{1,0:T(4,128)S(1)}, u32[]{:S(2)}, u32[]{:S(2)}) collective-permute-start(f32[4,1152]{1,0:T(4,128)S(1)} %get-tuple-element.45.order_ref.refs_0_), channel_id=1, source_target_pairs={{0,1},{1,0},{2,3},{3,2},{4,5},{5,4},{6,7},{7,6},{8,9},{9,8},{10,11... | collective-permute-start | bytes 55304 | tf_op jit(solution)/shard_map/ppermute | solution.py:24
  32.6 5.0 %collective-permute-start.10 = (bf16[4,3840]{1,0:T(4,128)(2,1)S(1)}, bf16[4,3840]{1,0:T(4,128)(2,1)S(1)}, u32[]{:S(2)}, u32[]{:S(2)}) collective-permute-start(bf16[4,3840]{1,0:T(4,128)(2,1)S(1)} %get-tuple-element.50.low_ref.order_ref), channel_id=1, source_target_pairs={{0,16},{2,18},{4,20},{6,22},{8,24},{10,26},{12,28},{14,30},{16,0},... | collective-permute-start | bytes 92168 | tf_op jit(solution)/shard_map/ppermute | solution.py:24
  32.9 4.7 %collective-permute-start.9 = (f32[2,1536]{1,0:T(2,128)S(1)}, f32[2,1536]{1,0:T(2,128)S(1)}, u32[]{:S(2)}, u32[]{:S(2)}) collective-permute-start(f32[2,1536]{1,0:T(2,128)S(1)} %get-tuple-element.49), channel_id=1, source_target_pairs={{0,1},{1,0},{2,3},{3,2},{4,5},{5,4},{6,7},{7,6},{8,9},{9,8},{10,11... | collective-permute-start | bytes 36872 | tf_op jit(solution)/shard_map/ppermute | solution.py:24
  44.8 1.5 %collective-permute-start.11 = (bf16[2,32,1536]{2,1,0:T(8,128)(2,1)S(1)}, bf16[2,32,1536]{2,1,0:T(8,128)(2,1)S(1)}, u32[]{:S(2)}, u32[]{:S(2)}) collective-permute-start(bf16[2,32,1536]{2,1,0:T(8,128)(2,1)S(1)} %get-tuple-element.60), channel_id=1, source_target_pairs={{0,2},{2,0},{4,6},{6,4},{8,10},{10,8},{12,14},{14,12},{16,18},{18,... | collective-permute-start | bytes 589832 | tf_op jit(solution)/shard_map/ppermute | solution.py:24
  44.9 4.4 %collective-permute-start.16 = (bf16[8,3840]{1,0:T(8,128)(2,1)S(1)}, bf16[8,3840]{1,0:T(8,128)(2,1)S(1)}, u32[]{:S(2)}, u32[]{:S(2)}) collective-permute-start(bf16[8,3840]{1,0:T(8,128)(2,1)S(1)} %stack_rows.11.refs_3_.low_ref), channel_id=1, source_target_pairs={{0,8},{2,10},{4,12},{6,14},{8,0},{10,2},{12,4},{14,6},{16,24},{18,... | collective-permute-start | bytes 184328 | tf_op jit(solution)/shard_map/ppermute | solution.py:24
  46.4 7.8 %collective-permute-start.12 = (bf16[32,1536]{1,0:T(8,128)(2,1)S(1)}, bf16[32,1536]{1,0:T(8,128)(2,1)S(1)}, u32[]{:S(2)}, u32[]{:S(2)}) collective-permute-start(bf16[32,1536]{1,0:T(8,128)(2,1)S(1)} %get-tuple-element.62), channel_id=1, source_target_pairs={{0,1},{1,0},{2,3},{3,2},{4,5},{5,4},{6,7},{7,6},{8,9},{9,8},{10,11... | collective-permute-start | bytes 294920 | tf_op jit(solution)/shard_map/ppermute | solution.py:24
  49.3 6.3 %collective-permute-start.17 = (bf16[16,3840]{1,0:T(8,128)(2,1)S(1)}, bf16[16,3840]{1,0:T(8,128)(2,1)S(1)}, u32[]{:S(2)}, u32[]{:S(2)}) collective-permute-start(bf16[16,3840]{1,0:T(8,128)(2,1)S(1)} %stack_rows.12.low_ref), channel_id=1, source_target_pairs={{0,4},{2,6},{4,0},{6,2},{8,12},{10,14},{12,8},{14,10},{16,20},{18,... | collective-permute-start | bytes 368648 | tf_op jit(solution)/shard_map/ppermute | solution.py:24
  50.0 16.9 %copy-start.1 = (bf16[2,1152]{1,0:T(2,128)(2,1)S(1)}, bf16[2,1152]{1,0:T(2,128)(2,1)}, u32[]{:S(2)}) copy-start(bf16[2,1152]{1,0:T(2,128)(2,1)} %refs_2_.3) | copy-start | bytes 13828
  54.2 5.8 %collective-permute-start.13 = (bf16[32,1536]{1,0:T(8,128)(2,1)S(1)}, bf16[32,1536]{1,0:T(8,128)(2,1)S(1)}, u32[]{:S(2)}, u32[]{:S(2)}) collective-permute-start(bf16[32,1536]{1,0:T(8,128)(2,1)S(1)} %add_all.4.refs_5_.refs_0_), channel_id=1, source_target_pairs={{0,4},{2,6},{4,0},{6,2},{8,12},{10,14},{12,8},{14,10},{16,20},{18,... | collective-permute-start | bytes 294920 | tf_op jit(solution)/shard_map/ppermute | solution.py:24
  55.7 11.2 %collective-permute-start.18 = (bf16[32,3840]{1,0:T(8,128)(2,1)S(1)}, bf16[32,3840]{1,0:T(8,128)(2,1)S(1)}, u32[]{:S(2)}, u32[]{:S(2)}) collective-permute-start(bf16[32,3840]{1,0:T(8,128)(2,1)S(1)} %stack_rows.13.refs_0_), channel_id=1, source_target_pairs={{0,2},{2,0},{4,6},{6,4},{8,10},{10,8},{12,14},{14,12},{16,18},{18,... | collective-permute-start | bytes 737288 | tf_op jit(solution)/shard_map/ppermute | solution.py:24
  60.0 5.3 %collective-permute-start.14 = (bf16[32,1536]{1,0:T(8,128)(2,1)S(1)}, bf16[32,1536]{1,0:T(8,128)(2,1)S(1)}, u32[]{:S(2)}, u32[]{:S(2)}) collective-permute-start(bf16[32,1536]{1,0:T(8,128)(2,1)S(1)} %add_all.5.refs_0_), channel_id=1, source_target_pairs={{0,8},{2,10},{4,12},{6,14},{8,0},{10,2},{12,4},{14,6},{16,24},{18,... | collective-permute-start | bytes 294920 | tf_op jit(solution)/shard_map/ppermute | solution.py:24
  65.2 7.2 %collective-permute-start.15 = (bf16[32,1536]{1,0:T(8,128)(2,1)S(1)}, bf16[32,1536]{1,0:T(8,128)(2,1)S(1)}, u32[]{:S(2)}, u32[]{:S(2)}) collective-permute-start(bf16[32,1536]{1,0:T(8,128)(2,1)S(1)} %add_all.6.refs_3_.refs_0_), channel_id=1, source_target_pairs={{0,16},{2,18},{4,20},{6,22},{8,24},{10,26},{12,28},{14,30},{16,0},... | collective-permute-start | bytes 294920 | tf_op jit(solution)/shard_map/ppermute | solution.py:24
  72.5 0.7 copy-start.2
  73.2 1.4 %collective-permute-start.19 = (bf16[32,1536]{1,0:T(8,128)(2,1)S(1)}, bf16[32,1536]{1,0:T(8,128)(2,1)S(1)}, u32[]{:S(2)}, u32[]{:S(2)}) collective-permute-start(bf16[32,1536]{1,0:T(8,128)(2,1)S(1)} %add_all.7.own_ref), channel_id=1, source_target_pairs={{0,2},{2,0},{4,6},{6,4},{8,10},{10,8},{12,14},{14,12},{16,18},{18,... | collective-permute-start | bytes 294920 | tf_op jit(solution)/shard_map/ppermute | solution.py:24

commit v4 on v3

--- a/solution.py
+++ b/solution.py
@@ -160,7 +160,7 @@
 
 
 def own_kernel(
-    members, place_ref, x_hbm, kernel_hbm, term_hbm, mixed_ref, sum_ref, weight_ref, x_ref, kernel_ref, term_ref, sems
+    members, place_ref, x_hbm, kernel_hbm, term_hbm, text_hbm, mixed_ref, sum_ref, weight_ref, x_ref, text_ref, kernel_ref, term_ref, sems
 ):
     share = kernel_hbm.shape[1]
     member = place_ref[0]
@@ -175,6 +175,7 @@
                 x_hbm.at[:, :, :, lanes], x_ref.at[:, :, :, lanes], sems.at[2 + m]
             )
         )
+    copies.append(pltpu.make_async_copy(text_hbm, text_ref, sems.at[2 + members]))
     for copy in copies:
         copy.start()
     sum_ref[...] = jnp.zeros_like(sum_ref)
@@ -187,7 +188,7 @@
         copy.wait()
 
 
-def own_block(place, image_maps, dw_kernel, channel_terms):
+def own_block(place, image_maps, dw_kernel, channel_terms, text_feats):
     images, height, width, channels = image_maps.shape
     share = dw_kernel.shape[1]
     members = channels // share
@@ -198,17 +199,18 @@
             SHAPE((images, height, width, LANES), F32),
             SHAPE((ROWS_PAD, share), F32),
             SHAPE(image_maps.shape, BF),
+            SHAPE(text_feats.shape, BF),
         ],
-        in_specs=[SM, HB, HB, HB],
-        out_specs=[VM] * 4,
+        in_specs=[SM, HB, HB, HB, HB],
+        out_specs=[VM] * 5,
         scratch_shapes=[
             pltpu.VMEM(dw_kernel.shape, BF),
             pltpu.VMEM(channel_terms.shape, BF),
-            pltpu.SemaphoreType.DMA((2 + members,)),
+            pltpu.SemaphoreType.DMA((3 + members,)),
         ],
         compiler_params=params(24),
         name="own_block",
-    )(place, *far([image_maps, dw_kernel, channel_terms]))
+    )(place, *far([image_maps, dw_kernel, channel_terms, text_feats]))
 
 
 def forward_kernel(members, place_ref, head_hbm, x_ref, mixed_own, sum_own, weight_own, order_ref, *refs):
@@ -531,11 +533,11 @@
     )(place, *near(grads), order, *near([x_here, *weights, *mixed, *saved]))
 
 
-def images_kernel(image, place_ref, flow_ref, weight_own, weight_rest, shared_ref, out_ref, token_ref):
+def images_kernel(image, base, place_ref, flow_ref, weight_own, weight_rest, shared_ref, out_ref, token_ref):
     height, width, channels = flow_ref.shape[1:]
     share = weight_own.shape[1]
     own_tiles = share // LANES
-    step = pl.program_id(0)
+    step = pl.program_id(0) + base
     token_ref[...] = jnp.zeros_like(token_ref)
 
     def piece(weight_ref, first):
@@ -549,34 +551,35 @@
             for h in range(height):
                 out_ref[0, h, :, lanes] = (sums[h] + shared_ref[image : image + 1, wide]).astype(BF)
 
-    @pl.when(step == 0)
-    def _():
-        piece(weight_own, 0)
+    if base == 0:
+
+        @pl.when(step == 0)
+        def _():
+            piece(weight_own, 0)
 
     @pl.when(step != 0)
     def _():
         piece(weight_rest, 1)
 
 
-def image_block(image, place, flow, weights, shared, order, out):
+def image_block(image, base, count, place, flow, weights, shared, order, out):
     first = out is None
     share = weights[0].shape[1]
-    members = flow.shape[3] // share
     operands = [place, *near([flow, *weights, shared]), order] + ([] if first else [out])
 
     def kernel(*refs):
-        images_kernel(image, *refs[:5], refs[-2], refs[-1])
+        images_kernel(image, base, *refs[:5], refs[-2], refs[-1])
 
     return pl.pallas_call(
         kernel,
         grid_spec=pltpu.PrefetchScalarGridSpec(
             num_scalar_prefetch=1,
-            grid=(members,),
+            grid=(count,),
             in_specs=[VM, VM, VM, VM, ANY] + ([] if first else [HB]),
             out_specs=[
                 pl.BlockSpec(
                     (1,) + flow.shape[1:3] + (share,),
-                    lambda step, place_ref: (image, 0, 0, place_ref[0] ^ step),
+                    lambda step, place_ref: (image, 0, 0, place_ref[0] ^ (step + base)),
                 ),
                 pl.BlockSpec((8, LANES), lambda step, place_ref: (0, 0)),
             ],
@@ -588,7 +591,7 @@
     )(*operands)
 
 
-def head_grads_kernel(block, packed_low, packed_high, text_ref, order_ref, head_ref, text_grad_ref):
+def head_grads_kernel(block, packed_low, packed_high, text_ref, order_ref, head_ref, text_grad_ref, token_ref):
     share = packed_low.shape[1] - 2 * text_ref.shape[1]
     width = text_ref.shape[1]
     step = pl.program_id(0)
@@ -602,6 +605,7 @@
 
     @pl.when(step == 0)
     def _():
+        token_ref[...] = jnp.zeros_like(token_ref)
         units = slice(share + width, share + 2 * width)
         unit_all = jnp.concatenate([packed_low[:, units], packed_high[:, units]], axis=0)
         raw = text_ref[...].astype(F32)
@@ -614,21 +618,26 @@
         text_grad_ref[...] = unit_back(unit, inverse, text_sum)
 
 
-def head_grads_block(packed, text_feats, share, order):
-    rows, width = text_feats.shape
+def head_grads_block(packed, text_here, share, order):
+    rows, width = text_here.shape
     block = 256 if share % 256 == 0 else LANES
     return pl.pallas_call(
         lambda *refs: head_grads_kernel(block, *refs),
         grid=(share // block,),
-        out_shape=[SHAPE((share, width), F32), SHAPE((rows, width), F32)],
+        out_shape=[
+            SHAPE((share, width), F32),
+            SHAPE((rows, width), F32),
+            SHAPE((8, LANES), F32),
+        ],
         in_specs=[VM, VM, VM, ANY],
         out_specs=[
             pl.BlockSpec((block, width), lambda step: (step, 0)),
             pl.BlockSpec((rows, width), lambda step: (0, 0)),
+            pl.BlockSpec((8, LANES), lambda step: (0, 0)),
         ],
         compiler_params=params(24),
         name="head_grads_block",
-    )(*near(packed), text_feats, order)
+    )(*near([*packed, text_here]), order)
 
 
 def split_kernel(place_ref, own_ref, other_ref, kernel_ref, term_ref):
@@ -676,10 +685,12 @@
 
     kernels = [swap(dw_kernel, "fsdp", m) for m in others]
     terms = [swap(channel_terms, "fsdp", m) for m in others]
-    mixed_own, sum_own, weight_own, x_here = own_block(place, image_maps, dw_kernel, channel_terms)
-
-    text_rows = text_feats
-    for mask in pair_masks:
+    mixed_own, sum_own, weight_own, x_here, text_here = own_block(
+        place, image_maps, dw_kernel, channel_terms, text_feats
+    )
+
+    text_rows = stack_rows(text_here, swap(text_feats, "fsdp", 1), sum_own)
+    for mask in pair_masks[1:]:
         text_rows = stack_rows(text_rows, swap(text_rows, "fsdp", mask), sum_own)
     text_rows = stack_rows(text_rows, swap(text_rows, "dp", 1), (terms or [sum_own])[-1])
     text_masks = down[:-1]
@@ -704,20 +715,37 @@
     keep, give, flow, shared = terms_block(
         place, grads, packed, x_here, weights, (mixed_own, mixed_rest), saved
     )
-    for mask in down[1:-1]:
-        packed = stack_rows(packed, swap(packed, "dp", mask), shared)
-    packed = (packed, swap(packed, "dp", down[-1]))
+
+    parts = [(image, base) for image in range(image_maps.shape[0]) for base in (0, members // 2)]
+    image_grads = None
+
+    def image_parts(count, order, image_grads):
+        token = order
+        for _ in range(min(count, len(parts))):
+            image, base = parts.pop(0)
+            image_grads, token = image_block(
+                image, base, members // 2, place, flow, weights, shared, order, image_grads
+            )
+        return image_grads, token
 
     chip = chip_sums(keep, swap(give, "dp", 1))
-    image_grads, token = image_block(0, place, flow, weights, shared, chip[0], None)
+    gather_masks = list(down[1:])
+    moving = swap(packed, "dp", gather_masks.pop(0))
+    image_grads, token = image_parts(1, chip[0], None)
     sent = add_all([chip[0]] + [swap(chip[m], "fsdp", m) for m in others], token)
-    for image in range(1, image_maps.shape[0]):
-        image_grads, token = image_block(image, place, flow, weights, shared, sent, image_grads)
     ring_masks = dp_masks[1:]
-    for mask in ring_masks[:-1]:
+    counts = [1] + [2] * len(ring_masks)
+    for mask, count in zip(ring_masks[:-1], counts):
+        packed = stack_rows(packed, moving, token)
+        moving = swap(packed, "dp", gather_masks.pop(0))
+        image_grads, token = image_parts(count, sent, image_grads)
         sent = add_all([sent, swap(sent, "dp", mask)], token)
-    head_grads, text_grads = head_grads_block(packed, text_feats, share, sent)
-    sent = add_all([sent, swap(sent, "dp", ring_masks[-1])], text_grads)
+    image_grads, token = image_parts(len(parts), sent, image_grads)
+    while gather_masks:
+        packed = stack_rows(packed, moving, token)
+        moving = swap(packed, "dp", gather_masks.pop(0))
+    head_grads, text_grads, token = head_grads_block((packed, moving), text_here, share, sent)
+    sent = add_all([sent, swap(sent, "dp", ring_masks[-1])], token)
     kernel_grads, term_grads = split_block(place, sent, swap(sent, "dp", 1))
     return (image_grads, kernel_grads, term_grads, head_grads, text_grads)
 

time: 76.1 us -> 72.1 us (0.947)
  waiting for transfers between devices: 21.9 us -> 17.7 us
  Pallas kernels: 33.6 us -> 35.8 us
  local copies, waits for them, and re-layouts: 1.39 us -> 0 us
    ppermute x20, waiting for transfers between devices: 21.9 us -> 17.7 us  [swap(): lax.ppermute(value, axis, [(source, source ^ mask) for source in range(co...]
    pallas_call x2 -> x4, Pallas kernels: 8.31 us -> 10.5 us  [image_block(): pl.pallas_call(kernel, grid_spec=pltpu.PrefetchScalarGridSpec(num_scalar_...]
    unnamed x6 -> x0, local copies, waits for them, and re-layouts: 1.39 us -> none
  transfers between devices with their start and end apart: 20 -> 20, of which waited for: 9 -> 10; matrix products, arithmetic and copies ran while one was open for 0% -> 0% of each run, Pallas kernels for 31% -> 36%
where the time goes in v4:
time: 72.1 us; the launch traced here: 72 us
  Pallas kernels  35.8 us (50%)
  starting transfers between devices  17.7 us (25%)
  waiting for transfers between devices  17.7 us (25%)
  between operations  0.79 us (1%)
    ppermute x20, waiting for transfers between devices, swap(): lax.ppermute(value, axis, [(source, source ^ mask) for source in range(co...  17.7 us
    ppermute x20, starting transfers between devices, swap(): lax.ppermute(value, axis, [(source, source ^ mask) for source in range(co...  17.7 us
    pallas_call x4, Pallas kernels, image_block(): pl.pallas_call(kernel, grid_spec=pltpu.PrefetchScalarGridSpec(num_scalar_...  10.5 us
    pallas_call x1, Pallas kernels, terms_block(): pl.pallas_call(lambda *refs: terms_kernel(members, *refs), out_shape=[hal...  7.19 us
    pallas_call x1, Pallas kernels, forward_block(): pl.pallas_call(lambda *refs: forward_kernel(members, *refs), out_shape=ou...  5.07 us
    pallas_call x1, Pallas kernels, head_grads_block(): pl.pallas_call(lambda *refs: head_grads_kernel(block, *refs), grid=(share...  5.04 us
    pallas_call x1, Pallas kernels, own_block(): pl.pallas_call(lambda *refs: own_kernel(members, *refs), out_shape=[SHAPE...  4.42 us
    pallas_call x1, Pallas kernels, loss_block(): pl.pallas_call(lambda *refs: loss_kernel(members, *refs), out_shape=[SHAP...  1.47 us
  transfers between devices with their start and end apart: 20, of which 10 were waited for; matrix products, arithmetic and copies ran while one was open for 0% of the time, Pallas kernels for 36%

profile of v4, /device:TPU:0, one launch (start us, length us, event | category | flops | bytes accessed | tf_op | source)
XLA Modules:
  0.0 72.0 jit_solution(1388147865041548670)
XLA Ops:
  0.6 3.0 %collective-permute-start.3 = (bf16[49,1536]{1,0:T(8,128)(2,1)}, bf16[49,1536]{1,0:T(8,128)(2,1)S(1)}, u32[]{:S(2)}, u32[]{:S(2)}) collective-permute-start(bf16[49,1536]{1,0:T(8,128)(2,1)} %refs_2_.1), channel_id=1, source_target_pairs={{0,1},{1,0},{2,3},{3,2},{4,5},{5,4},{6,7},{7,6},{8,9},{9,8},{10,11... | collective-permute-start | bytes 451592 | tf_op jit(solution)/shard_map/ppermute | solution.py:24
  3.7 0.1 collective-permute-start
  3.7 1.9 %collective-permute-start.2 = (bf16[4,1536]{1,0:T(4,128)(2,1)}, bf16[4,1536]{1,0:T(4,128)(2,1)S(1)}, u32[]{:S(2)}, u32[]{:S(2)}) collective-permute-start(bf16[4,1536]{1,0:T(4,128)(2,1)} %refs_3_.1), channel_id=1, source_target_pairs={{0,1},{1,0},{2,3},{3,2},{4,5},{5,4},{6,7},{7,6},{8,9},{9,8},{10,11... | collective-permute-start | bytes 36872 | tf_op jit(solution)/shard_map/ppermute | solution.py:24
  5.7 0.1 pad_add_fusion.refs_0_.place_ref
  5.8 4.4 %own_block.1 = (f32[2,8,8,1536]{3,2,1,0:T(8,128)S(1)}, f32[2,8,8,128]{3,2,1,0:T(8,128)S(1)}, f32[64,1536]{1,0:T(8,128)S(1)}, bf16[2,8,8,3072]{3,2,1,0:T(8,128)(2,1)S(1)}, bf16[2,1152]{1,0:T(2,128)(2,1)S(1)}) custom-call(s32[2]{0:T(128)S(1)} %pad_add_fusion.refs_0_.place_ref, bf16[2,8,8,3072]{3,2,1,0:T(8,128)(2,1)} %refs_1_.2, bf16[49,1536]{1,0:T(8,128)(2,1)} %refs_2_.1, ...), custom_call_target="tpu_custom_call" | custom-call | tf_op jit(solution)/shard_map/own_block/pallas_call | solution.py:195
  10.2 0.0 collective-permute-done.high_ref
  10.2 0.1 collective-permute-start.1
  10.3 0.0 collective-permute-done.2.order_ref.refs_8_
  10.3 1.1 %collective-permute-done.1.high_ref = bf16[4,1152]{1,0:T(4,128)(2,1)S(1)} collective-permute-done((bf16[4,1152]{1,0:T(4,128)(2,1)S(1)}, bf16[4,1152]{1,0:T(4,128)(2,1)S(1)}, u32[]{:S(2)}, u32[]{:S(2)}) %collective-permute-start.1) | collective-permute-done | bytes 9248 | tf_op jit(solution)/shard_map/ppermute | solution.py:24
  11.5 2.7 %collective-permute-start.6 = (bf16[8,1152]{1,0:T(8,128)(2,1)S(1)}, bf16[8,1152]{1,0:T(8,128)(2,1)S(1)}, u32[]{:S(2)}, u32[]{:S(2)}) collective-permute-start(bf16[8,1152]{1,0:T(8,128)(2,1)S(1)} %stack_rows.8.refs_6_.low_ref), channel_id=1, source_target_pairs={{0,16},{2,18},{4,20},{6,22},{8,24},{10,26},{12,28},{14,30},{16,0},... | collective-permute-start | bytes 55304 | tf_op jit(solution)/shard_map/ppermute | solution.py:24
  14.1 0.0 collective-permute-done.3.refs_7_
  14.1 5.1 %forward_block.1 = (bf16[2,1536]{1,0:T(2,128)(2,1)S(1)}, bf16[2,1536]{1,0:T(2,128)(2,1)S(1)}, bf16[1536,1152]{1,0:T(8,128)(2,1)S(1)}, f32[64,1536]{1,0:T(8,128)S...) custom-call(s32[2]{0:T(128)S(1)} %pad_add_fusion.refs_0_.place_ref, ...), custom_call_target="tpu_custom_call" | custom-call | tf_op jit(solution)/shard_map/forward_block/pallas_call | solution.py:306
  19.2 1.6 %collective-permute-start.7 = (bf16[16,1152]{1,0:T(8,128)(2,1)S(1)}, bf16[16,1152]{1,0:T(8,128)(2,1)S(1)}, u32[]{:S(2)}, u32[]{:S(2)}) collective-permute-start(bf16[16,1152]{1,0:T(8,128)(2,1)S(1)} %stack_rows.9.low_ref), channel_id=1, source_target_pairs={{0,8},{2,10},{4,12},{6,14},{8,0},{10,2},{12,4},{14,6},{16,24},{18,... | collective-permute-start | bytes 110600 | tf_op jit(solution)/shard_map/ppermute | solution.py:24
  20.9 0.5 collective-permute-start.4
  21.4 3.1 %collective-permute-done.4.refs_1_ = bf16[2,1536]{1,0:T(2,128)(2,1)S(1)} collective-permute-done((bf16[2,1536]{1,0:T(2,128)(2,1)S(1)}, bf16[2,1536]{1,0:T(2,128)(2,1)S(1)}, u32[]{:S(2)}, u32[]{:S(2)}) %collective-permute-start.4) | collective-permute-done | bytes 6176 | tf_op jit(solution)/shard_map/ppermute | solution.py:24
  24.5 0.6 head_project.1
  25.1 0.0 collective-permute-done.7.high_ref
  25.1 1.6 %collective-permute-start.8 = (bf16[32,1152]{1,0:T(8,128)(2,1)S(1)}, bf16[32,1152]{1,0:T(8,128)(2,1)S(1)}, u32[]{:S(2)}, u32[]{:S(2)}) collective-permute-start(bf16[32,1152]{1,0:T(8,128)(2,1)S(1)} %stack_rows.10.refs_2_), channel_id=1, source_target_pairs={{0,4},{2,6},{4,0},{6,2},{8,12},{10,14},{12,8},{14,10},{16,20},{18,... | collective-permute-start | bytes 221192 | tf_op jit(solution)/shard_map/ppermute | solution.py:24
  26.7 0.5 collective-permute-start.5
  27.2 3.3 %collective-permute-done.5.refs_1_ = f32[4,1152]{1,0:T(4,128)S(1)} collective-permute-done((f32[4,1152]{1,0:T(4,128)S(1)}, f32[4,1152]{1,0:T(4,128)S(1)}, u32[]{:S(2)}, u32[]{:S(2)}) %collective-permute-start.5) | collective-permute-done | bytes 18464 | tf_op jit(solution)/shard_map/ppermute | solution.py:24
  30.4 1.5 %loss_block.1 = (bf16[4,3840]{1,0:T(4,128)(2,1)S(1)}, f32[2,1536]{1,0:T(2,128)S(1)}, f32[2,1536]{1,0:T(2,128)S(1)}) custom-call(f32[4,1152]{1,0:T(4,128)S(1)} %get-tuple-element.51.order_ref.refs_0_, f32[4,1152]{1,0:T(4,128)S(1)} %collective-permute-done.5.refs_1_, bf16[32,1152]{1,0:T(8,128)(2,1)S(1)} %stack_rows.10.refs_2_, ...), custom_call_target="tpu_custom_call" | custom-call | tf_op jit(solution)/shard_map/loss_block/pallas_call | solution.py:398
  31.9 0.4 collective-permute-start.10
  32.2 0.5 collective-permute-start.9
  32.7 4.2 %collective-permute-done.10.high_ref = bf16[4,3840]{1,0:T(4,128)(2,1)S(1)} collective-permute-done((bf16[4,3840]{1,0:T(4,128)(2,1)S(1)}, bf16[4,3840]{1,0:T(4,128)(2,1)S(1)}, u32[]{:S(2)}, u32[]{:S(2)}) %collective-permute-start.10) | collective-permute-done | bytes 30752 | tf_op jit(solution)/shard_map/ppermute | solution.py:24
  36.9 7.2 %terms_block.1 = (bf16[2,32,1536]{2,1,0:T(8,128)(2,1)S(1)}, bf16[2,32,1536]{2,1,0:T(8,128)(2,1)S(1)}, f32[2,8,8,3072]{3,2,1,0:T(8,128)S(1)}, f32[2,3072]{1,0:T(2,128)S(1)}) custom-call(s32[2]{0:T(128)S(1)} %pad_add_fusion.refs_0_.place_ref, f32[2,1536]{1,0:T(2,128)S(1)} %get-tuple-element.54.refs_1_, f32[2,1536]{1,0:T(2,128)S(1)} %collective-permute-done.9.refs_2_, ...), custom_call_target="tpu_custom_call" | custom-call | tf_op jit(solution)/shard_map/terms_block/pallas_call | solution.py:520
  44.1 0.1 collective-permute-start.11
  44.2 0.3 collective-permute-start.16
  44.5 1.1 %collective-permute-done.11.give_ref = bf16[2,32,1536]{2,1,0:T(8,128)(2,1)S(1)} collective-permute-done((bf16[2,32,1536]{2,1,0:T(8,128)(2,1)S(1)}, bf16[2,32,1536]{2,1,0:T(8,128)(2,1)S(1)}, u32[]{:S(2)}, u32[]{:S(2)}) %collective-permute-start.11) | collective-permute-done | bytes 196640 | tf_op jit(solution)/shard_map/ppermute | solution.py:24
  45.6 0.1 chip_sums.1
  45.7 0.6 collective-permute-start.12
  46.3 2.6 %image_block.4 = (bf16[2,8,8,3072]{3,2,1,0:T(8,128)(2,1)}, f32[8,128]{1,0:T(8,128)S(1)}) custom-call(s32[2]{0:T(128)S(1)} %pad_add_fusion.refs_0_.place_ref, f32[2,8,8,3072]{3,2,1,0:T(8,128)S(1)} %get-tuple-element.63.refs_1_, f32[64,1536]{1,0:T(8,128)S(1)} %get-tuple-element.46.refs_5_.refs_2_, f32[64,1536]{1,0:T(8,128)S(1)} %get-tuple-element.57.refs_6_.refs_3_, ...), custom_call_target="tpu_custom_call" | custom-call | tf_op jit(solution)/shard_map/image_block/pallas_call | solution.py:573
  48.9 0.7 collective-permute-start.17
  49.5 1.1 %collective-permute-done.12.refs_1_ = bf16[32,1536]{1,0:T(8,128)(2,1)S(1)} collective-permute-done((bf16[32,1536]{1,0:T(8,128)(2,1)S(1)}, bf16[32,1536]{1,0:T(8,128)(2,1)S(1)}, u32[]{:S(2)}, u32[]{:S(2)}) %collective-permute-start.12) | collective-permute-done | bytes 98336 | tf_op jit(solution)/shard_map/ppermute | solution.py:24
  50.6 0.7 collective-permute-start.13
  51.3 2.6 %image_block.5 = (bf16[2,8,8,3072]{3,2,1,0:T(8,128)(2,1)}, f32[8,128]{1,0:T(8,128)S(1)}) custom-call(s32[2]{0:T(128)S(1)} %pad_add_fusion.refs_0_.place_ref, f32[2,8,8,3072]{3,2,1,0:T(8,128)S(1)} %get-tuple-element.63.refs_1_, f32[64,1536]{1,0:T(8,128)S(1)} %get-tuple-element.46.refs_5_.refs_2_, ...), custom_call_target="tpu_custom_call", output_to_operand_aliasing={{0}: (6, {})} | custom-call | tf_op jit(solution)/shard_map/image_block/pallas_call | solution.py:573
  53.9 1.2 %collective-permute-done.17.high_ref = bf16[16,3840]{1,0:T(8,128)(2,1)S(1)} collective-permute-done((bf16[16,3840]{1,0:T(8,128)(2,1)S(1)}, bf16[16,3840]{1,0:T(8,128)(2,1)S(1)}, u32[]{:S(2)}, u32[]{:S(2)}) %collective-permute-start.17) | collective-permute-done | bytes 122912 | tf_op jit(solution)/shard_map/ppermute | solution.py:24
  55.1 0.1 collective-permute-start.18
  55.2 1.0 %collective-permute-done.13.refs_1_ = bf16[32,1536]{1,0:T(8,128)(2,1)S(1)} collective-permute-done((bf16[32,1536]{1,0:T(8,128)(2,1)S(1)}, bf16[32,1536]{1,0:T(8,128)(2,1)S(1)}, u32[]{:S(2)}, u32[]{:S(2)}) %collective-permute-start.13) | collective-permute-done | bytes 98336 | tf_op jit(solution)/shard_map/ppermute | solution.py:24
  56.2 0.8 %collective-permute-start.14 = (bf16[32,1536]{1,0:T(8,128)(2,1)S(1)}, bf16[32,1536]{1,0:T(8,128)(2,1)S(1)}, u32[]{:S(2)}, u32[]{:S(2)}) collective-permute-start(bf16[32,1536]{1,0:T(8,128)(2,1)S(1)} %add_all.5.refs_5_.refs_0_), channel_id=1, source_target_pairs={{0,8},{2,10},{4,12},{6,14},{8,0},{10,2},{12,4},{14,6},{16,24},{18,... | collective-permute-start | bytes 294920 | tf_op jit(solution)/shard_map/ppermute | solution.py:24
  56.9 2.6 %image_block.6 = (bf16[2,8,8,3072]{3,2,1,0:T(8,128)(2,1)}, f32[8,128]{1,0:T(8,128)}) custom-call(s32[2]{0:T(128)S(1)} %pad_add_fusion.refs_0_.place_ref, f32[2,8,8,3072]{3,2,1,0:T(8,128)S(1)} %get-tuple-element.63.refs_1_, f32[64,1536]{1,0:T(8,128)S(1)} %get-tuple-element.46.refs_5_.refs_2_, ...), custom_call_target="tpu_custom_call", output_to_operand_aliasing={{0}: (6, {})} | custom-call | tf_op jit(solution)/shard_map/image_block/pallas_call | solution.py:573
  59.6 2.6 %image_block.7 = (bf16[2,8,8,3072]{3,2,1,0:T(8,128)(2,1)}, f32[8,128]{1,0:T(8,128)S(1)}) custom-call(s32[2]{0:T(128)S(1)} %pad_add_fusion.refs_0_.place_ref, f32[2,8,8,3072]{3,2,1,0:T(8,128)S(1)} %get-tuple-element.63.refs_1_, f32[64,1536]{1,0:T(8,128)S(1)} %get-tuple-element.46.refs_5_.refs_2_, ...), custom_call_target="tpu_custom_call", output_to_operand_aliasing={{0}: (6, {})} | custom-call | tf_op jit(solution)/shard_map/image_block/pallas_call | solution.py:573
  62.2 0.0 collective-permute-done.14.refs_1_
  62.2 1.6 %collective-permute-start.15 = (bf16[32,1536]{1,0:T(8,128)(2,1)S(1)}, bf16[32,1536]{1,0:T(8,128)(2,1)S(1)}, u32[]{:S(2)}, u32[]{:S(2)}) collective-permute-start(bf16[32,1536]{1,0:T(8,128)(2,1)S(1)} %add_all.6.refs_3_.refs_0_), channel_id=1, source_target_pairs={{0,16},{2,18},{4,20},{6,22},{8,24},{10,26},{12,28},{14,30},{16,0},... | collective-permute-start | bytes 294920 | tf_op jit(solution)/shard_map/ppermute | solution.py:24
  63.9 5.0 %head_grads_block.1 = (f32[1536,1152]{1,0:T(8,128)}, f32[2,1152]{1,0:T(2,128)}, f32[8,128]{1,0:T(8,128)S(1)}) custom-call(bf16[32,3840]{1,0:T(8,128)(2,1)S(1)} %stack_rows.13.refs_0_, bf16[32,3840]{1,0:T(8,128)(2,1)S(1)} %collective-permute-done.18.refs_1_, bf16[2,1152]{1,0:T(2,128)(2,1)S(1)} %get-tuple-element.47.low_ref.refs_2_, ...), custom_call_target="tpu_custom_call" | custom-call | tf_op jit(solution)/shard_map/head_grads_block/pallas_call | solution.py:624
  68.9 0.4 collective-permute-done.15.refs_1_
  69.3 0.1 collective-permute-start.19
  69.4 1.3 %collective-permute-done.19.other_ref = bf16[32,1536]{1,0:T(8,128)(2,1)S(1)} collective-permute-done((bf16[32,1536]{1,0:T(8,128)(2,1)S(1)}, bf16[32,1536]{1,0:T(8,128)(2,1)S(1)}, u32[]{:S(2)}, u32[]{:S(2)}) %collective-permute-start.19) | collective-permute-done | bytes 98336 | tf_op jit(solution)/shard_map/ppermute | solution.py:24
  70.6 1.3 %split_block.1 = (f32[49,1536]{1,0:T(8,128)}, f32[4,1536]{1,0:T(4,128)}) custom-call(s32[2]{0:T(128)S(1)} %pad_add_fusion.refs_0_.place_ref, bf16[32,1536]{1,0:T(8,128)(2,1)S(1)} %add_all.7.own_ref, bf16[32,1536]{1,0:T(8,128)(2,1)S(1)} %collective-permute-done.19.other_ref), custom_call_target="tpu_custom_call" | custom-call | tf_op jit(solution)/shard_map/split_block/pallas_call | solution.py:665
  (16 shorter events, 0.2 us)
Async XLA Ops:
  0.6 13.5 %collective-permute-start.3 = (bf16[49,1536]{1,0:T(8,128)(2,1)}, bf16[49,1536]{1,0:T(8,128)(2,1)S(1)}, u32[]{:S(2)}, u32[]{:S(2)}) collective-permute-start(bf16[49,1536]{1,0:T(8,128)(2,1)} %refs_2_.1), channel_id=1, source_target_pairs={{0,1},{1,0},{2,3},{3,2},{4,5},{5,4},{6,7},{7,6},{8,9},{9,8},{10,11... | collective-permute-start | bytes 451592 | tf_op jit(solution)/shard_map/ppermute | solution.py:24
  3.7 6.5 %collective-permute-start = (bf16[2,1152]{1,0:T(2,128)(2,1)}, bf16[2,1152]{1,0:T(2,128)(2,1)S(1)}, u32[]{:S(2)}, u32[]{:S(2)}) collective-permute-start(bf16[2,1152]{1,0:T(2,128)(2,1)} %refs_4_.1), channel_id=1, source_target_pairs={{0,1},{1,0},{2,3},{3,2},{4,5},{5,4},{6,7},{7,6},{8,9},{9,8},{10,11... | collective-permute-start | bytes 13832 | tf_op jit(solution)/shard_map/ppermute | solution.py:24
  3.7 6.6 %collective-permute-start.2 = (bf16[4,1536]{1,0:T(4,128)(2,1)}, bf16[4,1536]{1,0:T(4,128)(2,1)S(1)}, u32[]{:S(2)}, u32[]{:S(2)}) collective-permute-start(bf16[4,1536]{1,0:T(4,128)(2,1)} %refs_3_.1), channel_id=1, source_target_pairs={{0,1},{1,0},{2,3},{3,2},{4,5},{5,4},{6,7},{7,6},{8,9},{9,8},{10,11... | collective-permute-start | bytes 36872 | tf_op jit(solution)/shard_map/ppermute | solution.py:24
  10.2 1.2 %collective-permute-start.1 = (bf16[4,1152]{1,0:T(4,128)(2,1)S(1)}, bf16[4,1152]{1,0:T(4,128)(2,1)S(1)}, u32[]{:S(2)}, u32[]{:S(2)}) collective-permute-start(bf16[4,1152]{1,0:T(4,128)(2,1)S(1)} %stack_rows.7.low_ref), channel_id=1, source_target_pairs={{0,2},{2,0},{4,6},{6,4},{8,10},{10,8},{12,14},{14,12},{16,18},{18,... | collective-permute-start | bytes 27656 | tf_op jit(solution)/shard_map/ppermute | solution.py:24
  11.5 7.7 %collective-permute-start.6 = (bf16[8,1152]{1,0:T(8,128)(2,1)S(1)}, bf16[8,1152]{1,0:T(8,128)(2,1)S(1)}, u32[]{:S(2)}, u32[]{:S(2)}) collective-permute-start(bf16[8,1152]{1,0:T(8,128)(2,1)S(1)} %stack_rows.8.refs_6_.low_ref), channel_id=1, source_target_pairs={{0,16},{2,18},{4,20},{6,22},{8,24},{10,26},{12,28},{14,30},{16,0},... | collective-permute-start | bytes 55304 | tf_op jit(solution)/shard_map/ppermute | solution.py:24
  19.2 5.8 %collective-permute-start.7 = (bf16[16,1152]{1,0:T(8,128)(2,1)S(1)}, bf16[16,1152]{1,0:T(8,128)(2,1)S(1)}, u32[]{:S(2)}, u32[]{:S(2)}) collective-permute-start(bf16[16,1152]{1,0:T(8,128)(2,1)S(1)} %stack_rows.9.low_ref), channel_id=1, source_target_pairs={{0,8},{2,10},{4,12},{6,14},{8,0},{10,2},{12,4},{14,6},{16,24},{18,... | collective-permute-start | bytes 110600 | tf_op jit(solution)/shard_map/ppermute | solution.py:24
  20.9 3.6 %collective-permute-start.4 = (bf16[2,1536]{1,0:T(2,128)(2,1)S(1)}, bf16[2,1536]{1,0:T(2,128)(2,1)S(1)}, u32[]{:S(2)}, u32[]{:S(2)}) collective-permute-start(bf16[2,1536]{1,0:T(2,128)(2,1)S(1)} %get-tuple-element.49), channel_id=1, source_target_pairs={{0,1},{1,0},{2,3},{3,2},{4,5},{5,4},{6,7},{7,6},{8,9},{9,8},{10,11... | collective-permute-start | bytes 18440 | tf_op jit(solution)/shard_map/ppermute | solution.py:24
  25.1 5.3 %collective-permute-start.8 = (bf16[32,1152]{1,0:T(8,128)(2,1)S(1)}, bf16[32,1152]{1,0:T(8,128)(2,1)S(1)}, u32[]{:S(2)}, u32[]{:S(2)}) collective-permute-start(bf16[32,1152]{1,0:T(8,128)(2,1)S(1)} %stack_rows.10.refs_2_), channel_id=1, source_target_pairs={{0,4},{2,6},{4,0},{6,2},{8,12},{10,14},{12,8},{14,10},{16,20},{18,... | collective-permute-start | bytes 221192 | tf_op jit(solution)/shard_map/ppermute | solution.py:24
  26.7 3.8 %collective-permute-start.5 = (f32[4,1152]{1,0:T(4,128)S(1)}, f32[4,1152]{1,0:T(4,128)S(1)}, u32[]{:S(2)}, u32[]{:S(2)}) collective-permute-start(f32[4,1152]{1,0:T(4,128)S(1)} %get-tuple-element.51.order_ref.refs_0_), channel_id=1, source_target_pairs={{0,1},{1,0},{2,3},{3,2},{4,5},{5,4},{6,7},{7,6},{8,9},{9,8},{10,11... | collective-permute-start | bytes 55304 | tf_op jit(solution)/shard_map/ppermute | solution.py:24
  31.9 5.0 %collective-permute-start.10 = (bf16[4,3840]{1,0:T(4,128)(2,1)S(1)}, bf16[4,3840]{1,0:T(4,128)(2,1)S(1)}, u32[]{:S(2)}, u32[]{:S(2)}) collective-permute-start(bf16[4,3840]{1,0:T(4,128)(2,1)S(1)} %get-tuple-element.56.low_ref.order_ref), channel_id=1, source_target_pairs={{0,16},{2,18},{4,20},{6,22},{8,24},{10,26},{12,28},{14,30},{16,0},... | collective-permute-start | bytes 92168 | tf_op jit(solution)/shard_map/ppermute | solution.py:24
  32.2 4.7 %collective-permute-start.9 = (f32[2,1536]{1,0:T(2,128)S(1)}, f32[2,1536]{1,0:T(2,128)S(1)}, u32[]{:S(2)}, u32[]{:S(2)}) collective-permute-start(f32[2,1536]{1,0:T(2,128)S(1)} %get-tuple-element.55), channel_id=1, source_target_pairs={{0,1},{1,0},{2,3},{3,2},{4,5},{5,4},{6,7},{7,6},{8,9},{9,8},{10,11... | collective-permute-start | bytes 36872 | tf_op jit(solution)/shard_map/ppermute | solution.py:24
  44.1 1.5 %collective-permute-start.11 = (bf16[2,32,1536]{2,1,0:T(8,128)(2,1)S(1)}, bf16[2,32,1536]{2,1,0:T(8,128)(2,1)S(1)}, u32[]{:S(2)}, u32[]{:S(2)}) collective-permute-start(bf16[2,32,1536]{2,1,0:T(8,128)(2,1)S(1)} %get-tuple-element.66), channel_id=1, source_target_pairs={{0,2},{2,0},{4,6},{6,4},{8,10},{10,8},{12,14},{14,12},{16,18},{18,... | collective-permute-start | bytes 589832 | tf_op jit(solution)/shard_map/ppermute | solution.py:24
  44.2 4.7 %collective-permute-start.16 = (bf16[8,3840]{1,0:T(8,128)(2,1)S(1)}, bf16[8,3840]{1,0:T(8,128)(2,1)S(1)}, u32[]{:S(2)}, u32[]{:S(2)}) collective-permute-start(bf16[8,3840]{1,0:T(8,128)(2,1)S(1)} %stack_rows.11.refs_3_.low_ref), channel_id=1, source_target_pairs={{0,8},{2,10},{4,12},{6,14},{8,0},{10,2},{12,4},{14,6},{16,24},{18,... | collective-permute-start | bytes 184328 | tf_op jit(solution)/shard_map/ppermute | solution.py:24
  45.7 4.9 %collective-permute-start.12 = (bf16[32,1536]{1,0:T(8,128)(2,1)S(1)}, bf16[32,1536]{1,0:T(8,128)(2,1)S(1)}, u32[]{:S(2)}, u32[]{:S(2)}) collective-permute-start(bf16[32,1536]{1,0:T(8,128)(2,1)S(1)} %get-tuple-element.68), channel_id=1, source_target_pairs={{0,1},{1,0},{2,3},{3,2},{4,5},{5,4},{6,7},{7,6},{8,9},{9,8},{10,11... | collective-permute-start | bytes 294920 | tf_op jit(solution)/shard_map/ppermute | solution.py:24
  48.9 6.2 %collective-permute-start.17 = (bf16[16,3840]{1,0:T(8,128)(2,1)S(1)}, bf16[16,3840]{1,0:T(8,128)(2,1)S(1)}, u32[]{:S(2)}, u32[]{:S(2)}) collective-permute-start(bf16[16,3840]{1,0:T(8,128)(2,1)S(1)} %stack_rows.12.low_ref), channel_id=1, source_target_pairs={{0,4},{2,6},{4,0},{6,2},{8,12},{10,14},{12,8},{14,10},{16,20},{18,... | collective-permute-start | bytes 368648 | tf_op jit(solution)/shard_map/ppermute | solution.py:24
  50.6 5.5 %collective-permute-start.13 = (bf16[32,1536]{1,0:T(8,128)(2,1)S(1)}, bf16[32,1536]{1,0:T(8,128)(2,1)S(1)}, u32[]{:S(2)}, u32[]{:S(2)}) collective-permute-start(bf16[32,1536]{1,0:T(8,128)(2,1)S(1)} %add_all.4.refs_5_.refs_0_), channel_id=1, source_target_pairs={{0,4},{2,6},{4,0},{6,2},{8,12},{10,14},{12,8},{14,10},{16,20},{18,... | collective-permute-start | bytes 294920 | tf_op jit(solution)/shard_map/ppermute | solution.py:24
  55.1 8.7 %collective-permute-start.18 = (bf16[32,3840]{1,0:T(8,128)(2,1)S(1)}, bf16[32,3840]{1,0:T(8,128)(2,1)S(1)}, u32[]{:S(2)}, u32[]{:S(2)}) collective-permute-start(bf16[32,3840]{1,0:T(8,128)(2,1)S(1)} %stack_rows.13.refs_0_), channel_id=1, source_target_pairs={{0,2},{2,0},{4,6},{6,4},{8,10},{10,8},{12,14},{14,12},{16,18},{18,... | collective-permute-start | bytes 737288 | tf_op jit(solution)/shard_map/ppermute | solution.py:24
  56.2 6.0 %collective-permute-start.14 = (bf16[32,1536]{1,0:T(8,128)(2,1)S(1)}, bf16[32,1536]{1,0:T(8,128)(2,1)S(1)}, u32[]{:S(2)}, u32[]{:S(2)}) collective-permute-start(bf16[32,1536]{1,0:T(8,128)(2,1)S(1)} %add_all.5.refs_5_.refs_0_), channel_id=1, source_target_pairs={{0,8},{2,10},{4,12},{6,14},{8,0},{10,2},{12,4},{14,6},{16,24},{18,... | collective-permute-start | bytes 294920 | tf_op jit(solution)/shard_map/ppermute | solution.py:24
  62.2 7.0 %collective-permute-start.15 = (bf16[32,1536]{1,0:T(8,128)(2,1)S(1)}, bf16[32,1536]{1,0:T(8,128)(2,1)S(1)}, u32[]{:S(2)}, u32[]{:S(2)}) collective-permute-start(bf16[32,1536]{1,0:T(8,128)(2,1)S(1)} %add_all.6.refs_3_.refs_0_), channel_id=1, source_target_pairs={{0,16},{2,18},{4,20},{6,22},{8,24},{10,26},{12,28},{14,30},{16,0},... | collective-permute-start | bytes 294920 | tf_op jit(solution)/shard_map/ppermute | solution.py:24
  69.3 1.4 %collective-permute-start.19 = (bf16[32,1536]{1,0:T(8,128)(2,1)S(1)}, bf16[32,1536]{1,0:T(8,128)(2,1)S(1)}, u32[]{:S(2)}, u32[]{:S(2)}) collective-permute-start(bf16[32,1536]{1,0:T(8,128)(2,1)S(1)} %add_all.7.own_ref), channel_id=1, source_target_pairs={{0,2},{2,0},{4,6},{6,4},{8,10},{10,8},{12,14},{14,12},{16,18},{18,... | collective-permute-start | bytes 294920 | tf_op jit(solution)/shard_map/ppermute | solution.py:24

commit v5 on v4

--- a/solution.py
+++ b/solution.py
@@ -15,6 +15,10 @@
 ROWS_PAD = 64
 HALF_PAD = ROWS_PAD // 2
 TERM_ROW = 56
+GAIN_ROW = TAPS
+WEIGHT_ROWS = 56
+DOTS_COST = 3.0
+SUM_COST = 1.0
 BF = jnp.bfloat16
 F32 = jnp.float32
 
@@ -41,6 +45,10 @@
 
 def params(mebibytes):
     return pltpu.CompilerParams(vmem_limit_bytes=mebibytes * 1024 * 1024)
+
+
+def cost(micros):
+    return pl.CostEstimate(flops=int(micros * 1.1e9), bytes_accessed=0, transcendentals=0)
 
 
 def far(arrays):
@@ -119,21 +127,35 @@
     )(*values, order)
 
 
-def chip_sums(keep, give):
+def hold(value, order):
+    def kernel(value_ref, order_ref, out_ref):
+        out_ref[...] = value_ref[...]
+
+    return pl.pallas_call(
+        kernel,
+        out_shape=SHAPE(value.shape, value.dtype),
+        in_specs=[VM, ANY],
+        out_specs=VM,
+        compiler_params=params(24),
+        name="hold",
+    )(value, order)
+
+
+def chip_sums(keep, give, order):
     members = keep.shape[0]
 
-    def kernel(keep_ref, give_ref, *out_refs):
+    def kernel(keep_ref, give_ref, order_ref, *out_refs):
         for m in range(members):
             out_refs[m][...] = (keep_ref[m].astype(F32) + give_ref[m].astype(F32)).astype(BF)
 
     return pl.pallas_call(
         kernel,
         out_shape=[SHAPE(keep.shape[1:], BF)] * members,
-        in_specs=[VM, VM],
+        in_specs=[VM, VM, ANY],
         out_specs=[VM] * members,
         compiler_params=params(24),
         name="chip_sums",
-    )(keep, give)
+    )(keep, give, order)
 
 
 def tile_of(base_piece, t, member, share):
@@ -149,7 +171,7 @@
     def _(t):
         lanes = lane_block(t, LANES)
         source = tile_of(base_piece, t, member, share)
-        bias = weight_ref[TERM_ROW : TERM_ROW + 1, lanes]
+        bias = weight_ref[GAIN_ROW : GAIN_ROW + 1, lanes]
         for i in range(images):
             rows = [x_ref[i, h, :, source].astype(F32) for h in range(height)]
             sums = conv_rows(rows, lambda tap: weight_ref[tap : tap + 1, lanes], False)
@@ -159,63 +181,137 @@
                 sum_ref[i, h] += value
 
 
-def own_kernel(
-    members, place_ref, x_hbm, kernel_hbm, term_hbm, text_hbm, mixed_ref, sum_ref, weight_ref, x_ref, text_ref, kernel_ref, term_ref, sems
-):
-    share = kernel_hbm.shape[1]
-    member = place_ref[0]
+def text_chunks(embed_width, share):
+    return [
+        (chunk, first, min(share, embed_width - first))
+        for chunk, first in enumerate(range(0, embed_width, share))
+    ]
+
+
+def pack_rows(texts, embed_width, share):
+    return (4 + texts * len(text_chunks(embed_width, share)) + 7) // 8 * 8
+
+
+def load_kernel(x_hbm, kernel_hbm, term_hbm, text_hbm, x_ref, weight_ref, text_ref, kernel_ref, term_ref, sems):
     copies = [
         pltpu.make_async_copy(kernel_hbm, kernel_ref, sems.at[0]),
         pltpu.make_async_copy(term_hbm, term_ref, sems.at[1]),
+        pltpu.make_async_copy(text_hbm, text_ref, sems.at[2]),
+        pltpu.make_async_copy(x_hbm, x_ref, sems.at[3]),
     ]
-    for m in range(members):
-        lanes = lane_block(member ^ m, share)
-        copies.append(
-            pltpu.make_async_copy(
-                x_hbm.at[:, :, :, lanes], x_ref.at[:, :, :, lanes], sems.at[2 + m]
-            )
-        )
-    copies.append(pltpu.make_async_copy(text_hbm, text_ref, sems.at[2 + members]))
     for copy in copies:
         copy.start()
-    sum_ref[...] = jnp.zeros_like(sum_ref)
     for copy in copies[:3]:
         copy.wait()
     weight_ref[0:TAPS, :] = kernel_ref[...].astype(F32)
-    weight_ref[TERM_ROW : TERM_ROW + 4, :] = term_ref[...].astype(F32)
-    conv_tiles(share // LANES, 0, member, share, x_ref, weight_ref, mixed_ref, sum_ref)
-    for copy in copies[3:]:
-        copy.wait()
-
-
-def own_block(place, image_maps, dw_kernel, channel_terms, text_feats):
-    images, height, width, channels = image_maps.shape
+    weight_ref[GAIN_ROW : GAIN_ROW + 4, :] = term_ref[...].astype(F32)
+    copies[3].wait()
+
+
+def load_block(image_maps, dw_kernel, channel_terms, text_feats):
     share = dw_kernel.shape[1]
-    members = channels // share
-    return pl.pallas_call(
-        lambda *refs: own_kernel(members, *refs),
+    return pl.pallas_call(
+        load_kernel,
+        out_shape=[
+            SHAPE(image_maps.shape, BF),
+            SHAPE((WEIGHT_ROWS, share), F32),
+            SHAPE(text_feats.shape, BF),
+        ],
+        in_specs=[HB, HB, HB, HB],
+        out_specs=[VM] * 3,
+        scratch_shapes=[
+            pltpu.VMEM(dw_kernel.shape, BF),
+            pltpu.VMEM(channel_terms.shape, BF),
+            pltpu.SemaphoreType.DMA((4,)),
+        ],
+        compiler_params=params(24),
+        name="load_block",
+    )(*far([image_maps, dw_kernel, channel_terms, text_feats]))
+
+
+def pack_block(weight_own, text_here, text_core):
+    images, embed_width = text_here.shape
+    share = weight_own.shape[1]
+    texts = 2 * images
+    rows = pack_rows(texts, embed_width, share)
+
+    def kernel(weight_ref, here_ref, core_ref, packed_ref, rows_ref):
+        rows_ref[...] = jnp.zeros_like(rows_ref)
+        rows_ref[0:4, :] = weight_ref[GAIN_ROW : GAIN_ROW + 4, :]
+        both = jnp.concatenate([here_ref[...].astype(F32), core_ref[...].astype(F32)], axis=0)
+        for chunk, first, width in text_chunks(embed_width, share):
+            row = 4 + chunk * texts
+            rows_ref[row : row + texts, 0:width] = both[:, first : first + width]
+        packed_ref[...] = rows_ref[...].astype(BF)
+
+    return pl.pallas_call(
+        kernel,
+        out_shape=SHAPE((rows, share), BF),
+        in_specs=[VM] * 3,
+        out_specs=VM,
+        scratch_shapes=[pltpu.VMEM((rows, share), F32)],
+        compiler_params=params(24),
+        name="pack_block",
+    )(*near([weight_own, text_here, text_core]))
+
+
+def text_stack(text_here, text_core, packs, order):
+    images, embed_width = text_here.shape
+    share = packs[0].shape[1]
+    members = len(packs) + 1
+    total = 2 * members * images
+
+    def kernel(*refs):
+        here_ref, core_ref, pack_refs, out_ref, rows_ref = refs[0], refs[1], refs[2 : members + 1], refs[-2], refs[-1]
+        half = members * images
+        rows_ref[0:images, :] = here_ref[...].astype(F32)
+        rows_ref[half : half + images, :] = core_ref[...].astype(F32)
+        for m in range(1, members):
+            pack = pack_refs[m - 1][...].astype(F32)
+            for chunk, first, width in text_chunks(embed_width, share):
+                for core in range(2):
+                    row = 4 + (chunk * 2 + core) * images
+                    place = core * half + m * images
+                    rows_ref[place : place + images, first : first + width] = pack[
+                        row : row + images, 0:width
+                    ]
+        out_ref[...] = rows_ref[...].astype(BF)
+
+    return pl.pallas_call(
+        kernel,
+        out_shape=SHAPE((total, embed_width), BF),
+        in_specs=[VM] * (members + 1) + [ANY],
+        out_specs=VM,
+        scratch_shapes=[pltpu.VMEM((total, embed_width), F32)],
+        compiler_params=params(24),
+        name="text_stack",
+    )(text_here, text_core, *packs, order)
+
+
+def own_block(place, x_here, weight_own):
+    images, height, width, channels = x_here.shape
+    share = weight_own.shape[1]
+
+    def kernel(place_ref, x_ref, weight_ref, mixed_ref, sum_ref):
+        sum_ref[...] = jnp.zeros_like(sum_ref)
+        conv_tiles(share // LANES, 0, place_ref[0], share, x_ref, weight_ref, mixed_ref, sum_ref)
+
+    return pl.pallas_call(
+        kernel,
         out_shape=[
             SHAPE((images, height, width, share), F32),
             SHAPE((images, height, width, LANES), F32),
-            SHAPE((ROWS_PAD, share), F32),
-            SHAPE(image_maps.shape, BF),
-            SHAPE(text_feats.shape, BF),
         ],
-        in_specs=[SM, HB, HB, HB, HB],
-        out_specs=[VM] * 5,
-        scratch_shapes=[
-            pltpu.VMEM(dw_kernel.shape, BF),
-            pltpu.VMEM(channel_terms.shape, BF),
-            pltpu.SemaphoreType.DMA((3 + members,)),
-        ],
+        in_specs=[SM, VM, VM],
+        out_specs=[VM] * 2,
         compiler_params=params(24),
         name="own_block",
-    )(place, *far([image_maps, dw_kernel, channel_terms, text_feats]))
+    )(place, *near([x_here, weight_own]))
 
 
 def forward_kernel(members, place_ref, head_hbm, x_ref, mixed_own, sum_own, weight_own, order_ref, *refs):
     kernel_refs, refs = refs[: members - 1], refs[members - 1 :]
-    term_refs, refs = refs[: members - 1], refs[members - 1 :]
+    pack_refs, refs = refs[: members - 1], refs[members - 1 :]
     piece_refs, refs = refs[:members], refs[members:]
     head_ref, weight_rest, mixed_rest, mean_ref, rstd_ref, hatsum_ref, hat_ref, hrstd_ref, sum_ref, pool_ref, sem = refs
     images, height, width, channels = x_ref.shape
@@ -227,7 +323,7 @@
     for m in range(1, members):
         lanes = slice((m - 1) * share, m * share)
         weight_rest[0:TAPS, lanes] = kernel_refs[m - 1][...].astype(F32)
-        weight_rest[TERM_ROW : TERM_ROW + 4, lanes] = term_refs[m - 1][...].astype(F32)
+        weight_rest[GAIN_ROW : GAIN_ROW + 4, lanes] = pack_refs[m - 1][...].astype(F32)[0:4]
     sum_ref[...] = sum_own[...]
     own_tiles = share // LANES
     rest_tiles = (members - 1) * own_tiles
@@ -257,8 +353,8 @@
             wide = lane_block(t + base * own_tiles, LANES)
             source = tile_of(base, t, member, share)
             scale = (
-                weight_ref[TERM_ROW + 1 : TERM_ROW + 2, lanes]
-                * weight_ref[TERM_ROW + 2 : TERM_ROW + 3, lanes]
+                weight_ref[GAIN_ROW + 1 : GAIN_ROW + 2, lanes]
+                * weight_ref[GAIN_ROW + 2 : GAIN_ROW + 3, lanes]
             )
             for i in range(images):
                 hats = jnp.zeros((width, LANES), F32)
@@ -280,22 +376,22 @@
     hrstd_ref[...] = jnp.broadcast_to(head_rstd, hrstd_ref.shape)
     for m in range(members):
         gain = (
-            weight_own[TERM_ROW + 3 : TERM_ROW + 4, :]
+            weight_own[GAIN_ROW + 3 : GAIN_ROW + 4, :]
             if m == 0
-            else weight_rest[TERM_ROW + 3 : TERM_ROW + 4, (m - 1) * share : m * share]
+            else weight_rest[GAIN_ROW + 3 : GAIN_ROW + 4, (m - 1) * share : m * share]
         )
         piece_refs[m][...] = (hat[:, m * share : (m + 1) * share] * gain).astype(BF)
     head_copy.wait()
 
 
-def forward_block(place, head_weight, x_here, own, order, kernels, terms):
+def forward_block(place, head_weight, x_here, own, order, kernels, packs):
     images, height, width, channels = x_here.shape
-    members = len(kernels) + 1
+    members = len(packs) + 1
     share = channels // members
     cell = (images, height, width, LANES)
     outs = [SHAPE((images, share), BF)] * members + [
         SHAPE(head_weight.shape, BF),
-        SHAPE((ROWS_PAD, channels - share), F32),
+        SHAPE((WEIGHT_ROWS, channels - share), F32),
         SHAPE((images, height, width, channels - share), F32),
         SHAPE(cell, F32),
         SHAPE(cell, F32),
@@ -315,7 +411,7 @@
         ],
         compiler_params=params(24),
         name="forward_block",
-    )(place, *far([head_weight]), *near([x_here, *own]), order, *near([*kernels, *terms]))
+    )(place, *far([head_weight]), *near([x_here, *own]), order, *near([*kernels, *packs]))
     return result[:members], result[members], result[members + 1], result[members + 2], result[members + 3 :]
 
 
@@ -336,6 +432,7 @@
         in_specs=[VM] * (members + 1),
         out_specs=[VM, VM],
         compiler_params=params(24),
+        cost_estimate=cost(0.5),
         name="head_project",
     )(*near([*pieces, head_weight]))
 
@@ -360,18 +457,35 @@
     return inverse * (grad - unit * jnp.sum(unit * grad, axis=1, keepdims=True))
 
 
-def loss_kernel(members, *refs):
-    partials, refs = refs[:members], refs[members:]
-    text_low, text_high, group_ref, weight_ref, packed_ref = refs[:5]
-    piece_refs = refs[5:]
-    total_rows, width = partials[0].shape
+def embed_sum_kernel(members, *refs):
+    total_rows = refs[0].shape[0]
+    rows = total_rows // members
+    embed = refs[0][...]
+    for m in range(1, members):
+        embed = embed + jnp.concatenate(
+            [refs[m][(k ^ m) * rows : (k ^ m) * rows + rows, :] for k in range(members)], axis=0
+        )
+    refs[members][...] = embed
+
+
+def embed_sum(partials):
+    members = len(partials)
+    return pl.pallas_call(
+        lambda *refs: embed_sum_kernel(members, *refs),
+        out_shape=SHAPE(partials[0].shape, F32),
+        in_specs=[VM] * members,
+        out_specs=VM,
+        compiler_params=params(24),
+        cost_estimate=cost(SUM_COST),
+        name="embed_sum",
+    )(*near(partials))
+
+
+def loss_kernel(members, embed_ref, text_low, text_high, group_ref, weight_ref, packed_ref, *piece_refs):
+    total_rows, width = embed_ref.shape
     rows = total_rows // members
     share = group_ref.shape[1]
-    embed = partials[0][...]
-    for m in range(1, members):
-        embed = embed + jnp.concatenate(
-            [partials[m][(k ^ m) * rows : (k ^ m) * rows + rows, :] for k in range(members)], axis=0
-        )
+    embed = embed_ref[...]
     inverse = inverse_norm(embed)
     unit = embed * inverse
     unit_bf = unit.astype(BF)
@@ -391,45 +505,33 @@
         piece_refs[m][...] = part[m * rows : m * rows + rows]
 
 
-def loss_block(partials, texts, group, head_weight):
-    members = len(partials)
-    total_rows, embed_width = partials[0].shape
+def loss_block(members, embed, texts, group, head_weight):
+    total_rows, embed_width = embed.shape
     share = head_weight.shape[0]
     result = pl.pallas_call(
         lambda *refs: loss_kernel(members, *refs),
         out_shape=[SHAPE((total_rows, share + 2 * embed_width), BF)]
         + [SHAPE((total_rows // members, share), F32)] * members,
-        in_specs=[VM] * (members + 4),
+        in_specs=[VM] * 5,
         out_specs=[VM] * (members + 1),
         compiler_params=params(24),
         name="loss_block",
-    )(*near([*partials, *texts, group, head_weight]))
+    )(*near([embed, *texts, group, head_weight]))
     return result[0], result[1:]
 
 
-def terms_kernel(members, place_ref, *refs):
+def pool_grad_kernel(members, cells, *refs):
     grad_refs, refs = refs[:members], refs[members:]
-    order_ref, x_ref, weight_own, weight_rest, mixed_own, mixed_rest, mean_ref, rstd_ref, hatsum_ref, hat_ref, hrstd_ref = refs[:11]
-    keep_ref, give_ref, flow_ref, shared_ref, scaled_ref, dot_ref, sums_ref, taps_ref = refs[11:]
-    images, height, width, channels = x_ref.shape
-    share = channels // members
-    own_tiles = share // LANES
-    rest_tiles = (members - 1) * own_tiles
-    cells = height * width
-    member = place_ref[0]
-    core = place_ref[1]
-    parts = [(0, own_tiles, mixed_own), (1, rest_tiles, mixed_rest)]
+    weight_own, weight_rest, hatsum_ref, hat_ref, hrstd_ref, shared_ref, scaled_ref, rows_ref = refs
 
     def term_row(row):
         return jnp.concatenate(
-            [weight_own[TERM_ROW + row : TERM_ROW + row + 1, :], weight_rest[TERM_ROW + row : TERM_ROW + row + 1, :]],
+            [weight_own[GAIN_ROW + row : GAIN_ROW + row + 1, :], weight_rest[GAIN_ROW + row : GAIN_ROW + row + 1, :]],
             axis=1,
         )
 
     grad = jnp.concatenate([ref[...] for ref in grad_refs], axis=1)
     hat = hat_ref[...]
-    sums_ref[...] = jnp.zeros_like(sums_ref)
-    sums_ref[TERM_ROW + 3 : TERM_ROW + 4, :] = jnp.sum(grad * hat, axis=0, keepdims=True)
     inner = grad * term_row(3)
     shared = (
         hrstd_ref[:, 0:1]
@@ -444,17 +546,44 @@
     gain = term_row(1)
     scale = term_row(2)
     hat_total = jnp.sum(shared * hatsum_ref[...], axis=0, keepdims=True)
-    sums_ref[TERM_ROW + 1 : TERM_ROW + 2, :] = hat_total * scale
-    sums_ref[TERM_ROW + 2 : TERM_ROW + 3, :] = hat_total * gain
+    rows_ref[...] = jnp.zeros_like(rows_ref)
+    rows_ref[1:2, :] = hat_total * scale
+    rows_ref[2:3, :] = hat_total * gain
+    rows_ref[3:4, :] = jnp.sum(grad * hat, axis=0, keepdims=True)
     scaled = shared * (gain * scale)
     scaled_ref[...] = scaled - jnp.mean(scaled, axis=1, keepdims=True)
+
+
+def pool_grad_block(grads, cells, weights, hatsum, hat, hrstd):
+    members = len(grads)
+    images, channels = hat.shape
+    return pl.pallas_call(
+        lambda *refs: pool_grad_kernel(members, cells, *refs),
+        out_shape=[
+            SHAPE((images, channels), F32),
+            SHAPE((images, channels), F32),
+            SHAPE((8, channels), F32),
+        ],
+        in_specs=[VM] * (members + 5),
+        out_specs=[VM] * 3,
+        compiler_params=params(24),
+        cost_estimate=cost(0.4),
+        name="pool_grad_block",
+    )(*near([*grads, *weights, hatsum, hat, hrstd]))
+
+
+def dots_kernel(scaled_ref, mixed_own, mixed_rest, mean_ref, rstd_ref, dot_ref):
+    images, height = dot_ref.shape[:2]
+    channels = scaled_ref.shape[1]
+    own_tiles = mixed_own.shape[3] // LANES
+    rest_tiles = mixed_rest.shape[3] // LANES
     dot_ref[...] = jnp.zeros_like(dot_ref)
-    for base, tiles, mixed_ref in parts:
+    for first, tiles, mixed_ref in [(0, own_tiles, mixed_own), (own_tiles, rest_tiles, mixed_rest)]:
 
         @pl.loop(0, tiles)
         def _(t):
             lanes = lane_block(t, LANES)
-            wide = lane_block(t + base * own_tiles, LANES)
+            wide = lane_block(t + first, LANES)
             for i in range(images):
                 factor = scaled_ref[i : i + 1, wide]
                 for h in range(height):
@@ -462,91 +591,111 @@
 
     dots = jnp.sum(dot_ref[...], axis=-1, keepdims=True) * (1.0 / channels)
     dot_ref[...] = jnp.broadcast_to(dots, dot_ref.shape) * rstd_ref[...] * rstd_ref[...]
-    for base, tiles, mixed_ref in parts:
-
-        @pl.loop(0, tiles)
-        def _(t):
-            lanes = lane_block(t, LANES)
-            wide = lane_block(t + base * own_tiles, LANES)
-            source = tile_of(base, t, member, share)
-            flows = []
+
+
+def dots_block(scaled, mixed, mean, rstd):
+    return pl.pallas_call(
+        dots_kernel,
+        out_shape=SHAPE(mean.shape, F32),
+        in_specs=[VM] * 5,
+        out_specs=VM,
+        compiler_params=params(24),
+        cost_estimate=cost(DOTS_COST),
+        name="dots_block",
+    )(*near([scaled, *mixed, mean, rstd]))
+
+
+def terms_kernel(base, share, place_ref, x_ref, scaled_ref, rows_ref, mixed_ref, mean_ref, rstd_ref, dot_ref, *refs):
+    keep_ref, give_ref, flow_ref, sums_ref, taps_ref = refs
+    images, height, width = x_ref.shape[:3]
+    channels = mixed_ref.shape[3]
+    own_tiles = share // LANES
+    member = place_ref[0]
+    core = place_ref[1]
+    first = base * share
+    sums_ref[TAPS // 8 * 8 : TERM_ROW, :] = jnp.zeros((TERM_ROW - TAPS // 8 * 8, channels), F32)
+    sums_ref[TERM_ROW:ROWS_PAD, :] = rows_ref[:, first : first + channels]
+
+    @pl.loop(0, channels // LANES)
+    def _(t):
+        lanes = lane_block(t, LANES)
+        wide = lane_block(t + base * own_tiles, LANES)
+        source = tile_of(base, t, member, share)
+        flows = []
+        for i in range(images):
+            factor = scaled_ref[i : i + 1, wide]
+            flow_rows = []
+            for h in range(height):
+                centered = mixed_ref[i, h, :, lanes] - mean_ref[i, h]
+                flow = rstd_ref[i, h] * (factor - centered * dot_ref[i, h])
+                flow_ref[i, h, :, lanes] = flow
+                flow_rows.append(flow)
+            flows.append(flow_rows)
+        bias = flows[0][0]
+        for i in range(images):
+            for h in range(height):
+                if i or h:
+                    bias = bias + flows[i][h]
+        taps_ref[TAPS * width : TAPS * width + width, :] = bias
+        for b in range(KER):
+            totals = [None] * KER
             for i in range(images):
-                factor = scaled_ref[i : i + 1, wide]
-                flow_rows = []
-                for h in range(height):
-                    centered = mixed_ref[i, h, :, lanes] - mean_ref[i, h]
-                    flow = rstd_ref[i, h] * (factor - centered * dot_ref[i, h])
-                    flow_ref[i, h, :, wide] = flow
-                    flow_rows.append(flow)
-                flows.append(flow_rows)
-            bias = flows[0][0]
-            for i in range(images):
-                for h in range(height):
-                    if i or h:
-                        bias = bias + flows[i][h]
-            taps_ref[TAPS * width : TAPS * width + width, :] = bias
-            for b in range(KER):
-                totals = [None] * KER
-                for i in range(images):
-                    moved = [
-                        shift_cols(x_ref[i, h, :, source].astype(F32), b - REACH)
-                        for h in range(height)
-                    ]
-                    for a in range(KER):
-                        for h in range(max(0, REACH - a), min(height, height + REACH - a)):
-                            term = flows[i][h] * moved[h + a - REACH]
-                            totals[a] = term if totals[a] is None else totals[a] + term
+                moved = [
+                    shift_cols(x_ref[i, h, :, source].astype(F32), b - REACH)
+                    for h in range(height)
+                ]
                 for a in range(KER):
-                    tap = a * KER + b
-                    taps_ref[tap * width : tap * width + width, :] = totals[a]
-            rows = TAPS + 1
-            total = taps_ref[pl.ds(0, rows, stride=width), :]
-            for s in range(1, width):
-                total = total + taps_ref[pl.ds(s, rows, stride=width), :]
-            sums_ref[0:TAPS, wide] = total[0:TAPS]
-            sums_ref[TERM_ROW : TERM_ROW + 1, wide] = total[TAPS : TAPS + 1]
-
-    for m in range(members):
+                    for h in range(max(0, REACH - a), min(height, height + REACH - a)):
+                        term = flows[i][h] * moved[h + a - REACH]
+                        totals[a] = term if totals[a] is None else totals[a] + term
+            for a in range(KER):
+                tap = a * KER + b
+                taps_ref[tap * width : tap * width + width, :] = totals[a]
+        rows = TAPS + 1
+        total = taps_ref[pl.ds(0, rows, stride=width), :]
+        for s in range(1, width):
+            total = total + taps_ref[pl.ds(s, rows, stride=width), :]
+        sums_ref[0:TAPS, lanes] = total[0:TAPS]
+        sums_ref[TERM_ROW : TERM_ROW + 1, lanes] = total[TAPS : TAPS + 1]
+
+    for m in range(channels // share):
         lanes = slice(m * share, (m + 1) * share)
         keep_ref[m] = sums_ref[pl.ds(pl.multiple_of(core * HALF_PAD, HALF_PAD), HALF_PAD), lanes].astype(BF)
         give_ref[m] = sums_ref[pl.ds(pl.multiple_of((1 - core) * HALF_PAD, HALF_PAD), HALF_PAD), lanes].astype(BF)
 
 
-def terms_block(place, grads, order, x_here, weights, mixed, saved):
-    images, height, width, channels = x_here.shape
-    members = len(grads)
-    share = channels // members
-    half = SHAPE((members, HALF_PAD, share), BF)
-    return pl.pallas_call(
-        lambda *refs: terms_kernel(members, *refs),
-        out_shape=[half, half, SHAPE(x_here.shape, F32), SHAPE((images, channels), F32)],
-        in_specs=[SM] + [VM] * members + [ANY] + [VM] * 10,
-        out_specs=[VM] * 4,
+def terms_block(base, share, place, order, x_here, scaled, rows, mixed, mean, rstd, dots):
+    width = x_here.shape[2]
+    channels = mixed.shape[3]
+    half = SHAPE((channels // share, HALF_PAD, share), BF)
+    return pl.pallas_call(
+        lambda place_ref, order_ref, *refs: terms_kernel(base, share, place_ref, *refs),
+        out_shape=[half, half, SHAPE(mixed.shape, F32)],
+        in_specs=[SM, ANY] + [VM] * 7,
+        out_specs=[VM] * 3,
         scratch_shapes=[
-            pltpu.VMEM((images, channels), F32),
-            pltpu.VMEM((images, height, width, LANES), F32),
             pltpu.VMEM((ROWS_PAD, channels), F32),
             pltpu.VMEM(((TAPS + 1) * width, LANES), F32),
         ],
         compiler_params=params(24),
         name="terms_block",
-    )(place, *near(grads), order, *near([x_here, *weights, *mixed, *saved]))
-
-
-def images_kernel(image, base, place_ref, flow_ref, weight_own, weight_rest, shared_ref, out_ref, token_ref):
-    height, width, channels = flow_ref.shape[1:]
+    )(place, order, *near([x_here, scaled, rows, mixed, mean, rstd, dots]))
+
+
+def images_kernel(image, base, place_ref, flow_own, flow_rest, weight_own, weight_rest, shared_ref, out_ref, token_ref):
+    height = flow_own.shape[1]
     share = weight_own.shape[1]
     own_tiles = share // LANES
     step = pl.program_id(0) + base
     token_ref[...] = jnp.zeros_like(token_ref)
 
-    def piece(weight_ref, first):
+    def piece(flow_ref, weight_ref, first):
         @pl.loop(0, own_tiles)
         def _(t):
             lanes = lane_block(t, LANES)
             wide = lane_block(t + step * own_tiles, LANES)
             near_lanes = lane_block(t + (step - first) * own_tiles, LANES)
-            rows = [flow_ref[image, h, :, wide] for h in range(height)]
+            rows = [flow_ref[image, h, :, near_lanes] for h in range(height)]
             sums = conv_rows(rows, lambda tap: weight_ref[tap : tap + 1, near_lanes], True)
             for h in range(height):
                 out_ref[0, h, :, lanes] = (sums[h] + shared_ref[image : image + 1, wide]).astype(BF)
@@ -555,38 +704,42 @@
 
         @pl.when(step == 0)
         def _():
-            piece(weight_own, 0)
+            piece(flow_own, weight_own, 0)
 
     @pl.when(step != 0)
     def _():
-        piece(weight_rest, 1)
+        piece(flow_rest, weight_rest, 1)
 
 
 def image_block(image, base, count, place, flow, weights, shared, order, out):
     first = out is None
     share = weights[0].shape[1]
-    operands = [place, *near([flow, *weights, shared]), order] + ([] if first else [out])
+    operands = [place, *near([*flow, *weights, shared]), order] + ([] if first else [out])
 
     def kernel(*refs):
-        images_kernel(image, base, *refs[:5], refs[-2], refs[-1])
+        images_kernel(image, base, *refs[:6], refs[-2], refs[-1])
 
     return pl.pallas_call(
         kernel,
         grid_spec=pltpu.PrefetchScalarGridSpec(
             num_scalar_prefetch=1,
             grid=(count,),
-            in_specs=[VM, VM, VM, VM, ANY] + ([] if first else [HB]),
+            in_specs=[VM] * 5 + [ANY] + ([] if first else [HB]),
             out_specs=[
                 pl.BlockSpec(
-                    (1,) + flow.shape[1:3] + (share,),
+                    (1,) + flow[0].shape[1:3] + (share,),
                     lambda step, place_ref: (image, 0, 0, place_ref[0] ^ (step + base)),
                 ),
                 pl.BlockSpec((8, LANES), lambda step, place_ref: (0, 0)),
             ],
         ),
-        out_shape=[SHAPE(flow.shape, BF), SHAPE((8, LANES), F32)],
-        input_output_aliases={} if first else {6: 0},
-        compiler_params=params(24),
+        out_shape=[
+            SHAPE(flow[0].shape[:3] + (shared.shape[1],), BF),
+            SHAPE((8, LANES), F32),
+        ],
+        input_output_aliases={} if first else {7: 0},
+        compiler_params=params(24),
+        cost_estimate=cost(1.5),
         name="image_block",
     )(*operands)
 
@@ -678,24 +831,21 @@
     core = lax.axis_index("dp") % 2
     place = jnp.stack([member, core]).astype(jnp.int32)
     others = range(1, members)
-    pair_masks = bits_up(members)
     dp_masks = bits_up(lax.axis_size("dp"))
     down = dp_masks[::-1]
     share = head_weight.shape[0]
 
     kernels = [swap(dw_kernel, "fsdp", m) for m in others]
-    terms = [swap(channel_terms, "fsdp", m) for m in others]
-    mixed_own, sum_own, weight_own, x_here, text_here = own_block(
-        place, image_maps, dw_kernel, channel_terms, text_feats
-    )
-
-    text_rows = stack_rows(text_here, swap(text_feats, "fsdp", 1), sum_own)
-    for mask in pair_masks[1:]:
-        text_rows = stack_rows(text_rows, swap(text_rows, "fsdp", mask), sum_own)
-    text_rows = stack_rows(text_rows, swap(text_rows, "dp", 1), (terms or [sum_own])[-1])
+    text_core = swap(text_feats, "dp", 1)
+    x_here, weight_own, text_here = load_block(image_maps, dw_kernel, channel_terms, text_feats)
+    pack_own = pack_block(weight_own, text_here, text_core)
+    packs = [swap(pack_own, "fsdp", m) for m in others]
+    mixed_own, sum_own = own_block(place, x_here, weight_own)
+
+    text_rows = text_stack(text_here, text_core, packs, sum_own)
     text_masks = down[:-1]
     pieces, head_here, weight_rest, mixed_rest, saved = forward_block(
-        place, head_weight, x_here, (mixed_own, sum_own, weight_own), text_rows, kernels, terms
+        place, head_weight, x_here, (mixed_own, sum_own, weight_own), text_rows, kernels, packs
     )
     weights = (weight_own, weight_rest)
     far_rows = swap(text_rows, "dp", text_masks[0])
@@ -708,13 +858,25 @@
     texts = (text_rows, far_rows)
 
     partials = [partial] + [swap(partial, "fsdp", m) for m in others]
-    packed, grads = loss_block(partials, texts, group, head_here)
+    packed, grads = loss_block(members, embed_sum(partials), texts, group, head_here)
     grads = [grads[0]] + [swap(grads[m], "fsdp", m) for m in others]
 
-    packed = stack_rows(packed, swap(packed, "dp", down[0]), packed)
-    keep, give, flow, shared = terms_block(
-        place, grads, packed, x_here, weights, (mixed_own, mixed_rest), saved
-    )
+    mean, rstd, hatsum, hat, hrstd = saved
+    cells = image_maps.shape[1] * image_maps.shape[2]
+    shared, scaled, term_rows = pool_grad_block(grads, cells, weights, hatsum, hat, hrstd)
+    mixed = (mixed_own, mixed_rest)
+    dots = dots_block(scaled, mixed, mean, rstd)
+    moving = swap(packed, "dp", down[0])
+
+    def terms_part(base, mixed_part, order):
+        return terms_block(
+            base, share, place, order, x_here, scaled, term_rows, mixed_part, mean, rstd, dots
+        )
+
+    packed = stack_rows(packed, moving, dots)
+    keep_rest, give_rest, flow_rest = terms_part(1, mixed_rest, packed)
+    keep_own, give_own, flow_own = terms_part(0, mixed_own, keep_rest)
+    flow = (flow_own, flow_rest)
 
     parts = [(image, base) for image in range(image_maps.shape[0]) for base in (0, members // 2)]
     image_grads = None
@@ -728,17 +890,20 @@
             )
         return image_grads, token
 
-    chip = chip_sums(keep, swap(give, "dp", 1))
+    chip = chip_sums(keep_rest, swap(give_rest, "dp", 1), keep_own)
+    chip_own = chip_sums(keep_own, swap(give_own, "dp", 1), chip[0])[0]
     gather_masks = list(down[1:])
+    image_grads, token = image_parts(1, chip[0], None)
+    packed = hold(packed, token)
     moving = swap(packed, "dp", gather_masks.pop(0))
-    image_grads, token = image_parts(1, chip[0], None)
-    sent = add_all([chip[0]] + [swap(chip[m], "fsdp", m) for m in others], token)
+    sent = add_all([chip_own] + [swap(chip[m - 1], "fsdp", m) for m in others], token)
     ring_masks = dp_masks[1:]
     counts = [1] + [2] * len(ring_masks)
     for mask, count in zip(ring_masks[:-1], counts):
-        packed = stack_rows(packed, moving, token)
-        moving = swap(packed, "dp", gather_masks.pop(0))
         image_grads, token = image_parts(count, sent, image_grads)
+        if mask == ring_masks[0]:
+            packed = stack_rows(packed, moving, token)
+            moving = swap(packed, "dp", gather_masks.pop(0))
         sent = add_all([sent, swap(sent, "dp", mask)], token)
     image_grads, token = image_parts(len(parts), sent, image_grads)
     while gather_masks:

time: 72.1 us -> 69.6 us (0.965)
  waiting for transfers between devices: 17.7 us -> 11.4 us
  starting transfers between devices: 17.7 us -> 20.6 us
  Pallas kernels: 35.8 us -> 36.6 us
    ppermute x20, waiting for transfers between devices: 17.7 us -> 11.4 us  [swap(): lax.ppermute(value, axis, [(source, source ^ mask) for source in range(co...]
    ppermute x20, starting transfers between devices: 17.7 us -> 20.6 us  [swap(): lax.ppermute(value, axis, [(source, source ^ mask) for source in range(co...]
    pallas_call x2 -> x10, Pallas kernels: 11.6 us -> 12.4 us  [the longest x2 6.9 us: terms_block(): pl.pallas_call(lambda place_ref, order_ref, *refs: terms_kernel(base, sha...]
  transfers between devices with their start and end apart: 20 -> 20, of which waited for: 10 -> 10; matrix products, arithmetic and copies ran while one was open for 0% -> 0% of each run, Pallas kernels for 36% -> 44%
where the time goes in v5:
time: 69.6 us; the launch traced here: 69.5 us
  Pallas kernels  36.6 us (53%)
  starting transfers between devices  20.6 us (30%)
  waiting for transfers between devices  11.4 us (16%)
  between operations  0.78 us (1%)
    ppermute x20, starting transfers between devices, swap(): lax.ppermute(value, axis, [(source, source ^ mask) for source in range(co...  20.6 us
    ppermute x20, waiting for transfers between devices, swap(): lax.ppermute(value, axis, [(source, source ^ mask) for source in range(co...  11.4 us
    pallas_call x4, Pallas kernels, image_block(): pl.pallas_call(kernel, grid_spec=pltpu.PrefetchScalarGridSpec(num_scalar_...  10.5 us
    pallas_call x2, Pallas kernels, terms_block(): pl.pallas_call(lambda place_ref, order_ref, *refs: terms_kernel(base, sha...  6.9 us
    pallas_call x1, Pallas kernels, forward_block(): pl.pallas_call(lambda *refs: forward_kernel(members, *refs), out_shape=ou...  5.08 us
    pallas_call x1, Pallas kernels, head_grads_block(): pl.pallas_call(lambda *refs: head_grads_kernel(block, *refs), grid=(share...  5.05 us
    pallas_call x1, Pallas kernels, own_block(): pl.pallas_call(kernel, out_shape=[SHAPE((images, height, width, share), F...  3.31 us
    pallas_call x1, Pallas kernels, loss_block(): pl.pallas_call(lambda *refs: loss_kernel(members, *refs), out_shape=[SHAP...  1.47 us
  transfers between devices with their start and end apart: 20, of which 10 were waited for; matrix products, arithmetic and copies ran while one was open for 0% of the time, Pallas kernels for 44%

profile of v5, /device:TPU:0, one launch (start us, length us, event | category | flops | bytes accessed | tf_op | source)
XLA Modules:
  0.0 69.5 jit_solution(8866903953404967487)
XLA Ops:
  0.6 3.0 %collective-permute-start.2 = (bf16[49,1536]{1,0:T(8,128)(2,1)}, bf16[49,1536]{1,0:T(8,128)(2,1)S(1)}, u32[]{:S(2)}, u32[]{:S(2)}) collective-permute-start(bf16[49,1536]{1,0:T(8,128)(2,1)} %kernel_hbm.1), channel_id=1, source_target_pairs={{0,1},{1,0},{2,3},{3,2},{4,5},{5,4},{6,7},{7,6},{8,9},{9,8},{10,11... | collective-permute-start | bytes 451592 | tf_op jit(solution)/shard_map/ppermute | solution.py:28
  3.7 0.0 collective-permute-start
  3.7 1.3 %load_block.1 = (bf16[2,8,8,3072]{3,2,1,0:T(8,128)(2,1)S(1)}, f32[56,1536]{1,0:T(8,128)S(1)}, bf16[2,1152]{1,0:T(2,128)(2,1)S(1)}) custom-call(bf16[2,8,8,3072]{3,2,1,0:T(8,128)(2,1)} %x_hbm.1, bf16[49,1536]{1,0:T(8,128)(2,1)} %kernel_hbm.1, bf16[4,1536]{1,0:T(4,128)(2,1)} %term_hbm.1, bf16[2,1152]{1,0:T(2,128)(2,1)} %text_hbm.1), custom_call_target="tpu_custom_call" | custom-call | tf_op jit(solution)/shard_map/load_block/pallas_call | solution.py:213
  5.0 0.1 collective-permute-done.core_ref.refs_1_
  5.1 0.1 collective-permute-start.1
  5.2 0.1 pad_add_fusion.place_ref.refs_0_
  5.3 3.3 %own_block.1 = (f32[2,8,8,1536]{3,2,1,0:T(8,128)S(1)}, f32[2,8,8,128]{3,2,1,0:T(8,128)S(1)}) custom-call(s32[2]{0:T(128)S(1)} %pad_add_fusion.place_ref.refs_0_, bf16[2,8,8,3072]{3,2,1,0:T(8,128)(2,1)S(1)} %get-tuple-element.46.x_ref.refs_2_.refs_0_, f32[56,1536]{1,0:T(8,128)S(1)} %get-tuple-element.47.weight_ref.refs_5_.refs_2_.refs_3_), custom_call_target="tpu_custom_call" | custom-call | tf_op jit(solution)/shard_map/own_block/pallas_call | solution.py:299
  8.6 0.4 collective-permute-done.1.refs_2_.refs_8_
  9.0 2.7 %collective-permute-start.5 = (bf16[8,1152]{1,0:T(8,128)(2,1)S(1)}, bf16[8,1152]{1,0:T(8,128)(2,1)S(1)}, u32[]{:S(2)}, u32[]{:S(2)}) collective-permute-start(bf16[8,1152]{1,0:T(8,128)(2,1)S(1)} %text_stack.1.refs_6_.low_ref), channel_id=1, source_target_pairs={{0,16},{2,18},{4,20},{6,22},{8,24},{10,26},{12,28},{14,30},{16,0},... | collective-permute-start | bytes 55304 | tf_op jit(solution)/shard_map/ppermute | solution.py:28
  11.7 5.1 %forward_block.1 = (bf16[2,1536]{1,0:T(2,128)(2,1)S(1)}, bf16[2,1536]{1,0:T(2,128)(2,1)S(1)}, bf16[1536,1152]{1,0:T(8,128)(2,1)S(1)}, f32[56,1536]{1,0:T(8,128)S...) custom-call(s32[2]{0:T(128)S(1)} %pad_add_fusion.place_ref.refs_0_, ...), custom_call_target="tpu_custom_call" | custom-call | tf_op jit(solution)/shard_map/forward_block/pallas_call | solution.py:402
  16.8 1.6 %collective-permute-start.3 = (bf16[2,1536]{1,0:T(2,128)(2,1)S(1)}, bf16[2,1536]{1,0:T(2,128)(2,1)S(1)}, u32[]{:S(2)}, u32[]{:S(2)}) collective-permute-start(bf16[2,1536]{1,0:T(2,128)(2,1)S(1)} %get-tuple-element.52), channel_id=1, source_target_pairs={{0,1},{1,0},{2,3},{3,2},{4,5},{5,4},{6,7},{7,6},{8,9},{9,8},{10,11... | collective-permute-start | bytes 18440 | tf_op jit(solution)/shard_map/ppermute | solution.py:28
  18.4 1.6 %collective-permute-start.6 = (bf16[16,1152]{1,0:T(8,128)(2,1)S(1)}, bf16[16,1152]{1,0:T(8,128)(2,1)S(1)}, u32[]{:S(2)}, u32[]{:S(2)}) collective-permute-start(bf16[16,1152]{1,0:T(8,128)(2,1)S(1)} %stack_rows.5.low_ref), channel_id=1, source_target_pairs={{0,8},{2,10},{4,12},{6,14},{8,0},{10,2},{12,4},{14,6},{16,24},{18,... | collective-permute-start | bytes 110600 | tf_op jit(solution)/shard_map/ppermute | solution.py:28
  20.0 0.5 collective-permute-done.3.refs_1_
  20.5 0.6 head_project.1
  21.1 1.6 %collective-permute-start.4 = (f32[4,1152]{1,0:T(4,128)S(1)}, f32[4,1152]{1,0:T(4,128)S(1)}, u32[]{:S(2)}, u32[]{:S(2)}) collective-permute-start(f32[4,1152]{1,0:T(4,128)S(1)} %get-tuple-element.54.refs_0_.order_ref), channel_id=1, source_target_pairs={{0,1},{1,0},{2,3},{3,2},{4,5},{5,4},{6,7},{7,6},{8,9},{9,8},{10,11... | collective-permute-start | bytes 55304 | tf_op jit(solution)/shard_map/ppermute | solution.py:28
  22.6 1.6 %collective-permute-start.7 = (bf16[32,1152]{1,0:T(8,128)(2,1)S(1)}, bf16[32,1152]{1,0:T(8,128)(2,1)S(1)}, u32[]{:S(2)}, u32[]{:S(2)}) collective-permute-start(bf16[32,1152]{1,0:T(8,128)(2,1)S(1)} %stack_rows.6.refs_1_), channel_id=1, source_target_pairs={{0,4},{2,6},{4,0},{6,2},{8,12},{10,14},{12,8},{14,10},{16,20},{18,... | collective-permute-start | bytes 221192 | tf_op jit(solution)/shard_map/ppermute | solution.py:28
  24.2 0.7 collective-permute-done.4.refs_1_
  24.9 2.2 %collective-permute-done.7.refs_2_ = bf16[32,1152]{1,0:T(8,128)(2,1)S(1)} collective-permute-done((bf16[32,1152]{1,0:T(8,128)(2,1)S(1)}, bf16[32,1152]{1,0:T(8,128)(2,1)S(1)}, u32[]{:S(2)}, u32[]{:S(2)}) %collective-permute-start.7) | collective-permute-done | bytes 73760 | tf_op jit(solution)/shard_map/ppermute | solution.py:28
  27.1 1.5 %loss_block.1 = (bf16[4,3840]{1,0:T(4,128)(2,1)S(1)}, f32[2,1536]{1,0:T(2,128)S(1)}, f32[2,1536]{1,0:T(2,128)S(1)}) custom-call(f32[4,1152]{1,0:T(4,128)S(1)} %embed_sum.1.refs_0_, bf16[32,1152]{1,0:T(8,128)(2,1)S(1)} %stack_rows.6.refs_1_, bf16[32,1152]{1,0:T(8,128)(2,1)S(1)} %collective-permute-done.7.refs_2_, ...), custom_call_target="tpu_custom_call" | custom-call | tf_op jit(solution)/shard_map/loss_block/pallas_call | solution.py:511
  28.5 0.5 collective-permute-start.9
  29.1 0.3 collective-permute-start.8
  29.3 2.9 %collective-permute-done.9.refs_1_ = f32[2,1536]{1,0:T(2,128)S(1)} collective-permute-done((f32[2,1536]{1,0:T(2,128)S(1)}, f32[2,1536]{1,0:T(2,128)S(1)}, u32[]{:S(2)}, u32[]{:S(2)}) %collective-permute-start.9) | collective-permute-done | bytes 12320 | tf_op jit(solution)/shard_map/ppermute | solution.py:28
  32.2 0.3 pool_grad_block.1
  32.5 0.6 dots_block.1.order_ref.refs_6_
  33.1 0.8 %collective-permute-done.8.high_ref = bf16[4,3840]{1,0:T(4,128)(2,1)S(1)} collective-permute-done((bf16[4,3840]{1,0:T(4,128)(2,1)S(1)}, bf16[4,3840]{1,0:T(4,128)(2,1)S(1)}, u32[]{:S(2)}, u32[]{:S(2)}) %collective-permute-start.8) | collective-permute-done | bytes 30752 | tf_op jit(solution)/shard_map/ppermute | solution.py:28
  33.9 3.4 %terms_block.2 = (bf16[1,32,1536]{2,1,0:T(8,128)(2,1)S(1)}, bf16[1,32,1536]{2,1,0:T(8,128)(2,1)S(1)}, f32[2,8,8,1536]{3,2,1,0:T(8,128)S(1)}) custom-call(s32[2]{0:T(128)S(1)} %pad_add_fusion.place_ref.refs_0_, bf16[8,3840]{1,0:T(8,128)(2,1)S(1)} %stack_rows.7.order_ref.value_ref, bf16[2,8,8,3072]{3,2,1,0:T(8,128)(2,1)S(1)} %get-tuple-element.46.x_ref.refs_2_.refs_0_, ...), custom_call_target="tpu_custom_call" | custom-call | tf_op jit(solution)/shard_map/terms_block/pallas_call | solution.py:671
  37.3 0.1 collective-permute-start.11
  37.4 3.5 %terms_block.3 = (bf16[1,32,1536]{2,1,0:T(8,128)(2,1)S(1)}, bf16[1,32,1536]{2,1,0:T(8,128)(2,1)S(1)}, f32[2,8,8,1536]{3,2,1,0:T(8,128)S(1)}) custom-call(s32[2]{0:T(128)S(1)} %pad_add_fusion.place_ref.refs_0_, bf16[1,32,1536]{2,1,0:T(8,128)(2,1)S(1)} %get-tuple-element.68.order_ref.keep_ref, ...), custom_call_target="tpu_custom_call" | custom-call | tf_op jit(solution)/shard_map/terms_block/pallas_call | solution.py:671
  40.9 0.6 collective-permute-start.10
  41.5 1.6 %collective-permute-start.12 = (bf16[32,1536]{1,0:T(8,128)(2,1)S(1)}, bf16[32,1536]{1,0:T(8,128)(2,1)S(1)}, u32[]{:S(2)}, u32[]{:S(2)}) collective-permute-start(bf16[32,1536]{1,0:T(8,128)(2,1)S(1)} %chip_sums.2.order_ref.refs_6_), channel_id=1, source_target_pairs={{0,1},{1,0},{2,3},{3,2},{4,5},{5,4},{6,7},{7,6},{8,9},{9,8},{10,11... | collective-permute-start | bytes 294920 | tf_op jit(solution)/shard_map/ppermute | solution.py:28
  43.0 2.6 %image_block.4 = (bf16[2,8,8,3072]{3,2,1,0:T(8,128)(2,1)}, f32[8,128]{1,0:T(8,128)S(1)}) custom-call(s32[2]{0:T(128)S(1)} %pad_add_fusion.place_ref.refs_0_, f32[2,8,8,1536]{3,2,1,0:T(8,128)S(1)} %get-tuple-element.69.refs_1_, f32[2,8,8,1536]{3,2,1,0:T(8,128)S(1)} %get-tuple-element.70.refs_2_, ...), custom_call_target="tpu_custom_call" | custom-call | flops 1650000000 | tf_op jit(solution)/shard_map/image_block/pallas_call | solution.py:722
  45.7 1.6 %collective-permute-start.16 = (bf16[8,3840]{1,0:T(8,128)(2,1)S(1)}, bf16[8,3840]{1,0:T(8,128)(2,1)S(1)}, u32[]{:S(2)}, u32[]{:S(2)}) collective-permute-start(bf16[8,3840]{1,0:T(8,128)(2,1)S(1)} %hold.1.low_ref), channel_id=1, source_target_pairs={{0,8},{2,10},{4,12},{6,14},{8,0},{10,2},{12,4},{14,6},{16,24},{18,... | collective-permute-start | bytes 184328 | tf_op jit(solution)/shard_map/ppermute | solution.py:28
  47.2 0.0 collective-permute-done.10.give_ref
  47.3 0.0 collective-permute-done.12.refs_1_
  47.3 1.6 %collective-permute-start.13 = (bf16[32,1536]{1,0:T(8,128)(2,1)S(1)}, bf16[32,1536]{1,0:T(8,128)(2,1)S(1)}, u32[]{:S(2)}, u32[]{:S(2)}) collective-permute-start(bf16[32,1536]{1,0:T(8,128)(2,1)S(1)} %add_all.4.refs_6_.refs_0_), channel_id=1, source_target_pairs={{0,4},{2,6},{4,0},{6,2},{8,12},{10,14},{12,8},{14,10},{16,20},{18,... | collective-permute-start | bytes 294920 | tf_op jit(solution)/shard_map/ppermute | solution.py:28
  48.9 2.7 %image_block.5 = (bf16[2,8,8,3072]{3,2,1,0:T(8,128)(2,1)}, f32[8,128]{1,0:T(8,128)S(1)}) custom-call(s32[2]{0:T(128)S(1)} %pad_add_fusion.place_ref.refs_0_, f32[2,8,8,1536]{3,2,1,0:T(8,128)S(1)} %get-tuple-element.69.refs_1_, f32[2,8,8,1536]{3,2,1,0:T(8,128)S(1)} %get-tuple-element.70.refs_2_, ...), custom_call_target="tpu_custom_call", output_to_operand_aliasing={{0}: (7, {})} | custom-call | flops 1650000000 | tf_op jit(solution)/shard_map/image_block/pallas_call | solution.py:722
  51.5 0.6 collective-permute-start.17
  52.2 0.9 %collective-permute-start.14 = (bf16[32,1536]{1,0:T(8,128)(2,1)S(1)}, bf16[32,1536]{1,0:T(8,128)(2,1)S(1)}, u32[]{:S(2)}, u32[]{:S(2)}) collective-permute-start(bf16[32,1536]{1,0:T(8,128)(2,1)S(1)} %add_all.5.refs_6_.refs_0_), channel_id=1, source_target_pairs={{0,8},{2,10},{4,12},{6,14},{8,0},{10,2},{12,4},{14,6},{16,24},{18,... | collective-permute-start | bytes 294920 | tf_op jit(solution)/shard_map/ppermute | solution.py:28
  53.1 2.6 %image_block.6 = (bf16[2,8,8,3072]{3,2,1,0:T(8,128)(2,1)}, f32[8,128]{1,0:T(8,128)}) custom-call(s32[2]{0:T(128)S(1)} %pad_add_fusion.place_ref.refs_0_, f32[2,8,8,1536]{3,2,1,0:T(8,128)S(1)} %get-tuple-element.69.refs_1_, f32[2,8,8,1536]{3,2,1,0:T(8,128)S(1)} %get-tuple-element.70.refs_2_, ...), custom_call_target="tpu_custom_call", output_to_operand_aliasing={{0}: (7, {})} | custom-call | flops 1650000000 | tf_op jit(solution)/shard_map/image_block/pallas_call | solution.py:722
  55.7 2.7 %image_block.7 = (bf16[2,8,8,3072]{3,2,1,0:T(8,128)(2,1)}, f32[8,128]{1,0:T(8,128)S(1)}) custom-call(s32[2]{0:T(128)S(1)} %pad_add_fusion.place_ref.refs_0_, f32[2,8,8,1536]{3,2,1,0:T(8,128)S(1)} %get-tuple-element.69.refs_1_, f32[2,8,8,1536]{3,2,1,0:T(8,128)S(1)} %get-tuple-element.70.refs_2_, ...), custom_call_target="tpu_custom_call", output_to_operand_aliasing={{0}: (7, {})} | custom-call | flops 1650000000 | tf_op jit(solution)/shard_map/image_block/pallas_call | solution.py:722
  58.5 0.1 collective-permute-start.18
  58.5 0.6 collective-permute-start.15
  59.2 0.9 %collective-permute-done.18.refs_1_ = bf16[32,3840]{1,0:T(8,128)(2,1)S(1)} collective-permute-done((bf16[32,3840]{1,0:T(8,128)(2,1)S(1)}, bf16[32,3840]{1,0:T(8,128)(2,1)S(1)}, u32[]{:S(2)}, u32[]{:S(2)}) %collective-permute-start.18) | collective-permute-done | bytes 245792 | tf_op jit(solution)/shard_map/ppermute | solution.py:28
  60.0 5.1 %head_grads_block.1 = (f32[1536,1152]{1,0:T(8,128)}, f32[2,1152]{1,0:T(2,128)}, f32[8,128]{1,0:T(8,128)S(1)}) custom-call(bf16[32,3840]{1,0:T(8,128)(2,1)S(1)} %stack_rows.9.refs_0_, bf16[32,3840]{1,0:T(8,128)(2,1)S(1)} %collective-permute-done.18.refs_1_, bf16[2,1152]{1,0:T(2,128)(2,1)S(1)} %get-tuple-element.50.here_ref.refs_0_.refs_2_, ...), custom_call_target="tpu_custom_call" | custom-call | tf_op jit(solution)/shard_map/head_grads_block/pallas_call | solution.py:777
  65.1 1.7 %collective-permute-done.15.refs_1_ = bf16[32,1536]{1,0:T(8,128)(2,1)S(1)} collective-permute-done((bf16[32,1536]{1,0:T(8,128)(2,1)S(1)}, bf16[32,1536]{1,0:T(8,128)(2,1)S(1)}, u32[]{:S(2)}, u32[]{:S(2)}) %collective-permute-start.15) | collective-permute-done | bytes 98336 | tf_op jit(solution)/shard_map/ppermute | solution.py:28
  66.8 0.1 collective-permute-start.19
  66.9 1.3 %collective-permute-done.19.other_ref = bf16[32,1536]{1,0:T(8,128)(2,1)S(1)} collective-permute-done((bf16[32,1536]{1,0:T(8,128)(2,1)S(1)}, bf16[32,1536]{1,0:T(8,128)(2,1)S(1)}, u32[]{:S(2)}, u32[]{:S(2)}) %collective-permute-start.19) | collective-permute-done | bytes 98336 | tf_op jit(solution)/shard_map/ppermute | solution.py:28
  68.2 1.3 %split_block.1 = (f32[49,1536]{1,0:T(8,128)}, f32[4,1536]{1,0:T(4,128)}) custom-call(s32[2]{0:T(128)S(1)} %pad_add_fusion.place_ref.refs_0_, bf16[32,1536]{1,0:T(8,128)(2,1)S(1)} %add_all.7.own_ref, bf16[32,1536]{1,0:T(8,128)(2,1)S(1)} %collective-permute-done.19.other_ref), custom_call_target="tpu_custom_call" | custom-call | tf_op jit(solution)/shard_map/split_block/pallas_call | solution.py:818
  (23 shorter events, 0.3 us)
Async XLA Ops:
  0.6 11.1 %collective-permute-start.2 = (bf16[49,1536]{1,0:T(8,128)(2,1)}, bf16[49,1536]{1,0:T(8,128)(2,1)S(1)}, u32[]{:S(2)}, u32[]{:S(2)}) collective-permute-start(bf16[49,1536]{1,0:T(8,128)(2,1)} %kernel_hbm.1), channel_id=1, source_target_pairs={{0,1},{1,0},{2,3},{3,2},{4,5},{5,4},{6,7},{7,6},{8,9},{9,8},{10,11... | collective-permute-start | bytes 451592 | tf_op jit(solution)/shard_map/ppermute | solution.py:28
  3.7 1.4 %collective-permute-start = (bf16[2,1152]{1,0:T(2,128)(2,1)}, bf16[2,1152]{1,0:T(2,128)(2,1)S(1)}, u32[]{:S(2)}, u32[]{:S(2)}) collective-permute-start(bf16[2,1152]{1,0:T(2,128)(2,1)} %text_hbm.1), channel_id=1, source_target_pairs={{0,2},{2,0},{4,6},{6,4},{8,10},{10,8},{12,14},{14,12},{16,18},{18,... | collective-permute-start | bytes 13832 | tf_op jit(solution)/shard_map/ppermute | solution.py:28
  5.1 3.9 %collective-permute-start.1 = (bf16[8,1536]{1,0:T(8,128)(2,1)S(1)}, bf16[8,1536]{1,0:T(8,128)(2,1)S(1)}, u32[]{:S(2)}, u32[]{:S(2)}) collective-permute-start(bf16[8,1536]{1,0:T(8,128)(2,1)S(1)} %pack_block.1), channel_id=1, source_target_pairs={{0,1},{1,0},{2,3},{3,2},{4,5},{5,4},{6,7},{7,6},{8,9},{9,8},{10,11... | collective-permute-start | bytes 73736 | tf_op jit(solution)/shard_map/ppermute | solution.py:28
  9.0 9.4 %collective-permute-start.5 = (bf16[8,1152]{1,0:T(8,128)(2,1)S(1)}, bf16[8,1152]{1,0:T(8,128)(2,1)S(1)}, u32[]{:S(2)}, u32[]{:S(2)}) collective-permute-start(bf16[8,1152]{1,0:T(8,128)(2,1)S(1)} %text_stack.1.refs_6_.low_ref), channel_id=1, source_target_pairs={{0,16},{2,18},{4,20},{6,22},{8,24},{10,26},{12,28},{14,30},{16,0},... | collective-permute-start | bytes 55304 | tf_op jit(solution)/shard_map/ppermute | solution.py:28
  16.8 3.7 %collective-permute-start.3 = (bf16[2,1536]{1,0:T(2,128)(2,1)S(1)}, bf16[2,1536]{1,0:T(2,128)(2,1)S(1)}, u32[]{:S(2)}, u32[]{:S(2)}) collective-permute-start(bf16[2,1536]{1,0:T(2,128)(2,1)S(1)} %get-tuple-element.52), channel_id=1, source_target_pairs={{0,1},{1,0},{2,3},{3,2},{4,5},{5,4},{6,7},{7,6},{8,9},{9,8},{10,11... | collective-permute-start | bytes 18440 | tf_op jit(solution)/shard_map/ppermute | solution.py:28
  18.4 4.2 %collective-permute-start.6 = (bf16[16,1152]{1,0:T(8,128)(2,1)S(1)}, bf16[16,1152]{1,0:T(8,128)(2,1)S(1)}, u32[]{:S(2)}, u32[]{:S(2)}) collective-permute-start(bf16[16,1152]{1,0:T(8,128)(2,1)S(1)} %stack_rows.5.low_ref), channel_id=1, source_target_pairs={{0,8},{2,10},{4,12},{6,14},{8,0},{10,2},{12,4},{14,6},{16,24},{18,... | collective-permute-start | bytes 110600 | tf_op jit(solution)/shard_map/ppermute | solution.py:28
  21.1 3.8 %collective-permute-start.4 = (f32[4,1152]{1,0:T(4,128)S(1)}, f32[4,1152]{1,0:T(4,128)S(1)}, u32[]{:S(2)}, u32[]{:S(2)}) collective-permute-start(f32[4,1152]{1,0:T(4,128)S(1)} %get-tuple-element.54.refs_0_.order_ref), channel_id=1, source_target_pairs={{0,1},{1,0},{2,3},{3,2},{4,5},{5,4},{6,7},{7,6},{8,9},{9,8},{10,11... | collective-permute-start | bytes 55304 | tf_op jit(solution)/shard_map/ppermute | solution.py:28
  22.6 4.4 %collective-permute-start.7 = (bf16[32,1152]{1,0:T(8,128)(2,1)S(1)}, bf16[32,1152]{1,0:T(8,128)(2,1)S(1)}, u32[]{:S(2)}, u32[]{:S(2)}) collective-permute-start(bf16[32,1152]{1,0:T(8,128)(2,1)S(1)} %stack_rows.6.refs_1_), channel_id=1, source_target_pairs={{0,4},{2,6},{4,0},{6,2},{8,12},{10,14},{12,8},{14,10},{16,20},{18,... | collective-permute-start | bytes 221192 | tf_op jit(solution)/shard_map/ppermute | solution.py:28
  28.5 3.7 %collective-permute-start.9 = (f32[2,1536]{1,0:T(2,128)S(1)}, f32[2,1536]{1,0:T(2,128)S(1)}, u32[]{:S(2)}, u32[]{:S(2)}) collective-permute-start(f32[2,1536]{1,0:T(2,128)S(1)} %get-tuple-element.59), channel_id=1, source_target_pairs={{0,1},{1,0},{2,3},{3,2},{4,5},{5,4},{6,7},{7,6},{8,9},{9,8},{10,11... | collective-permute-start | bytes 36872 | tf_op jit(solution)/shard_map/ppermute | solution.py:28
  29.1 4.8 %collective-permute-start.8 = (bf16[4,3840]{1,0:T(4,128)(2,1)S(1)}, bf16[4,3840]{1,0:T(4,128)(2,1)S(1)}, u32[]{:S(2)}, u32[]{:S(2)}) collective-permute-start(bf16[4,3840]{1,0:T(4,128)(2,1)S(1)} %get-tuple-element.57.low_ref), channel_id=1, source_target_pairs={{0,16},{2,18},{4,20},{6,22},{8,24},{10,26},{12,28},{14,30},{16,0},... | collective-permute-start | bytes 92168 | tf_op jit(solution)/shard_map/ppermute | solution.py:28
  37.3 4.1 %collective-permute-start.11 = (bf16[1,32,1536]{2,1,0:T(8,128)(2,1)S(1)}, bf16[1,32,1536]{2,1,0:T(8,128)(2,1)S(1)}, u32[]{:S(2)}, u32[]{:S(2)}) collective-permute-start(bf16[1,32,1536]{2,1,0:T(8,128)(2,1)S(1)} %get-tuple-element.74), channel_id=1, source_target_pairs={{0,2},{2,0},{4,6},{6,4},{8,10},{10,8},{12,14},{14,12},{16,18},{18,... | collective-permute-start | bytes 294920 | tf_op jit(solution)/shard_map/ppermute | solution.py:28
  40.9 6.4 %collective-permute-start.10 = (bf16[1,32,1536]{2,1,0:T(8,128)(2,1)S(1)}, bf16[1,32,1536]{2,1,0:T(8,128)(2,1)S(1)}, u32[]{:S(2)}, u32[]{:S(2)}) collective-permute-start(bf16[1,32,1536]{2,1,0:T(8,128)(2,1)S(1)} %get-tuple-element.73), channel_id=1, source_target_pairs={{0,2},{2,0},{4,6},{6,4},{8,10},{10,8},{12,14},{14,12},{16,18},{18,... | collective-permute-start | bytes 294920 | tf_op jit(solution)/shard_map/ppermute | solution.py:28
  41.5 5.8 %collective-permute-start.12 = (bf16[32,1536]{1,0:T(8,128)(2,1)S(1)}, bf16[32,1536]{1,0:T(8,128)(2,1)S(1)}, u32[]{:S(2)}, u32[]{:S(2)}) collective-permute-start(bf16[32,1536]{1,0:T(8,128)(2,1)S(1)} %chip_sums.2.order_ref.refs_6_), channel_id=1, source_target_pairs={{0,1},{1,0},{2,3},{3,2},{4,5},{5,4},{6,7},{7,6},{8,9},{9,8},{10,11... | collective-permute-start | bytes 294920 | tf_op jit(solution)/shard_map/ppermute | solution.py:28
  45.7 5.9 %collective-permute-start.16 = (bf16[8,3840]{1,0:T(8,128)(2,1)S(1)}, bf16[8,3840]{1,0:T(8,128)(2,1)S(1)}, u32[]{:S(2)}, u32[]{:S(2)}) collective-permute-start(bf16[8,3840]{1,0:T(8,128)(2,1)S(1)} %hold.1.low_ref), channel_id=1, source_target_pairs={{0,8},{2,10},{4,12},{6,14},{8,0},{10,2},{12,4},{14,6},{16,24},{18,... | collective-permute-start | bytes 184328 | tf_op jit(solution)/shard_map/ppermute | solution.py:28
  47.3 4.8 %collective-permute-start.13 = (bf16[32,1536]{1,0:T(8,128)(2,1)S(1)}, bf16[32,1536]{1,0:T(8,128)(2,1)S(1)}, u32[]{:S(2)}, u32[]{:S(2)}) collective-permute-start(bf16[32,1536]{1,0:T(8,128)(2,1)S(1)} %add_all.4.refs_6_.refs_0_), channel_id=1, source_target_pairs={{0,4},{2,6},{4,0},{6,2},{8,12},{10,14},{12,8},{14,10},{16,20},{18,... | collective-permute-start | bytes 294920 | tf_op jit(solution)/shard_map/ppermute | solution.py:28
  51.5 6.9 %collective-permute-start.17 = (bf16[16,3840]{1,0:T(8,128)(2,1)S(1)}, bf16[16,3840]{1,0:T(8,128)(2,1)S(1)}, u32[]{:S(2)}, u32[]{:S(2)}) collective-permute-start(bf16[16,3840]{1,0:T(8,128)(2,1)S(1)} %stack_rows.8.low_ref), channel_id=1, source_target_pairs={{0,4},{2,6},{4,0},{6,2},{8,12},{10,14},{12,8},{14,10},{16,20},{18,... | collective-permute-start | bytes 368648 | tf_op jit(solution)/shard_map/ppermute | solution.py:28
  52.2 6.2 %collective-permute-start.14 = (bf16[32,1536]{1,0:T(8,128)(2,1)S(1)}, bf16[32,1536]{1,0:T(8,128)(2,1)S(1)}, u32[]{:S(2)}, u32[]{:S(2)}) collective-permute-start(bf16[32,1536]{1,0:T(8,128)(2,1)S(1)} %add_all.5.refs_6_.refs_0_), channel_id=1, source_target_pairs={{0,8},{2,10},{4,12},{6,14},{8,0},{10,2},{12,4},{14,6},{16,24},{18,... | collective-permute-start | bytes 294920 | tf_op jit(solution)/shard_map/ppermute | solution.py:28
  58.5 1.6 %collective-permute-start.18 = (bf16[32,3840]{1,0:T(8,128)(2,1)S(1)}, bf16[32,3840]{1,0:T(8,128)(2,1)S(1)}, u32[]{:S(2)}, u32[]{:S(2)}) collective-permute-start(bf16[32,3840]{1,0:T(8,128)(2,1)S(1)} %stack_rows.9.refs_0_), channel_id=1, source_target_pairs={{0,2},{2,0},{4,6},{6,4},{8,10},{10,8},{12,14},{14,12},{16,18},{18,... | collective-permute-start | bytes 737288 | tf_op jit(solution)/shard_map/ppermute | solution.py:28
  58.5 8.2 %collective-permute-start.15 = (bf16[32,1536]{1,0:T(8,128)(2,1)S(1)}, bf16[32,1536]{1,0:T(8,128)(2,1)S(1)}, u32[]{:S(2)}, u32[]{:S(2)}) collective-permute-start(bf16[32,1536]{1,0:T(8,128)(2,1)S(1)} %add_all.6.order_ref.refs_3_.refs_0_), channel_id=1, source_target_pairs={{0,16},{2,18},{4,20},{6,22},{8,24},{10,26},{12,28},{14,30},{16,0},... | collective-permute-start | bytes 294920 | tf_op jit(solution)/shard_map/ppermute | solution.py:28
  66.8 1.4 %collective-permute-start.19 = (bf16[32,1536]{1,0:T(8,128)(2,1)S(1)}, bf16[32,1536]{1,0:T(8,128)(2,1)S(1)}, u32[]{:S(2)}, u32[]{:S(2)}) collective-permute-start(bf16[32,1536]{1,0:T(8,128)(2,1)S(1)} %add_all.7.own_ref), channel_id=1, source_target_pairs={{0,2},{2,0},{4,6},{6,4},{8,10},{10,8},{12,14},{14,12},{16,18},{18,... | collective-permute-start | bytes 294920 | tf_op jit(solution)/shard_map/ppermute | solution.py:28

commit v6 on v5

--- a/solution.py
+++ b/solution.py
@@ -17,6 +17,7 @@
 TERM_ROW = 56
 GAIN_ROW = TAPS
 WEIGHT_ROWS = 56
+GROUP = 4
 DOTS_COST = 3.0
 SUM_COST = 1.0
 BF = jnp.bfloat16
@@ -164,8 +165,72 @@
     return lane_block((member ^ piece) * per_piece + t % per_piece, LANES)
 
 
-def conv_tiles(tiles, base_piece, member, share, x_ref, weight_ref, mixed_ref, sum_ref):
-    images, height = x_ref.shape[:2]
+def cells_fit(images, height, width, share):
+    return images == 2 and height == 8 and width == 8 and share % (GROUP * LANES) == 0
+
+
+def conv_scratch():
+    return [
+        pltpu.VMEM((8, 64, LANES), F32),
+        pltpu.VMEM((8, 8, 8, LANES), F32),
+        pltpu.VMEM((8 * WEIGHT_ROWS, LANES), F32),
+        pltpu.VMEM((TAPS, 8, LANES), F32),
+    ]
+
+
+def load_cells(turn_ref, cell_ref):
+    for h in range(8):
+        for w in range(8):
+            cell_ref[h, w] = turn_ref[h, pl.ds(w, 8, stride=8), :]
+
+
+def conv_cells(groups, base_piece, member, share, x_ref, weight_ref, mixed_ref, sum_ref, scratch):
+    turn_ref, cell_ref, spread_ref, tap_ref = scratch
+    per_piece = share // (GROUP * LANES)
+
+    @pl.loop(0, groups)
+    def _(g):
+        piece = base_piece + g // per_piece
+        start = ((member ^ piece) * per_piece + g % per_piece) * GROUP * LANES
+        for c in range(GROUP):
+            lanes = pl.ds(pl.multiple_of(g * GROUP * LANES + c * LANES, LANES), LANES)
+            source = pl.ds(pl.multiple_of(start + c * LANES, LANES), LANES)
+            column = weight_ref[:, lanes]
+            for i in range(2):
+                slot = i * GROUP + c
+                spread_ref[slot * WEIGHT_ROWS : (slot + 1) * WEIGHT_ROWS, :] = column
+                for h in range(8):
+                    turn_ref[h, slot * 8 : slot * 8 + 8, :] = x_ref[i, h, :, source].astype(F32)
+        for tap in range(TAPS):
+            tap_ref[tap] = spread_ref[pl.ds(tap, 8, stride=WEIGHT_ROWS), :]
+        bias = spread_ref[pl.ds(GAIN_ROW, 8, stride=WEIGHT_ROWS), :]
+        load_cells(turn_ref, cell_ref)
+        for h in range(8):
+            sums = [bias] * 8
+            for a in range(max(0, REACH - h), min(KER, 8 + REACH - h)):
+                row = [cell_ref[h + a - REACH, w] for w in range(8)]
+                for b in range(KER):
+                    weight = tap_ref[a * KER + b]
+                    for w in range(max(0, REACH - b), min(8, 8 + REACH - b)):
+                        sums[w] = sums[w] + row[w + b - REACH] * weight
+            for w in range(8):
+                turn_ref[h, w * 8 : w * 8 + 8, :] = sums[w]
+        for h in range(8):
+            for i in range(2):
+                for c in range(GROUP):
+                    lanes = pl.ds(pl.multiple_of(g * GROUP * LANES + c * LANES, LANES), LANES)
+                    value = turn_ref[h, pl.ds(i * GROUP + c, 8, stride=8), :]
+                    mixed_ref[i, h, :, lanes] = value
+                    sum_ref[i, h] += value
+
+
+def conv_tiles(tiles, base_piece, member, share, x_ref, weight_ref, mixed_ref, sum_ref, scratch):
+    images, height, width = x_ref.shape[:3]
+    if cells_fit(images, height, width, share):
+        conv_cells(
+            tiles // GROUP, base_piece, member, share, x_ref, weight_ref, mixed_ref, sum_ref, scratch
+        )
+        return
 
     @pl.loop(0, tiles)
     def _(t):
@@ -292,9 +357,11 @@
     images, height, width, channels = x_here.shape
     share = weight_own.shape[1]
 
-    def kernel(place_ref, x_ref, weight_ref, mixed_ref, sum_ref):
+    def kernel(place_ref, x_ref, weight_ref, mixed_ref, sum_ref, *scratch):
         sum_ref[...] = jnp.zeros_like(sum_ref)
-        conv_tiles(share // LANES, 0, place_ref[0], share, x_ref, weight_ref, mixed_ref, sum_ref)
+        conv_tiles(
+            share // LANES, 0, place_ref[0], share, x_ref, weight_ref, mixed_ref, sum_ref, scratch
+        )
 
     return pl.pallas_call(
         kernel,
@@ -304,6 +371,7 @@
         ],
         in_specs=[SM, VM, VM],
         out_specs=[VM] * 2,
+        scratch_shapes=conv_scratch(),
         compiler_params=params(24),
         name="own_block",
     )(place, *near([x_here, weight_own]))
@@ -313,7 +381,8 @@
     kernel_refs, refs = refs[: members - 1], refs[members - 1 :]
     pack_refs, refs = refs[: members - 1], refs[members - 1 :]
     piece_refs, refs = refs[:members], refs[members:]
-    head_ref, weight_rest, mixed_rest, mean_ref, rstd_ref, hatsum_ref, hat_ref, hrstd_ref, sum_ref, pool_ref, sem = refs
+    head_ref, weight_rest, mixed_rest, mean_ref, rstd_ref, hatsum_ref, hat_ref, hrstd_ref, sum_ref, pool_ref, sem = refs[:11]
+    scratch = refs[11:]
     images, height, width, channels = x_ref.shape
     share = channels // members
     cells = height * width
@@ -327,7 +396,7 @@
     sum_ref[...] = sum_own[...]
     own_tiles = share // LANES
     rest_tiles = (members - 1) * own_tiles
-    conv_tiles(rest_tiles, 1, member, share, x_ref, weight_rest, mixed_rest, sum_ref)
+    conv_tiles(rest_tiles, 1, member, share, x_ref, weight_rest, mixed_rest, sum_ref, scratch)
     parts = [(0, own_tiles, mixed_own, weight_own), (1, rest_tiles, mixed_rest, weight_rest)]
 
     mean = jnp.sum(sum_ref[...], axis=-1, keepdims=True) * (1.0 / channels)
@@ -408,7 +477,8 @@
             pltpu.VMEM(cell, F32),
             pltpu.VMEM((images, channels), F32),
             pltpu.SemaphoreType.DMA,
-        ],
+        ]
+        + conv_scratch(),
         compiler_params=params(24),
         name="forward_block",
     )(place, *far([head_weight]), *near([x_here, *own]), order, *near([*kernels, *packs]))
@@ -606,7 +676,7 @@
 
 
 def terms_kernel(base, share, place_ref, x_ref, scaled_ref, rows_ref, mixed_ref, mean_ref, rstd_ref, dot_ref, *refs):
-    keep_ref, give_ref, flow_ref, sums_ref, taps_ref = refs
+    keep_ref, give_ref, flow_ref, sums_ref, taps_ref, turn_x, turn_flow, cell_x, cell_flow = refs
     images, height, width = x_ref.shape[:3]
     channels = mixed_ref.shape[3]
     own_tiles = share // LANES
@@ -616,47 +686,97 @@
     sums_ref[TAPS // 8 * 8 : TERM_ROW, :] = jnp.zeros((TERM_ROW - TAPS // 8 * 8, channels), F32)
     sums_ref[TERM_ROW:ROWS_PAD, :] = rows_ref[:, first : first + channels]
 
-    @pl.loop(0, channels // LANES)
-    def _(t):
-        lanes = lane_block(t, LANES)
-        wide = lane_block(t + base * own_tiles, LANES)
-        source = tile_of(base, t, member, share)
-        flows = []
-        for i in range(images):
-            factor = scaled_ref[i : i + 1, wide]
-            flow_rows = []
-            for h in range(height):
-                centered = mixed_ref[i, h, :, lanes] - mean_ref[i, h]
-                flow = rstd_ref[i, h] * (factor - centered * dot_ref[i, h])
-                flow_ref[i, h, :, lanes] = flow
-                flow_rows.append(flow)
-            flows.append(flow_rows)
-        bias = flows[0][0]
-        for i in range(images):
-            for h in range(height):
-                if i or h:
-                    bias = bias + flows[i][h]
-        taps_ref[TAPS * width : TAPS * width + width, :] = bias
-        for b in range(KER):
-            totals = [None] * KER
+    if cells_fit(images, height, width, share):
+        per_piece = share // (GROUP * LANES)
+
+        @pl.loop(0, channels // (GROUP * LANES))
+        def _(g):
+            piece = base + g // per_piece
+            start = ((member ^ piece) * per_piece + g % per_piece) * GROUP * LANES
+            for c in range(GROUP):
+                here = g * GROUP * LANES + c * LANES
+                lanes = pl.ds(pl.multiple_of(here, LANES), LANES)
+                wide = pl.ds(pl.multiple_of(first + here, LANES), LANES)
+                source = pl.ds(pl.multiple_of(start + c * LANES, LANES), LANES)
+                for i in range(images):
+                    slot = (i * GROUP + c) * width
+                    factor = scaled_ref[i : i + 1, wide]
+                    for h in range(height):
+                        centered = mixed_ref[i, h, :, lanes] - mean_ref[i, h]
+                        flow = rstd_ref[i, h] * (factor - centered * dot_ref[i, h])
+                        flow_ref[i, h, :, lanes] = flow
+                        turn_flow[h, slot : slot + width, :] = flow
+                        turn_x[h, slot : slot + width, :] = x_ref[i, h, :, source].astype(F32)
+            load_cells(turn_flow, cell_flow)
+            load_cells(turn_x, cell_x)
+            bias = None
+            for a in range(KER):
+                totals = [None] * KER
+                for h in range(max(0, REACH - a), min(height, height + REACH - a)):
+                    flows = [cell_flow[h, w] for w in range(width)]
+                    row = [cell_x[h + a - REACH, w] for w in range(width)]
+                    for b in range(KER):
+                        for w in range(max(0, REACH - b), min(width, width + REACH - b)):
+                            term = flows[w] * row[w + b - REACH]
+                            totals[b] = term if totals[b] is None else totals[b] + term
+                    if a == REACH:
+                        for w in range(width):
+                            bias = flows[w] if bias is None else bias + flows[w]
+                for b in range(KER):
+                    tap = a * KER + b
+                    taps_ref[tap * 8 : tap * 8 + 8, :] = totals[b]
+            taps_ref[TAPS * 8 : TAPS * 8 + 8, :] = bias
+            for c in range(GROUP):
+                lanes = pl.ds(pl.multiple_of(g * GROUP * LANES + c * LANES, LANES), LANES)
+                total = (
+                    taps_ref[pl.ds(c, TAPS + 1, stride=8), :]
+                    + taps_ref[pl.ds(GROUP + c, TAPS + 1, stride=8), :]
+                )
+                sums_ref[0:TAPS, lanes] = total[0:TAPS]
+                sums_ref[TERM_ROW : TERM_ROW + 1, lanes] = total[TAPS : TAPS + 1]
+
+    else:
+        @pl.loop(0, channels // LANES)
+        def _(t):
+            lanes = lane_block(t, LANES)
+            wide = lane_block(t + base * own_tiles, LANES)
+            source = tile_of(base, t, member, share)
+            flows = []
             for i in range(images):
-                moved = [
-                    shift_cols(x_ref[i, h, :, source].astype(F32), b - REACH)
-                    for h in range(height)
-                ]
+                factor = scaled_ref[i : i + 1, wide]
+                flow_rows = []
+                for h in range(height):
+                    centered = mixed_ref[i, h, :, lanes] - mean_ref[i, h]
+                    flow = rstd_ref[i, h] * (factor - centered * dot_ref[i, h])
+                    flow_ref[i, h, :, lanes] = flow
+                    flow_rows.append(flow)
+                flows.append(flow_rows)
+            bias = flows[0][0]
+            for i in range(images):
+                for h in range(height):
+                    if i or h:
+                        bias = bias + flows[i][h]
+            taps_ref[TAPS * width : TAPS * width + width, :] = bias
+            for b in range(KER):
+                totals = [None] * KER
+                for i in range(images):
+                    moved = [
+                        shift_cols(x_ref[i, h, :, source].astype(F32), b - REACH)
+                        for h in range(height)
+                    ]
+                    for a in range(KER):
+                        for h in range(max(0, REACH - a), min(height, height + REACH - a)):
+                            term = flows[i][h] * moved[h + a - REACH]
+                            totals[a] = term if totals[a] is None else totals[a] + term
                 for a in range(KER):
-                    for h in range(max(0, REACH - a), min(height, height + REACH - a)):
-                        term = flows[i][h] * moved[h + a - REACH]
-                        totals[a] = term if totals[a] is None else totals[a] + term
-            for a in range(KER):
-                tap = a * KER + b
-                taps_ref[tap * width : tap * width + width, :] = totals[a]
-        rows = TAPS + 1
-        total = taps_ref[pl.ds(0, rows, stride=width), :]
-        for s in range(1, width):
-            total = total + taps_ref[pl.ds(s, rows, stride=width), :]
-        sums_ref[0:TAPS, lanes] = total[0:TAPS]
-        sums_ref[TERM_ROW : TERM_ROW + 1, lanes] = total[TAPS : TAPS + 1]
+                    tap = a * KER + b
+                    taps_ref[tap * width : tap * width + width, :] = totals[a]
+            rows = TAPS + 1
+            total = taps_ref[pl.ds(0, rows, stride=width), :]
+            for s in range(1, width):
+                total = total + taps_ref[pl.ds(s, rows, stride=width), :]
+            sums_ref[0:TAPS, lanes] = total[0:TAPS]
+            sums_ref[TERM_ROW : TERM_ROW + 1, lanes] = total[TAPS : TAPS + 1]
 
     for m in range(channels // share):
         lanes = slice(m * share, (m + 1) * share)
@@ -676,6 +796,10 @@
         scratch_shapes=[
             pltpu.VMEM((ROWS_PAD, channels), F32),
             pltpu.VMEM(((TAPS + 1) * width, LANES), F32),
+            pltpu.VMEM((8, 64, LANES), F32),
+            pltpu.VMEM((8, 64, LANES), F32),
+            pltpu.VMEM((8, 8, 8, LANES), F32),
+            pltpu.VMEM((8, 8, 8, LANES), F32),
         ],
         compiler_params=params(24),
         name="terms_block",

time: 69.6 us -> 67.3 us (0.967)
  Pallas kernels: 36.6 us -> 33.6 us
  waiting for transfers between devices: 11.4 us -> 12.1 us
    pallas_call x2, Pallas kernels: 6.9 us -> 5.39 us  [terms_block(): pl.pallas_call(lambda place_ref, order_ref, *refs: terms_kernel(base, sha...]
    pallas_call x1, Pallas kernels: 3.31 us -> 2.55 us  [own_block(): pl.pallas_call(kernel, out_shape=[SHAPE((images, height, width, share), F...]
    ppermute x20, waiting for transfers between devices: 11.4 us -> 12.1 us  [swap(): lax.ppermute(value, axis, [(source, source ^ mask) for source in range(co...]
    pallas_call x1, Pallas kernels: 5.08 us -> 4.36 us  [forward_block(): pl.pallas_call(lambda *refs: forward_kernel(members, *refs), out_shape=ou...]
  transfers between devices with their start and end apart: 20 -> 20, of which waited for: 10 -> 10; matrix products, arithmetic and copies ran while one was open for 0% -> 0% of each run, Pallas kernels for 44% -> 42%
where the time goes in v6:
time: 67.3 us; the launch traced here: 67.2 us
  Pallas kernels  33.6 us (50%)
  starting transfers between devices  20.6 us (31%)
  waiting for transfers between devices  12.1 us (18%)
  between operations  0.78 us (1%)
    ppermute x20, starting transfers between devices, swap(): lax.ppermute(value, axis, [(source, source ^ mask) for source in range(co...  20.6 us
    ppermute x20, waiting for transfers between devices, swap(): lax.ppermute(value, axis, [(source, source ^ mask) for source in range(co...  12.1 us
    pallas_call x4, Pallas kernels, image_block(): pl.pallas_call(kernel, grid_spec=pltpu.PrefetchScalarGridSpec(num_scalar_...  10.5 us
    pallas_call x2, Pallas kernels, terms_block(): pl.pallas_call(lambda place_ref, order_ref, *refs: terms_kernel(base, sha...  5.39 us
    pallas_call x1, Pallas kernels, head_grads_block(): pl.pallas_call(lambda *refs: head_grads_kernel(block, *refs), grid=(share...  5.05 us
    pallas_call x1, Pallas kernels, forward_block(): pl.pallas_call(lambda *refs: forward_kernel(members, *refs), out_shape=ou...  4.36 us
    pallas_call x1, Pallas kernels, own_block(): pl.pallas_call(kernel, out_shape=[SHAPE((images, height, width, share), F...  2.55 us
    pallas_call x1, Pallas kernels, loss_block(): pl.pallas_call(lambda *refs: loss_kernel(members, *refs), out_shape=[SHAP...  1.47 us
  transfers between devices with their start and end apart: 20, of which 10 were waited for; matrix products, arithmetic and copies ran while one was open for 0% of the time, Pallas kernels for 42%

profile of v6, /device:TPU:0, one launch (start us, length us, event | category | flops | bytes accessed | tf_op | source)
XLA Modules:
  0.0 67.2 jit_solution(10265150332064022766)
XLA Ops:
  0.6 3.0 %collective-permute-start.2 = (bf16[49,1536]{1,0:T(8,128)(2,1)}, bf16[49,1536]{1,0:T(8,128)(2,1)S(1)}, u32[]{:S(2)}, u32[]{:S(2)}) collective-permute-start(bf16[49,1536]{1,0:T(8,128)(2,1)} %kernel_hbm.1), channel_id=1, source_target_pairs={{0,1},{1,0},{2,3},{3,2},{4,5},{5,4},{6,7},{7,6},{8,9},{9,8},{10,11... | collective-permute-start | bytes 451592 | tf_op jit(solution)/shard_map/ppermute | solution.py:29
  3.7 0.0 collective-permute-start
  3.7 1.3 %load_block.1 = (bf16[2,8,8,3072]{3,2,1,0:T(8,128)(2,1)S(1)}, f32[56,1536]{1,0:T(8,128)S(1)}, bf16[2,1152]{1,0:T(2,128)(2,1)S(1)}) custom-call(bf16[2,8,8,3072]{3,2,1,0:T(8,128)(2,1)} %x_hbm.1, bf16[49,1536]{1,0:T(8,128)(2,1)} %kernel_hbm.1, bf16[4,1536]{1,0:T(4,128)(2,1)} %term_hbm.1, bf16[2,1152]{1,0:T(2,128)(2,1)} %text_hbm.1), custom_call_target="tpu_custom_call" | custom-call | tf_op jit(solution)/shard_map/load_block/pallas_call | solution.py:278
  5.0 0.1 collective-permute-done.core_ref.refs_1_
  5.1 0.1 collective-permute-start.1
  5.2 0.1 pad_add_fusion.place_ref.refs_0_
  5.3 2.6 %own_block.1 = (f32[2,8,8,1536]{3,2,1,0:T(8,128)S(1)}, f32[2,8,8,128]{3,2,1,0:T(8,128)S(1)}) custom-call(s32[2]{0:T(128)S(1)} %pad_add_fusion.place_ref.refs_0_, bf16[2,8,8,3072]{3,2,1,0:T(8,128)(2,1)S(1)} %get-tuple-element.46.x_ref.refs_2_.refs_0_, f32[56,1536]{1,0:T(8,128)S(1)} %get-tuple-element.47.weight_ref.refs_5_.refs_2_.refs_3_), custom_call_target="tpu_custom_call" | custom-call | tf_op jit(solution)/shard_map/own_block/pallas_call | solution.py:366
  7.8 1.1 %collective-permute-done.1.refs_2_.refs_8_ = bf16[8,1536]{1,0:T(8,128)(2,1)S(1)} collective-permute-done((bf16[8,1536]{1,0:T(8,128)(2,1)S(1)}, bf16[8,1536]{1,0:T(8,128)(2,1)S(1)}, u32[]{:S(2)}, u32[]{:S(2)}) %collective-permute-start.1) | collective-permute-done | bytes 24608 | tf_op jit(solution)/shard_map/ppermute | solution.py:29
  9.0 2.7 %collective-permute-start.5 = (bf16[8,1152]{1,0:T(8,128)(2,1)S(1)}, bf16[8,1152]{1,0:T(8,128)(2,1)S(1)}, u32[]{:S(2)}, u32[]{:S(2)}) collective-permute-start(bf16[8,1152]{1,0:T(8,128)(2,1)S(1)} %text_stack.1.refs_6_.low_ref), channel_id=1, source_target_pairs={{0,16},{2,18},{4,20},{6,22},{8,24},{10,26},{12,28},{14,30},{16,0},... | collective-permute-start | bytes 55304 | tf_op jit(solution)/shard_map/ppermute | solution.py:29
  11.7 4.4 %forward_block.1 = (bf16[2,1536]{1,0:T(2,128)(2,1)S(1)}, bf16[2,1536]{1,0:T(2,128)(2,1)S(1)}, bf16[1536,1152]{1,0:T(8,128)(2,1)S(1)}, f32[56,1536]{1,0:T(8,128)S...) custom-call(s32[2]{0:T(128)S(1)} %pad_add_fusion.place_ref.refs_0_, ...), custom_call_target="tpu_custom_call" | custom-call | tf_op jit(solution)/shard_map/forward_block/pallas_call | solution.py:471
  16.0 1.6 %collective-permute-start.3 = (bf16[2,1536]{1,0:T(2,128)(2,1)S(1)}, bf16[2,1536]{1,0:T(2,128)(2,1)S(1)}, u32[]{:S(2)}, u32[]{:S(2)}) collective-permute-start(bf16[2,1536]{1,0:T(2,128)(2,1)S(1)} %get-tuple-element.52), channel_id=1, source_target_pairs={{0,1},{1,0},{2,3},{3,2},{4,5},{5,4},{6,7},{7,6},{8,9},{9,8},{10,11... | collective-permute-start | bytes 18440 | tf_op jit(solution)/shard_map/ppermute | solution.py:29
  17.6 1.6 %collective-permute-start.6 = (bf16[16,1152]{1,0:T(8,128)(2,1)S(1)}, bf16[16,1152]{1,0:T(8,128)(2,1)S(1)}, u32[]{:S(2)}, u32[]{:S(2)}) collective-permute-start(bf16[16,1152]{1,0:T(8,128)(2,1)S(1)} %stack_rows.5.low_ref), channel_id=1, source_target_pairs={{0,8},{2,10},{4,12},{6,14},{8,0},{10,2},{12,4},{14,6},{16,24},{18,... | collective-permute-start | bytes 110600 | tf_op jit(solution)/shard_map/ppermute | solution.py:29
  19.2 0.5 collective-permute-done.3.refs_1_
  19.7 0.6 head_project.1
  20.3 1.6 %collective-permute-start.4 = (f32[4,1152]{1,0:T(4,128)S(1)}, f32[4,1152]{1,0:T(4,128)S(1)}, u32[]{:S(2)}, u32[]{:S(2)}) collective-permute-start(f32[4,1152]{1,0:T(4,128)S(1)} %get-tuple-element.54.refs_0_.order_ref), channel_id=1, source_target_pairs={{0,1},{1,0},{2,3},{3,2},{4,5},{5,4},{6,7},{7,6},{8,9},{9,8},{10,11... | collective-permute-start | bytes 55304 | tf_op jit(solution)/shard_map/ppermute | solution.py:29
  21.9 1.6 %collective-permute-start.7 = (bf16[32,1152]{1,0:T(8,128)(2,1)S(1)}, bf16[32,1152]{1,0:T(8,128)(2,1)S(1)}, u32[]{:S(2)}, u32[]{:S(2)}) collective-permute-start(bf16[32,1152]{1,0:T(8,128)(2,1)S(1)} %stack_rows.6.refs_1_), channel_id=1, source_target_pairs={{0,4},{2,6},{4,0},{6,2},{8,12},{10,14},{12,8},{14,10},{16,20},{18,... | collective-permute-start | bytes 221192 | tf_op jit(solution)/shard_map/ppermute | solution.py:29
  23.4 0.7 collective-permute-done.4.refs_1_
  24.1 2.2 %collective-permute-done.7.refs_2_ = bf16[32,1152]{1,0:T(8,128)(2,1)S(1)} collective-permute-done((bf16[32,1152]{1,0:T(8,128)(2,1)S(1)}, bf16[32,1152]{1,0:T(8,128)(2,1)S(1)}, u32[]{:S(2)}, u32[]{:S(2)}) %collective-permute-start.7) | collective-permute-done | bytes 73760 | tf_op jit(solution)/shard_map/ppermute | solution.py:29
  26.3 1.5 %loss_block.1 = (bf16[4,3840]{1,0:T(4,128)(2,1)S(1)}, f32[2,1536]{1,0:T(2,128)S(1)}, f32[2,1536]{1,0:T(2,128)S(1)}) custom-call(f32[4,1152]{1,0:T(4,128)S(1)} %embed_sum.1.refs_0_, bf16[32,1152]{1,0:T(8,128)(2,1)S(1)} %stack_rows.6.refs_1_, bf16[32,1152]{1,0:T(8,128)(2,1)S(1)} %collective-permute-done.7.refs_2_, ...), custom_call_target="tpu_custom_call" | custom-call | tf_op jit(solution)/shard_map/loss_block/pallas_call | solution.py:581
  27.8 0.5 collective-permute-start.9
  28.3 0.3 collective-permute-start.8
  28.6 2.9 %collective-permute-done.9.refs_1_ = f32[2,1536]{1,0:T(2,128)S(1)} collective-permute-done((f32[2,1536]{1,0:T(2,128)S(1)}, f32[2,1536]{1,0:T(2,128)S(1)}, u32[]{:S(2)}, u32[]{:S(2)}) %collective-permute-start.9) | collective-permute-done | bytes 12320 | tf_op jit(solution)/shard_map/ppermute | solution.py:29
  31.5 0.3 pool_grad_block.1
  31.7 0.6 dots_block.1.order_ref.refs_6_
  32.3 0.8 %collective-permute-done.8.high_ref = bf16[4,3840]{1,0:T(4,128)(2,1)S(1)} collective-permute-done((bf16[4,3840]{1,0:T(4,128)(2,1)S(1)}, bf16[4,3840]{1,0:T(4,128)(2,1)S(1)}, u32[]{:S(2)}, u32[]{:S(2)}) %collective-permute-start.8) | collective-permute-done | bytes 30752 | tf_op jit(solution)/shard_map/ppermute | solution.py:29
  33.1 2.7 %terms_block.2 = (bf16[1,32,1536]{2,1,0:T(8,128)(2,1)S(1)}, bf16[1,32,1536]{2,1,0:T(8,128)(2,1)S(1)}, f32[2,8,8,1536]{3,2,1,0:T(8,128)S(1)}) custom-call(s32[2]{0:T(128)S(1)} %pad_add_fusion.place_ref.refs_0_, bf16[8,3840]{1,0:T(8,128)(2,1)S(1)} %stack_rows.7.order_ref.value_ref, bf16[2,8,8,3072]{3,2,1,0:T(8,128)(2,1)S(1)} %get-tuple-element.46.x_ref.refs_2_.refs_0_, ...), custom_call_target="tpu_custom_call" | custom-call | tf_op jit(solution)/shard_map/terms_block/pallas_call | solution.py:791
  35.8 0.1 collective-permute-start.11
  35.9 2.7 %terms_block.3 = (bf16[1,32,1536]{2,1,0:T(8,128)(2,1)S(1)}, bf16[1,32,1536]{2,1,0:T(8,128)(2,1)S(1)}, f32[2,8,8,1536]{3,2,1,0:T(8,128)S(1)}) custom-call(s32[2]{0:T(128)S(1)} %pad_add_fusion.place_ref.refs_0_, bf16[1,32,1536]{2,1,0:T(8,128)(2,1)S(1)} %get-tuple-element.68.order_ref.keep_ref, ...), custom_call_target="tpu_custom_call" | custom-call | tf_op jit(solution)/shard_map/terms_block/pallas_call | solution.py:791
  38.6 0.6 collective-permute-start.10
  39.2 0.0 collective-permute-done.11.give_ref
  39.2 1.6 %collective-permute-start.12 = (bf16[32,1536]{1,0:T(8,128)(2,1)S(1)}, bf16[32,1536]{1,0:T(8,128)(2,1)S(1)}, u32[]{:S(2)}, u32[]{:S(2)}) collective-permute-start(bf16[32,1536]{1,0:T(8,128)(2,1)S(1)} %chip_sums.2.order_ref.refs_6_), channel_id=1, source_target_pairs={{0,1},{1,0},{2,3},{3,2},{4,5},{5,4},{6,7},{7,6},{8,9},{9,8},{10,11... | collective-permute-start | bytes 294920 | tf_op jit(solution)/shard_map/ppermute | solution.py:29
  40.8 2.6 %image_block.4 = (bf16[2,8,8,3072]{3,2,1,0:T(8,128)(2,1)}, f32[8,128]{1,0:T(8,128)S(1)}) custom-call(s32[2]{0:T(128)S(1)} %pad_add_fusion.place_ref.refs_0_, f32[2,8,8,1536]{3,2,1,0:T(8,128)S(1)} %get-tuple-element.69.refs_1_, f32[2,8,8,1536]{3,2,1,0:T(8,128)S(1)} %get-tuple-element.70.refs_2_, ...), custom_call_target="tpu_custom_call" | custom-call | flops 1650000000 | tf_op jit(solution)/shard_map/image_block/pallas_call | solution.py:846
  43.4 1.6 %collective-permute-start.16 = (bf16[8,3840]{1,0:T(8,128)(2,1)S(1)}, bf16[8,3840]{1,0:T(8,128)(2,1)S(1)}, u32[]{:S(2)}, u32[]{:S(2)}) collective-permute-start(bf16[8,3840]{1,0:T(8,128)(2,1)S(1)} %hold.1.low_ref), channel_id=1, source_target_pairs={{0,8},{2,10},{4,12},{6,14},{8,0},{10,2},{12,4},{14,6},{16,24},{18,... | collective-permute-start | bytes 184328 | tf_op jit(solution)/shard_map/ppermute | solution.py:29
  45.0 0.0 collective-permute-done.10.give_ref
  45.0 1.6 %collective-permute-start.13 = (bf16[32,1536]{1,0:T(8,128)(2,1)S(1)}, bf16[32,1536]{1,0:T(8,128)(2,1)S(1)}, u32[]{:S(2)}, u32[]{:S(2)}) collective-permute-start(bf16[32,1536]{1,0:T(8,128)(2,1)S(1)} %add_all.4.refs_6_.refs_0_), channel_id=1, source_target_pairs={{0,4},{2,6},{4,0},{6,2},{8,12},{10,14},{12,8},{14,10},{16,20},{18,... | collective-permute-start | bytes 294920 | tf_op jit(solution)/shard_map/ppermute | solution.py:29
  46.6 2.7 %image_block.5 = (bf16[2,8,8,3072]{3,2,1,0:T(8,128)(2,1)}, f32[8,128]{1,0:T(8,128)S(1)}) custom-call(s32[2]{0:T(128)S(1)} %pad_add_fusion.place_ref.refs_0_, f32[2,8,8,1536]{3,2,1,0:T(8,128)S(1)} %get-tuple-element.69.refs_1_, f32[2,8,8,1536]{3,2,1,0:T(8,128)S(1)} %get-tuple-element.70.refs_2_, ...), custom_call_target="tpu_custom_call", output_to_operand_aliasing={{0}: (7, {})} | custom-call | flops 1650000000 | tf_op jit(solution)/shard_map/image_block/pallas_call | solution.py:846
  49.3 0.6 collective-permute-start.17
  49.9 0.9 %collective-permute-start.14 = (bf16[32,1536]{1,0:T(8,128)(2,1)S(1)}, bf16[32,1536]{1,0:T(8,128)(2,1)S(1)}, u32[]{:S(2)}, u32[]{:S(2)}) collective-permute-start(bf16[32,1536]{1,0:T(8,128)(2,1)S(1)} %add_all.5.refs_6_.refs_0_), channel_id=1, source_target_pairs={{0,8},{2,10},{4,12},{6,14},{8,0},{10,2},{12,4},{14,6},{16,24},{18,... | collective-permute-start | bytes 294920 | tf_op jit(solution)/shard_map/ppermute | solution.py:29
  50.8 2.6 %image_block.6 = (bf16[2,8,8,3072]{3,2,1,0:T(8,128)(2,1)}, f32[8,128]{1,0:T(8,128)}) custom-call(s32[2]{0:T(128)S(1)} %pad_add_fusion.place_ref.refs_0_, f32[2,8,8,1536]{3,2,1,0:T(8,128)S(1)} %get-tuple-element.69.refs_1_, f32[2,8,8,1536]{3,2,1,0:T(8,128)S(1)} %get-tuple-element.70.refs_2_, ...), custom_call_target="tpu_custom_call", output_to_operand_aliasing={{0}: (7, {})} | custom-call | flops 1650000000 | tf_op jit(solution)/shard_map/image_block/pallas_call | solution.py:846
  53.5 2.7 %image_block.7 = (bf16[2,8,8,3072]{3,2,1,0:T(8,128)(2,1)}, f32[8,128]{1,0:T(8,128)S(1)}) custom-call(s32[2]{0:T(128)S(1)} %pad_add_fusion.place_ref.refs_0_, f32[2,8,8,1536]{3,2,1,0:T(8,128)S(1)} %get-tuple-element.69.refs_1_, f32[2,8,8,1536]{3,2,1,0:T(8,128)S(1)} %get-tuple-element.70.refs_2_, ...), custom_call_target="tpu_custom_call", output_to_operand_aliasing={{0}: (7, {})} | custom-call | flops 1650000000 | tf_op jit(solution)/shard_map/image_block/pallas_call | solution.py:846
  56.2 0.1 collective-permute-start.18
  56.3 0.6 collective-permute-start.15
  56.9 0.9 %collective-permute-done.18.refs_1_ = bf16[32,3840]{1,0:T(8,128)(2,1)S(1)} collective-permute-done((bf16[32,3840]{1,0:T(8,128)(2,1)S(1)}, bf16[32,3840]{1,0:T(8,128)(2,1)S(1)}, u32[]{:S(2)}, u32[]{:S(2)}) %collective-permute-start.18) | collective-permute-done | bytes 245792 | tf_op jit(solution)/shard_map/ppermute | solution.py:29
  57.8 5.1 %head_grads_block.1 = (f32[1536,1152]{1,0:T(8,128)}, f32[2,1152]{1,0:T(2,128)}, f32[8,128]{1,0:T(8,128)S(1)}) custom-call(bf16[32,3840]{1,0:T(8,128)(2,1)S(1)} %stack_rows.9.refs_0_, bf16[32,3840]{1,0:T(8,128)(2,1)S(1)} %collective-permute-done.18.refs_1_, bf16[2,1152]{1,0:T(2,128)(2,1)S(1)} %get-tuple-element.50.here_ref.refs_0_.refs_2_, ...), custom_call_target="tpu_custom_call" | custom-call | tf_op jit(solution)/shard_map/head_grads_block/pallas_call | solution.py:901
  62.8 1.7 %collective-permute-done.15.refs_1_ = bf16[32,1536]{1,0:T(8,128)(2,1)S(1)} collective-permute-done((bf16[32,1536]{1,0:T(8,128)(2,1)S(1)}, bf16[32,1536]{1,0:T(8,128)(2,1)S(1)}, u32[]{:S(2)}, u32[]{:S(2)}) %collective-permute-start.15) | collective-permute-done | bytes 98336 | tf_op jit(solution)/shard_map/ppermute | solution.py:29
  64.5 0.1 collective-permute-start.19
  64.6 1.3 %collective-permute-done.19.other_ref = bf16[32,1536]{1,0:T(8,128)(2,1)S(1)} collective-permute-done((bf16[32,1536]{1,0:T(8,128)(2,1)S(1)}, bf16[32,1536]{1,0:T(8,128)(2,1)S(1)}, u32[]{:S(2)}, u32[]{:S(2)}) %collective-permute-start.19) | collective-permute-done | bytes 98336 | tf_op jit(solution)/shard_map/ppermute | solution.py:29
  65.9 1.3 %split_block.1 = (f32[49,1536]{1,0:T(8,128)}, f32[4,1536]{1,0:T(4,128)}) custom-call(s32[2]{0:T(128)S(1)} %pad_add_fusion.place_ref.refs_0_, bf16[32,1536]{1,0:T(8,128)(2,1)S(1)} %add_all.7.own_ref, bf16[32,1536]{1,0:T(8,128)(2,1)S(1)} %collective-permute-done.19.other_ref), custom_call_target="tpu_custom_call" | custom-call | tf_op jit(solution)/shard_map/split_block/pallas_call | solution.py:942
  (23 shorter events, 0.3 us)
Async XLA Ops:
  0.6 11.0 %collective-permute-start.2 = (bf16[49,1536]{1,0:T(8,128)(2,1)}, bf16[49,1536]{1,0:T(8,128)(2,1)S(1)}, u32[]{:S(2)}, u32[]{:S(2)}) collective-permute-start(bf16[49,1536]{1,0:T(8,128)(2,1)} %kernel_hbm.1), channel_id=1, source_target_pairs={{0,1},{1,0},{2,3},{3,2},{4,5},{5,4},{6,7},{7,6},{8,9},{9,8},{10,11... | collective-permute-start | bytes 451592 | tf_op jit(solution)/shard_map/ppermute | solution.py:29
  3.7 1.4 %collective-permute-start = (bf16[2,1152]{1,0:T(2,128)(2,1)}, bf16[2,1152]{1,0:T(2,128)(2,1)S(1)}, u32[]{:S(2)}, u32[]{:S(2)}) collective-permute-start(bf16[2,1152]{1,0:T(2,128)(2,1)} %text_hbm.1), channel_id=1, source_target_pairs={{0,2},{2,0},{4,6},{6,4},{8,10},{10,8},{12,14},{14,12},{16,18},{18,... | collective-permute-start | bytes 13832 | tf_op jit(solution)/shard_map/ppermute | solution.py:29
  5.1 3.9 %collective-permute-start.1 = (bf16[8,1536]{1,0:T(8,128)(2,1)S(1)}, bf16[8,1536]{1,0:T(8,128)(2,1)S(1)}, u32[]{:S(2)}, u32[]{:S(2)}) collective-permute-start(bf16[8,1536]{1,0:T(8,128)(2,1)S(1)} %pack_block.1), channel_id=1, source_target_pairs={{0,1},{1,0},{2,3},{3,2},{4,5},{5,4},{6,7},{7,6},{8,9},{9,8},{10,11... | collective-permute-start | bytes 73736 | tf_op jit(solution)/shard_map/ppermute | solution.py:29
  9.0 8.7 %collective-permute-start.5 = (bf16[8,1152]{1,0:T(8,128)(2,1)S(1)}, bf16[8,1152]{1,0:T(8,128)(2,1)S(1)}, u32[]{:S(2)}, u32[]{:S(2)}) collective-permute-start(bf16[8,1152]{1,0:T(8,128)(2,1)S(1)} %text_stack.1.refs_6_.low_ref), channel_id=1, source_target_pairs={{0,16},{2,18},{4,20},{6,22},{8,24},{10,26},{12,28},{14,30},{16,0},... | collective-permute-start | bytes 55304 | tf_op jit(solution)/shard_map/ppermute | solution.py:29
  16.0 3.7 %collective-permute-start.3 = (bf16[2,1536]{1,0:T(2,128)(2,1)S(1)}, bf16[2,1536]{1,0:T(2,128)(2,1)S(1)}, u32[]{:S(2)}, u32[]{:S(2)}) collective-permute-start(bf16[2,1536]{1,0:T(2,128)(2,1)S(1)} %get-tuple-element.52), channel_id=1, source_target_pairs={{0,1},{1,0},{2,3},{3,2},{4,5},{5,4},{6,7},{7,6},{8,9},{9,8},{10,11... | collective-permute-start | bytes 18440 | tf_op jit(solution)/shard_map/ppermute | solution.py:29
  17.6 4.2 %collective-permute-start.6 = (bf16[16,1152]{1,0:T(8,128)(2,1)S(1)}, bf16[16,1152]{1,0:T(8,128)(2,1)S(1)}, u32[]{:S(2)}, u32[]{:S(2)}) collective-permute-start(bf16[16,1152]{1,0:T(8,128)(2,1)S(1)} %stack_rows.5.low_ref), channel_id=1, source_target_pairs={{0,8},{2,10},{4,12},{6,14},{8,0},{10,2},{12,4},{14,6},{16,24},{18,... | collective-permute-start | bytes 110600 | tf_op jit(solution)/shard_map/ppermute | solution.py:29
  20.3 3.8 %collective-permute-start.4 = (f32[4,1152]{1,0:T(4,128)S(1)}, f32[4,1152]{1,0:T(4,128)S(1)}, u32[]{:S(2)}, u32[]{:S(2)}) collective-permute-start(f32[4,1152]{1,0:T(4,128)S(1)} %get-tuple-element.54.refs_0_.order_ref), channel_id=1, source_target_pairs={{0,1},{1,0},{2,3},{3,2},{4,5},{5,4},{6,7},{7,6},{8,9},{9,8},{10,11... | collective-permute-start | bytes 55304 | tf_op jit(solution)/shard_map/ppermute | solution.py:29
  21.9 4.4 %collective-permute-start.7 = (bf16[32,1152]{1,0:T(8,128)(2,1)S(1)}, bf16[32,1152]{1,0:T(8,128)(2,1)S(1)}, u32[]{:S(2)}, u32[]{:S(2)}) collective-permute-start(bf16[32,1152]{1,0:T(8,128)(2,1)S(1)} %stack_rows.6.refs_1_), channel_id=1, source_target_pairs={{0,4},{2,6},{4,0},{6,2},{8,12},{10,14},{12,8},{14,10},{16,20},{18,... | collective-permute-start | bytes 221192 | tf_op jit(solution)/shard_map/ppermute | solution.py:29
  27.8 3.7 %collective-permute-start.9 = (f32[2,1536]{1,0:T(2,128)S(1)}, f32[2,1536]{1,0:T(2,128)S(1)}, u32[]{:S(2)}, u32[]{:S(2)}) collective-permute-start(f32[2,1536]{1,0:T(2,128)S(1)} %get-tuple-element.59), channel_id=1, source_target_pairs={{0,1},{1,0},{2,3},{3,2},{4,5},{5,4},{6,7},{7,6},{8,9},{9,8},{10,11... | collective-permute-start | bytes 36872 | tf_op jit(solution)/shard_map/ppermute | solution.py:29
  28.3 4.8 %collective-permute-start.8 = (bf16[4,3840]{1,0:T(4,128)(2,1)S(1)}, bf16[4,3840]{1,0:T(4,128)(2,1)S(1)}, u32[]{:S(2)}, u32[]{:S(2)}) collective-permute-start(bf16[4,3840]{1,0:T(4,128)(2,1)S(1)} %get-tuple-element.57.low_ref), channel_id=1, source_target_pairs={{0,16},{2,18},{4,20},{6,22},{8,24},{10,26},{12,28},{14,30},{16,0},... | collective-permute-start | bytes 92168 | tf_op jit(solution)/shard_map/ppermute | solution.py:29
  35.8 3.3 %collective-permute-start.11 = (bf16[1,32,1536]{2,1,0:T(8,128)(2,1)S(1)}, bf16[1,32,1536]{2,1,0:T(8,128)(2,1)S(1)}, u32[]{:S(2)}, u32[]{:S(2)}) collective-permute-start(bf16[1,32,1536]{2,1,0:T(8,128)(2,1)S(1)} %get-tuple-element.74), channel_id=1, source_target_pairs={{0,2},{2,0},{4,6},{6,4},{8,10},{10,8},{12,14},{14,12},{16,18},{18,... | collective-permute-start | bytes 294920 | tf_op jit(solution)/shard_map/ppermute | solution.py:29
  38.6 6.4 %collective-permute-start.10 = (bf16[1,32,1536]{2,1,0:T(8,128)(2,1)S(1)}, bf16[1,32,1536]{2,1,0:T(8,128)(2,1)S(1)}, u32[]{:S(2)}, u32[]{:S(2)}) collective-permute-start(bf16[1,32,1536]{2,1,0:T(8,128)(2,1)S(1)} %get-tuple-element.73), channel_id=1, source_target_pairs={{0,2},{2,0},{4,6},{6,4},{8,10},{10,8},{12,14},{14,12},{16,18},{18,... | collective-permute-start | bytes 294920 | tf_op jit(solution)/shard_map/ppermute | solution.py:29
  39.2 5.8 %collective-permute-start.12 = (bf16[32,1536]{1,0:T(8,128)(2,1)S(1)}, bf16[32,1536]{1,0:T(8,128)(2,1)S(1)}, u32[]{:S(2)}, u32[]{:S(2)}) collective-permute-start(bf16[32,1536]{1,0:T(8,128)(2,1)S(1)} %chip_sums.2.order_ref.refs_6_), channel_id=1, source_target_pairs={{0,1},{1,0},{2,3},{3,2},{4,5},{5,4},{6,7},{7,6},{8,9},{9,8},{10,11... | collective-permute-start | bytes 294920 | tf_op jit(solution)/shard_map/ppermute | solution.py:29
  43.4 5.9 %collective-permute-start.16 = (bf16[8,3840]{1,0:T(8,128)(2,1)S(1)}, bf16[8,3840]{1,0:T(8,128)(2,1)S(1)}, u32[]{:S(2)}, u32[]{:S(2)}) collective-permute-start(bf16[8,3840]{1,0:T(8,128)(2,1)S(1)} %hold.1.low_ref), channel_id=1, source_target_pairs={{0,8},{2,10},{4,12},{6,14},{8,0},{10,2},{12,4},{14,6},{16,24},{18,... | collective-permute-start | bytes 184328 | tf_op jit(solution)/shard_map/ppermute | solution.py:29
  45.0 4.8 %collective-permute-start.13 = (bf16[32,1536]{1,0:T(8,128)(2,1)S(1)}, bf16[32,1536]{1,0:T(8,128)(2,1)S(1)}, u32[]{:S(2)}, u32[]{:S(2)}) collective-permute-start(bf16[32,1536]{1,0:T(8,128)(2,1)S(1)} %add_all.4.refs_6_.refs_0_), channel_id=1, source_target_pairs={{0,4},{2,6},{4,0},{6,2},{8,12},{10,14},{12,8},{14,10},{16,20},{18,... | collective-permute-start | bytes 294920 | tf_op jit(solution)/shard_map/ppermute | solution.py:29
  49.3 6.9 %collective-permute-start.17 = (bf16[16,3840]{1,0:T(8,128)(2,1)S(1)}, bf16[16,3840]{1,0:T(8,128)(2,1)S(1)}, u32[]{:S(2)}, u32[]{:S(2)}) collective-permute-start(bf16[16,3840]{1,0:T(8,128)(2,1)S(1)} %stack_rows.8.low_ref), channel_id=1, source_target_pairs={{0,4},{2,6},{4,0},{6,2},{8,12},{10,14},{12,8},{14,10},{16,20},{18,... | collective-permute-start | bytes 368648 | tf_op jit(solution)/shard_map/ppermute | solution.py:29
  49.9 6.2 %collective-permute-start.14 = (bf16[32,1536]{1,0:T(8,128)(2,1)S(1)}, bf16[32,1536]{1,0:T(8,128)(2,1)S(1)}, u32[]{:S(2)}, u32[]{:S(2)}) collective-permute-start(bf16[32,1536]{1,0:T(8,128)(2,1)S(1)} %add_all.5.refs_6_.refs_0_), channel_id=1, source_target_pairs={{0,8},{2,10},{4,12},{6,14},{8,0},{10,2},{12,4},{14,6},{16,24},{18,... | collective-permute-start | bytes 294920 | tf_op jit(solution)/shard_map/ppermute | solution.py:29
  56.2 1.6 %collective-permute-start.18 = (bf16[32,3840]{1,0:T(8,128)(2,1)S(1)}, bf16[32,3840]{1,0:T(8,128)(2,1)S(1)}, u32[]{:S(2)}, u32[]{:S(2)}) collective-permute-start(bf16[32,3840]{1,0:T(8,128)(2,1)S(1)} %stack_rows.9.refs_0_), channel_id=1, source_target_pairs={{0,2},{2,0},{4,6},{6,4},{8,10},{10,8},{12,14},{14,12},{16,18},{18,... | collective-permute-start | bytes 737288 | tf_op jit(solution)/shard_map/ppermute | solution.py:29
  56.3 8.2 %collective-permute-start.15 = (bf16[32,1536]{1,0:T(8,128)(2,1)S(1)}, bf16[32,1536]{1,0:T(8,128)(2,1)S(1)}, u32[]{:S(2)}, u32[]{:S(2)}) collective-permute-start(bf16[32,1536]{1,0:T(8,128)(2,1)S(1)} %add_all.6.order_ref.refs_3_.refs_0_), channel_id=1, source_target_pairs={{0,16},{2,18},{4,20},{6,22},{8,24},{10,26},{12,28},{14,30},{16,0},... | collective-permute-start | bytes 294920 | tf_op jit(solution)/shard_map/ppermute | solution.py:29
  64.5 1.4 %collective-permute-start.19 = (bf16[32,1536]{1,0:T(8,128)(2,1)S(1)}, bf16[32,1536]{1,0:T(8,128)(2,1)S(1)}, u32[]{:S(2)}, u32[]{:S(2)}) collective-permute-start(bf16[32,1536]{1,0:T(8,128)(2,1)S(1)} %add_all.7.own_ref), channel_id=1, source_target_pairs={{0,2},{2,0},{4,6},{6,4},{8,10},{10,8},{12,14},{14,12},{16,18},{18,... | collective-permute-start | bytes 294920 | tf_op jit(solution)/shard_map/ppermute | solution.py:29

commit v7 on v6

--- a/solution.py
+++ b/solution.py
@@ -29,12 +29,6 @@
     return lax.ppermute(value, axis, [(source, source ^ mask) for source in range(count)])
 
 
-def tree_gather(value, axis, masks):
-    for mask in masks:
-        value = jnp.concatenate([value, swap(value, axis, mask)], axis=0)
-    return value
-
-
 def bits_up(count):
     masks = []
     mask = 1
@@ -182,6 +176,25 @@
     for h in range(8):
         for w in range(8):
             cell_ref[h, w] = turn_ref[h, pl.ds(w, 8, stride=8), :]
+
+
+def conv_group(scratch, start, flip):
+    turn_ref, cell_ref, spread_ref, tap_ref = scratch
+    for tap in range(TAPS):
+        source = TAPS - 1 - tap if flip else tap
+        tap_ref[tap] = spread_ref[pl.ds(source, 8, stride=WEIGHT_ROWS), :]
+    load_cells(turn_ref, cell_ref)
+    for h in range(8):
+        sums = [start] * 8
+        for a in range(max(0, REACH - h), min(KER, 8 + REACH - h)):
+            row = [cell_ref[h + a - REACH, w] for w in range(8)]
+            for b in range(KER):
+                weight = tap_ref[a * KER + b]
+                for w in range(max(0, REACH - b), min(8, 8 + REACH - b)):
+                    term = row[w + b - REACH] * weight
+                    sums[w] = term if sums[w] is None else sums[w] + term
+        for w in range(8):
+            turn_ref[h, w * 8 : w * 8 + 8, :] = sums[w]
 
 
 def conv_cells(groups, base_piece, member, share, x_ref, weight_ref, mixed_ref, sum_ref, scratch):
@@ -201,20 +214,8 @@
                 spread_ref[slot * WEIGHT_ROWS : (slot + 1) * WEIGHT_ROWS, :] = column
                 for h in range(8):
                     turn_ref[h, slot * 8 : slot * 8 + 8, :] = x_ref[i, h, :, source].astype(F32)
-        for tap in range(TAPS):
-            tap_ref[tap] = spread_ref[pl.ds(tap, 8, stride=WEIGHT_ROWS), :]
         bias = spread_ref[pl.ds(GAIN_ROW, 8, stride=WEIGHT_ROWS), :]
-        load_cells(turn_ref, cell_ref)
-        for h in range(8):
-            sums = [bias] * 8
-            for a in range(max(0, REACH - h), min(KER, 8 + REACH - h)):
-                row = [cell_ref[h + a - REACH, w] for w in range(8)]
-                for b in range(KER):
-                    weight = tap_ref[a * KER + b]
-                    for w in range(max(0, REACH - b), min(8, 8 + REACH - b)):
-                        sums[w] = sums[w] + row[w + b - REACH] * weight
-            for w in range(8):
-                turn_ref[h, w * 8 : w * 8 + 8, :] = sums[w]
+        conv_group(scratch, bias, False)
         for h in range(8):
             for i in range(2):
                 for c in range(GROUP):
@@ -340,7 +341,8 @@
                     rows_ref[place : place + images, first : first + width] = pack[
                         row : row + images, 0:width
                     ]
-        out_ref[...] = rows_ref[...].astype(BF)
+        raw = rows_ref[...]
+        out_ref[...] = (raw * inverse_norm(raw)).astype(BF)
 
     return pl.pallas_call(
         kernel,
@@ -559,8 +561,7 @@
     inverse = inverse_norm(embed)
     unit = embed * inverse
     unit_bf = unit.astype(BF)
-    raw = jnp.concatenate([text_low[...], text_high[...]], axis=0).astype(F32)
-    texts = (raw * inverse_norm(raw)).astype(BF)
+    texts = jnp.concatenate([text_low[...], text_high[...]], axis=0)
     unit_grad = LOGIT_SCALE * jnp.dot(
         pair_weights(unit_bf, texts), texts, preferred_element_type=F32
     )
@@ -868,6 +869,75 @@
     )(*operands)
 
 
+def image_cells_kernel(base, place_ref, flow_own, flow_rest, weight_own, weight_rest, shared_ref, out_ref, token_ref, *scratch):
+    turn_ref, _, spread_ref, _ = scratch
+    own_groups = weight_own.shape[1] // (GROUP * LANES)
+    group = pl.program_id(0) + base
+    token_ref[...] = jnp.zeros_like(token_ref)
+
+    def one(flow_ref, weight_ref, g):
+        for c in range(GROUP):
+            lanes = pl.ds(pl.multiple_of(g * GROUP * LANES + c * LANES, LANES), LANES)
+            column = weight_ref[:, lanes]
+            for i in range(2):
+                slot = i * GROUP + c
+                spread_ref[slot * WEIGHT_ROWS : (slot + 1) * WEIGHT_ROWS, :] = column
+                for h in range(8):
+                    turn_ref[h, slot * 8 : slot * 8 + 8, :] = flow_ref[i, h, :, lanes]
+        conv_group(scratch, None, True)
+        for c in range(GROUP):
+            wide = pl.ds(pl.multiple_of(group * GROUP * LANES + c * LANES, LANES), LANES)
+            for i in range(2):
+                shared = shared_ref[i : i + 1, wide]
+                for h in range(8):
+                    value = turn_ref[h, pl.ds(i * GROUP + c, 8, stride=8), :]
+                    out_ref[i, h, :, c * LANES : (c + 1) * LANES] = (value + shared).astype(BF)
+
+    @pl.when(group < own_groups)
+    def _():
+        one(flow_own, weight_own, group)
+
+    @pl.when(group >= own_groups)
+    def _():
+        one(flow_rest, weight_rest, group - own_groups)
+
+
+def image_cells(base, count, place, flow, weights, shared, order, out):
+    first = out is None
+    groups = weights[0].shape[1] // (GROUP * LANES)
+    images, height, width = flow[0].shape[:3]
+    operands = [place, *near([*flow, *weights, shared]), order] + ([] if first else [out])
+
+    def kernel(*refs):
+        image_cells_kernel(base, *refs[:6], *refs[-6:])
+
+    def index(step, place_ref):
+        group = step + base
+        return (0, 0, 0, (place_ref[0] ^ (group // groups)) * groups + group % groups)
+
+    return pl.pallas_call(
+        kernel,
+        grid_spec=pltpu.PrefetchScalarGridSpec(
+            num_scalar_prefetch=1,
+            grid=(count,),
+            in_specs=[VM] * 5 + [ANY] + ([] if first else [HB]),
+            out_specs=[
+                pl.BlockSpec((images, height, width, GROUP * LANES), index),
+                pl.BlockSpec((8, LANES), lambda step, place_ref: (0, 0)),
+            ],
+            scratch_shapes=conv_scratch(),
+        ),
+        out_shape=[
+            SHAPE((images, height, width, shared.shape[1]), BF),
+            SHAPE((8, LANES), F32),
+        ],
+        input_output_aliases={} if first else {7: 0},
+        compiler_params=params(24),
+        cost_estimate=cost(1.5),
+        name="image_cells",
+    )(*operands)
+
+
 def head_grads_kernel(block, packed_low, packed_high, text_ref, order_ref, head_ref, text_grad_ref, token_ref):
     share = packed_low.shape[1] - 2 * text_ref.shape[1]
     width = text_ref.shape[1]
@@ -897,7 +967,7 @@
 
 def head_grads_block(packed, text_here, share, order):
     rows, width = text_here.shape
-    block = 256 if share % 256 == 0 else LANES
+    block = 512 if share % 512 == 0 else LANES
     return pl.pallas_call(
         lambda *refs: head_grads_kernel(block, *refs),
         grid=(share // block,),
@@ -990,7 +1060,8 @@
     shared, scaled, term_rows = pool_grad_block(grads, cells, weights, hatsum, hat, hrstd)
     mixed = (mixed_own, mixed_rest)
     dots = dots_block(scaled, mixed, mean, rstd)
-    moving = swap(packed, "dp", down[0])
+    gather_masks = [down[1], down[0]] + list(down[2:])
+    moving = swap(packed, "dp", gather_masks.pop(0))
 
     def terms_part(base, mixed_part, order):
         return terms_block(
@@ -1002,21 +1073,31 @@
     keep_own, give_own, flow_own = terms_part(0, mixed_own, keep_rest)
     flow = (flow_own, flow_rest)
 
-    parts = [(image, base) for image in range(image_maps.shape[0]) for base in (0, members // 2)]
+    fits = cells_fit(*image_maps.shape[:3], share)
     image_grads = None
+    if fits:
+        groups = image_maps.shape[3] // (GROUP * LANES)
+        edges = [0, groups // 6, groups // 2, groups]
+        parts = [(low, high - low) for low, high in zip(edges, edges[1:]) if high > low]
+    else:
+        parts = [(image, base) for image in range(image_maps.shape[0]) for base in (0, members // 2)]
 
     def image_parts(count, order, image_grads):
         token = order
         for _ in range(min(count, len(parts))):
-            image, base = parts.pop(0)
-            image_grads, token = image_block(
-                image, base, members // 2, place, flow, weights, shared, order, image_grads
-            )
+            first, second = parts.pop(0)
+            if fits:
+                image_grads, token = image_cells(
+                    first, second, place, flow, weights, shared, order, image_grads
+                )
+            else:
+                image_grads, token = image_block(
+                    first, second, members // 2, place, flow, weights, shared, order, image_grads
+                )
         return image_grads, token
 
     chip = chip_sums(keep_rest, swap(give_rest, "dp", 1), keep_own)
     chip_own = chip_sums(keep_own, swap(give_own, "dp", 1), chip[0])[0]
-    gather_masks = list(down[1:])
     image_grads, token = image_parts(1, chip[0], None)
     packed = hold(packed, token)
     moving = swap(packed, "dp", gather_masks.pop(0))

time: 67.3 us -> 64.8 us (0.963)
  Pallas kernels: 33.6 us -> 30.3 us
  starting transfers between devices: 20.6 us -> 22 us
  waiting for transfers between devices: 12.1 us -> 11.4 us
    pallas_call x4 -> x3, Pallas kernels: 10.5 us -> 7.85 us  [image_cells(): pl.pallas_call(kernel, grid_spec=pltpu.PrefetchScalarGridSpec(num_scalar_...]
    ppermute x20, starting transfers between devices: 20.6 us -> 22 us  [swap(): lax.ppermute(value, axis, [(source, source ^ mask) for source in range(co...]
  transfers between devices with their start and end apart: 20 -> 20, of which waited for: 10 -> 10; matrix products, arithmetic and copies ran while one was open for 0% -> 0% of each run, Pallas kernels for 42% -> 38%
where the time goes in v7:
time: 64.8 us; the launch traced here: 64.7 us
  Pallas kernels  30.3 us (47%)
  starting transfers between devices  22 us (34%)
  waiting for transfers between devices  11.4 us (18%)
  between operations  0.78 us (1%)
    ppermute x20, starting transfers between devices, swap(): lax.ppermute(value, axis, [(source, source ^ mask) for source in range(co...  22 us
    ppermute x20, waiting for transfers between devices, swap(): lax.ppermute(value, axis, [(source, source ^ mask) for source in range(co...  11.4 us
    pallas_call x3, Pallas kernels, image_cells(): pl.pallas_call(kernel, grid_spec=pltpu.PrefetchScalarGridSpec(num_scalar_...  7.85 us
    pallas_call x2, Pallas kernels, terms_block(): pl.pallas_call(lambda place_ref, order_ref, *refs: terms_kernel(base, sha...  5.39 us
    pallas_call x1, Pallas kernels, head_grads_block(): pl.pallas_call(lambda *refs: head_grads_kernel(block, *refs), grid=(share...  4.38 us
    pallas_call x1, Pallas kernels, forward_block(): pl.pallas_call(lambda *refs: forward_kernel(members, *refs), out_shape=ou...  4.36 us
    pallas_call x1, Pallas kernels, own_block(): pl.pallas_call(kernel, out_shape=[SHAPE((images, height, width, share), F...  2.55 us
    pallas_call x1, Pallas kernels, loss_block(): pl.pallas_call(lambda *refs: loss_kernel(members, *refs), out_shape=[SHAP...  1.45 us
  transfers between devices with their start and end apart: 20, of which 10 were waited for; matrix products, arithmetic and copies ran while one was open for 0% of the time, Pallas kernels for 38%

profile of v7, /device:TPU:0, one launch (start us, length us, event | category | flops | bytes accessed | tf_op | source)
XLA Modules:
  0.0 64.7 jit_solution(15588399271626454122)
XLA Ops:
  0.6 3.0 %collective-permute-start.2 = (bf16[49,1536]{1,0:T(8,128)(2,1)}, bf16[49,1536]{1,0:T(8,128)(2,1)S(1)}, u32[]{:S(2)}, u32[]{:S(2)}) collective-permute-start(bf16[49,1536]{1,0:T(8,128)(2,1)} %kernel_hbm.1), channel_id=1, source_target_pairs={{0,1},{1,0},{2,3},{3,2},{4,5},{5,4},{6,7},{7,6},{8,9},{9,8},{10,11... | collective-permute-start | bytes 451592 | tf_op jit(solution)/shard_map/ppermute | solution.py:29
  3.7 1.3 %load_block.1 = (bf16[2,8,8,3072]{3,2,1,0:T(8,128)(2,1)S(1)}, f32[56,1536]{1,0:T(8,128)S(1)}, bf16[2,1152]{1,0:T(2,128)(2,1)S(1)}) custom-call(bf16[2,8,8,3072]{3,2,1,0:T(8,128)(2,1)} %x_hbm.1, bf16[49,1536]{1,0:T(8,128)(2,1)} %kernel_hbm.1, bf16[4,1536]{1,0:T(4,128)(2,1)} %term_hbm.1, bf16[2,1152]{1,0:T(2,128)(2,1)} %text_hbm.1), custom_call_target="tpu_custom_call" | custom-call | tf_op jit(solution)/shard_map/load_block/pallas_call | solution.py:279
  5.0 0.1 collective-permute-done.core_ref.refs_1_
  5.1 0.1 collective-permute-start.1
  5.2 0.1 pad_add_fusion.place_ref.refs_0_
  5.3 2.6 %own_block.1 = (f32[2,8,8,1536]{3,2,1,0:T(8,128)S(1)}, f32[2,8,8,128]{3,2,1,0:T(8,128)S(1)}) custom-call(s32[2]{0:T(128)S(1)} %pad_add_fusion.place_ref.refs_0_, bf16[2,8,8,3072]{3,2,1,0:T(8,128)(2,1)S(1)} %get-tuple-element.45.x_ref.refs_2_.refs_0_, f32[56,1536]{1,0:T(8,128)S(1)} %get-tuple-element.46.weight_ref.refs_5_.refs_2_.refs_3_), custom_call_target="tpu_custom_call" | custom-call | tf_op jit(solution)/shard_map/own_block/pallas_call | solution.py:368
  7.8 1.1 %collective-permute-done.1.refs_2_.refs_8_ = bf16[8,1536]{1,0:T(8,128)(2,1)S(1)} collective-permute-done((bf16[8,1536]{1,0:T(8,128)(2,1)S(1)}, bf16[8,1536]{1,0:T(8,128)(2,1)S(1)}, u32[]{:S(2)}, u32[]{:S(2)}) %collective-permute-start.1) | collective-permute-done | bytes 24608 | tf_op jit(solution)/shard_map/ppermute | solution.py:29
  9.0 0.1 text_stack.1.refs_6_.low_ref
  9.1 2.6 %collective-permute-start.5 = (bf16[8,1152]{1,0:T(8,128)(2,1)S(1)}, bf16[8,1152]{1,0:T(8,128)(2,1)S(1)}, u32[]{:S(2)}, u32[]{:S(2)}) collective-permute-start(bf16[8,1152]{1,0:T(8,128)(2,1)S(1)} %text_stack.1.refs_6_.low_ref), channel_id=1, source_target_pairs={{0,16},{2,18},{4,20},{6,22},{8,24},{10,26},{12,28},{14,30},{16,0},... | collective-permute-start | bytes 55304 | tf_op jit(solution)/shard_map/ppermute | solution.py:29
  11.7 0.0 collective-permute-done.2.refs_7_
  11.7 4.4 %forward_block.1 = (bf16[2,1536]{1,0:T(2,128)(2,1)S(1)}, bf16[2,1536]{1,0:T(2,128)(2,1)S(1)}, bf16[1536,1152]{1,0:T(8,128)(2,1)S(1)}, f32[56,1536]{1,0:T(8,128)S...) custom-call(s32[2]{0:T(128)S(1)} %pad_add_fusion.place_ref.refs_0_, ...), custom_call_target="tpu_custom_call" | custom-call | tf_op jit(solution)/shard_map/forward_block/pallas_call | solution.py:473
  16.1 1.6 %collective-permute-start.3 = (bf16[2,1536]{1,0:T(2,128)(2,1)S(1)}, bf16[2,1536]{1,0:T(2,128)(2,1)S(1)}, u32[]{:S(2)}, u32[]{:S(2)}) collective-permute-start(bf16[2,1536]{1,0:T(2,128)(2,1)S(1)} %get-tuple-element.51), channel_id=1, source_target_pairs={{0,1},{1,0},{2,3},{3,2},{4,5},{5,4},{6,7},{7,6},{8,9},{9,8},{10,11... | collective-permute-start | bytes 18440 | tf_op jit(solution)/shard_map/ppermute | solution.py:29
  17.7 0.0 collective-permute-done.5.high_ref
  17.7 1.6 %collective-permute-start.6 = (bf16[16,1152]{1,0:T(8,128)(2,1)S(1)}, bf16[16,1152]{1,0:T(8,128)(2,1)S(1)}, u32[]{:S(2)}, u32[]{:S(2)}) collective-permute-start(bf16[16,1152]{1,0:T(8,128)(2,1)S(1)} %stack_rows.5.low_ref), channel_id=1, source_target_pairs={{0,8},{2,10},{4,12},{6,14},{8,0},{10,2},{12,4},{14,6},{16,24},{18,... | collective-permute-start | bytes 110600 | tf_op jit(solution)/shard_map/ppermute | solution.py:29
  19.2 0.5 collective-permute-done.3.refs_1_
  19.8 0.6 head_project.1
  20.3 1.6 %collective-permute-start.4 = (f32[4,1152]{1,0:T(4,128)S(1)}, f32[4,1152]{1,0:T(4,128)S(1)}, u32[]{:S(2)}, u32[]{:S(2)}) collective-permute-start(f32[4,1152]{1,0:T(4,128)S(1)} %get-tuple-element.53.refs_0_.order_ref), channel_id=1, source_target_pairs={{0,1},{1,0},{2,3},{3,2},{4,5},{5,4},{6,7},{7,6},{8,9},{9,8},{10,11... | collective-permute-start | bytes 55304 | tf_op jit(solution)/shard_map/ppermute | solution.py:29
  21.9 1.6 %collective-permute-start.7 = (bf16[32,1152]{1,0:T(8,128)(2,1)S(1)}, bf16[32,1152]{1,0:T(8,128)(2,1)S(1)}, u32[]{:S(2)}, u32[]{:S(2)}) collective-permute-start(bf16[32,1152]{1,0:T(8,128)(2,1)S(1)} %stack_rows.6.refs_1_), channel_id=1, source_target_pairs={{0,4},{2,6},{4,0},{6,2},{8,12},{10,14},{12,8},{14,10},{16,20},{18,... | collective-permute-start | bytes 221192 | tf_op jit(solution)/shard_map/ppermute | solution.py:29
  23.5 0.7 %collective-permute-done.4.refs_1_ = f32[4,1152]{1,0:T(4,128)S(1)} collective-permute-done((f32[4,1152]{1,0:T(4,128)S(1)}, f32[4,1152]{1,0:T(4,128)S(1)}, u32[]{:S(2)}, u32[]{:S(2)}) %collective-permute-start.4) | collective-permute-done | bytes 18464 | tf_op jit(solution)/shard_map/ppermute | solution.py:29
  24.1 2.2 %collective-permute-done.7.refs_2_ = bf16[32,1152]{1,0:T(8,128)(2,1)S(1)} collective-permute-done((bf16[32,1152]{1,0:T(8,128)(2,1)S(1)}, bf16[32,1152]{1,0:T(8,128)(2,1)S(1)}, u32[]{:S(2)}, u32[]{:S(2)}) %collective-permute-start.7) | collective-permute-done | bytes 73760 | tf_op jit(solution)/shard_map/ppermute | solution.py:29
  26.3 1.5 %loss_block.1 = (bf16[4,3840]{1,0:T(4,128)(2,1)S(1)}, f32[2,1536]{1,0:T(2,128)S(1)}, f32[2,1536]{1,0:T(2,128)S(1)}) custom-call(f32[4,1152]{1,0:T(4,128)S(1)} %embed_sum.1.refs_0_, bf16[32,1152]{1,0:T(8,128)(2,1)S(1)} %stack_rows.6.refs_1_, bf16[32,1152]{1,0:T(8,128)(2,1)S(1)} %collective-permute-done.7.refs_2_, ...), custom_call_target="tpu_custom_call" | custom-call | tf_op jit(solution)/shard_map/loss_block/pallas_call | solution.py:582
  27.8 0.5 collective-permute-start.9
  28.3 1.6 %collective-permute-start.8 = (bf16[4,3840]{1,0:T(4,128)(2,1)S(1)}, bf16[4,3840]{1,0:T(4,128)(2,1)S(1)}, u32[]{:S(2)}, u32[]{:S(2)}) collective-permute-start(bf16[4,3840]{1,0:T(4,128)(2,1)S(1)} %get-tuple-element.56.low_ref), channel_id=1, source_target_pairs={{0,8},{2,10},{4,12},{6,14},{8,0},{10,2},{12,4},{14,6},{16,24},{18,... | collective-permute-start | bytes 92168 | tf_op jit(solution)/shard_map/ppermute | solution.py:29
  29.9 1.6 %collective-permute-done.9.refs_1_ = f32[2,1536]{1,0:T(2,128)S(1)} collective-permute-done((f32[2,1536]{1,0:T(2,128)S(1)}, f32[2,1536]{1,0:T(2,128)S(1)}, u32[]{:S(2)}, u32[]{:S(2)}) %collective-permute-start.9) | collective-permute-done | bytes 12320 | tf_op jit(solution)/shard_map/ppermute | solution.py:29
  31.5 0.3 pool_grad_block.1
  31.8 0.6 dots_block.1.order_ref.refs_6_
  32.4 2.7 %terms_block.2 = (bf16[1,32,1536]{2,1,0:T(8,128)(2,1)S(1)}, bf16[1,32,1536]{2,1,0:T(8,128)(2,1)S(1)}, f32[2,8,8,1536]{3,2,1,0:T(8,128)S(1)}) custom-call(s32[2]{0:T(128)S(1)} %pad_add_fusion.place_ref.refs_0_, bf16[8,3840]{1,0:T(8,128)(2,1)S(1)} %stack_rows.7.order_ref.value_ref, bf16[2,8,8,3072]{3,2,1,0:T(8,128)(2,1)S(1)} %get-tuple-element.45.x_ref.refs_2_.refs_0_, ...), custom_call_target="tpu_custom_call" | custom-call | tf_op jit(solution)/shard_map/terms_block/pallas_call | solution.py:792
  35.1 0.1 collective-permute-start.11
  35.1 2.7 %terms_block.3 = (bf16[1,32,1536]{2,1,0:T(8,128)(2,1)S(1)}, bf16[1,32,1536]{2,1,0:T(8,128)(2,1)S(1)}, f32[2,8,8,1536]{3,2,1,0:T(8,128)S(1)}) custom-call(s32[2]{0:T(128)S(1)} %pad_add_fusion.place_ref.refs_0_, bf16[1,32,1536]{2,1,0:T(8,128)(2,1)S(1)} %get-tuple-element.67.order_ref.keep_ref, ...), custom_call_target="tpu_custom_call" | custom-call | tf_op jit(solution)/shard_map/terms_block/pallas_call | solution.py:792
  37.8 0.6 collective-permute-start.10
  38.4 1.4 %collective-permute-start.12 = (bf16[32,1536]{1,0:T(8,128)(2,1)S(1)}, bf16[32,1536]{1,0:T(8,128)(2,1)S(1)}, u32[]{:S(2)}, u32[]{:S(2)}) collective-permute-start(bf16[32,1536]{1,0:T(8,128)(2,1)S(1)} %chip_sums.2.order_ref.refs_6_), channel_id=1, source_target_pairs={{0,1},{1,0},{2,3},{3,2},{4,5},{5,4},{6,7},{7,6},{8,9},{9,8},{10,11... | collective-permute-start | bytes 294920 | tf_op jit(solution)/shard_map/ppermute | solution.py:29
  39.9 1.8 %image_cells.3 = (bf16[2,8,8,3072]{3,2,1,0:T(8,128)(2,1)}, f32[8,128]{1,0:T(8,128)S(1)}) custom-call(s32[2]{0:T(128)S(1)} %pad_add_fusion.place_ref.refs_0_, f32[2,8,8,1536]{3,2,1,0:T(8,128)S(1)} %get-tuple-element.68.refs_1_, f32[2,8,8,1536]{3,2,1,0:T(8,128)S(1)} %get-tuple-element.69.refs_2_, ...), custom_call_target="tpu_custom_call" | custom-call | flops 1650000000 | tf_op jit(solution)/shard_map/image_cells/pallas_call | solution.py:918
  41.7 0.3 collective-permute-start.16
  42.1 1.1 %collective-permute-done.12.refs_1_ = bf16[32,1536]{1,0:T(8,128)(2,1)S(1)} collective-permute-done((bf16[32,1536]{1,0:T(8,128)(2,1)S(1)}, bf16[32,1536]{1,0:T(8,128)(2,1)S(1)}, u32[]{:S(2)}, u32[]{:S(2)}) %collective-permute-start.12) | collective-permute-done | bytes 98336 | tf_op jit(solution)/shard_map/ppermute | solution.py:29
  43.3 1.6 %collective-permute-start.13 = (bf16[32,1536]{1,0:T(8,128)(2,1)S(1)}, bf16[32,1536]{1,0:T(8,128)(2,1)S(1)}, u32[]{:S(2)}, u32[]{:S(2)}) collective-permute-start(bf16[32,1536]{1,0:T(8,128)(2,1)S(1)} %add_all.4.refs_6_.refs_0_), channel_id=1, source_target_pairs={{0,4},{2,6},{4,0},{6,2},{8,12},{10,14},{12,8},{14,10},{16,20},{18,... | collective-permute-start | bytes 294920 | tf_op jit(solution)/shard_map/ppermute | solution.py:29
  44.8 2.7 %image_cells.4 = (bf16[2,8,8,3072]{3,2,1,0:T(8,128)(2,1)}, f32[8,128]{1,0:T(8,128)S(1)}) custom-call(s32[2]{0:T(128)S(1)} %pad_add_fusion.place_ref.refs_0_, f32[2,8,8,1536]{3,2,1,0:T(8,128)S(1)} %get-tuple-element.68.refs_1_, f32[2,8,8,1536]{3,2,1,0:T(8,128)S(1)} %get-tuple-element.69.refs_2_, ...), custom_call_target="tpu_custom_call", output_to_operand_aliasing={{0}: (7, {})} | custom-call | flops 1650000000 | tf_op jit(solution)/shard_map/image_cells/pallas_call | solution.py:918
  47.5 1.4 %collective-permute-start.17 = (bf16[16,3840]{1,0:T(8,128)(2,1)S(1)}, bf16[16,3840]{1,0:T(8,128)(2,1)S(1)}, u32[]{:S(2)}, u32[]{:S(2)}) collective-permute-start(bf16[16,3840]{1,0:T(8,128)(2,1)S(1)} %stack_rows.8.low_ref), channel_id=1, source_target_pairs={{0,4},{2,6},{4,0},{6,2},{8,12},{10,14},{12,8},{14,10},{16,20},{18,... | collective-permute-start | bytes 368648 | tf_op jit(solution)/shard_map/ppermute | solution.py:29
  48.9 1.3 %collective-permute-start.14 = (bf16[32,1536]{1,0:T(8,128)(2,1)S(1)}, bf16[32,1536]{1,0:T(8,128)(2,1)S(1)}, u32[]{:S(2)}, u32[]{:S(2)}) collective-permute-start(bf16[32,1536]{1,0:T(8,128)(2,1)S(1)} %add_all.5.refs_6_.refs_0_), channel_id=1, source_target_pairs={{0,8},{2,10},{4,12},{6,14},{8,0},{10,2},{12,4},{14,6},{16,24},{18,... | collective-permute-start | bytes 294920 | tf_op jit(solution)/shard_map/ppermute | solution.py:29
  50.2 3.4 %image_cells.5 = (bf16[2,8,8,3072]{3,2,1,0:T(8,128)(2,1)}, f32[8,128]{1,0:T(8,128)S(1)}) custom-call(s32[2]{0:T(128)S(1)} %pad_add_fusion.place_ref.refs_0_, f32[2,8,8,1536]{3,2,1,0:T(8,128)S(1)} %get-tuple-element.68.refs_1_, f32[2,8,8,1536]{3,2,1,0:T(8,128)S(1)} %get-tuple-element.69.refs_2_, ...), custom_call_target="tpu_custom_call", output_to_operand_aliasing={{0}: (7, {})} | custom-call | flops 1650000000 | tf_op jit(solution)/shard_map/image_cells/pallas_call | solution.py:918
  53.5 0.0 collective-permute-done.14.refs_1_
  53.7 0.1 collective-permute-start.18
  53.7 1.1 %collective-permute-start.15 = (bf16[32,1536]{1,0:T(8,128)(2,1)S(1)}, bf16[32,1536]{1,0:T(8,128)(2,1)S(1)}, u32[]{:S(2)}, u32[]{:S(2)}) collective-permute-start(bf16[32,1536]{1,0:T(8,128)(2,1)S(1)} %add_all.6.order_ref.refs_3_.refs_0_), channel_id=1, source_target_pairs={{0,16},{2,18},{4,20},{6,22},{8,24},{10,26},{12,28},{14,30},{16,0},... | collective-permute-start | bytes 294920 | tf_op jit(solution)/shard_map/ppermute | solution.py:29
  54.8 0.4 collective-permute-done.18.refs_1_
  55.2 4.4 %head_grads_block.1 = (f32[1536,1152]{1,0:T(8,128)}, f32[2,1152]{1,0:T(2,128)}, f32[8,128]{1,0:T(8,128)S(1)}) custom-call(bf16[32,3840]{1,0:T(8,128)(2,1)S(1)} %stack_rows.9.refs_0_, bf16[32,3840]{1,0:T(8,128)(2,1)S(1)} %collective-permute-done.18.refs_1_, bf16[2,1152]{1,0:T(2,128)(2,1)S(1)} %get-tuple-element.49.here_ref.refs_0_.refs_2_, ...), custom_call_target="tpu_custom_call" | custom-call | tf_op jit(solution)/shard_map/head_grads_block/pallas_call | solution.py:971
  59.6 2.3 %collective-permute-done.15.refs_1_ = bf16[32,1536]{1,0:T(8,128)(2,1)S(1)} collective-permute-done((bf16[32,1536]{1,0:T(8,128)(2,1)S(1)}, bf16[32,1536]{1,0:T(8,128)(2,1)S(1)}, u32[]{:S(2)}, u32[]{:S(2)}) %collective-permute-start.15) | collective-permute-done | bytes 98336 | tf_op jit(solution)/shard_map/ppermute | solution.py:29
  62.0 0.1 collective-permute-start.19
  62.1 1.3 %collective-permute-done.19.other_ref = bf16[32,1536]{1,0:T(8,128)(2,1)S(1)} collective-permute-done((bf16[32,1536]{1,0:T(8,128)(2,1)S(1)}, bf16[32,1536]{1,0:T(8,128)(2,1)S(1)}, u32[]{:S(2)}, u32[]{:S(2)}) %collective-permute-start.19) | collective-permute-done | bytes 98336 | tf_op jit(solution)/shard_map/ppermute | solution.py:29
  63.3 1.3 %split_block.1 = (f32[49,1536]{1,0:T(8,128)}, f32[4,1536]{1,0:T(4,128)}) custom-call(s32[2]{0:T(128)S(1)} %pad_add_fusion.place_ref.refs_0_, bf16[32,1536]{1,0:T(8,128)(2,1)S(1)} %add_all.7.own_ref, bf16[32,1536]{1,0:T(8,128)(2,1)S(1)} %collective-permute-done.19.other_ref), custom_call_target="tpu_custom_call" | custom-call | tf_op jit(solution)/shard_map/split_block/pallas_call | solution.py:1012
  (22 shorter events, 0.3 us)
Async XLA Ops:
  0.6 11.1 %collective-permute-start.2 = (bf16[49,1536]{1,0:T(8,128)(2,1)}, bf16[49,1536]{1,0:T(8,128)(2,1)S(1)}, u32[]{:S(2)}, u32[]{:S(2)}) collective-permute-start(bf16[49,1536]{1,0:T(8,128)(2,1)} %kernel_hbm.1), channel_id=1, source_target_pairs={{0,1},{1,0},{2,3},{3,2},{4,5},{5,4},{6,7},{7,6},{8,9},{9,8},{10,11... | collective-permute-start | bytes 451592 | tf_op jit(solution)/shard_map/ppermute | solution.py:29
  3.7 1.4 %collective-permute-start = (bf16[2,1152]{1,0:T(2,128)(2,1)}, bf16[2,1152]{1,0:T(2,128)(2,1)S(1)}, u32[]{:S(2)}, u32[]{:S(2)}) collective-permute-start(bf16[2,1152]{1,0:T(2,128)(2,1)} %text_hbm.1), channel_id=1, source_target_pairs={{0,2},{2,0},{4,6},{6,4},{8,10},{10,8},{12,14},{14,12},{16,18},{18,... | collective-permute-start | bytes 13832 | tf_op jit(solution)/shard_map/ppermute | solution.py:29
  5.1 3.9 %collective-permute-start.1 = (bf16[8,1536]{1,0:T(8,128)(2,1)S(1)}, bf16[8,1536]{1,0:T(8,128)(2,1)S(1)}, u32[]{:S(2)}, u32[]{:S(2)}) collective-permute-start(bf16[8,1536]{1,0:T(8,128)(2,1)S(1)} %pack_block.1), channel_id=1, source_target_pairs={{0,1},{1,0},{2,3},{3,2},{4,5},{5,4},{6,7},{7,6},{8,9},{9,8},{10,11... | collective-permute-start | bytes 73736 | tf_op jit(solution)/shard_map/ppermute | solution.py:29
  9.1 8.6 %collective-permute-start.5 = (bf16[8,1152]{1,0:T(8,128)(2,1)S(1)}, bf16[8,1152]{1,0:T(8,128)(2,1)S(1)}, u32[]{:S(2)}, u32[]{:S(2)}) collective-permute-start(bf16[8,1152]{1,0:T(8,128)(2,1)S(1)} %text_stack.1.refs_6_.low_ref), channel_id=1, source_target_pairs={{0,16},{2,18},{4,20},{6,22},{8,24},{10,26},{12,28},{14,30},{16,0},... | collective-permute-start | bytes 55304 | tf_op jit(solution)/shard_map/ppermute | solution.py:29
  16.1 3.7 %collective-permute-start.3 = (bf16[2,1536]{1,0:T(2,128)(2,1)S(1)}, bf16[2,1536]{1,0:T(2,128)(2,1)S(1)}, u32[]{:S(2)}, u32[]{:S(2)}) collective-permute-start(bf16[2,1536]{1,0:T(2,128)(2,1)S(1)} %get-tuple-element.51), channel_id=1, source_target_pairs={{0,1},{1,0},{2,3},{3,2},{4,5},{5,4},{6,7},{7,6},{8,9},{9,8},{10,11... | collective-permute-start | bytes 18440 | tf_op jit(solution)/shard_map/ppermute | solution.py:29
  17.7 4.2 %collective-permute-start.6 = (bf16[16,1152]{1,0:T(8,128)(2,1)S(1)}, bf16[16,1152]{1,0:T(8,128)(2,1)S(1)}, u32[]{:S(2)}, u32[]{:S(2)}) collective-permute-start(bf16[16,1152]{1,0:T(8,128)(2,1)S(1)} %stack_rows.5.low_ref), channel_id=1, source_target_pairs={{0,8},{2,10},{4,12},{6,14},{8,0},{10,2},{12,4},{14,6},{16,24},{18,... | collective-permute-start | bytes 110600 | tf_op jit(solution)/shard_map/ppermute | solution.py:29
  20.3 3.8 %collective-permute-start.4 = (f32[4,1152]{1,0:T(4,128)S(1)}, f32[4,1152]{1,0:T(4,128)S(1)}, u32[]{:S(2)}, u32[]{:S(2)}) collective-permute-start(f32[4,1152]{1,0:T(4,128)S(1)} %get-tuple-element.53.refs_0_.order_ref), channel_id=1, source_target_pairs={{0,1},{1,0},{2,3},{3,2},{4,5},{5,4},{6,7},{7,6},{8,9},{9,8},{10,11... | collective-permute-start | bytes 55304 | tf_op jit(solution)/shard_map/ppermute | solution.py:29
  21.9 4.4 %collective-permute-start.7 = (bf16[32,1152]{1,0:T(8,128)(2,1)S(1)}, bf16[32,1152]{1,0:T(8,128)(2,1)S(1)}, u32[]{:S(2)}, u32[]{:S(2)}) collective-permute-start(bf16[32,1152]{1,0:T(8,128)(2,1)S(1)} %stack_rows.6.refs_1_), channel_id=1, source_target_pairs={{0,4},{2,6},{4,0},{6,2},{8,12},{10,14},{12,8},{14,10},{16,20},{18,... | collective-permute-start | bytes 221192 | tf_op jit(solution)/shard_map/ppermute | solution.py:29
  27.8 3.7 %collective-permute-start.9 = (f32[2,1536]{1,0:T(2,128)S(1)}, f32[2,1536]{1,0:T(2,128)S(1)}, u32[]{:S(2)}, u32[]{:S(2)}) collective-permute-start(f32[2,1536]{1,0:T(2,128)S(1)} %get-tuple-element.58), channel_id=1, source_target_pairs={{0,1},{1,0},{2,3},{3,2},{4,5},{5,4},{6,7},{7,6},{8,9},{9,8},{10,11... | collective-permute-start | bytes 36872 | tf_op jit(solution)/shard_map/ppermute | solution.py:29
  28.3 4.0 %collective-permute-start.8 = (bf16[4,3840]{1,0:T(4,128)(2,1)S(1)}, bf16[4,3840]{1,0:T(4,128)(2,1)S(1)}, u32[]{:S(2)}, u32[]{:S(2)}) collective-permute-start(bf16[4,3840]{1,0:T(4,128)(2,1)S(1)} %get-tuple-element.56.low_ref), channel_id=1, source_target_pairs={{0,8},{2,10},{4,12},{6,14},{8,0},{10,2},{12,4},{14,6},{16,24},{18,... | collective-permute-start | bytes 92168 | tf_op jit(solution)/shard_map/ppermute | solution.py:29
  35.1 3.3 %collective-permute-start.11 = (bf16[1,32,1536]{2,1,0:T(8,128)(2,1)S(1)}, bf16[1,32,1536]{2,1,0:T(8,128)(2,1)S(1)}, u32[]{:S(2)}, u32[]{:S(2)}) collective-permute-start(bf16[1,32,1536]{2,1,0:T(8,128)(2,1)S(1)} %get-tuple-element.73), channel_id=1, source_target_pairs={{0,2},{2,0},{4,6},{6,4},{8,10},{10,8},{12,14},{14,12},{16,18},{18,... | collective-permute-start | bytes 294920 | tf_op jit(solution)/shard_map/ppermute | solution.py:29
  37.8 4.2 %collective-permute-start.10 = (bf16[1,32,1536]{2,1,0:T(8,128)(2,1)S(1)}, bf16[1,32,1536]{2,1,0:T(8,128)(2,1)S(1)}, u32[]{:S(2)}, u32[]{:S(2)}) collective-permute-start(bf16[1,32,1536]{2,1,0:T(8,128)(2,1)S(1)} %get-tuple-element.72), channel_id=1, source_target_pairs={{0,2},{2,0},{4,6},{6,4},{8,10},{10,8},{12,14},{14,12},{16,18},{18,... | collective-permute-start | bytes 294920 | tf_op jit(solution)/shard_map/ppermute | solution.py:29
  38.4 4.8 %collective-permute-start.12 = (bf16[32,1536]{1,0:T(8,128)(2,1)S(1)}, bf16[32,1536]{1,0:T(8,128)(2,1)S(1)}, u32[]{:S(2)}, u32[]{:S(2)}) collective-permute-start(bf16[32,1536]{1,0:T(8,128)(2,1)S(1)} %chip_sums.2.order_ref.refs_6_), channel_id=1, source_target_pairs={{0,1},{1,0},{2,3},{3,2},{4,5},{5,4},{6,7},{7,6},{8,9},{9,8},{10,11... | collective-permute-start | bytes 294920 | tf_op jit(solution)/shard_map/ppermute | solution.py:29
  41.7 5.7 %collective-permute-start.16 = (bf16[8,3840]{1,0:T(8,128)(2,1)S(1)}, bf16[8,3840]{1,0:T(8,128)(2,1)S(1)}, u32[]{:S(2)}, u32[]{:S(2)}) collective-permute-start(bf16[8,3840]{1,0:T(8,128)(2,1)S(1)} %hold.1.low_ref), channel_id=1, source_target_pairs={{0,16},{2,18},{4,20},{6,22},{8,24},{10,26},{12,28},{14,30},{16,0},... | collective-permute-start | bytes 184328 | tf_op jit(solution)/shard_map/ppermute | solution.py:29
  43.3 5.6 %collective-permute-start.13 = (bf16[32,1536]{1,0:T(8,128)(2,1)S(1)}, bf16[32,1536]{1,0:T(8,128)(2,1)S(1)}, u32[]{:S(2)}, u32[]{:S(2)}) collective-permute-start(bf16[32,1536]{1,0:T(8,128)(2,1)S(1)} %add_all.4.refs_6_.refs_0_), channel_id=1, source_target_pairs={{0,4},{2,6},{4,0},{6,2},{8,12},{10,14},{12,8},{14,10},{16,20},{18,... | collective-permute-start | bytes 294920 | tf_op jit(solution)/shard_map/ppermute | solution.py:29
  47.5 6.1 %collective-permute-start.17 = (bf16[16,3840]{1,0:T(8,128)(2,1)S(1)}, bf16[16,3840]{1,0:T(8,128)(2,1)S(1)}, u32[]{:S(2)}, u32[]{:S(2)}) collective-permute-start(bf16[16,3840]{1,0:T(8,128)(2,1)S(1)} %stack_rows.8.low_ref), channel_id=1, source_target_pairs={{0,4},{2,6},{4,0},{6,2},{8,12},{10,14},{12,8},{14,10},{16,20},{18,... | collective-permute-start | bytes 368648 | tf_op jit(solution)/shard_map/ppermute | solution.py:29
  48.9 4.7 %collective-permute-start.14 = (bf16[32,1536]{1,0:T(8,128)(2,1)S(1)}, bf16[32,1536]{1,0:T(8,128)(2,1)S(1)}, u32[]{:S(2)}, u32[]{:S(2)}) collective-permute-start(bf16[32,1536]{1,0:T(8,128)(2,1)S(1)} %add_all.5.refs_6_.refs_0_), channel_id=1, source_target_pairs={{0,8},{2,10},{4,12},{6,14},{8,0},{10,2},{12,4},{14,6},{16,24},{18,... | collective-permute-start | bytes 294920 | tf_op jit(solution)/shard_map/ppermute | solution.py:29
  53.7 1.6 %collective-permute-start.18 = (bf16[32,3840]{1,0:T(8,128)(2,1)S(1)}, bf16[32,3840]{1,0:T(8,128)(2,1)S(1)}, u32[]{:S(2)}, u32[]{:S(2)}) collective-permute-start(bf16[32,3840]{1,0:T(8,128)(2,1)S(1)} %stack_rows.9.refs_0_), channel_id=1, source_target_pairs={{0,2},{2,0},{4,6},{6,4},{8,10},{10,8},{12,14},{14,12},{16,18},{18,... | collective-permute-start | bytes 737288 | tf_op jit(solution)/shard_map/ppermute | solution.py:29
  53.7 8.2 %collective-permute-start.15 = (bf16[32,1536]{1,0:T(8,128)(2,1)S(1)}, bf16[32,1536]{1,0:T(8,128)(2,1)S(1)}, u32[]{:S(2)}, u32[]{:S(2)}) collective-permute-start(bf16[32,1536]{1,0:T(8,128)(2,1)S(1)} %add_all.6.order_ref.refs_3_.refs_0_), channel_id=1, source_target_pairs={{0,16},{2,18},{4,20},{6,22},{8,24},{10,26},{12,28},{14,30},{16,0},... | collective-permute-start | bytes 294920 | tf_op jit(solution)/shard_map/ppermute | solution.py:29
  62.0 1.4 %collective-permute-start.19 = (bf16[32,1536]{1,0:T(8,128)(2,1)S(1)}, bf16[32,1536]{1,0:T(8,128)(2,1)S(1)}, u32[]{:S(2)}, u32[]{:S(2)}) collective-permute-start(bf16[32,1536]{1,0:T(8,128)(2,1)S(1)} %add_all.7.own_ref), channel_id=1, source_target_pairs={{0,2},{2,0},{4,6},{6,4},{8,10},{10,8},{12,14},{14,12},{16,18},{18,... | collective-permute-start | bytes 294920 | tf_op jit(solution)/shard_map/ppermute | solution.py:29

commit v8 on v7

--- a/solution.py
+++ b/solution.py
@@ -153,6 +153,10 @@
     )(keep, give, order)
 
 
+def together(tiles):
+    return GROUP if tiles % GROUP == 0 else 1
+
+
 def tile_of(base_piece, t, member, share):
     per_piece = share // LANES
     piece = base_piece + t // per_piece
@@ -218,11 +222,13 @@
         conv_group(scratch, bias, False)
         for h in range(8):
             for i in range(2):
+                total = None
                 for c in range(GROUP):
                     lanes = pl.ds(pl.multiple_of(g * GROUP * LANES + c * LANES, LANES), LANES)
                     value = turn_ref[h, pl.ds(i * GROUP + c, 8, stride=8), :]
                     mixed_ref[i, h, :, lanes] = value
-                    sum_ref[i, h] += value
+                    total = value if total is None else total + value
+                sum_ref[i, h] += total
 
 
 def conv_tiles(tiles, base_piece, member, share, x_ref, weight_ref, mixed_ref, sum_ref, scratch):
@@ -406,38 +412,43 @@
     sum_ref[...] = jnp.zeros_like(sum_ref)
     for base, tiles, mixed_ref, weight_ref in parts:
 
-        @pl.loop(0, tiles)
+        @pl.loop(0, tiles // together(tiles))
         def _(t):
-            lanes = lane_block(t, LANES)
             for i in range(images):
                 for h in range(height):
-                    value = mixed_ref[i, h, :, lanes] - mean_ref[i, h]
-                    sum_ref[i, h] += value * value
+                    total = None
+                    for k in range(together(tiles)):
+                        lanes = lane_block(t * together(tiles) + k, LANES)
+                        value = mixed_ref[i, h, :, lanes] - mean_ref[i, h]
+                        total = value * value if total is None else total + value * value
+                    sum_ref[i, h] += total
 
     var = jnp.sum(sum_ref[...], axis=-1, keepdims=True) * (1.0 / channels)
     rstd_ref[...] = jnp.broadcast_to(lax.rsqrt(var + EPS), rstd_ref.shape)
     for base, tiles, mixed_ref, weight_ref in parts:
 
-        @pl.loop(0, tiles)
-        def _(t):
-            lanes = lane_block(t, LANES)
-            wide = lane_block(t + base * own_tiles, LANES)
-            source = tile_of(base, t, member, share)
-            scale = (
-                weight_ref[GAIN_ROW + 1 : GAIN_ROW + 2, lanes]
-                * weight_ref[GAIN_ROW + 2 : GAIN_ROW + 3, lanes]
-            )
-            for i in range(images):
-                hats = jnp.zeros((width, LANES), F32)
-                plain = jnp.zeros((width, LANES), F32)
-                for h in range(height):
-                    hats = hats + (mixed_ref[i, h, :, lanes] - mean_ref[i, h]) * rstd_ref[i, h]
-                    plain = plain + x_ref[i, h, :, source].astype(F32)
-                hat_row = jnp.sum(hats, axis=0, keepdims=True)
-                hatsum_ref[i : i + 1, wide] = hat_row
-                pool_ref[i : i + 1, wide] = (
-                    jnp.sum(plain, axis=0, keepdims=True) + scale * hat_row
-                ) * (1.0 / cells)
+        @pl.loop(0, tiles // together(tiles))
+        def _(step):
+            for k in range(together(tiles)):
+                t = step * together(tiles) + k
+                lanes = lane_block(t, LANES)
+                wide = lane_block(t + base * own_tiles, LANES)
+                source = tile_of(base, t, member, share)
+                scale = (
+                    weight_ref[GAIN_ROW + 1 : GAIN_ROW + 2, lanes]
+                    * weight_ref[GAIN_ROW + 2 : GAIN_ROW + 3, lanes]
+                )
+                for i in range(images):
+                    hats = jnp.zeros((width, LANES), F32)
+                    plain = jnp.zeros((width, LANES), F32)
+                    for h in range(height):
+                        hats = hats + (mixed_ref[i, h, :, lanes] - mean_ref[i, h]) * rstd_ref[i, h]
+                        plain = plain + x_ref[i, h, :, source].astype(F32)
+                    hat_row = jnp.sum(hats, axis=0, keepdims=True)
+                    hatsum_ref[i : i + 1, wide] = hat_row
+                    pool_ref[i : i + 1, wide] = (
+                        jnp.sum(plain, axis=0, keepdims=True) + scale * hat_row
+                    ) * (1.0 / cells)
 
     pooled = pool_ref[...]
     centered = pooled - jnp.mean(pooled, axis=1, keepdims=True)
@@ -651,14 +662,17 @@
     dot_ref[...] = jnp.zeros_like(dot_ref)
     for first, tiles, mixed_ref in [(0, own_tiles, mixed_own), (own_tiles, rest_tiles, mixed_rest)]:
 
-        @pl.loop(0, tiles)
+        @pl.loop(0, tiles // together(tiles))
         def _(t):
-            lanes = lane_block(t, LANES)
-            wide = lane_block(t + first, LANES)
             for i in range(images):
-                factor = scaled_ref[i : i + 1, wide]
                 for h in range(height):
-                    dot_ref[i, h] += factor * (mixed_ref[i, h, :, lanes] - mean_ref[i, h])
+                    total = None
+                    for k in range(together(tiles)):
+                        tile = t * together(tiles) + k
+                        factor = scaled_ref[i : i + 1, lane_block(tile + first, LANES)]
+                        term = factor * (mixed_ref[i, h, :, lane_block(tile, LANES)] - mean_ref[i, h])
+                        total = term if total is None else total + term
+                    dot_ref[i, h] += total
 
     dots = jnp.sum(dot_ref[...], axis=-1, keepdims=True) * (1.0 / channels)
     dot_ref[...] = jnp.broadcast_to(dots, dot_ref.shape) * rstd_ref[...] * rstd_ref[...]

time: 64.8 us -> 64.3 us (level)
  no operation moved by 1% of the time
where the time goes in v8:
time: 64.3 us; the launch traced here: 64.2 us
  Pallas kernels  29.7 us (46%)
  starting transfers between devices  22.3 us (35%)
  waiting for transfers between devices  11.3 us (18%)
  between operations  0.77 us (1%)
    ppermute x20, starting transfers between devices, swap(): lax.ppermute(value, axis, [(source, source ^ mask) for source in range(co...  22.3 us
    ppermute x20, waiting for transfers between devices, swap(): lax.ppermute(value, axis, [(source, source ^ mask) for source in range(co...  11.3 us
    pallas_call x3, Pallas kernels, image_cells(): pl.pallas_call(kernel, grid_spec=pltpu.PrefetchScalarGridSpec(num_scalar_...  7.85 us
    pallas_call x2, Pallas kernels, terms_block(): pl.pallas_call(lambda place_ref, order_ref, *refs: terms_kernel(base, sha...  5.39 us
    pallas_call x1, Pallas kernels, head_grads_block(): pl.pallas_call(lambda *refs: head_grads_kernel(block, *refs), grid=(share...  4.39 us
    pallas_call x1, Pallas kernels, forward_block(): pl.pallas_call(lambda *refs: forward_kernel(members, *refs), out_shape=ou...  3.87 us
    pallas_call x1, Pallas kernels, own_block(): pl.pallas_call(kernel, out_shape=[SHAPE((images, height, width, share), F...  2.55 us
    pallas_call x1, Pallas kernels, loss_block(): pl.pallas_call(lambda *refs: loss_kernel(members, *refs), out_shape=[SHAP...  1.45 us
  transfers between devices with their start and end apart: 20, of which 10 were waited for; matrix products, arithmetic and copies ran while one was open for 0% of the time, Pallas kernels for 38%

profile of v8, /device:TPU:0, one launch (start us, length us, event | category | flops | bytes accessed | tf_op | source)
XLA Modules:
  0.0 64.2 jit_solution(6681967427808826148)
XLA Ops:
  0.6 3.0 %collective-permute-start.2 = (bf16[49,1536]{1,0:T(8,128)(2,1)}, bf16[49,1536]{1,0:T(8,128)(2,1)S(1)}, u32[]{:S(2)}, u32[]{:S(2)}) collective-permute-start(bf16[49,1536]{1,0:T(8,128)(2,1)} %kernel_hbm.1), channel_id=1, source_target_pairs={{0,1},{1,0},{2,3},{3,2},{4,5},{5,4},{6,7},{7,6},{8,9},{9,8},{10,11... | collective-permute-start | bytes 451592 | tf_op jit(solution)/shard_map/ppermute | solution.py:29
  3.7 1.3 %load_block.1 = (bf16[2,8,8,3072]{3,2,1,0:T(8,128)(2,1)S(1)}, f32[56,1536]{1,0:T(8,128)S(1)}, bf16[2,1152]{1,0:T(2,128)(2,1)S(1)}) custom-call(bf16[2,8,8,3072]{3,2,1,0:T(8,128)(2,1)} %x_hbm.1, bf16[49,1536]{1,0:T(8,128)(2,1)} %kernel_hbm.1, bf16[4,1536]{1,0:T(4,128)(2,1)} %term_hbm.1, bf16[2,1152]{1,0:T(2,128)(2,1)} %text_hbm.1), custom_call_target="tpu_custom_call" | custom-call | tf_op jit(solution)/shard_map/load_block/pallas_call | solution.py:285
  5.0 0.1 collective-permute-done.core_ref.refs_1_
  5.1 0.1 collective-permute-start.1
  5.2 0.1 pad_add_fusion.place_ref.refs_0_
  5.3 2.5 %own_block.1 = (f32[2,8,8,1536]{3,2,1,0:T(8,128)S(1)}, f32[2,8,8,128]{3,2,1,0:T(8,128)S(1)}) custom-call(s32[2]{0:T(128)S(1)} %pad_add_fusion.place_ref.refs_0_, bf16[2,8,8,3072]{3,2,1,0:T(8,128)(2,1)S(1)} %get-tuple-element.45.x_ref.refs_2_.refs_0_, f32[56,1536]{1,0:T(8,128)S(1)} %get-tuple-element.46.weight_ref.refs_5_.refs_2_.refs_3_), custom_call_target="tpu_custom_call" | custom-call | tf_op jit(solution)/shard_map/own_block/pallas_call | solution.py:374
  7.8 1.1 %collective-permute-done.1.refs_2_.refs_8_ = bf16[8,1536]{1,0:T(8,128)(2,1)S(1)} collective-permute-done((bf16[8,1536]{1,0:T(8,128)(2,1)S(1)}, bf16[8,1536]{1,0:T(8,128)(2,1)S(1)}, u32[]{:S(2)}, u32[]{:S(2)}) %collective-permute-start.1) | collective-permute-done | bytes 24608 | tf_op jit(solution)/shard_map/ppermute | solution.py:29
  9.0 0.1 text_stack.1.refs_6_.low_ref
  9.1 2.6 %collective-permute-start.5 = (bf16[8,1152]{1,0:T(8,128)(2,1)S(1)}, bf16[8,1152]{1,0:T(8,128)(2,1)S(1)}, u32[]{:S(2)}, u32[]{:S(2)}) collective-permute-start(bf16[8,1152]{1,0:T(8,128)(2,1)S(1)} %text_stack.1.refs_6_.low_ref), channel_id=1, source_target_pairs={{0,16},{2,18},{4,20},{6,22},{8,24},{10,26},{12,28},{14,30},{16,0},... | collective-permute-start | bytes 55304 | tf_op jit(solution)/shard_map/ppermute | solution.py:29
  11.7 0.0 collective-permute-done.2.refs_7_
  11.7 3.9 %forward_block.1 = (bf16[2,1536]{1,0:T(2,128)(2,1)S(1)}, bf16[2,1536]{1,0:T(2,128)(2,1)S(1)}, bf16[1536,1152]{1,0:T(8,128)(2,1)S(1)}, f32[56,1536]{1,0:T(8,128)S...) custom-call(s32[2]{0:T(128)S(1)} %pad_add_fusion.place_ref.refs_0_, ...), custom_call_target="tpu_custom_call" | custom-call | tf_op jit(solution)/shard_map/forward_block/pallas_call | solution.py:484
  15.6 1.6 %collective-permute-start.3 = (bf16[2,1536]{1,0:T(2,128)(2,1)S(1)}, bf16[2,1536]{1,0:T(2,128)(2,1)S(1)}, u32[]{:S(2)}, u32[]{:S(2)}) collective-permute-start(bf16[2,1536]{1,0:T(2,128)(2,1)S(1)} %get-tuple-element.51), channel_id=1, source_target_pairs={{0,1},{1,0},{2,3},{3,2},{4,5},{5,4},{6,7},{7,6},{8,9},{9,8},{10,11... | collective-permute-start | bytes 18440 | tf_op jit(solution)/shard_map/ppermute | solution.py:29
  17.2 1.6 %collective-permute-start.6 = (bf16[16,1152]{1,0:T(8,128)(2,1)S(1)}, bf16[16,1152]{1,0:T(8,128)(2,1)S(1)}, u32[]{:S(2)}, u32[]{:S(2)}) collective-permute-start(bf16[16,1152]{1,0:T(8,128)(2,1)S(1)} %stack_rows.5.low_ref), channel_id=1, source_target_pairs={{0,8},{2,10},{4,12},{6,14},{8,0},{10,2},{12,4},{14,6},{16,24},{18,... | collective-permute-start | bytes 110600 | tf_op jit(solution)/shard_map/ppermute | solution.py:29
  18.8 0.5 collective-permute-done.3.refs_1_
  19.3 0.6 head_project.1
  19.8 1.6 %collective-permute-start.4 = (f32[4,1152]{1,0:T(4,128)S(1)}, f32[4,1152]{1,0:T(4,128)S(1)}, u32[]{:S(2)}, u32[]{:S(2)}) collective-permute-start(f32[4,1152]{1,0:T(4,128)S(1)} %get-tuple-element.53.refs_0_.order_ref), channel_id=1, source_target_pairs={{0,1},{1,0},{2,3},{3,2},{4,5},{5,4},{6,7},{7,6},{8,9},{9,8},{10,11... | collective-permute-start | bytes 55304 | tf_op jit(solution)/shard_map/ppermute | solution.py:29
  21.4 1.6 %collective-permute-start.7 = (bf16[32,1152]{1,0:T(8,128)(2,1)S(1)}, bf16[32,1152]{1,0:T(8,128)(2,1)S(1)}, u32[]{:S(2)}, u32[]{:S(2)}) collective-permute-start(bf16[32,1152]{1,0:T(8,128)(2,1)S(1)} %stack_rows.6.refs_1_), channel_id=1, source_target_pairs={{0,4},{2,6},{4,0},{6,2},{8,12},{10,14},{12,8},{14,10},{16,20},{18,... | collective-permute-start | bytes 221192 | tf_op jit(solution)/shard_map/ppermute | solution.py:29
  23.0 0.7 %collective-permute-done.4.refs_1_ = f32[4,1152]{1,0:T(4,128)S(1)} collective-permute-done((f32[4,1152]{1,0:T(4,128)S(1)}, f32[4,1152]{1,0:T(4,128)S(1)}, u32[]{:S(2)}, u32[]{:S(2)}) %collective-permute-start.4) | collective-permute-done | bytes 18464 | tf_op jit(solution)/shard_map/ppermute | solution.py:29
  23.7 2.2 %collective-permute-done.7.refs_2_ = bf16[32,1152]{1,0:T(8,128)(2,1)S(1)} collective-permute-done((bf16[32,1152]{1,0:T(8,128)(2,1)S(1)}, bf16[32,1152]{1,0:T(8,128)(2,1)S(1)}, u32[]{:S(2)}, u32[]{:S(2)}) %collective-permute-start.7) | collective-permute-done | bytes 73760 | tf_op jit(solution)/shard_map/ppermute | solution.py:29
  25.8 1.5 %loss_block.1 = (bf16[4,3840]{1,0:T(4,128)(2,1)S(1)}, f32[2,1536]{1,0:T(2,128)S(1)}, f32[2,1536]{1,0:T(2,128)S(1)}) custom-call(f32[4,1152]{1,0:T(4,128)S(1)} %embed_sum.1.refs_0_, bf16[32,1152]{1,0:T(8,128)(2,1)S(1)} %stack_rows.6.refs_1_, bf16[32,1152]{1,0:T(8,128)(2,1)S(1)} %collective-permute-done.7.refs_2_, ...), custom_call_target="tpu_custom_call" | custom-call | tf_op jit(solution)/shard_map/loss_block/pallas_call | solution.py:593
  27.3 0.5 collective-permute-start.9
  27.8 1.6 %collective-permute-start.8 = (bf16[4,3840]{1,0:T(4,128)(2,1)S(1)}, bf16[4,3840]{1,0:T(4,128)(2,1)S(1)}, u32[]{:S(2)}, u32[]{:S(2)}) collective-permute-start(bf16[4,3840]{1,0:T(4,128)(2,1)S(1)} %get-tuple-element.56.low_ref), channel_id=1, source_target_pairs={{0,8},{2,10},{4,12},{6,14},{8,0},{10,2},{12,4},{14,6},{16,24},{18,... | collective-permute-start | bytes 92168 | tf_op jit(solution)/shard_map/ppermute | solution.py:29
  29.4 1.6 %collective-permute-done.9.refs_1_ = f32[2,1536]{1,0:T(2,128)S(1)} collective-permute-done((f32[2,1536]{1,0:T(2,128)S(1)}, f32[2,1536]{1,0:T(2,128)S(1)}, u32[]{:S(2)}, u32[]{:S(2)}) %collective-permute-start.9) | collective-permute-done | bytes 12320 | tf_op jit(solution)/shard_map/ppermute | solution.py:29
  31.0 0.3 pool_grad_block.1
  31.3 0.4 dots_block.1.order_ref.refs_6_
  31.7 0.0 collective-permute-done.8.high_ref
  31.7 2.7 %terms_block.2 = (bf16[1,32,1536]{2,1,0:T(8,128)(2,1)S(1)}, bf16[1,32,1536]{2,1,0:T(8,128)(2,1)S(1)}, f32[2,8,8,1536]{3,2,1,0:T(8,128)S(1)}) custom-call(s32[2]{0:T(128)S(1)} %pad_add_fusion.place_ref.refs_0_, bf16[8,3840]{1,0:T(8,128)(2,1)S(1)} %stack_rows.7.order_ref.value_ref, bf16[2,8,8,3072]{3,2,1,0:T(8,128)(2,1)S(1)} %get-tuple-element.45.x_ref.refs_2_.refs_0_, ...), custom_call_target="tpu_custom_call" | custom-call | tf_op jit(solution)/shard_map/terms_block/pallas_call | solution.py:806
  34.4 0.1 collective-permute-start.11
  34.5 2.7 %terms_block.3 = (bf16[1,32,1536]{2,1,0:T(8,128)(2,1)S(1)}, bf16[1,32,1536]{2,1,0:T(8,128)(2,1)S(1)}, f32[2,8,8,1536]{3,2,1,0:T(8,128)S(1)}) custom-call(s32[2]{0:T(128)S(1)} %pad_add_fusion.place_ref.refs_0_, bf16[1,32,1536]{2,1,0:T(8,128)(2,1)S(1)} %get-tuple-element.67.order_ref.keep_ref, ...), custom_call_target="tpu_custom_call" | custom-call | tf_op jit(solution)/shard_map/terms_block/pallas_call | solution.py:806
  37.2 0.6 collective-permute-start.10
  37.8 1.6 %collective-permute-start.12 = (bf16[32,1536]{1,0:T(8,128)(2,1)S(1)}, bf16[32,1536]{1,0:T(8,128)(2,1)S(1)}, u32[]{:S(2)}, u32[]{:S(2)}) collective-permute-start(bf16[32,1536]{1,0:T(8,128)(2,1)S(1)} %chip_sums.2.order_ref.refs_6_), channel_id=1, source_target_pairs={{0,1},{1,0},{2,3},{3,2},{4,5},{5,4},{6,7},{7,6},{8,9},{9,8},{10,11... | collective-permute-start | bytes 294920 | tf_op jit(solution)/shard_map/ppermute | solution.py:29
  39.4 1.8 %image_cells.3 = (bf16[2,8,8,3072]{3,2,1,0:T(8,128)(2,1)}, f32[8,128]{1,0:T(8,128)S(1)}) custom-call(s32[2]{0:T(128)S(1)} %pad_add_fusion.place_ref.refs_0_, f32[2,8,8,1536]{3,2,1,0:T(8,128)S(1)} %get-tuple-element.68.refs_1_, f32[2,8,8,1536]{3,2,1,0:T(8,128)S(1)} %get-tuple-element.69.refs_2_, ...), custom_call_target="tpu_custom_call" | custom-call | flops 1650000000 | tf_op jit(solution)/shard_map/image_cells/pallas_call | solution.py:932
  41.2 0.3 collective-permute-start.16
  41.6 1.0 %collective-permute-done.12.refs_1_ = bf16[32,1536]{1,0:T(8,128)(2,1)S(1)} collective-permute-done((bf16[32,1536]{1,0:T(8,128)(2,1)S(1)}, bf16[32,1536]{1,0:T(8,128)(2,1)S(1)}, u32[]{:S(2)}, u32[]{:S(2)}) %collective-permute-start.12) | collective-permute-done | bytes 98336 | tf_op jit(solution)/shard_map/ppermute | solution.py:29
  42.6 1.6 %collective-permute-start.13 = (bf16[32,1536]{1,0:T(8,128)(2,1)S(1)}, bf16[32,1536]{1,0:T(8,128)(2,1)S(1)}, u32[]{:S(2)}, u32[]{:S(2)}) collective-permute-start(bf16[32,1536]{1,0:T(8,128)(2,1)S(1)} %add_all.4.refs_6_.refs_0_), channel_id=1, source_target_pairs={{0,4},{2,6},{4,0},{6,2},{8,12},{10,14},{12,8},{14,10},{16,20},{18,... | collective-permute-start | bytes 294920 | tf_op jit(solution)/shard_map/ppermute | solution.py:29
  44.2 2.7 %image_cells.4 = (bf16[2,8,8,3072]{3,2,1,0:T(8,128)(2,1)}, f32[8,128]{1,0:T(8,128)S(1)}) custom-call(s32[2]{0:T(128)S(1)} %pad_add_fusion.place_ref.refs_0_, f32[2,8,8,1536]{3,2,1,0:T(8,128)S(1)} %get-tuple-element.68.refs_1_, f32[2,8,8,1536]{3,2,1,0:T(8,128)S(1)} %get-tuple-element.69.refs_2_, ...), custom_call_target="tpu_custom_call", output_to_operand_aliasing={{0}: (7, {})} | custom-call | flops 1650000000 | tf_op jit(solution)/shard_map/image_cells/pallas_call | solution.py:932
  46.9 1.5 %collective-permute-start.17 = (bf16[16,3840]{1,0:T(8,128)(2,1)S(1)}, bf16[16,3840]{1,0:T(8,128)(2,1)S(1)}, u32[]{:S(2)}, u32[]{:S(2)}) collective-permute-start(bf16[16,3840]{1,0:T(8,128)(2,1)S(1)} %stack_rows.8.low_ref), channel_id=1, source_target_pairs={{0,4},{2,6},{4,0},{6,2},{8,12},{10,14},{12,8},{14,10},{16,20},{18,... | collective-permute-start | bytes 368648 | tf_op jit(solution)/shard_map/ppermute | solution.py:29
  48.4 1.3 %collective-permute-start.14 = (bf16[32,1536]{1,0:T(8,128)(2,1)S(1)}, bf16[32,1536]{1,0:T(8,128)(2,1)S(1)}, u32[]{:S(2)}, u32[]{:S(2)}) collective-permute-start(bf16[32,1536]{1,0:T(8,128)(2,1)S(1)} %add_all.5.refs_6_.refs_0_), channel_id=1, source_target_pairs={{0,8},{2,10},{4,12},{6,14},{8,0},{10,2},{12,4},{14,6},{16,24},{18,... | collective-permute-start | bytes 294920 | tf_op jit(solution)/shard_map/ppermute | solution.py:29
  49.7 3.4 %image_cells.5 = (bf16[2,8,8,3072]{3,2,1,0:T(8,128)(2,1)}, f32[8,128]{1,0:T(8,128)S(1)}) custom-call(s32[2]{0:T(128)S(1)} %pad_add_fusion.place_ref.refs_0_, f32[2,8,8,1536]{3,2,1,0:T(8,128)S(1)} %get-tuple-element.68.refs_1_, f32[2,8,8,1536]{3,2,1,0:T(8,128)S(1)} %get-tuple-element.69.refs_2_, ...), custom_call_target="tpu_custom_call", output_to_operand_aliasing={{0}: (7, {})} | custom-call | flops 1650000000 | tf_op jit(solution)/shard_map/image_cells/pallas_call | solution.py:932
  53.1 0.0 collective-permute-done.14.refs_1_
  53.2 0.1 collective-permute-start.18
  53.2 1.1 %collective-permute-start.15 = (bf16[32,1536]{1,0:T(8,128)(2,1)S(1)}, bf16[32,1536]{1,0:T(8,128)(2,1)S(1)}, u32[]{:S(2)}, u32[]{:S(2)}) collective-permute-start(bf16[32,1536]{1,0:T(8,128)(2,1)S(1)} %add_all.6.order_ref.refs_3_.refs_0_), channel_id=1, source_target_pairs={{0,16},{2,18},{4,20},{6,22},{8,24},{10,26},{12,28},{14,30},{16,0},... | collective-permute-start | bytes 294920 | tf_op jit(solution)/shard_map/ppermute | solution.py:29
  54.3 0.4 collective-permute-done.18.refs_1_
  54.7 4.4 %head_grads_block.1 = (f32[1536,1152]{1,0:T(8,128)}, f32[2,1152]{1,0:T(2,128)}, f32[8,128]{1,0:T(8,128)S(1)}) custom-call(bf16[32,3840]{1,0:T(8,128)(2,1)S(1)} %stack_rows.9.refs_0_, bf16[32,3840]{1,0:T(8,128)(2,1)S(1)} %collective-permute-done.18.refs_1_, bf16[2,1152]{1,0:T(2,128)(2,1)S(1)} %get-tuple-element.49.here_ref.refs_0_.refs_2_, ...), custom_call_target="tpu_custom_call" | custom-call | tf_op jit(solution)/shard_map/head_grads_block/pallas_call | solution.py:985
  59.1 2.3 %collective-permute-done.15.refs_1_ = bf16[32,1536]{1,0:T(8,128)(2,1)S(1)} collective-permute-done((bf16[32,1536]{1,0:T(8,128)(2,1)S(1)}, bf16[32,1536]{1,0:T(8,128)(2,1)S(1)}, u32[]{:S(2)}, u32[]{:S(2)}) %collective-permute-start.15) | collective-permute-done | bytes 98336 | tf_op jit(solution)/shard_map/ppermute | solution.py:29
  61.5 0.1 collective-permute-start.19
  61.6 1.3 %collective-permute-done.19.other_ref = bf16[32,1536]{1,0:T(8,128)(2,1)S(1)} collective-permute-done((bf16[32,1536]{1,0:T(8,128)(2,1)S(1)}, bf16[32,1536]{1,0:T(8,128)(2,1)S(1)}, u32[]{:S(2)}, u32[]{:S(2)}) %collective-permute-start.19) | collective-permute-done | bytes 98336 | tf_op jit(solution)/shard_map/ppermute | solution.py:29
  62.9 1.3 %split_block.1 = (f32[49,1536]{1,0:T(8,128)}, f32[4,1536]{1,0:T(4,128)}) custom-call(s32[2]{0:T(128)S(1)} %pad_add_fusion.place_ref.refs_0_, bf16[32,1536]{1,0:T(8,128)(2,1)S(1)} %add_all.7.own_ref, bf16[32,1536]{1,0:T(8,128)(2,1)S(1)} %collective-permute-done.19.other_ref), custom_call_target="tpu_custom_call" | custom-call | tf_op jit(solution)/shard_map/split_block/pallas_call | solution.py:1026
  (22 shorter events, 0.3 us)
Async XLA Ops:
  0.6 11.1 %collective-permute-start.2 = (bf16[49,1536]{1,0:T(8,128)(2,1)}, bf16[49,1536]{1,0:T(8,128)(2,1)S(1)}, u32[]{:S(2)}, u32[]{:S(2)}) collective-permute-start(bf16[49,1536]{1,0:T(8,128)(2,1)} %kernel_hbm.1), channel_id=1, source_target_pairs={{0,1},{1,0},{2,3},{3,2},{4,5},{5,4},{6,7},{7,6},{8,9},{9,8},{10,11... | collective-permute-start | bytes 451592 | tf_op jit(solution)/shard_map/ppermute | solution.py:29
  3.7 1.4 %collective-permute-start = (bf16[2,1152]{1,0:T(2,128)(2,1)}, bf16[2,1152]{1,0:T(2,128)(2,1)S(1)}, u32[]{:S(2)}, u32[]{:S(2)}) collective-permute-start(bf16[2,1152]{1,0:T(2,128)(2,1)} %text_hbm.1), channel_id=1, source_target_pairs={{0,2},{2,0},{4,6},{6,4},{8,10},{10,8},{12,14},{14,12},{16,18},{18,... | collective-permute-start | bytes 13832 | tf_op jit(solution)/shard_map/ppermute | solution.py:29
  5.1 3.9 %collective-permute-start.1 = (bf16[8,1536]{1,0:T(8,128)(2,1)S(1)}, bf16[8,1536]{1,0:T(8,128)(2,1)S(1)}, u32[]{:S(2)}, u32[]{:S(2)}) collective-permute-start(bf16[8,1536]{1,0:T(8,128)(2,1)S(1)} %pack_block.1), channel_id=1, source_target_pairs={{0,1},{1,0},{2,3},{3,2},{4,5},{5,4},{6,7},{7,6},{8,9},{9,8},{10,11... | collective-permute-start | bytes 73736 | tf_op jit(solution)/shard_map/ppermute | solution.py:29
  9.1 8.1 %collective-permute-start.5 = (bf16[8,1152]{1,0:T(8,128)(2,1)S(1)}, bf16[8,1152]{1,0:T(8,128)(2,1)S(1)}, u32[]{:S(2)}, u32[]{:S(2)}) collective-permute-start(bf16[8,1152]{1,0:T(8,128)(2,1)S(1)} %text_stack.1.refs_6_.low_ref), channel_id=1, source_target_pairs={{0,16},{2,18},{4,20},{6,22},{8,24},{10,26},{12,28},{14,30},{16,0},... | collective-permute-start | bytes 55304 | tf_op jit(solution)/shard_map/ppermute | solution.py:29
  15.6 3.7 %collective-permute-start.3 = (bf16[2,1536]{1,0:T(2,128)(2,1)S(1)}, bf16[2,1536]{1,0:T(2,128)(2,1)S(1)}, u32[]{:S(2)}, u32[]{:S(2)}) collective-permute-start(bf16[2,1536]{1,0:T(2,128)(2,1)S(1)} %get-tuple-element.51), channel_id=1, source_target_pairs={{0,1},{1,0},{2,3},{3,2},{4,5},{5,4},{6,7},{7,6},{8,9},{9,8},{10,11... | collective-permute-start | bytes 18440 | tf_op jit(solution)/shard_map/ppermute | solution.py:29
  17.2 4.2 %collective-permute-start.6 = (bf16[16,1152]{1,0:T(8,128)(2,1)S(1)}, bf16[16,1152]{1,0:T(8,128)(2,1)S(1)}, u32[]{:S(2)}, u32[]{:S(2)}) collective-permute-start(bf16[16,1152]{1,0:T(8,128)(2,1)S(1)} %stack_rows.5.low_ref), channel_id=1, source_target_pairs={{0,8},{2,10},{4,12},{6,14},{8,0},{10,2},{12,4},{14,6},{16,24},{18,... | collective-permute-start | bytes 110600 | tf_op jit(solution)/shard_map/ppermute | solution.py:29
  19.8 3.8 %collective-permute-start.4 = (f32[4,1152]{1,0:T(4,128)S(1)}, f32[4,1152]{1,0:T(4,128)S(1)}, u32[]{:S(2)}, u32[]{:S(2)}) collective-permute-start(f32[4,1152]{1,0:T(4,128)S(1)} %get-tuple-element.53.refs_0_.order_ref), channel_id=1, source_target_pairs={{0,1},{1,0},{2,3},{3,2},{4,5},{5,4},{6,7},{7,6},{8,9},{9,8},{10,11... | collective-permute-start | bytes 55304 | tf_op jit(solution)/shard_map/ppermute | solution.py:29
  21.4 4.4 %collective-permute-start.7 = (bf16[32,1152]{1,0:T(8,128)(2,1)S(1)}, bf16[32,1152]{1,0:T(8,128)(2,1)S(1)}, u32[]{:S(2)}, u32[]{:S(2)}) collective-permute-start(bf16[32,1152]{1,0:T(8,128)(2,1)S(1)} %stack_rows.6.refs_1_), channel_id=1, source_target_pairs={{0,4},{2,6},{4,0},{6,2},{8,12},{10,14},{12,8},{14,10},{16,20},{18,... | collective-permute-start | bytes 221192 | tf_op jit(solution)/shard_map/ppermute | solution.py:29
  27.3 3.7 %collective-permute-start.9 = (f32[2,1536]{1,0:T(2,128)S(1)}, f32[2,1536]{1,0:T(2,128)S(1)}, u32[]{:S(2)}, u32[]{:S(2)}) collective-permute-start(f32[2,1536]{1,0:T(2,128)S(1)} %get-tuple-element.58), channel_id=1, source_target_pairs={{0,1},{1,0},{2,3},{3,2},{4,5},{5,4},{6,7},{7,6},{8,9},{9,8},{10,11... | collective-permute-start | bytes 36872 | tf_op jit(solution)/shard_map/ppermute | solution.py:29
  27.8 3.9 %collective-permute-start.8 = (bf16[4,3840]{1,0:T(4,128)(2,1)S(1)}, bf16[4,3840]{1,0:T(4,128)(2,1)S(1)}, u32[]{:S(2)}, u32[]{:S(2)}) collective-permute-start(bf16[4,3840]{1,0:T(4,128)(2,1)S(1)} %get-tuple-element.56.low_ref), channel_id=1, source_target_pairs={{0,8},{2,10},{4,12},{6,14},{8,0},{10,2},{12,4},{14,6},{16,24},{18,... | collective-permute-start | bytes 92168 | tf_op jit(solution)/shard_map/ppermute | solution.py:29
  34.4 3.3 %collective-permute-start.11 = (bf16[1,32,1536]{2,1,0:T(8,128)(2,1)S(1)}, bf16[1,32,1536]{2,1,0:T(8,128)(2,1)S(1)}, u32[]{:S(2)}, u32[]{:S(2)}) collective-permute-start(bf16[1,32,1536]{2,1,0:T(8,128)(2,1)S(1)} %get-tuple-element.73), channel_id=1, source_target_pairs={{0,2},{2,0},{4,6},{6,4},{8,10},{10,8},{12,14},{14,12},{16,18},{18,... | collective-permute-start | bytes 294920 | tf_op jit(solution)/shard_map/ppermute | solution.py:29
  37.2 4.4 %collective-permute-start.10 = (bf16[1,32,1536]{2,1,0:T(8,128)(2,1)S(1)}, bf16[1,32,1536]{2,1,0:T(8,128)(2,1)S(1)}, u32[]{:S(2)}, u32[]{:S(2)}) collective-permute-start(bf16[1,32,1536]{2,1,0:T(8,128)(2,1)S(1)} %get-tuple-element.72), channel_id=1, source_target_pairs={{0,2},{2,0},{4,6},{6,4},{8,10},{10,8},{12,14},{14,12},{16,18},{18,... | collective-permute-start | bytes 294920 | tf_op jit(solution)/shard_map/ppermute | solution.py:29
  37.8 4.8 %collective-permute-start.12 = (bf16[32,1536]{1,0:T(8,128)(2,1)S(1)}, bf16[32,1536]{1,0:T(8,128)(2,1)S(1)}, u32[]{:S(2)}, u32[]{:S(2)}) collective-permute-start(bf16[32,1536]{1,0:T(8,128)(2,1)S(1)} %chip_sums.2.order_ref.refs_6_), channel_id=1, source_target_pairs={{0,1},{1,0},{2,3},{3,2},{4,5},{5,4},{6,7},{7,6},{8,9},{9,8},{10,11... | collective-permute-start | bytes 294920 | tf_op jit(solution)/shard_map/ppermute | solution.py:29
  41.2 5.6 %collective-permute-start.16 = (bf16[8,3840]{1,0:T(8,128)(2,1)S(1)}, bf16[8,3840]{1,0:T(8,128)(2,1)S(1)}, u32[]{:S(2)}, u32[]{:S(2)}) collective-permute-start(bf16[8,3840]{1,0:T(8,128)(2,1)S(1)} %hold.1.low_ref), channel_id=1, source_target_pairs={{0,16},{2,18},{4,20},{6,22},{8,24},{10,26},{12,28},{14,30},{16,0},... | collective-permute-start | bytes 184328 | tf_op jit(solution)/shard_map/ppermute | solution.py:29
  42.6 5.8 %collective-permute-start.13 = (bf16[32,1536]{1,0:T(8,128)(2,1)S(1)}, bf16[32,1536]{1,0:T(8,128)(2,1)S(1)}, u32[]{:S(2)}, u32[]{:S(2)}) collective-permute-start(bf16[32,1536]{1,0:T(8,128)(2,1)S(1)} %add_all.4.refs_6_.refs_0_), channel_id=1, source_target_pairs={{0,4},{2,6},{4,0},{6,2},{8,12},{10,14},{12,8},{14,10},{16,20},{18,... | collective-permute-start | bytes 294920 | tf_op jit(solution)/shard_map/ppermute | solution.py:29
  46.9 6.3 %collective-permute-start.17 = (bf16[16,3840]{1,0:T(8,128)(2,1)S(1)}, bf16[16,3840]{1,0:T(8,128)(2,1)S(1)}, u32[]{:S(2)}, u32[]{:S(2)}) collective-permute-start(bf16[16,3840]{1,0:T(8,128)(2,1)S(1)} %stack_rows.8.low_ref), channel_id=1, source_target_pairs={{0,4},{2,6},{4,0},{6,2},{8,12},{10,14},{12,8},{14,10},{16,20},{18,... | collective-permute-start | bytes 368648 | tf_op jit(solution)/shard_map/ppermute | solution.py:29
  48.4 4.7 %collective-permute-start.14 = (bf16[32,1536]{1,0:T(8,128)(2,1)S(1)}, bf16[32,1536]{1,0:T(8,128)(2,1)S(1)}, u32[]{:S(2)}, u32[]{:S(2)}) collective-permute-start(bf16[32,1536]{1,0:T(8,128)(2,1)S(1)} %add_all.5.refs_6_.refs_0_), channel_id=1, source_target_pairs={{0,8},{2,10},{4,12},{6,14},{8,0},{10,2},{12,4},{14,6},{16,24},{18,... | collective-permute-start | bytes 294920 | tf_op jit(solution)/shard_map/ppermute | solution.py:29
  53.2 1.6 %collective-permute-start.18 = (bf16[32,3840]{1,0:T(8,128)(2,1)S(1)}, bf16[32,3840]{1,0:T(8,128)(2,1)S(1)}, u32[]{:S(2)}, u32[]{:S(2)}) collective-permute-start(bf16[32,3840]{1,0:T(8,128)(2,1)S(1)} %stack_rows.9.refs_0_), channel_id=1, source_target_pairs={{0,2},{2,0},{4,6},{6,4},{8,10},{10,8},{12,14},{14,12},{16,18},{18,... | collective-permute-start | bytes 737288 | tf_op jit(solution)/shard_map/ppermute | solution.py:29
  53.2 8.2 %collective-permute-start.15 = (bf16[32,1536]{1,0:T(8,128)(2,1)S(1)}, bf16[32,1536]{1,0:T(8,128)(2,1)S(1)}, u32[]{:S(2)}, u32[]{:S(2)}) collective-permute-start(bf16[32,1536]{1,0:T(8,128)(2,1)S(1)} %add_all.6.order_ref.refs_3_.refs_0_), channel_id=1, source_target_pairs={{0,16},{2,18},{4,20},{6,22},{8,24},{10,26},{12,28},{14,30},{16,0},... | collective-permute-start | bytes 294920 | tf_op jit(solution)/shard_map/ppermute | solution.py:29
  61.5 1.4 %collective-permute-start.19 = (bf16[32,1536]{1,0:T(8,128)(2,1)S(1)}, bf16[32,1536]{1,0:T(8,128)(2,1)S(1)}, u32[]{:S(2)}, u32[]{:S(2)}) collective-permute-start(bf16[32,1536]{1,0:T(8,128)(2,1)S(1)} %add_all.7.own_ref), channel_id=1, source_target_pairs={{0,2},{2,0},{4,6},{6,4},{8,10},{10,8},{12,14},{14,12},{16,18},{18,... | collective-permute-start | bytes 294920 | tf_op jit(solution)/shard_map/ppermute | solution.py:29

commit v9 on v8

--- a/solution.py
+++ b/solution.py
@@ -981,7 +981,7 @@
 
 def head_grads_block(packed, text_here, share, order):
     rows, width = text_here.shape
-    block = 512 if share % 512 == 0 else LANES
+    block = 768 if share % 768 == 0 else LANES
     return pl.pallas_call(
         lambda *refs: head_grads_kernel(block, *refs),
         grid=(share // block,),

time: 64.3 us -> 64.3 us (level)
  transfers between devices with their start and end apart: 20 -> 20, of which waited for: 10 -> 10; matrix products, arithmetic and copies ran while one was open for 0% -> 0% of each run, Pallas kernels for 38% -> 37%
where the time goes in v9:
time: 64.3 us; the launch traced here: 64.2 us
  Pallas kernels  29.5 us (46%)
  starting transfers between devices  22.3 us (35%)
  waiting for transfers between devices  11.5 us (18%)
  between operations  0.77 us (1%)
    ppermute x20, starting transfers between devices, swap(): lax.ppermute(value, axis, [(source, source ^ mask) for source in range(co...  22.3 us
    ppermute x20, waiting for transfers between devices, swap(): lax.ppermute(value, axis, [(source, source ^ mask) for source in range(co...  11.5 us
    pallas_call x3, Pallas kernels, image_cells(): pl.pallas_call(kernel, grid_spec=pltpu.PrefetchScalarGridSpec(num_scalar_...  7.85 us
    pallas_call x2, Pallas kernels, terms_block(): pl.pallas_call(lambda place_ref, order_ref, *refs: terms_kernel(base, sha...  5.39 us
    pallas_call x1, Pallas kernels, head_grads_block(): pl.pallas_call(lambda *refs: head_grads_kernel(block, *refs), grid=(share...  4.2 us
    pallas_call x1, Pallas kernels, forward_block(): pl.pallas_call(lambda *refs: forward_kernel(members, *refs), out_shape=ou...  3.87 us
    pallas_call x1, Pallas kernels, own_block(): pl.pallas_call(kernel, out_shape=[SHAPE((images, height, width, share), F...  2.55 us
    pallas_call x1, Pallas kernels, loss_block(): pl.pallas_call(lambda *refs: loss_kernel(members, *refs), out_shape=[SHAP...  1.45 us
  transfers between devices with their start and end apart: 20, of which 10 were waited for; matrix products, arithmetic and copies ran while one was open for 0% of the time, Pallas kernels for 37%

profile of v9, /device:TPU:0, one launch (start us, length us, event | category | flops | bytes accessed | tf_op | source)
XLA Modules:
  0.0 64.2 jit_solution(11476464539032080903)
XLA Ops:
  0.6 3.0 %collective-permute-start.2 = (bf16[49,1536]{1,0:T(8,128)(2,1)}, bf16[49,1536]{1,0:T(8,128)(2,1)S(1)}, u32[]{:S(2)}, u32[]{:S(2)}) collective-permute-start(bf16[49,1536]{1,0:T(8,128)(2,1)} %kernel_hbm.1), channel_id=1, source_target_pairs={{0,1},{1,0},{2,3},{3,2},{4,5},{5,4},{6,7},{7,6},{8,9},{9,8},{10,11... | collective-permute-start | bytes 451592 | tf_op jit(solution)/shard_map/ppermute | solution.py:29
  3.7 1.3 %load_block.1 = (bf16[2,8,8,3072]{3,2,1,0:T(8,128)(2,1)S(1)}, f32[56,1536]{1,0:T(8,128)S(1)}, bf16[2,1152]{1,0:T(2,128)(2,1)S(1)}) custom-call(bf16[2,8,8,3072]{3,2,1,0:T(8,128)(2,1)} %x_hbm.1, bf16[49,1536]{1,0:T(8,128)(2,1)} %kernel_hbm.1, bf16[4,1536]{1,0:T(4,128)(2,1)} %term_hbm.1, bf16[2,1152]{1,0:T(2,128)(2,1)} %text_hbm.1), custom_call_target="tpu_custom_call" | custom-call | tf_op jit(solution)/shard_map/load_block/pallas_call | solution.py:285
  5.0 0.1 collective-permute-done.core_ref.refs_1_
  5.1 0.1 collective-permute-start.1
  5.2 0.1 pad_add_fusion.place_ref.refs_0_
  5.3 2.5 %own_block.1 = (f32[2,8,8,1536]{3,2,1,0:T(8,128)S(1)}, f32[2,8,8,128]{3,2,1,0:T(8,128)S(1)}) custom-call(s32[2]{0:T(128)S(1)} %pad_add_fusion.place_ref.refs_0_, bf16[2,8,8,3072]{3,2,1,0:T(8,128)(2,1)S(1)} %get-tuple-element.45.x_ref.refs_2_.refs_0_, f32[56,1536]{1,0:T(8,128)S(1)} %get-tuple-element.46.weight_ref.refs_5_.refs_2_.refs_3_), custom_call_target="tpu_custom_call" | custom-call | tf_op jit(solution)/shard_map/own_block/pallas_call | solution.py:374
  7.8 1.1 %collective-permute-done.1.refs_2_.refs_8_ = bf16[8,1536]{1,0:T(8,128)(2,1)S(1)} collective-permute-done((bf16[8,1536]{1,0:T(8,128)(2,1)S(1)}, bf16[8,1536]{1,0:T(8,128)(2,1)S(1)}, u32[]{:S(2)}, u32[]{:S(2)}) %collective-permute-start.1) | collective-permute-done | bytes 24608 | tf_op jit(solution)/shard_map/ppermute | solution.py:29
  9.0 0.1 text_stack.1.refs_6_.low_ref
  9.1 2.6 %collective-permute-start.5 = (bf16[8,1152]{1,0:T(8,128)(2,1)S(1)}, bf16[8,1152]{1,0:T(8,128)(2,1)S(1)}, u32[]{:S(2)}, u32[]{:S(2)}) collective-permute-start(bf16[8,1152]{1,0:T(8,128)(2,1)S(1)} %text_stack.1.refs_6_.low_ref), channel_id=1, source_target_pairs={{0,16},{2,18},{4,20},{6,22},{8,24},{10,26},{12,28},{14,30},{16,0},... | collective-permute-start | bytes 55304 | tf_op jit(solution)/shard_map/ppermute | solution.py:29
  11.7 0.0 collective-permute-done.2.refs_7_
  11.7 3.9 %forward_block.1 = (bf16[2,1536]{1,0:T(2,128)(2,1)S(1)}, bf16[2,1536]{1,0:T(2,128)(2,1)S(1)}, bf16[1536,1152]{1,0:T(8,128)(2,1)S(1)}, f32[56,1536]{1,0:T(8,128)S...) custom-call(s32[2]{0:T(128)S(1)} %pad_add_fusion.place_ref.refs_0_, ...), custom_call_target="tpu_custom_call" | custom-call | tf_op jit(solution)/shard_map/forward_block/pallas_call | solution.py:484
  15.6 1.6 %collective-permute-start.3 = (bf16[2,1536]{1,0:T(2,128)(2,1)S(1)}, bf16[2,1536]{1,0:T(2,128)(2,1)S(1)}, u32[]{:S(2)}, u32[]{:S(2)}) collective-permute-start(bf16[2,1536]{1,0:T(2,128)(2,1)S(1)} %get-tuple-element.51), channel_id=1, source_target_pairs={{0,1},{1,0},{2,3},{3,2},{4,5},{5,4},{6,7},{7,6},{8,9},{9,8},{10,11... | collective-permute-start | bytes 18440 | tf_op jit(solution)/shard_map/ppermute | solution.py:29
  17.2 1.6 %collective-permute-start.6 = (bf16[16,1152]{1,0:T(8,128)(2,1)S(1)}, bf16[16,1152]{1,0:T(8,128)(2,1)S(1)}, u32[]{:S(2)}, u32[]{:S(2)}) collective-permute-start(bf16[16,1152]{1,0:T(8,128)(2,1)S(1)} %stack_rows.5.low_ref), channel_id=1, source_target_pairs={{0,8},{2,10},{4,12},{6,14},{8,0},{10,2},{12,4},{14,6},{16,24},{18,... | collective-permute-start | bytes 110600 | tf_op jit(solution)/shard_map/ppermute | solution.py:29
  18.8 0.5 collective-permute-done.3.refs_1_
  19.3 0.6 head_project.1
  19.8 1.6 %collective-permute-start.4 = (f32[4,1152]{1,0:T(4,128)S(1)}, f32[4,1152]{1,0:T(4,128)S(1)}, u32[]{:S(2)}, u32[]{:S(2)}) collective-permute-start(f32[4,1152]{1,0:T(4,128)S(1)} %get-tuple-element.53.refs_0_.order_ref), channel_id=1, source_target_pairs={{0,1},{1,0},{2,3},{3,2},{4,5},{5,4},{6,7},{7,6},{8,9},{9,8},{10,11... | collective-permute-start | bytes 55304 | tf_op jit(solution)/shard_map/ppermute | solution.py:29
  21.4 1.6 %collective-permute-start.7 = (bf16[32,1152]{1,0:T(8,128)(2,1)S(1)}, bf16[32,1152]{1,0:T(8,128)(2,1)S(1)}, u32[]{:S(2)}, u32[]{:S(2)}) collective-permute-start(bf16[32,1152]{1,0:T(8,128)(2,1)S(1)} %stack_rows.6.refs_1_), channel_id=1, source_target_pairs={{0,4},{2,6},{4,0},{6,2},{8,12},{10,14},{12,8},{14,10},{16,20},{18,... | collective-permute-start | bytes 221192 | tf_op jit(solution)/shard_map/ppermute | solution.py:29
  23.0 0.7 %collective-permute-done.4.refs_1_ = f32[4,1152]{1,0:T(4,128)S(1)} collective-permute-done((f32[4,1152]{1,0:T(4,128)S(1)}, f32[4,1152]{1,0:T(4,128)S(1)}, u32[]{:S(2)}, u32[]{:S(2)}) %collective-permute-start.4) | collective-permute-done | bytes 18464 | tf_op jit(solution)/shard_map/ppermute | solution.py:29
  23.7 2.2 %collective-permute-done.7.refs_2_ = bf16[32,1152]{1,0:T(8,128)(2,1)S(1)} collective-permute-done((bf16[32,1152]{1,0:T(8,128)(2,1)S(1)}, bf16[32,1152]{1,0:T(8,128)(2,1)S(1)}, u32[]{:S(2)}, u32[]{:S(2)}) %collective-permute-start.7) | collective-permute-done | bytes 73760 | tf_op jit(solution)/shard_map/ppermute | solution.py:29
  25.8 1.5 %loss_block.1 = (bf16[4,3840]{1,0:T(4,128)(2,1)S(1)}, f32[2,1536]{1,0:T(2,128)S(1)}, f32[2,1536]{1,0:T(2,128)S(1)}) custom-call(f32[4,1152]{1,0:T(4,128)S(1)} %embed_sum.1.refs_0_, bf16[32,1152]{1,0:T(8,128)(2,1)S(1)} %stack_rows.6.refs_1_, bf16[32,1152]{1,0:T(8,128)(2,1)S(1)} %collective-permute-done.7.refs_2_, ...), custom_call_target="tpu_custom_call" | custom-call | tf_op jit(solution)/shard_map/loss_block/pallas_call | solution.py:593
  27.3 0.5 collective-permute-start.9
  27.8 1.6 %collective-permute-start.8 = (bf16[4,3840]{1,0:T(4,128)(2,1)S(1)}, bf16[4,3840]{1,0:T(4,128)(2,1)S(1)}, u32[]{:S(2)}, u32[]{:S(2)}) collective-permute-start(bf16[4,3840]{1,0:T(4,128)(2,1)S(1)} %get-tuple-element.56.low_ref), channel_id=1, source_target_pairs={{0,8},{2,10},{4,12},{6,14},{8,0},{10,2},{12,4},{14,6},{16,24},{18,... | collective-permute-start | bytes 92168 | tf_op jit(solution)/shard_map/ppermute | solution.py:29
  29.4 1.6 %collective-permute-done.9.refs_1_ = f32[2,1536]{1,0:T(2,128)S(1)} collective-permute-done((f32[2,1536]{1,0:T(2,128)S(1)}, f32[2,1536]{1,0:T(2,128)S(1)}, u32[]{:S(2)}, u32[]{:S(2)}) %collective-permute-start.9) | collective-permute-done | bytes 12320 | tf_op jit(solution)/shard_map/ppermute | solution.py:29
  31.0 0.3 pool_grad_block.1
  31.3 0.4 dots_block.1.order_ref.refs_6_
  31.7 0.0 collective-permute-done.8.high_ref
  31.7 2.7 %terms_block.2 = (bf16[1,32,1536]{2,1,0:T(8,128)(2,1)S(1)}, bf16[1,32,1536]{2,1,0:T(8,128)(2,1)S(1)}, f32[2,8,8,1536]{3,2,1,0:T(8,128)S(1)}) custom-call(s32[2]{0:T(128)S(1)} %pad_add_fusion.place_ref.refs_0_, bf16[8,3840]{1,0:T(8,128)(2,1)S(1)} %stack_rows.7.order_ref.value_ref, bf16[2,8,8,3072]{3,2,1,0:T(8,128)(2,1)S(1)} %get-tuple-element.45.x_ref.refs_2_.refs_0_, ...), custom_call_target="tpu_custom_call" | custom-call | tf_op jit(solution)/shard_map/terms_block/pallas_call | solution.py:806
  34.4 0.1 collective-permute-start.11
  34.5 2.7 %terms_block.3 = (bf16[1,32,1536]{2,1,0:T(8,128)(2,1)S(1)}, bf16[1,32,1536]{2,1,0:T(8,128)(2,1)S(1)}, f32[2,8,8,1536]{3,2,1,0:T(8,128)S(1)}) custom-call(s32[2]{0:T(128)S(1)} %pad_add_fusion.place_ref.refs_0_, bf16[1,32,1536]{2,1,0:T(8,128)(2,1)S(1)} %get-tuple-element.67.order_ref.keep_ref, ...), custom_call_target="tpu_custom_call" | custom-call | tf_op jit(solution)/shard_map/terms_block/pallas_call | solution.py:806
  37.2 0.6 collective-permute-start.10
  37.8 1.6 %collective-permute-start.12 = (bf16[32,1536]{1,0:T(8,128)(2,1)S(1)}, bf16[32,1536]{1,0:T(8,128)(2,1)S(1)}, u32[]{:S(2)}, u32[]{:S(2)}) collective-permute-start(bf16[32,1536]{1,0:T(8,128)(2,1)S(1)} %chip_sums.2.order_ref.refs_6_), channel_id=1, source_target_pairs={{0,1},{1,0},{2,3},{3,2},{4,5},{5,4},{6,7},{7,6},{8,9},{9,8},{10,11... | collective-permute-start | bytes 294920 | tf_op jit(solution)/shard_map/ppermute | solution.py:29
  39.4 1.8 %image_cells.3 = (bf16[2,8,8,3072]{3,2,1,0:T(8,128)(2,1)}, f32[8,128]{1,0:T(8,128)S(1)}) custom-call(s32[2]{0:T(128)S(1)} %pad_add_fusion.place_ref.refs_0_, f32[2,8,8,1536]{3,2,1,0:T(8,128)S(1)} %get-tuple-element.68.refs_1_, f32[2,8,8,1536]{3,2,1,0:T(8,128)S(1)} %get-tuple-element.69.refs_2_, ...), custom_call_target="tpu_custom_call" | custom-call | flops 1650000000 | tf_op jit(solution)/shard_map/image_cells/pallas_call | solution.py:932
  41.2 0.3 collective-permute-start.16
  41.6 1.0 %collective-permute-done.12.refs_1_ = bf16[32,1536]{1,0:T(8,128)(2,1)S(1)} collective-permute-done((bf16[32,1536]{1,0:T(8,128)(2,1)S(1)}, bf16[32,1536]{1,0:T(8,128)(2,1)S(1)}, u32[]{:S(2)}, u32[]{:S(2)}) %collective-permute-start.12) | collective-permute-done | bytes 98336 | tf_op jit(solution)/shard_map/ppermute | solution.py:29
  42.6 1.6 %collective-permute-start.13 = (bf16[32,1536]{1,0:T(8,128)(2,1)S(1)}, bf16[32,1536]{1,0:T(8,128)(2,1)S(1)}, u32[]{:S(2)}, u32[]{:S(2)}) collective-permute-start(bf16[32,1536]{1,0:T(8,128)(2,1)S(1)} %add_all.4.refs_6_.refs_0_), channel_id=1, source_target_pairs={{0,4},{2,6},{4,0},{6,2},{8,12},{10,14},{12,8},{14,10},{16,20},{18,... | collective-permute-start | bytes 294920 | tf_op jit(solution)/shard_map/ppermute | solution.py:29
  44.2 2.7 %image_cells.4 = (bf16[2,8,8,3072]{3,2,1,0:T(8,128)(2,1)}, f32[8,128]{1,0:T(8,128)S(1)}) custom-call(s32[2]{0:T(128)S(1)} %pad_add_fusion.place_ref.refs_0_, f32[2,8,8,1536]{3,2,1,0:T(8,128)S(1)} %get-tuple-element.68.refs_1_, f32[2,8,8,1536]{3,2,1,0:T(8,128)S(1)} %get-tuple-element.69.refs_2_, ...), custom_call_target="tpu_custom_call", output_to_operand_aliasing={{0}: (7, {})} | custom-call | flops 1650000000 | tf_op jit(solution)/shard_map/image_cells/pallas_call | solution.py:932
  46.9 1.5 %collective-permute-start.17 = (bf16[16,3840]{1,0:T(8,128)(2,1)S(1)}, bf16[16,3840]{1,0:T(8,128)(2,1)S(1)}, u32[]{:S(2)}, u32[]{:S(2)}) collective-permute-start(bf16[16,3840]{1,0:T(8,128)(2,1)S(1)} %stack_rows.8.low_ref), channel_id=1, source_target_pairs={{0,4},{2,6},{4,0},{6,2},{8,12},{10,14},{12,8},{14,10},{16,20},{18,... | collective-permute-start | bytes 368648 | tf_op jit(solution)/shard_map/ppermute | solution.py:29
  48.4 1.3 %collective-permute-start.14 = (bf16[32,1536]{1,0:T(8,128)(2,1)S(1)}, bf16[32,1536]{1,0:T(8,128)(2,1)S(1)}, u32[]{:S(2)}, u32[]{:S(2)}) collective-permute-start(bf16[32,1536]{1,0:T(8,128)(2,1)S(1)} %add_all.5.refs_6_.refs_0_), channel_id=1, source_target_pairs={{0,8},{2,10},{4,12},{6,14},{8,0},{10,2},{12,4},{14,6},{16,24},{18,... | collective-permute-start | bytes 294920 | tf_op jit(solution)/shard_map/ppermute | solution.py:29
  49.7 3.4 %image_cells.5 = (bf16[2,8,8,3072]{3,2,1,0:T(8,128)(2,1)}, f32[8,128]{1,0:T(8,128)S(1)}) custom-call(s32[2]{0:T(128)S(1)} %pad_add_fusion.place_ref.refs_0_, f32[2,8,8,1536]{3,2,1,0:T(8,128)S(1)} %get-tuple-element.68.refs_1_, f32[2,8,8,1536]{3,2,1,0:T(8,128)S(1)} %get-tuple-element.69.refs_2_, ...), custom_call_target="tpu_custom_call", output_to_operand_aliasing={{0}: (7, {})} | custom-call | flops 1650000000 | tf_op jit(solution)/shard_map/image_cells/pallas_call | solution.py:932
  53.1 0.0 collective-permute-done.14.refs_1_
  53.2 0.1 collective-permute-start.18
  53.2 1.1 %collective-permute-start.15 = (bf16[32,1536]{1,0:T(8,128)(2,1)S(1)}, bf16[32,1536]{1,0:T(8,128)(2,1)S(1)}, u32[]{:S(2)}, u32[]{:S(2)}) collective-permute-start(bf16[32,1536]{1,0:T(8,128)(2,1)S(1)} %add_all.6.order_ref.refs_3_.refs_0_), channel_id=1, source_target_pairs={{0,16},{2,18},{4,20},{6,22},{8,24},{10,26},{12,28},{14,30},{16,0},... | collective-permute-start | bytes 294920 | tf_op jit(solution)/shard_map/ppermute | solution.py:29
  54.3 0.4 collective-permute-done.18.refs_1_
  54.7 4.2 %head_grads_block.1 = (f32[1536,1152]{1,0:T(8,128)}, f32[2,1152]{1,0:T(2,128)}, f32[8,128]{1,0:T(8,128)S(1)}) custom-call(bf16[32,3840]{1,0:T(8,128)(2,1)S(1)} %stack_rows.9.refs_0_, bf16[32,3840]{1,0:T(8,128)(2,1)S(1)} %collective-permute-done.18.refs_1_, bf16[2,1152]{1,0:T(2,128)(2,1)S(1)} %get-tuple-element.49.here_ref.refs_0_.refs_2_, ...), custom_call_target="tpu_custom_call" | custom-call | tf_op jit(solution)/shard_map/head_grads_block/pallas_call | solution.py:985
  58.9 2.5 %collective-permute-done.15.refs_1_ = bf16[32,1536]{1,0:T(8,128)(2,1)S(1)} collective-permute-done((bf16[32,1536]{1,0:T(8,128)(2,1)S(1)}, bf16[32,1536]{1,0:T(8,128)(2,1)S(1)}, u32[]{:S(2)}, u32[]{:S(2)}) %collective-permute-start.15) | collective-permute-done | bytes 98336 | tf_op jit(solution)/shard_map/ppermute | solution.py:29
  61.5 0.1 collective-permute-start.19
  61.6 1.3 %collective-permute-done.19.other_ref = bf16[32,1536]{1,0:T(8,128)(2,1)S(1)} collective-permute-done((bf16[32,1536]{1,0:T(8,128)(2,1)S(1)}, bf16[32,1536]{1,0:T(8,128)(2,1)S(1)}, u32[]{:S(2)}, u32[]{:S(2)}) %collective-permute-start.19) | collective-permute-done | bytes 98336 | tf_op jit(solution)/shard_map/ppermute | solution.py:29
  62.9 1.3 %split_block.1 = (f32[49,1536]{1,0:T(8,128)}, f32[4,1536]{1,0:T(4,128)}) custom-call(s32[2]{0:T(128)S(1)} %pad_add_fusion.place_ref.refs_0_, bf16[32,1536]{1,0:T(8,128)(2,1)S(1)} %add_all.7.own_ref, bf16[32,1536]{1,0:T(8,128)(2,1)S(1)} %collective-permute-done.19.other_ref), custom_call_target="tpu_custom_call" | custom-call | tf_op jit(solution)/shard_map/split_block/pallas_call | solution.py:1026
  (22 shorter events, 0.3 us)
Async XLA Ops:
  0.6 11.1 %collective-permute-start.2 = (bf16[49,1536]{1,0:T(8,128)(2,1)}, bf16[49,1536]{1,0:T(8,128)(2,1)S(1)}, u32[]{:S(2)}, u32[]{:S(2)}) collective-permute-start(bf16[49,1536]{1,0:T(8,128)(2,1)} %kernel_hbm.1), channel_id=1, source_target_pairs={{0,1},{1,0},{2,3},{3,2},{4,5},{5,4},{6,7},{7,6},{8,9},{9,8},{10,11... | collective-permute-start | bytes 451592 | tf_op jit(solution)/shard_map/ppermute | solution.py:29
  3.7 1.4 %collective-permute-start = (bf16[2,1152]{1,0:T(2,128)(2,1)}, bf16[2,1152]{1,0:T(2,128)(2,1)S(1)}, u32[]{:S(2)}, u32[]{:S(2)}) collective-permute-start(bf16[2,1152]{1,0:T(2,128)(2,1)} %text_hbm.1), channel_id=1, source_target_pairs={{0,2},{2,0},{4,6},{6,4},{8,10},{10,8},{12,14},{14,12},{16,18},{18,... | collective-permute-start | bytes 13832 | tf_op jit(solution)/shard_map/ppermute | solution.py:29
  5.1 3.9 %collective-permute-start.1 = (bf16[8,1536]{1,0:T(8,128)(2,1)S(1)}, bf16[8,1536]{1,0:T(8,128)(2,1)S(1)}, u32[]{:S(2)}, u32[]{:S(2)}) collective-permute-start(bf16[8,1536]{1,0:T(8,128)(2,1)S(1)} %pack_block.1), channel_id=1, source_target_pairs={{0,1},{1,0},{2,3},{3,2},{4,5},{5,4},{6,7},{7,6},{8,9},{9,8},{10,11... | collective-permute-start | bytes 73736 | tf_op jit(solution)/shard_map/ppermute | solution.py:29
  9.1 8.1 %collective-permute-start.5 = (bf16[8,1152]{1,0:T(8,128)(2,1)S(1)}, bf16[8,1152]{1,0:T(8,128)(2,1)S(1)}, u32[]{:S(2)}, u32[]{:S(2)}) collective-permute-start(bf16[8,1152]{1,0:T(8,128)(2,1)S(1)} %text_stack.1.refs_6_.low_ref), channel_id=1, source_target_pairs={{0,16},{2,18},{4,20},{6,22},{8,24},{10,26},{12,28},{14,30},{16,0},... | collective-permute-start | bytes 55304 | tf_op jit(solution)/shard_map/ppermute | solution.py:29
  15.6 3.7 %collective-permute-start.3 = (bf16[2,1536]{1,0:T(2,128)(2,1)S(1)}, bf16[2,1536]{1,0:T(2,128)(2,1)S(1)}, u32[]{:S(2)}, u32[]{:S(2)}) collective-permute-start(bf16[2,1536]{1,0:T(2,128)(2,1)S(1)} %get-tuple-element.51), channel_id=1, source_target_pairs={{0,1},{1,0},{2,3},{3,2},{4,5},{5,4},{6,7},{7,6},{8,9},{9,8},{10,11... | collective-permute-start | bytes 18440 | tf_op jit(solution)/shard_map/ppermute | solution.py:29
  17.2 4.2 %collective-permute-start.6 = (bf16[16,1152]{1,0:T(8,128)(2,1)S(1)}, bf16[16,1152]{1,0:T(8,128)(2,1)S(1)}, u32[]{:S(2)}, u32[]{:S(2)}) collective-permute-start(bf16[16,1152]{1,0:T(8,128)(2,1)S(1)} %stack_rows.5.low_ref), channel_id=1, source_target_pairs={{0,8},{2,10},{4,12},{6,14},{8,0},{10,2},{12,4},{14,6},{16,24},{18,... | collective-permute-start | bytes 110600 | tf_op jit(solution)/shard_map/ppermute | solution.py:29
  19.8 3.8 %collective-permute-start.4 = (f32[4,1152]{1,0:T(4,128)S(1)}, f32[4,1152]{1,0:T(4,128)S(1)}, u32[]{:S(2)}, u32[]{:S(2)}) collective-permute-start(f32[4,1152]{1,0:T(4,128)S(1)} %get-tuple-element.53.refs_0_.order_ref), channel_id=1, source_target_pairs={{0,1},{1,0},{2,3},{3,2},{4,5},{5,4},{6,7},{7,6},{8,9},{9,8},{10,11... | collective-permute-start | bytes 55304 | tf_op jit(solution)/shard_map/ppermute | solution.py:29
  21.4 4.4 %collective-permute-start.7 = (bf16[32,1152]{1,0:T(8,128)(2,1)S(1)}, bf16[32,1152]{1,0:T(8,128)(2,1)S(1)}, u32[]{:S(2)}, u32[]{:S(2)}) collective-permute-start(bf16[32,1152]{1,0:T(8,128)(2,1)S(1)} %stack_rows.6.refs_1_), channel_id=1, source_target_pairs={{0,4},{2,6},{4,0},{6,2},{8,12},{10,14},{12,8},{14,10},{16,20},{18,... | collective-permute-start | bytes 221192 | tf_op jit(solution)/shard_map/ppermute | solution.py:29
  27.3 3.7 %collective-permute-start.9 = (f32[2,1536]{1,0:T(2,128)S(1)}, f32[2,1536]{1,0:T(2,128)S(1)}, u32[]{:S(2)}, u32[]{:S(2)}) collective-permute-start(f32[2,1536]{1,0:T(2,128)S(1)} %get-tuple-element.58), channel_id=1, source_target_pairs={{0,1},{1,0},{2,3},{3,2},{4,5},{5,4},{6,7},{7,6},{8,9},{9,8},{10,11... | collective-permute-start | bytes 36872 | tf_op jit(solution)/shard_map/ppermute | solution.py:29
  27.8 3.9 %collective-permute-start.8 = (bf16[4,3840]{1,0:T(4,128)(2,1)S(1)}, bf16[4,3840]{1,0:T(4,128)(2,1)S(1)}, u32[]{:S(2)}, u32[]{:S(2)}) collective-permute-start(bf16[4,3840]{1,0:T(4,128)(2,1)S(1)} %get-tuple-element.56.low_ref), channel_id=1, source_target_pairs={{0,8},{2,10},{4,12},{6,14},{8,0},{10,2},{12,4},{14,6},{16,24},{18,... | collective-permute-start | bytes 92168 | tf_op jit(solution)/shard_map/ppermute | solution.py:29
  34.4 3.3 %collective-permute-start.11 = (bf16[1,32,1536]{2,1,0:T(8,128)(2,1)S(1)}, bf16[1,32,1536]{2,1,0:T(8,128)(2,1)S(1)}, u32[]{:S(2)}, u32[]{:S(2)}) collective-permute-start(bf16[1,32,1536]{2,1,0:T(8,128)(2,1)S(1)} %get-tuple-element.73), channel_id=1, source_target_pairs={{0,2},{2,0},{4,6},{6,4},{8,10},{10,8},{12,14},{14,12},{16,18},{18,... | collective-permute-start | bytes 294920 | tf_op jit(solution)/shard_map/ppermute | solution.py:29
  37.2 4.4 %collective-permute-start.10 = (bf16[1,32,1536]{2,1,0:T(8,128)(2,1)S(1)}, bf16[1,32,1536]{2,1,0:T(8,128)(2,1)S(1)}, u32[]{:S(2)}, u32[]{:S(2)}) collective-permute-start(bf16[1,32,1536]{2,1,0:T(8,128)(2,1)S(1)} %get-tuple-element.72), channel_id=1, source_target_pairs={{0,2},{2,0},{4,6},{6,4},{8,10},{10,8},{12,14},{14,12},{16,18},{18,... | collective-permute-start | bytes 294920 | tf_op jit(solution)/shard_map/ppermute | solution.py:29
  37.8 4.8 %collective-permute-start.12 = (bf16[32,1536]{1,0:T(8,128)(2,1)S(1)}, bf16[32,1536]{1,0:T(8,128)(2,1)S(1)}, u32[]{:S(2)}, u32[]{:S(2)}) collective-permute-start(bf16[32,1536]{1,0:T(8,128)(2,1)S(1)} %chip_sums.2.order_ref.refs_6_), channel_id=1, source_target_pairs={{0,1},{1,0},{2,3},{3,2},{4,5},{5,4},{6,7},{7,6},{8,9},{9,8},{10,11... | collective-permute-start | bytes 294920 | tf_op jit(solution)/shard_map/ppermute | solution.py:29
  41.2 5.6 %collective-permute-start.16 = (bf16[8,3840]{1,0:T(8,128)(2,1)S(1)}, bf16[8,3840]{1,0:T(8,128)(2,1)S(1)}, u32[]{:S(2)}, u32[]{:S(2)}) collective-permute-start(bf16[8,3840]{1,0:T(8,128)(2,1)S(1)} %hold.1.low_ref), channel_id=1, source_target_pairs={{0,16},{2,18},{4,20},{6,22},{8,24},{10,26},{12,28},{14,30},{16,0},... | collective-permute-start | bytes 184328 | tf_op jit(solution)/shard_map/ppermute | solution.py:29
  42.6 5.8 %collective-permute-start.13 = (bf16[32,1536]{1,0:T(8,128)(2,1)S(1)}, bf16[32,1536]{1,0:T(8,128)(2,1)S(1)}, u32[]{:S(2)}, u32[]{:S(2)}) collective-permute-start(bf16[32,1536]{1,0:T(8,128)(2,1)S(1)} %add_all.4.refs_6_.refs_0_), channel_id=1, source_target_pairs={{0,4},{2,6},{4,0},{6,2},{8,12},{10,14},{12,8},{14,10},{16,20},{18,... | collective-permute-start | bytes 294920 | tf_op jit(solution)/shard_map/ppermute | solution.py:29
  46.9 6.3 %collective-permute-start.17 = (bf16[16,3840]{1,0:T(8,128)(2,1)S(1)}, bf16[16,3840]{1,0:T(8,128)(2,1)S(1)}, u32[]{:S(2)}, u32[]{:S(2)}) collective-permute-start(bf16[16,3840]{1,0:T(8,128)(2,1)S(1)} %stack_rows.8.low_ref), channel_id=1, source_target_pairs={{0,4},{2,6},{4,0},{6,2},{8,12},{10,14},{12,8},{14,10},{16,20},{18,... | collective-permute-start | bytes 368648 | tf_op jit(solution)/shard_map/ppermute | solution.py:29
  48.4 4.7 %collective-permute-start.14 = (bf16[32,1536]{1,0:T(8,128)(2,1)S(1)}, bf16[32,1536]{1,0:T(8,128)(2,1)S(1)}, u32[]{:S(2)}, u32[]{:S(2)}) collective-permute-start(bf16[32,1536]{1,0:T(8,128)(2,1)S(1)} %add_all.5.refs_6_.refs_0_), channel_id=1, source_target_pairs={{0,8},{2,10},{4,12},{6,14},{8,0},{10,2},{12,4},{14,6},{16,24},{18,... | collective-permute-start | bytes 294920 | tf_op jit(solution)/shard_map/ppermute | solution.py:29
  53.2 1.6 %collective-permute-start.18 = (bf16[32,3840]{1,0:T(8,128)(2,1)S(1)}, bf16[32,3840]{1,0:T(8,128)(2,1)S(1)}, u32[]{:S(2)}, u32[]{:S(2)}) collective-permute-start(bf16[32,3840]{1,0:T(8,128)(2,1)S(1)} %stack_rows.9.refs_0_), channel_id=1, source_target_pairs={{0,2},{2,0},{4,6},{6,4},{8,10},{10,8},{12,14},{14,12},{16,18},{18,... | collective-permute-start | bytes 737288 | tf_op jit(solution)/shard_map/ppermute | solution.py:29
  53.2 8.2 %collective-permute-start.15 = (bf16[32,1536]{1,0:T(8,128)(2,1)S(1)}, bf16[32,1536]{1,0:T(8,128)(2,1)S(1)}, u32[]{:S(2)}, u32[]{:S(2)}) collective-permute-start(bf16[32,1536]{1,0:T(8,128)(2,1)S(1)} %add_all.6.order_ref.refs_3_.refs_0_), channel_id=1, source_target_pairs={{0,16},{2,18},{4,20},{6,22},{8,24},{10,26},{12,28},{14,30},{16,0},... | collective-permute-start | bytes 294920 | tf_op jit(solution)/shard_map/ppermute | solution.py:29
  61.5 1.4 %collective-permute-start.19 = (bf16[32,1536]{1,0:T(8,128)(2,1)S(1)}, bf16[32,1536]{1,0:T(8,128)(2,1)S(1)}, u32[]{:S(2)}, u32[]{:S(2)}) collective-permute-start(bf16[32,1536]{1,0:T(8,128)(2,1)S(1)} %add_all.7.own_ref), channel_id=1, source_target_pairs={{0,2},{2,0},{4,6},{6,4},{8,10},{10,8},{12,14},{14,12},{16,18},{18,... | collective-permute-start | bytes 294920 | tf_op jit(solution)/shard_map/ppermute | solution.py:29
